TPU v7x, 32 devices: a whole 2x2x4 slice. The times are simulated.
32 devices in a mesh: expert: 8 (over y, x, core), fsdp: 4 (over z).
Axes of the slice: x: 2, y: 2, z: 4, core: 2. Of those that a mesh axis runs over, the one named last changes fastest.
Arguments:
- tokens: bfloat16 [1024, 7168], P('expert', 'fsdp'), may hold values from -6 to 6
- counts: int32 [8, 4], P('expert'), may hold values from 1 to 64, as said below
- gate_values: bfloat16 [8, 7168, 1024], P('expert', 'fsdp'), may hold values from -0.0625 to 0.0625
- up_values: bfloat16 [8, 7168, 1024], P('expert', 'fsdp'), may hold values from -0.0625 to 0.0625
- gate_scales: float32 [8, 56, 8], P('expert'), may hold values from 0.5 to 2
- up_scales: float32 [8, 56, 8], P('expert'), may hold values from 0.5 to 2
- grad_hidden: bfloat16 [8, 512, 1024], P('expert', 'fsdp'), may hold values from -6 to 6
Outputs:
- hidden: bfloat16 [8, 512, 1024], P('expert', 'fsdp')
- grad_gate: bfloat16 [8, 7168, 1024], P('expert', 'fsdp')
- grad_up: bfloat16 [8, 7168, 1024], P('expert', 'fsdp')
- grad_tokens: bfloat16 [1024, 7168], P('expert', 'fsdp')
Inputs may be any that keep to these rules, and one draw needn't show every extreme that they name: Each row of counts sums to 128. In every draw one expert, drawn from the seed, receives exactly 64 rows from every source index.
All inputs are finite; a program needn't handle non-finite values.
Results may differ from a plain program's by a relative error of at most 0.025.
Values may be sent and summed in bfloat16 or wider, within the bound.
No kernel may reach another device: no remote copies, remote signals or barrier semaphores. Data moves between devices by JAX's collectives and lax.ppermute only.
A program may use at most 64 MiB of HBM per device.

v0:
```python
import math

import jax
import jax.numpy as jnp
from jax import lax
from jax.experimental import pallas as pl
from jax.experimental.pallas import tpu as pltpu
from jax.sharding import PartitionSpec as P


def swap(value, axis, mask):
    pairs = [(source, source ^ mask) for source in range(lax.axis_size(axis))]
    return lax.ppermute(value, axis, pairs)


def pick(blocks, index):
    return lax.dynamic_index_in_dim(blocks, index, 0, keepdims=False)


def scale_kernel(
    sub,
    start_ref,
    gate_ref,
    up_ref,
    gate_scale_ref,
    up_scale_ref,
    out_ref,
    gate_held,
    up_held,
    gate_rows,
    up_rows,
    sems,
):
    rows = out_ref.shape[0]
    half_units = gate_held.shape[1]
    step = pl.program_id(0)

    def arrival(which, turn):
        here = pl.ds(pl.multiple_of(turn * rows, rows), rows)
        value_ref, held = ((gate_ref, gate_held), (up_ref, up_held))[which]
        return pltpu.make_async_copy(
            value_ref.at[0, here, :], held.at[here, :], sems.at[which, turn]
        )

    @pl.when(step == 0)
    def _():
        for turn in range(gate_held.shape[0] // rows):
            for which in range(2):
                arrival(which, turn).start()
        shape = (gate_scale_ref.shape[1], half_units)
        spread = (
            lax.broadcasted_iota(jnp.int32, shape, 0)
            == lax.broadcasted_iota(jnp.int32, shape, 1) // 128
        ).astype(jnp.float32)
        for scale_ref, grown in ((gate_scale_ref, gate_rows), (up_scale_ref, up_rows)):
            grown[...] = lax.dot_general(
                scale_ref[0],
                spread,
                (((0,), (0,)), ((), ())),
                precision=lax.Precision.HIGHEST,
                preferred_element_type=jnp.float32,
            )

    for which, held, grown in ((0, gate_held, gate_rows), (1, up_held, up_rows)):
        arrival(which, step).wait()
        for piece in range(rows // sub):
            block = (start_ref[0] + step * rows + piece * sub) // 128
            there = pl.ds(pl.multiple_of(step * rows + piece * sub, sub), sub)
            scaled = held[there, :].astype(jnp.float32) * grown[pl.ds(block, 1), :]
            out_ref[piece * sub : (piece + 1) * sub, which * half_units : (which + 1) * half_units] = (
                scaled.astype(jnp.bfloat16)
            )


def scaled_weights(gate_values, up_values, gate_scales, up_scales, start_row):
    feat_cols, half_units = gate_values.shape[1:]
    sub = math.gcd(feat_cols, 128)
    rows = max(r for r in range(sub, 257, sub) if feat_cols % r == 0)
    gate_scales, up_scales = (jnp.swapaxes(value, 1, 2) for value in (gate_scales, up_scales))
    any_spec = pl.BlockSpec(memory_space=pl.ANY)
    scale_spec = pl.BlockSpec(gate_scales.shape, lambda i, start: (0, 0, 0))
    held = pltpu.VMEM((feat_cols, half_units), jnp.bfloat16)
    grown = pltpu.VMEM((gate_scales.shape[2], half_units), jnp.float32)
    return pl.pallas_call(
        lambda *refs: scale_kernel(sub, *refs),
        out_shape=jax.ShapeDtypeStruct((feat_cols, 2 * half_units), jnp.bfloat16),
        grid_spec=pltpu.PrefetchScalarGridSpec(
            num_scalar_prefetch=1,
            grid=(feat_cols // rows,),
            in_specs=[any_spec, any_spec, scale_spec, scale_spec],
            out_specs=pl.BlockSpec((rows, 2 * half_units), lambda i, start: (i, 0)),
            scratch_shapes=[
                held,
                held,
                grown,
                grown,
                pltpu.SemaphoreType.DMA((2, feat_cols // rows)),
            ],
        ),
        compiler_params=pltpu.CompilerParams(vmem_limit_bytes=16 * 2**20),
        cost_estimate=pl.CostEstimate(
            flops=2 * feat_cols * half_units,
            bytes_accessed=8 * feat_cols * half_units,
            transcendentals=0,
        ),
        name="scale_weights",
    )(
        start_row[None],
        pltpu.with_memory_space_constraint(gate_values, pltpu.HBM),
        pltpu.with_memory_space_constraint(up_values, pltpu.HBM),
        gate_scales,
        up_scales,
    )


def rows_of(counts_ref, expert):
    first = jnp.int32(0)
    live = jnp.int32(0)
    for other in range(counts_ref.shape[1]):
        count = counts_ref[0, other]
        first = first + jnp.where(other < expert, count, 0)
        live = jnp.where(other == expert, count, live)
    return first, live


def pack_kernel(chip_ref, counts_ref, tokens_ref, chooser_ref, *out_refs):
    row_total = tokens_ref.shape[0]
    capacity = out_refs[0].shape[0]
    row = lax.broadcasted_iota(jnp.int32, (capacity, row_total), 1)
    slot = lax.broadcasted_iota(jnp.int32, (capacity, row_total), 0)
    hits = []
    for mask in range(len(out_refs)):
        first, live = rows_of(counts_ref, chip_ref[0] ^ mask)
        hits.append(((row == first + slot) & (slot < live)).astype(jnp.float32))
    chooser = jnp.concatenate(hits, 0).astype(jnp.bfloat16)
    chooser_ref[...] = chooser
    chosen = jnp.dot(chooser, tokens_ref[...], preferred_element_type=jnp.float32)
    for mask, out_ref in enumerate(out_refs):
        out_ref[...] = chosen[mask * capacity : (mask + 1) * capacity].astype(jnp.bfloat16)


def packed_rows(tokens, counts, chip, capacity):
    row_total, feat_cols = tokens.shape
    experts = counts.shape[1]
    smem = pl.BlockSpec(memory_space=pltpu.SMEM)
    vmem = pl.BlockSpec(memory_space=pltpu.VMEM)
    block = jax.ShapeDtypeStruct((capacity, feat_cols), jnp.bfloat16)
    chooser, *packed = pl.pallas_call(
        pack_kernel,
        out_shape=(jax.ShapeDtypeStruct((experts * capacity, row_total), jnp.bfloat16),)
        + (block,) * experts,
        in_specs=[smem, smem, vmem],
        out_specs=(vmem,) * (experts + 1),
        cost_estimate=pl.CostEstimate(
            flops=2 * experts * capacity * row_total * feat_cols,
            bytes_accessed=2 * (row_total + experts * capacity) * feat_cols,
            transcendentals=0,
        ),
        name="pack_rows",
    )(chip[None], counts, tokens)
    return chooser, packed


def project_kernel(*refs):
    *block_refs, weight_ref, out_ref, held = refs
    capacity = block_refs[0].shape[0]

    @pl.when(pl.program_id(0) == 0)
    def _():
        for place, block_ref in enumerate(block_refs):
            held[place * capacity : (place + 1) * capacity, :] = block_ref[...]

    sums = jnp.dot(held[...], weight_ref[...], preferred_element_type=jnp.float32)
    for place in range(len(block_refs)):
        out_ref[place] = sums[place * capacity : (place + 1) * capacity].astype(jnp.bfloat16)


def projected(blocks, weights):
    count = len(blocks)
    capacity, feat_cols = blocks[0].shape
    units = weights.shape[1]
    tile = math.gcd(units, 512)
    return pl.pallas_call(
        project_kernel,
        out_shape=jax.ShapeDtypeStruct((count, capacity, units), jnp.bfloat16),
        grid=(units // tile,),
        in_specs=[pl.BlockSpec((capacity, feat_cols), lambda i: (0, 0))] * count
        + [pl.BlockSpec((feat_cols, tile), lambda i: (0, i))],
        out_specs=pl.BlockSpec((count, capacity, tile), lambda i: (0, 0, i)),
        scratch_shapes=[pltpu.VMEM((count * capacity, feat_cols), jnp.bfloat16)],
        compiler_params=pltpu.CompilerParams(vmem_limit_bytes=16 * 2**20),
        cost_estimate=pl.CostEstimate(
            flops=2 * count * capacity * feat_cols * units,
            bytes_accessed=2 * (count * capacity * (feat_cols + units) + feat_cols * units),
            transcendentals=0,
        ),
        name="project",
    )(*blocks, pltpu.with_memory_space_constraint(weights, pltpu.VMEM))


def weight_kernel(count, *refs):
    input_refs, grad_refs = refs[:count], refs[count:-3]
    gate_ref, up_ref, held = refs[-3:]
    half_units = gate_ref.shape[2]

    @pl.when(pl.program_id(0) == 0)
    def _():
        place = 0
        for grad_ref in grad_refs:
            held[place : place + grad_ref.shape[0], :] = grad_ref[...]
            place += grad_ref.shape[0]

    inputs = jnp.concatenate([input_ref[...] for input_ref in input_refs], 0)
    for out_ref, offset in ((gate_ref, 0), (up_ref, half_units)):
        out_ref[0] = lax.dot_general(
            inputs,
            held[:, offset : offset + half_units],
            (((0,), (0,)), ((), ())),
            preferred_element_type=jnp.float32,
        ).astype(jnp.bfloat16)


def weight_grads(inputs, grads):
    count = len(inputs)
    rows = sum(value.shape[0] for value in inputs)
    feat_cols = inputs[0].shape[1]
    units = grads[0].shape[1]
    tile = 256 if feat_cols % 256 == 0 else feat_cols
    out = jax.ShapeDtypeStruct((1, feat_cols, units // 2), jnp.bfloat16)
    out_spec = pl.BlockSpec((1, tile, units // 2), lambda i: (0, i, 0))
    return pl.pallas_call(
        lambda *refs: weight_kernel(count, *refs),
        out_shape=(out, out),
        grid=(feat_cols // tile,),
        in_specs=[pl.BlockSpec((value.shape[0], tile), lambda i: (0, i)) for value in inputs]
        + [pl.BlockSpec(value.shape, lambda i: (0, 0)) for value in grads],
        out_specs=(out_spec, out_spec),
        scratch_shapes=[pltpu.VMEM((rows, units), jnp.bfloat16)],
        compiler_params=pltpu.CompilerParams(vmem_limit_bytes=16 * 2**20),
        cost_estimate=pl.CostEstimate(
            flops=2 * rows * feat_cols * units,
            bytes_accessed=2 * (rows * (feat_cols + units) + feat_cols * units),
            transcendentals=0,
        ),
        name="weight_grads",
    )(*inputs, *grads)


def earlier(value, *needed):
    return lax.optimization_barrier((value,) + needed)[0]


def add_rounded(first, second):
    return (first.astype(jnp.float32) + second.astype(jnp.float32)).astype(jnp.bfloat16)


class Chain:
    def __init__(self, chip, size):
        self.chip = chip
        self.size = size
        self.index = lax.axis_index("fsdp")
        self.reach = {1: size // 2, -1: size - 1 - size // 2}
        self.partial = None
        self.whole = None
        self.came = {}

    def owner(self, steps):
        return lax.rem(self.index + self.size + steps, self.size)

    def block(self, steps):
        return pick(self.partial, self.owner(steps) ^ self.chip)

    def send(self, way, value):
        ring = [(source, (source + way) % self.size) for source in range(self.size)]
        self.came[way] = lax.ppermute(value, "fsdp", ring)

    def place(self, value, steps):
        self.whole = lax.dynamic_update_index_in_dim(
            self.whole, value, self.owner(steps) ^ self.chip, 0
        )


def on_device(tokens, counts, gate_values, up_values, gate_scales, up_scales, grad_hidden):
    row_total, feat_cols = tokens.shape
    experts = counts.shape[1]
    capacity = min(4 * row_total // experts, row_total // 2)
    n_fsdp = lax.axis_size("fsdp")
    chips = lax.axis_size("expert") // 2
    half_units = gate_values.shape[2]
    parity = lax.axis_index("expert") % 2
    chip = lax.axis_index("expert") // 2
    index = lax.axis_index("fsdp")
    masks = range(chips)

    chooser, packed = packed_rows(tokens, counts, chip, capacity)
    weights = scaled_weights(
        gate_values, up_values, gate_scales, up_scales, index * feat_cols
    )
    cots = grad_hidden[0].reshape(2, capacity, half_units)
    chains = [Chain(chip, n_fsdp) for _ in range(2)]
    hiddens = [None, None]
    token = None

    def ordered(value):
        return value if token is None else earlier(value, token)

    def begin(group):
        nonlocal token
        chain = chains[group]
        chain.partial = projected(inputs[group], weights)
        for way, reach in chain.reach.items():
            if reach:
                token = ordered(chain.block(way * reach))
                chain.send(way, token)

    def reduce(group, way, step):
        nonlocal token
        chain = chains[group]
        token = add_rounded(
            chain.block(way * (chain.reach[way] - step)), ordered(chain.came[way])
        )
        chain.send(way, token)

    def activate(group):
        nonlocal token
        chain = chains[group]
        pre = chain.block(0).astype(jnp.float32)
        for came in chain.came.values():
            pre = pre + ordered(came).astype(jnp.float32)
        gate_pre = pre[:, :half_units]
        up_pre = pre[:, half_units:]
        cot = pick(cots, parity ^ (1 - group)).astype(jnp.float32)
        sigmoid_gate = jax.nn.sigmoid(gate_pre)
        hiddens[group] = (gate_pre * sigmoid_gate * up_pre).astype(jnp.bfloat16)
        grad_gate_pre = cot * up_pre * sigmoid_gate * (1.0 + gate_pre * (1.0 - sigmoid_gate))
        grad_up_pre = cot * gate_pre * sigmoid_gate
        token = jnp.concatenate(
            [grad_gate_pre.astype(jnp.bfloat16), grad_up_pre.astype(jnp.bfloat16)], 1
        )
        for way, reach in chain.reach.items():
            if reach:
                chain.send(way, token)
        chain.whole = jnp.zeros((chips, capacity, 2 * half_units), jnp.bfloat16)
        chain.place(token, 0)

    def gather(group, way, step):
        nonlocal token
        chain = chains[group]
        token = ordered(chain.came[way])
        chain.place(token, -way * step)
        if step < chain.reach[way]:
            chain.send(way, token)

    def back(whole):
        return lax.dot_general(
            whole, weights, (((1,), (1,)), ((), ())), preferred_element_type=jnp.float32
        ).astype(jnp.bfloat16)

    arrived = [swap(packed[mask], "expert", 2 * mask + 1) for mask in masks]
    inputs = [arrived, [swap(rows, "expert", 1) for rows in arrived]]
    for group in range(2):
        begin(group)
    steps = range(1, n_fsdp)
    for step in steps:
        for group in range(2):
            for way, reach in chains[group].reach.items():
                if step < reach:
                    reduce(group, way, step)
    for group in range(2):
        activate(group)
    for step in steps:
        for group in range(2):
            for way, reach in chains[group].reach.items():
                if step <= reach:
                    gather(group, way, step)
    wholes = [chain.whole.reshape(chips * capacity, 2 * half_units) for chain in chains]

    taken = swap(back(wholes[0]), "expert", 1)
    kept = back(earlier(wholes[1], taken))
    pieces = []
    for mask in masks:
        rows = slice(mask * capacity, (mask + 1) * capacity)
        both = add_rounded(kept[rows], taken[rows])
        pieces.append(swap(both, "expert", 2 * mask) if mask else both)

    hidden = jnp.where(
        parity == 0, jnp.concatenate([hiddens[1], hiddens[0]], 0), jnp.concatenate(hiddens, 0)
    )
    grad_gate, grad_up = weight_grads(inputs[0] + inputs[1], wholes)
    grad_tokens = lax.dot_general(
        chooser,
        jnp.concatenate(pieces, 0),
        (((0,), (0,)), ((), ())),
        preferred_element_type=jnp.float32,
    ).astype(jnp.bfloat16)
    return (hidden[None], grad_gate, grad_up, grad_tokens)


def solution(mesh):
    in_specs = (
        P("expert", "fsdp"),
        P("expert", None),
        P("expert", "fsdp", None),
        P("expert", "fsdp", None),
        P("expert", None, None),
        P("expert", None, None),
        P("expert", "fsdp", None),
    )
    out_specs = (
        P("expert", "fsdp", None),
        P("expert", "fsdp", None),
        P("expert", "fsdp", None),
        P("expert", "fsdp"),
    )
    return jax.shard_map(
        on_device, mesh=mesh, in_specs=in_specs, out_specs=out_specs, check_vma=False
    )
```

profile of v0, /device:TPU:0, one launch (start us, length us, event | category | flops | bytes accessed | tf_op | source)
XLA Modules:
  0.0 111.8 jit_solution(7912813423846397352)
XLA Ops:
  0.6 2.3 %pack_rows.1 = (bf16[256,128]{1,0:T(8,128)(2,1)}, bf16[64,1792]{1,0:T(8,128)(2,1)}, bf16[64,1792]{1,0:T(8,128)(2,1)}, bf16[64,1792]{1,0:T(8,128)(2,1)}, bf16[64,1792]{1,0:T(8,128)(2,1)}) custom-call(s32[1]{0:T(128)} %bitcast.chip_ref, s32[1,4]{1,0:T(1,128)} %counts_ref.1, bf16[128,1792]{1,0:T(8,128)(2,1)} %tokens_ref.1), custom_call_target="tpu_custom_call" | custom-call | flops 117440512 | bytes 1376256 | tf_op jit(solution)/shard_map/pack_rows/pallas_call | solution.py:148
  3.4 2.6 %collective-permute-start.2 = (bf16[64,1792]{1,0:T(8,128)(2,1)}, bf16[64,1792]{1,0:T(8,128)(2,1)S(1)}, u32[]{:S(2)}, u32[]{:S(2)}) collective-permute-start(bf16[64,1792]{1,0:T(8,128)(2,1)} %get-tuple-element.28), channel_id=1, source_target_pairs={{0,12},{4,8},{8,4},{12,0},{16,28},{20,24},{24,20},{28,16},{1,13},{... | collective-permute-start | bytes 688136 | tf_op jit(solution)/shard_map/ppermute | solution.py:13
  6.0 1.1 %collective-permute-start.4 = (bf16[64,1792]{1,0:T(8,128)(2,1)}, bf16[64,1792]{1,0:T(8,128)(2,1)S(1)}, u32[]{:S(2)}, u32[]{:S(2)}) collective-permute-start(bf16[64,1792]{1,0:T(8,128)(2,1)} %get-tuple-element.29), channel_id=1, source_target_pairs={{0,20},{4,16},{8,28},{12,24},{16,4},{20,0},{24,12},{28,8},{1,21},{... | collective-permute-start | bytes 688136 | tf_op jit(solution)/shard_map/ppermute | solution.py:13
  8.5 3.3 %scale_weights.1.refs_4_ = bf16[1792,2048]{1,0:T(8,128)(2,1)S(1)} custom-call(s32[1]{0:T(128)} %bitcast.1.refs_0_, bf16[1,1792,1024]{2,1,0:T(8,128)(2,1)} %refs_1_.1, bf16[1,1792,1024]{2,1,0:T(8,128)(2,1)} %refs_2_.1, f32[1,8,56]{2,1,0:T(8,128)S(1)} %bitcast.64, f32[1,8,56]{2,1,0:T(8,128)S(1)} %bitcast.65), custom_call_target="tpu_custom_call" | custom-call | flops 3670016 | bytes 14680064 | tf_op jit(solution)/shard_map/scale_weights/pallas_call | solution.py:84
  12.7 6.2 %collective-permute-done.4.refs_2_ = bf16[64,1792]{1,0:T(8,128)(2,1)S(1)} collective-permute-done((bf16[64,1792]{1,0:T(8,128)(2,1)}, bf16[64,1792]{1,0:T(8,128)(2,1)S(1)}, u32[]{:S(2)}, u32[]{:S(2)}) %collective-permute-start.4) | collective-permute-done | bytes 229408 | tf_op jit(solution)/shard_map/ppermute | solution.py:13
  19.4 3.3 %project.3 = bf16[4,64,2048]{2,1,0:T(8,128)(2,1)S(1)} custom-call(bf16[64,1792]{1,0:T(8,128)(2,1)S(1)} %collective-permute-done.refs_0_, bf16[64,1792]{1,0:T(8,128)(2,1)S(1)} %collective-permute-done.2.refs_1_, bf16[64,1792]{1,0:T(8,128)(2,1)S(1)} %collective-permute-done.4.refs_2_, bf16[64,1792]{1,0:T(8,128)(2,1)S(1)} %collective-permute-done.6.refs_3_, ...), custom_call_target="tpu_custom_call" | custom-call | flops 1879048192 | bytes 9306112 | tf_op jit(solution)/shard_map/project/pallas_call | solution.py:183
  22.7 1.6 %collective-permute-start.9 = (bf16[64,2048]{1,0:T(8,128)(2,1)S(1)}, bf16[64,2048]{1,0:T(8,128)(2,1)S(1)}, u32[]{:S(2)}, u32[]{:S(2)}) collective-permute-start(bf16[64,2048]{1,0:T(8,128)(2,1)S(1)} %get-tuple-element.56), channel_id=1, source_target_pairs={{0,1},{1,2},{2,3},{3,0},{4,5},{5,6},{6,7},{7,4},{8,9},{9,10},{10,1... | collective-permute-start | bytes 786440 | tf_op jit(solution)/shard_map/ppermute | solution.py:275
  24.3 2.2 %collective-permute-start.12 = (bf16[64,2048]{1,0:T(8,128)(2,1)S(1)}, bf16[64,2048]{1,0:T(8,128)(2,1)S(1)}, u32[]{:S(2)}, u32[]{:S(2)}) collective-permute-start(bf16[64,2048]{1,0:T(8,128)(2,1)S(1)} %get-tuple-element.31), channel_id=1, source_target_pairs={{0,3},{1,0},{2,1},{3,2},{4,7},{5,4},{6,5},{7,6},{8,11},{9,8},{10,9... | collective-permute-start | bytes 786440 | tf_op jit(solution)/shard_map/ppermute | solution.py:275
  26.6 3.3 %project.2 = bf16[4,64,2048]{2,1,0:T(8,128)(2,1)S(1)} custom-call(bf16[64,1792]{1,0:T(8,128)(2,1)S(1)} %collective-permute-done.1.refs_0_.refs_4_, bf16[64,1792]{1,0:T(8,128)(2,1)S(1)} %collective-permute-done.3.refs_1_.refs_5_, bf16[64,1792]{1,0:T(8,128)(2,1)S(1)} %collective-permute-done.5.refs_2_.refs_6_, ...), custom_call_target="tpu_custom_call" | custom-call | flops 1879048192 | bytes 9306112 | tf_op jit(solution)/shard_map/project/pallas_call | solution.py:183
  30.0 3.8 %collective-permute-start.13 = (bf16[64,2048]{1,0:T(8,128)(2,1)S(1)}, bf16[64,2048]{1,0:T(8,128)(2,1)S(1)}, u32[]{:S(2)}, u32[]{:S(2)}) collective-permute-start(bf16[64,2048]{1,0:T(8,128)(2,1)S(1)} %get-tuple-element.33), channel_id=1, source_target_pairs={{0,3},{1,0},{2,1},{3,2},{4,7},{5,4},{6,5},{7,6},{8,11},{9,8},{10,9... | collective-permute-start | bytes 786440 | tf_op jit(solution)/shard_map/ppermute | solution.py:275
  33.9 3.8 %collective-permute-start.11 = (bf16[64,2048]{1,0:T(8,128)(2,1)S(1)}, bf16[64,2048]{1,0:T(8,128)(2,1)S(1)}, u32[]{:S(2)}, u32[]{:S(2)}) collective-permute-start(bf16[64,2048]{1,0:T(8,128)(2,1)S(1)} %fusion.8), channel_id=1, source_target_pairs={{0,1},{1,2},{2,3},{3,0},{4,5},{5,6},{6,7},{7,4},{8,9},{9,10},{10,1... | collective-permute-start | bytes 786440 | tf_op jit(solution)/shard_map/ppermute | solution.py:275
  37.7 7.3 %collective-permute-done.8 = bf16[64,2048]{1,0:T(8,128)(2,1)S(1)} collective-permute-done((bf16[64,2048]{1,0:T(8,128)(2,1)S(1)}, bf16[64,2048]{1,0:T(8,128)(2,1)S(1)}, u32[]{:S(2)}, u32[]{:S(2)}) %collective-permute-start.8) | collective-permute-done | bytes 262176 | tf_op jit(solution)/shard_map/ppermute | solution.py:275
  45.1 3.9 %collective-permute-start.10 = (bf16[64,2048]{1,0:T(8,128)(2,1)S(1)}, bf16[64,2048]{1,0:T(8,128)(2,1)S(1)}, u32[]{:S(2)}, u32[]{:S(2)}) collective-permute-start(bf16[64,2048]{1,0:T(8,128)(2,1)S(1)} %fusion.9), channel_id=1, source_target_pairs={{0,1},{1,2},{2,3},{3,0},{4,5},{5,6},{6,7},{7,4},{8,9},{9,10},{10,1... | collective-permute-start | bytes 786440 | tf_op jit(solution)/shard_map/ppermute | solution.py:275
  48.9 7.3 %collective-permute-done.11 = bf16[64,2048]{1,0:T(8,128)(2,1)S(1)} collective-permute-done((bf16[64,2048]{1,0:T(8,128)(2,1)S(1)}, bf16[64,2048]{1,0:T(8,128)(2,1)S(1)}, u32[]{:S(2)}, u32[]{:S(2)}) %collective-permute-start.11) | collective-permute-done | bytes 262176 | tf_op jit(solution)/shard_map/ppermute | solution.py:275
  56.6 3.8 %collective-permute-start.15 = (bf16[64,2048]{1,0:T(8,128)(2,1)S(1)}, bf16[64,2048]{1,0:T(8,128)(2,1)S(1)}, u32[]{:S(2)}, u32[]{:S(2)}) collective-permute-start(bf16[64,2048]{1,0:T(8,128)(2,1)S(1)} %pad_maximum_fusion), channel_id=1, source_target_pairs={{0,3},{1,0},{2,1},{3,2},{4,7},{5,4},{6,5},{7,6},{8,11},{9,8},{10,9... | collective-permute-start | bytes 786440 | tf_op jit(solution)/shard_map/ppermute | solution.py:275
  60.6 1.4 %collective-permute-done.10 = bf16[64,2048]{1,0:T(8,128)(2,1)S(1)} collective-permute-done((bf16[64,2048]{1,0:T(8,128)(2,1)S(1)}, bf16[64,2048]{1,0:T(8,128)(2,1)S(1)}, u32[]{:S(2)}, u32[]{:S(2)}) %collective-permute-start.10) | collective-permute-done | bytes 262176 | tf_op jit(solution)/shard_map/ppermute | solution.py:275
  62.4 3.8 %collective-permute-start.17 = (bf16[64,2048]{1,0:T(8,128)(2,1)S(1)}, bf16[64,2048]{1,0:T(8,128)(2,1)S(1)}, u32[]{:S(2)}, u32[]{:S(2)}) collective-permute-start(bf16[64,2048]{1,0:T(8,128)(2,1)S(1)} %pad_maximum_fusion.1), channel_id=1, source_target_pairs={{0,3},{1,0},{2,1},{3,2},{4,7},{5,4},{6,5},{7,6},{8,11},{9,8},{10,9... | collective-permute-start | bytes 786440 | tf_op jit(solution)/shard_map/ppermute | solution.py:275
  67.6 3.6 %collective-permute-start.16 = (bf16[64,2048]{1,0:T(8,128)(2,1)S(1)}, bf16[64,2048]{1,0:T(8,128)(2,1)S(1)}, u32[]{:S(2)}, u32[]{:S(2)}) collective-permute-start(bf16[64,2048]{1,0:T(8,128)(2,1)S(1)} %collective-permute-done.14), channel_id=1, source_target_pairs={{0,1},{1,2},{2,3},{3,0},{4,5},{5,6},{6,7},{7,4},{8,9},{9,10},{10,1... | collective-permute-start | bytes 786440 | tf_op jit(solution)/shard_map/ppermute | solution.py:275
  71.2 2.2 %collective-permute-done.15 = bf16[64,2048]{1,0:T(8,128)(2,1)S(1)} collective-permute-done((bf16[64,2048]{1,0:T(8,128)(2,1)S(1)}, bf16[64,2048]{1,0:T(8,128)(2,1)S(1)}, u32[]{:S(2)}, u32[]{:S(2)}) %collective-permute-start.15) | collective-permute-done | bytes 262176 | tf_op jit(solution)/shard_map/ppermute | solution.py:275
  73.5 5.4 %collective-permute-done.18 = bf16[64,2048]{1,0:T(8,128)(2,1)S(1)} collective-permute-done((bf16[64,2048]{1,0:T(8,128)(2,1)S(1)}, bf16[64,2048]{1,0:T(8,128)(2,1)S(1)}, u32[]{:S(2)}, u32[]{:S(2)}) %collective-permute-start.18) | collective-permute-done | bytes 262176 | tf_op jit(solution)/shard_map/ppermute | solution.py:275
  78.9 3.5 %collective-permute-start.19 = (bf16[64,2048]{1,0:T(8,128)(2,1)S(1)}, bf16[64,2048]{1,0:T(8,128)(2,1)S(1)}, u32[]{:S(2)}, u32[]{:S(2)}) collective-permute-start(bf16[64,2048]{1,0:T(8,128)(2,1)S(1)} %collective-permute-done.18), channel_id=1, source_target_pairs={{0,1},{1,2},{2,3},{3,0},{4,5},{5,6},{6,7},{7,4},{8,9},{9,10},{10,1... | collective-permute-start | bytes 786440 | tf_op jit(solution)/shard_map/ppermute | solution.py:275
  82.4 1.9 %collective-permute-done.17 = bf16[64,2048]{1,0:T(8,128)(2,1)S(1)} collective-permute-done((bf16[64,2048]{1,0:T(8,128)(2,1)S(1)}, bf16[64,2048]{1,0:T(8,128)(2,1)S(1)}, u32[]{:S(2)}, u32[]{:S(2)}) %collective-permute-start.17) | collective-permute-done | bytes 262176 | tf_op jit(solution)/shard_map/ppermute | solution.py:275
  84.4 5.8 %collective-permute-done.16 = bf16[64,2048]{1,0:T(8,128)(2,1)S(1)} collective-permute-done((bf16[64,2048]{1,0:T(8,128)(2,1)S(1)}, bf16[64,2048]{1,0:T(8,128)(2,1)S(1)}, u32[]{:S(2)}, u32[]{:S(2)}) %collective-permute-start.16) | collective-permute-done | bytes 262176 | tf_op jit(solution)/shard_map/ppermute | solution.py:275
  90.2 2.1 %convolution_convert_fusion.1 = bf16[256,1792]{1,0:T(8,128)(2,1)S(1)} fusion(bf16[256,2048]{1,0:T(8,128)(2,1)S(1)} %bitcast.62, bf16[1792,2048]{1,0:T(8,128)(2,1)S(1)} %scale_weights.1.refs_4_), kind=kOutput, calls=%fused_computation.1 | convolution fusion | flops 1879506944 | bytes 9306112 | tf_op jit(solution)/shard_map/dot_general | solution.py:355
  92.4 2.5 %collective-permute-done.19 = bf16[64,2048]{1,0:T(8,128)(2,1)S(1)} collective-permute-done((bf16[64,2048]{1,0:T(8,128)(2,1)S(1)}, bf16[64,2048]{1,0:T(8,128)(2,1)S(1)}, u32[]{:S(2)}, u32[]{:S(2)}) %collective-permute-start.19) | collective-permute-done | bytes 262176 | tf_op jit(solution)/shard_map/ppermute | solution.py:275
  94.9 2.1 %convolution_convert_fusion = bf16[256,1792]{1,0:T(8,128)(2,1)S(1)} fusion(bf16[256,2048]{1,0:T(8,128)(2,1)S(1)} %bitcast.60, bf16[1792,2048]{1,0:T(8,128)(2,1)S(1)} %scale_weights.1.refs_4_), kind=kOutput, calls=%fused_computation | convolution fusion | flops 1879506944 | bytes 9306112 | tf_op jit(solution)/shard_map/dot_general | solution.py:355
  97.6 1.8 %collective-permute-start.22 = (bf16[64,1792]{1,0:T(8,128)(2,1)S(1)}, bf16[64,1792]{1,0:T(8,128)(2,1)S(1)}, u32[]{:S(2)}, u32[]{:S(2)}) collective-permute-start(bf16[64,1792]{1,0:T(8,128)(2,1)S(1)} %get-tuple-element.52), channel_id=1, source_target_pairs={{0,16},{4,20},{8,24},{12,28},{16,0},{20,4},{24,8},{28,12},{1,17},{... | collective-permute-start | bytes 688136 | tf_op jit(solution)/shard_map/ppermute | solution.py:13
  99.4 1.4 %collective-permute-start.23 = (bf16[64,1792]{1,0:T(8,128)(2,1)S(1)}, bf16[64,1792]{1,0:T(8,128)(2,1)S(1)}, u32[]{:S(2)}, u32[]{:S(2)}) collective-permute-start(bf16[64,1792]{1,0:T(8,128)(2,1)S(1)} %get-tuple-element.51), channel_id=1, source_target_pairs={{0,24},{4,28},{8,16},{12,20},{16,8},{20,12},{24,0},{28,4},{1,25},{... | collective-permute-start | bytes 688136 | tf_op jit(solution)/shard_map/ppermute | solution.py:13
  100.8 6.6 %weight_grads.1 = (bf16[1,1792,1024]{2,1,0:T(8,128)(2,1)}, bf16[1,1792,1024]{2,1,0:T(8,128)(2,1)}) custom-call(bf16[64,1792]{1,0:T(8,128)(2,1)S(1)} %collective-permute-done.refs_0_, bf16[64,1792]{1,0:T(8,128)(2,1)S(1)} %collective-permute-done.2.refs_1_, bf16[64,1792]{1,0:T(8,128)(2,1)S(1)} %collective-permute-done.4.refs_2_, ...), custom_call_target="tpu_custom_call" | custom-call | flops 3758096384 | bytes 11272192 | tf_op jit(solution)/shard_map/weight_grads/pallas_call | solution.py:231
  107.4 1.7 %collective-permute-done.22 = bf16[64,1792]{1,0:T(8,128)(2,1)S(1)} collective-permute-done((bf16[64,1792]{1,0:T(8,128)(2,1)S(1)}, bf16[64,1792]{1,0:T(8,128)(2,1)S(1)}, u32[]{:S(2)}, u32[]{:S(2)}) %collective-permute-start.22) | collective-permute-done | bytes 229408 | tf_op jit(solution)/shard_map/ppermute | solution.py:13
  109.1 1.6 %collective-permute-done.23 = bf16[64,1792]{1,0:T(8,128)(2,1)S(1)} collective-permute-done((bf16[64,1792]{1,0:T(8,128)(2,1)S(1)}, bf16[64,1792]{1,0:T(8,128)(2,1)S(1)}, u32[]{:S(2)}, u32[]{:S(2)}) %collective-permute-start.23) | collective-permute-done | bytes 229408 | tf_op jit(solution)/shard_map/ppermute | solution.py:13
  110.8 1.1 convolution_convert_fusion.2
  (54 shorter events, 6.5 us)
Async XLA Ops:
  2.9 8.9 %collective-permute-start = (bf16[64,1792]{1,0:T(8,128)(2,1)}, bf16[64,1792]{1,0:T(8,128)(2,1)S(1)}, u32[]{:S(2)}, u32[]{:S(2)}) collective-permute-start(bf16[64,1792]{1,0:T(8,128)(2,1)} %get-tuple-element.27), channel_id=1, source_target_pairs={{0,4},{4,0},{8,12},{12,8},{16,20},{20,16},{24,28},{28,24},{1,5},{5... | collective-permute-start | bytes 688136 | tf_op jit(solution)/shard_map/ppermute | solution.py:13
  3.4 9.0 %collective-permute-start.2 = (bf16[64,1792]{1,0:T(8,128)(2,1)}, bf16[64,1792]{1,0:T(8,128)(2,1)S(1)}, u32[]{:S(2)}, u32[]{:S(2)}) collective-permute-start(bf16[64,1792]{1,0:T(8,128)(2,1)} %get-tuple-element.28), channel_id=1, source_target_pairs={{0,12},{4,8},{8,4},{12,0},{16,28},{20,24},{24,20},{28,16},{1,13},{... | collective-permute-start | bytes 688136 | tf_op jit(solution)/shard_map/ppermute | solution.py:13
  6.0 12.8 %collective-permute-start.4 = (bf16[64,1792]{1,0:T(8,128)(2,1)}, bf16[64,1792]{1,0:T(8,128)(2,1)S(1)}, u32[]{:S(2)}, u32[]{:S(2)}) collective-permute-start(bf16[64,1792]{1,0:T(8,128)(2,1)} %get-tuple-element.29), channel_id=1, source_target_pairs={{0,20},{4,16},{8,28},{12,24},{16,4},{20,0},{24,12},{28,8},{1,21},{... | collective-permute-start | bytes 688136 | tf_op jit(solution)/shard_map/ppermute | solution.py:13
  7.1 11.8 %collective-permute-start.6 = (bf16[64,1792]{1,0:T(8,128)(2,1)}, bf16[64,1792]{1,0:T(8,128)(2,1)S(1)}, u32[]{:S(2)}, u32[]{:S(2)}) collective-permute-start(bf16[64,1792]{1,0:T(8,128)(2,1)} %get-tuple-element.30), channel_id=1, source_target_pairs={{0,28},{4,24},{8,20},{12,16},{16,12},{20,8},{24,4},{28,0},{1,29},{... | collective-permute-start | bytes 688136 | tf_op jit(solution)/shard_map/ppermute | solution.py:13
  7.1 0.7 copy-start
  7.8 0.7 copy-start.1
  11.8 12.5 %collective-permute-start.1 = (bf16[64,1792]{1,0:T(8,128)(2,1)S(1)}, bf16[64,1792]{1,0:T(8,128)(2,1)S(1)}, u32[]{:S(2)}, u32[]{:S(2)}) collective-permute-start(bf16[64,1792]{1,0:T(8,128)(2,1)S(1)} %collective-permute-done.refs_0_), channel_id=1, source_target_pairs={{0,4},{4,0},{8,12},{12,8},{16,20},{20,16},{24,28},{28,24},{1,5},{5... | collective-permute-start | bytes 688136 | tf_op jit(solution)/shard_map/ppermute | solution.py:13
  12.4 14.2 %collective-permute-start.3 = (bf16[64,1792]{1,0:T(8,128)(2,1)S(1)}, bf16[64,1792]{1,0:T(8,128)(2,1)S(1)}, u32[]{:S(2)}, u32[]{:S(2)}) collective-permute-start(bf16[64,1792]{1,0:T(8,128)(2,1)S(1)} %collective-permute-done.2.refs_1_), channel_id=1, source_target_pairs={{0,4},{4,0},{8,12},{12,8},{16,20},{20,16},{24,28},{28,24},{1,5},{5... | collective-permute-start | bytes 688136 | tf_op jit(solution)/shard_map/ppermute | solution.py:13
  18.8 7.7 %collective-permute-start.5 = (bf16[64,1792]{1,0:T(8,128)(2,1)S(1)}, bf16[64,1792]{1,0:T(8,128)(2,1)S(1)}, u32[]{:S(2)}, u32[]{:S(2)}) collective-permute-start(bf16[64,1792]{1,0:T(8,128)(2,1)S(1)} %collective-permute-done.4.refs_2_), channel_id=1, source_target_pairs={{0,4},{4,0},{8,12},{12,8},{16,20},{20,16},{24,28},{28,24},{1,5},{5... | collective-permute-start | bytes 688136 | tf_op jit(solution)/shard_map/ppermute | solution.py:13
  19.0 7.6 %collective-permute-start.7 = (bf16[64,1792]{1,0:T(8,128)(2,1)S(1)}, bf16[64,1792]{1,0:T(8,128)(2,1)S(1)}, u32[]{:S(2)}, u32[]{:S(2)}) collective-permute-start(bf16[64,1792]{1,0:T(8,128)(2,1)S(1)} %collective-permute-done.6.refs_3_), channel_id=1, source_target_pairs={{0,4},{4,0},{8,12},{12,8},{16,20},{20,16},{24,28},{28,24},{1,5},{5... | collective-permute-start | bytes 688136 | tf_op jit(solution)/shard_map/ppermute | solution.py:13
  22.7 11.1 %collective-permute-start.9 = (bf16[64,2048]{1,0:T(8,128)(2,1)S(1)}, bf16[64,2048]{1,0:T(8,128)(2,1)S(1)}, u32[]{:S(2)}, u32[]{:S(2)}) collective-permute-start(bf16[64,2048]{1,0:T(8,128)(2,1)S(1)} %get-tuple-element.56), channel_id=1, source_target_pairs={{0,1},{1,2},{2,3},{3,0},{4,5},{5,6},{6,7},{7,4},{8,9},{9,10},{10,1... | collective-permute-start | bytes 786440 | tf_op jit(solution)/shard_map/ppermute | solution.py:275
  24.3 24.6 %collective-permute-start.12 = (bf16[64,2048]{1,0:T(8,128)(2,1)S(1)}, bf16[64,2048]{1,0:T(8,128)(2,1)S(1)}, u32[]{:S(2)}, u32[]{:S(2)}) collective-permute-start(bf16[64,2048]{1,0:T(8,128)(2,1)S(1)} %get-tuple-element.31), channel_id=1, source_target_pairs={{0,3},{1,0},{2,1},{3,2},{4,7},{5,4},{6,5},{7,6},{8,11},{9,8},{10,9... | collective-permute-start | bytes 786440 | tf_op jit(solution)/shard_map/ppermute | solution.py:275
  29.9 26.5 %copy-start.2 = (bf16[1,128,1024]{2,1,0:T(8,128)(2,1)S(1)}, bf16[1,128,1024]{2,1,0:T(8,128)(2,1)}, u32[]{:S(2)}) copy-start(bf16[1,128,1024]{2,1,0:T(8,128)(2,1)} %param.13) | copy-start | bytes 786436
  29.9 15.1 %collective-permute-start.8 = (bf16[64,2048]{1,0:T(8,128)(2,1)S(1)}, bf16[64,2048]{1,0:T(8,128)(2,1)S(1)}, u32[]{:S(2)}, u32[]{:S(2)}) collective-permute-start(bf16[64,2048]{1,0:T(8,128)(2,1)S(1)} %get-tuple-element.32), channel_id=1, source_target_pairs={{0,1},{1,2},{2,3},{3,0},{4,5},{5,6},{6,7},{7,4},{8,9},{9,10},{10,1... | collective-permute-start | bytes 786440 | tf_op jit(solution)/shard_map/ppermute | solution.py:275
  30.0 30.4 %collective-permute-start.13 = (bf16[64,2048]{1,0:T(8,128)(2,1)S(1)}, bf16[64,2048]{1,0:T(8,128)(2,1)S(1)}, u32[]{:S(2)}, u32[]{:S(2)}) collective-permute-start(bf16[64,2048]{1,0:T(8,128)(2,1)S(1)} %get-tuple-element.33), channel_id=1, source_target_pairs={{0,3},{1,0},{2,1},{3,2},{4,7},{5,4},{6,5},{7,6},{8,11},{9,8},{10,9... | collective-permute-start | bytes 786440 | tf_op jit(solution)/shard_map/ppermute | solution.py:275
  33.9 22.3 %collective-permute-start.11 = (bf16[64,2048]{1,0:T(8,128)(2,1)S(1)}, bf16[64,2048]{1,0:T(8,128)(2,1)S(1)}, u32[]{:S(2)}, u32[]{:S(2)}) collective-permute-start(bf16[64,2048]{1,0:T(8,128)(2,1)S(1)} %fusion.8), channel_id=1, source_target_pairs={{0,1},{1,2},{2,3},{3,0},{4,5},{5,6},{6,7},{7,4},{8,9},{9,10},{10,1... | collective-permute-start | bytes 786440 | tf_op jit(solution)/shard_map/ppermute | solution.py:275
  45.1 16.9 %collective-permute-start.10 = (bf16[64,2048]{1,0:T(8,128)(2,1)S(1)}, bf16[64,2048]{1,0:T(8,128)(2,1)S(1)}, u32[]{:S(2)}, u32[]{:S(2)}) collective-permute-start(bf16[64,2048]{1,0:T(8,128)(2,1)S(1)} %fusion.9), channel_id=1, source_target_pairs={{0,1},{1,2},{2,3},{3,0},{4,5},{5,6},{6,7},{7,4},{8,9},{9,10},{10,1... | collective-permute-start | bytes 786440 | tf_op jit(solution)/shard_map/ppermute | solution.py:275
  56.5 11.1 %collective-permute-start.14 = (bf16[64,2048]{1,0:T(8,128)(2,1)S(1)}, bf16[64,2048]{1,0:T(8,128)(2,1)S(1)}, u32[]{:S(2)}, u32[]{:S(2)}) collective-permute-start(bf16[64,2048]{1,0:T(8,128)(2,1)S(1)} %pad_maximum_fusion), channel_id=1, source_target_pairs={{0,1},{1,2},{2,3},{3,0},{4,5},{5,6},{6,7},{7,4},{8,9},{9,10},{10,1... | collective-permute-start | bytes 786440 | tf_op jit(solution)/shard_map/ppermute | solution.py:275
  56.6 16.8 %collective-permute-start.15 = (bf16[64,2048]{1,0:T(8,128)(2,1)S(1)}, bf16[64,2048]{1,0:T(8,128)(2,1)S(1)}, u32[]{:S(2)}, u32[]{:S(2)}) collective-permute-start(bf16[64,2048]{1,0:T(8,128)(2,1)S(1)} %pad_maximum_fusion), channel_id=1, source_target_pairs={{0,3},{1,0},{2,1},{3,2},{4,7},{5,4},{6,5},{7,6},{8,11},{9,8},{10,9... | collective-permute-start | bytes 786440 | tf_op jit(solution)/shard_map/ppermute | solution.py:275
  62.3 16.6 %collective-permute-start.18 = (bf16[64,2048]{1,0:T(8,128)(2,1)S(1)}, bf16[64,2048]{1,0:T(8,128)(2,1)S(1)}, u32[]{:S(2)}, u32[]{:S(2)}) collective-permute-start(bf16[64,2048]{1,0:T(8,128)(2,1)S(1)} %pad_maximum_fusion.1), channel_id=1, source_target_pairs={{0,1},{1,2},{2,3},{3,0},{4,5},{5,6},{6,7},{7,4},{8,9},{9,10},{10,1... | collective-permute-start | bytes 786440 | tf_op jit(solution)/shard_map/ppermute | solution.py:275
  62.4 22.0 %collective-permute-start.17 = (bf16[64,2048]{1,0:T(8,128)(2,1)S(1)}, bf16[64,2048]{1,0:T(8,128)(2,1)S(1)}, u32[]{:S(2)}, u32[]{:S(2)}) collective-permute-start(bf16[64,2048]{1,0:T(8,128)(2,1)S(1)} %pad_maximum_fusion.1), channel_id=1, source_target_pairs={{0,3},{1,0},{2,1},{3,2},{4,7},{5,4},{6,5},{7,6},{8,11},{9,8},{10,9... | collective-permute-start | bytes 786440 | tf_op jit(solution)/shard_map/ppermute | solution.py:275
  67.6 22.5 %collective-permute-start.16 = (bf16[64,2048]{1,0:T(8,128)(2,1)S(1)}, bf16[64,2048]{1,0:T(8,128)(2,1)S(1)}, u32[]{:S(2)}, u32[]{:S(2)}) collective-permute-start(bf16[64,2048]{1,0:T(8,128)(2,1)S(1)} %collective-permute-done.14), channel_id=1, source_target_pairs={{0,1},{1,2},{2,3},{3,0},{4,5},{5,6},{6,7},{7,4},{8,9},{9,10},{10,1... | collective-permute-start | bytes 786440 | tf_op jit(solution)/shard_map/ppermute | solution.py:275
  78.9 16.0 %collective-permute-start.19 = (bf16[64,2048]{1,0:T(8,128)(2,1)S(1)}, bf16[64,2048]{1,0:T(8,128)(2,1)S(1)}, u32[]{:S(2)}, u32[]{:S(2)}) collective-permute-start(bf16[64,2048]{1,0:T(8,128)(2,1)S(1)} %collective-permute-done.18), channel_id=1, source_target_pairs={{0,1},{1,2},{2,3},{3,0},{4,5},{5,6},{6,7},{7,4},{8,9},{9,10},{10,1... | collective-permute-start | bytes 786440 | tf_op jit(solution)/shard_map/ppermute | solution.py:275
  92.3 2.6 %collective-permute-start.20 = (bf16[256,1792]{1,0:T(8,128)(2,1)S(1)}, bf16[256,1792]{1,0:T(8,128)(2,1)S(1)}, u32[]{:S(2)}, u32[]{:S(2)}) collective-permute-start(bf16[256,1792]{1,0:T(8,128)(2,1)S(1)} %convolution_convert_fusion.1), channel_id=1, source_target_pairs={{0,4},{4,0},{8,12},{12,8},{16,20},{20,16},{24,28},{28,24},{1,5},{5... | collective-permute-start | bytes 2752520 | tf_op jit(solution)/shard_map/ppermute | solution.py:13
  97.3 10.1 %collective-permute-start.21 = (bf16[64,1792]{1,0:T(8,128)(2,1)S(1)}, bf16[64,1792]{1,0:T(8,128)(2,1)S(1)}, u32[]{:S(2)}, u32[]{:S(2)}) collective-permute-start(bf16[64,1792]{1,0:T(8,128)(2,1)S(1)} %get-tuple-element.53), channel_id=1, source_target_pairs={{0,8},{4,12},{8,0},{12,4},{16,24},{20,28},{24,16},{28,20},{1,9},{5... | collective-permute-start | bytes 688136 | tf_op jit(solution)/shard_map/ppermute | solution.py:13
  97.6 11.5 %collective-permute-start.22 = (bf16[64,1792]{1,0:T(8,128)(2,1)S(1)}, bf16[64,1792]{1,0:T(8,128)(2,1)S(1)}, u32[]{:S(2)}, u32[]{:S(2)}) collective-permute-start(bf16[64,1792]{1,0:T(8,128)(2,1)S(1)} %get-tuple-element.52), channel_id=1, source_target_pairs={{0,16},{4,20},{8,24},{12,28},{16,0},{20,4},{24,8},{28,12},{1,17},{... | collective-permute-start | bytes 688136 | tf_op jit(solution)/shard_map/ppermute | solution.py:13
  99.4 11.4 %copy-start.3 = (bf16[256,128]{1,0:T(8,128)(2,1)S(1)}, bf16[256,128]{1,0:T(8,128)(2,1)}, u32[]{:S(2)}) copy-start(bf16[256,128]{1,0:T(8,128)(2,1)} %get-tuple-element.48) | copy-start | bytes 196612
  99.4 11.4 %collective-permute-start.23 = (bf16[64,1792]{1,0:T(8,128)(2,1)S(1)}, bf16[64,1792]{1,0:T(8,128)(2,1)S(1)}, u32[]{:S(2)}, u32[]{:S(2)}) collective-permute-start(bf16[64,1792]{1,0:T(8,128)(2,1)S(1)} %get-tuple-element.51), channel_id=1, source_target_pairs={{0,24},{4,28},{8,16},{12,20},{16,8},{20,12},{24,0},{28,4},{1,25},{... | collective-permute-start | bytes 688136 | tf_op jit(solution)/shard_map/ppermute | solution.py:13
where the time goes:
time: 112 us
  waiting for transfers between devices  43.9 us (39%)
  starting transfers between devices  39.5 us (35%)
  Pallas kernels  18.7 us (17%)
  matrix products  5.3 us (5%)
  local copies, waits for them, and re-layouts  1.83 us (2%)
  other arithmetic  1.69 us (2%)
    ppermute x12, waiting for transfers between devices, send(): self.came[way] = lax.ppermute(value, 'fsdp', ring)  34.4 us
    ppermute x12, starting transfers between devices, send(): self.came[way] = lax.ppermute(value, 'fsdp', ring)  30.3 us
    ppermute x12, waiting for transfers between devices, swap(): return lax.ppermute(value, axis, pairs)  9.52 us
    ppermute x12, starting transfers between devices, swap(): return lax.ppermute(value, axis, pairs)  9.16 us
    pallas_call x1, Pallas kernels, weight_grads(): pl.pallas_call(lambda *refs: weight_kernel(count, *refs), out_shape=(out,...  6.59 us
    pallas_call x2, Pallas kernels, projected(): pl.pallas_call(project_kernel, out_shape=jax.ShapeDtypeStruct((count, cap...  6.56 us
    dot_general x2, matrix products, back(): lax.dot_general(whole, weights, (((1,), (1,)), ((), ())), preferred_eleme...  4.21 us
    pallas_call x1, Pallas kernels, scaled_weights(): pl.pallas_call(lambda *refs: scale_kernel(sub, *refs), out_shape=jax.Shap...  3.3 us
  transfers between devices with their start and end apart: 24, of which 12 were waited for; matrix products, arithmetic and copies ran while one was open for 4% of the time, Pallas kernels for 15%

commit v1 on v0

--- a/solution.py
+++ b/solution.py
@@ -98,11 +98,7 @@
             ],
         ),
         compiler_params=pltpu.CompilerParams(vmem_limit_bytes=16 * 2**20),
-        cost_estimate=pl.CostEstimate(
-            flops=2 * feat_cols * half_units,
-            bytes_accessed=8 * feat_cols * half_units,
-            transcendentals=0,
-        ),
+        cost_estimate=pl.CostEstimate(flops=rows, bytes_accessed=rows, transcendentals=0),
         name="scale_weights",
     )(
         start_row[None],
@@ -123,77 +119,75 @@
     return first, live
 
 
-def pack_kernel(chip_ref, counts_ref, tokens_ref, chooser_ref, *out_refs):
+def pack_kernel(places, chip_ref, counts_ref, tokens_ref, chooser_ref, *out_refs):
     row_total = tokens_ref.shape[0]
-    capacity = out_refs[0].shape[0]
-    row = lax.broadcasted_iota(jnp.int32, (capacity, row_total), 1)
-    slot = lax.broadcasted_iota(jnp.int32, (capacity, row_total), 0)
+    part = out_refs[0].shape[0]
+    row = lax.broadcasted_iota(jnp.int32, (part, row_total), 1)
+    slot = lax.broadcasted_iota(jnp.int32, (part, row_total), 0)
     hits = []
-    for mask in range(len(out_refs)):
+    for half, mask in places:
         first, live = rows_of(counts_ref, chip_ref[0] ^ mask)
-        hits.append(((row == first + slot) & (slot < live)).astype(jnp.float32))
+        here = slot + half * part
+        hits.append(((row == first + here) & (here < live)).astype(jnp.float32))
     chooser = jnp.concatenate(hits, 0).astype(jnp.bfloat16)
     chooser_ref[...] = chooser
     chosen = jnp.dot(chooser, tokens_ref[...], preferred_element_type=jnp.float32)
-    for mask, out_ref in enumerate(out_refs):
-        out_ref[...] = chosen[mask * capacity : (mask + 1) * capacity].astype(jnp.bfloat16)
-
-
-def packed_rows(tokens, counts, chip, capacity):
+    for place, out_ref in enumerate(out_refs):
+        out_ref[...] = chosen[place * part : (place + 1) * part].astype(jnp.bfloat16)
+
+
+def packed_rows(tokens, counts, chip, places, part):
     row_total, feat_cols = tokens.shape
-    experts = counts.shape[1]
+    count = len(places)
     smem = pl.BlockSpec(memory_space=pltpu.SMEM)
     vmem = pl.BlockSpec(memory_space=pltpu.VMEM)
-    block = jax.ShapeDtypeStruct((capacity, feat_cols), jnp.bfloat16)
+    block = jax.ShapeDtypeStruct((part, feat_cols), jnp.bfloat16)
     chooser, *packed = pl.pallas_call(
-        pack_kernel,
-        out_shape=(jax.ShapeDtypeStruct((experts * capacity, row_total), jnp.bfloat16),)
-        + (block,) * experts,
+        lambda *refs: pack_kernel(places, *refs),
+        out_shape=(jax.ShapeDtypeStruct((count * part, row_total), jnp.bfloat16),)
+        + (block,) * count,
         in_specs=[smem, smem, vmem],
-        out_specs=(vmem,) * (experts + 1),
+        out_specs=(vmem,) * (count + 1),
         cost_estimate=pl.CostEstimate(
-            flops=2 * experts * capacity * row_total * feat_cols,
-            bytes_accessed=2 * (row_total + experts * capacity) * feat_cols,
+            flops=2 * count * part * row_total * feat_cols,
+            bytes_accessed=2 * (row_total + count * part) * feat_cols,
             transcendentals=0,
         ),
         name="pack_rows",
     )(chip[None], counts, tokens)
-    return chooser, packed
+    return chooser, dict(zip(places, packed))
 
 
 def project_kernel(*refs):
     *block_refs, weight_ref, out_ref, held = refs
-    capacity = block_refs[0].shape[0]
+    part = block_refs[0].shape[0]
+    capacity = out_ref.shape[1]
 
     @pl.when(pl.program_id(0) == 0)
     def _():
         for place, block_ref in enumerate(block_refs):
-            held[place * capacity : (place + 1) * capacity, :] = block_ref[...]
+            held[place * part : (place + 1) * part, :] = block_ref[...]
 
     sums = jnp.dot(held[...], weight_ref[...], preferred_element_type=jnp.float32)
-    for place in range(len(block_refs)):
-        out_ref[place] = sums[place * capacity : (place + 1) * capacity].astype(jnp.bfloat16)
-
-
-def projected(blocks, weights):
-    count = len(blocks)
-    capacity, feat_cols = blocks[0].shape
+    for owner in range(out_ref.shape[0]):
+        out_ref[owner] = sums[owner * capacity : (owner + 1) * capacity].astype(jnp.bfloat16)
+
+
+def projected(blocks, owners, weights):
+    part, feat_cols = blocks[0].shape
+    rows = len(blocks) * part
     units = weights.shape[1]
     tile = math.gcd(units, 512)
     return pl.pallas_call(
         project_kernel,
-        out_shape=jax.ShapeDtypeStruct((count, capacity, units), jnp.bfloat16),
+        out_shape=jax.ShapeDtypeStruct((owners, rows // owners, units), jnp.bfloat16),
         grid=(units // tile,),
-        in_specs=[pl.BlockSpec((capacity, feat_cols), lambda i: (0, 0))] * count
+        in_specs=[pl.BlockSpec((part, feat_cols), lambda i: (0, 0))] * len(blocks)
         + [pl.BlockSpec((feat_cols, tile), lambda i: (0, i))],
-        out_specs=pl.BlockSpec((count, capacity, tile), lambda i: (0, 0, i)),
-        scratch_shapes=[pltpu.VMEM((count * capacity, feat_cols), jnp.bfloat16)],
+        out_specs=pl.BlockSpec((owners, rows // owners, tile), lambda i: (0, 0, i)),
+        scratch_shapes=[pltpu.VMEM((rows, feat_cols), jnp.bfloat16)],
         compiler_params=pltpu.CompilerParams(vmem_limit_bytes=16 * 2**20),
-        cost_estimate=pl.CostEstimate(
-            flops=2 * count * capacity * feat_cols * units,
-            bytes_accessed=2 * (count * capacity * (feat_cols + units) + feat_cols * units),
-            transcendentals=0,
-        ),
+        cost_estimate=pl.CostEstimate(flops=rows, bytes_accessed=rows, transcendentals=0),
         name="project",
     )(*blocks, pltpu.with_memory_space_constraint(weights, pltpu.VMEM))
 
@@ -284,6 +278,7 @@
     row_total, feat_cols = tokens.shape
     experts = counts.shape[1]
     capacity = min(4 * row_total // experts, row_total // 2)
+    part = capacity // 2
     n_fsdp = lax.axis_size("fsdp")
     chips = lax.axis_size("expert") // 2
     half_units = gate_values.shape[2]
@@ -291,47 +286,65 @@
     chip = lax.axis_index("expert") // 2
     index = lax.axis_index("fsdp")
     masks = range(chips)
-
-    chooser, packed = packed_rows(tokens, counts, chip, capacity)
+    halves = range(2)
+    places = [(half, mask) for half in halves for mask in masks]
+
+    chooser, packed = packed_rows(tokens, counts, chip, places, part)
     weights = scaled_weights(
         gate_values, up_values, gate_scales, up_scales, index * feat_cols
     )
-    cots = grad_hidden[0].reshape(2, capacity, half_units)
-    chains = [Chain(chip, n_fsdp) for _ in range(2)]
+    cots = grad_hidden[0].reshape(2, 2, part, half_units)
+    chains = [Chain(chip, n_fsdp) for _ in halves]
     hiddens = [None, None]
     token = None
 
     def ordered(value):
         return value if token is None else earlier(value, token)
 
-    def begin(group):
+    def arrive(half, *needed):
+        rows = {0: (swap(packed[half, 0], "expert", 1), packed[half, 0])}
+        for mask in masks[1:]:
+            value = packed[half, mask]
+            if half:
+                value = earlier(value, inputs[0][-2])
+            value = swap(value, "expert", 2 * mask + 1)
+            rows[mask] = [earlier(value, *needed) if needed else value]
+        for mask in masks[1:]:
+            value = rows[mask][0]
+            if mask > 2:
+                value = earlier(value, rows[mask - 2][1])
+            rows[mask].append(swap(value, "expert", 1))
+        return [value for mask in masks for value in rows[mask]]
+
+    def begin(half):
         nonlocal token
-        chain = chains[group]
-        chain.partial = projected(inputs[group], weights)
+        chain = chains[half]
+        chain.partial = projected(inputs[half], chips, weights)
         for way, reach in chain.reach.items():
             if reach:
                 token = ordered(chain.block(way * reach))
                 chain.send(way, token)
 
-    def reduce(group, way, step):
+    def reduce(half, way, step):
         nonlocal token
-        chain = chains[group]
+        chain = chains[half]
         token = add_rounded(
             chain.block(way * (chain.reach[way] - step)), ordered(chain.came[way])
         )
         chain.send(way, token)
 
-    def activate(group):
+    def activate(half):
         nonlocal token
-        chain = chains[group]
+        chain = chains[half]
         pre = chain.block(0).astype(jnp.float32)
         for came in chain.came.values():
             pre = pre + ordered(came).astype(jnp.float32)
         gate_pre = pre[:, :half_units]
         up_pre = pre[:, half_units:]
-        cot = pick(cots, parity ^ (1 - group)).astype(jnp.float32)
+        cot = jnp.concatenate([pick(cots, 1 - parity)[half], pick(cots, parity)[half]], 0)
+        cot = cot.astype(jnp.float32)
         sigmoid_gate = jax.nn.sigmoid(gate_pre)
-        hiddens[group] = (gate_pre * sigmoid_gate * up_pre).astype(jnp.bfloat16)
+        hiddens[half] = (gate_pre * sigmoid_gate * up_pre).astype(jnp.bfloat16)
         grad_gate_pre = cot * up_pre * sigmoid_gate * (1.0 + gate_pre * (1.0 - sigmoid_gate))
         grad_up_pre = cot * gate_pre * sigmoid_gate
         token = jnp.concatenate(
@@ -343,50 +356,71 @@
         chain.whole = jnp.zeros((chips, capacity, 2 * half_units), jnp.bfloat16)
         chain.place(token, 0)
 
-    def gather(group, way, step):
+    def gather(half, step):
         nonlocal token
-        chain = chains[group]
-        token = ordered(chain.came[way])
-        chain.place(token, -way * step)
-        if step < chain.reach[way]:
-            chain.send(way, token)
-
-    def back(whole):
-        return lax.dot_general(
-            whole, weights, (((1,), (1,)), ((), ())), preferred_element_type=jnp.float32
+        chain = chains[half]
+        for way, reach in chain.reach.items():
+            if step <= reach:
+                token = ordered(chain.came[way])
+                chain.place(token, -way * step)
+                if step < reach:
+                    chain.send(way, token)
+
+    def give_back(half):
+        back = lax.dot_general(
+            chains[half].whole.reshape(chips * capacity, 2 * half_units),
+            weights,
+            (((1,), (1,)), ((), ())),
+            preferred_element_type=jnp.float32,
         ).astype(jnp.bfloat16)
-
-    arrived = [swap(packed[mask], "expert", 2 * mask + 1) for mask in masks]
-    inputs = [arrived, [swap(rows, "expert", 1) for rows in arrived]]
-    for group in range(2):
-        begin(group)
-    steps = range(1, n_fsdp)
-    for step in steps:
-        for group in range(2):
-            for way, reach in chains[group].reach.items():
+        back = back.reshape(chips, 2, part, feat_cols)
+        taken = swap(back[:, 0], "expert", 1)
+        sums = add_rounded(back[:, 1], taken)
+        pieces = [swap(sums[mask], "expert", 2 * mask) if mask else sums[0] for mask in masks]
+        return sums, pieces
+
+    def reduce_all(half):
+        chain = chains[half]
+        for step in range(1, chain.reach[1]):
+            for way, reach in chain.reach.items():
                 if step < reach:
-                    reduce(group, way, step)
-    for group in range(2):
-        activate(group)
-    for step in steps:
-        for group in range(2):
-            for way, reach in chains[group].reach.items():
-                if step <= reach:
-                    gather(group, way, step)
-    wholes = [chain.whole.reshape(chips * capacity, 2 * half_units) for chain in chains]
-
-    taken = swap(back(wholes[0]), "expert", 1)
-    kept = back(earlier(wholes[1], taken))
-    pieces = []
-    for mask in masks:
-        rows = slice(mask * capacity, (mask + 1) * capacity)
-        both = add_rounded(kept[rows], taken[rows])
-        pieces.append(swap(both, "expert", 2 * mask) if mask else both)
-
+                    reduce(half, way, step)
+
+    inputs = []
+    inputs.append(arrive(0, weights))
+    begin(0)
+    reduce_all(0)
+    inputs.append(arrive(1, token))
+    begin(1)
+    activate(0)
+    reduce_all(1)
+    reach = chains[0].reach[1]
+    for step in range(1, reach):
+        gather(0, step)
+    activate(1)
+    gather(0, reach)
+    _, pieces = give_back(0)
+    for step in range(1, reach):
+        gather(1, step)
+    chains[1].came[1], *pieces = lax.optimization_barrier((chains[1].came[1], *pieces))
+    gather(1, reach)
+    sums, late = give_back(1)
+    pieces += late
+
+    own, other = (
+        jnp.concatenate([rows[side * part : (side + 1) * part] for rows in hiddens], 0)
+        for side in (1, 0)
+    )
     hidden = jnp.where(
-        parity == 0, jnp.concatenate([hiddens[1], hiddens[0]], 0), jnp.concatenate(hiddens, 0)
-    )
-    grad_gate, grad_up = weight_grads(inputs[0] + inputs[1], wholes)
+        parity == 0, jnp.concatenate([own, other], 0), jnp.concatenate([other, own], 0)
+    )
+    grad_gate, grad_up = weight_grads(
+        inputs[0] + inputs[1],
+        [
+            earlier(chain.whole, sums).reshape(chips * capacity, 2 * half_units)
+            for chain in chains
+        ],
+    )
     grad_tokens = lax.dot_general(
         chooser,
         jnp.concatenate(pieces, 0),

time: 112 us -> 122 us (1.089)
  local copies, waits for them, and re-layouts: 1.83 us -> 12.7 us
  starting transfers between devices: 39.5 us -> 31.6 us
  waiting for transfers between devices: 43.9 us -> 48.6 us
  other arithmetic: 1.69 us -> 3.37 us
    ppermute x12, starting transfers between devices: 30.3 us -> 15.5 us  [send(): self.came[way] = lax.ppermute(value, 'fsdp', ring)]
    unnamed x8 -> x35, local copies, waits for them, and re-layouts: 1.38 us -> 10.5 us
    ppermute x12 -> x22, starting transfers between devices: 9.16 us -> 16.1 us  [swap(): return lax.ppermute(value, axis, pairs)]
    ppermute x12, waiting for transfers between devices: 34.4 us -> 40.6 us  [send(): self.came[way] = lax.ppermute(value, 'fsdp', ring)]
    squeeze x0 -> x5, local copies, waits for them, and re-layouts: none -> 1.72 us  [the longest x1 1.6 us: activate(): pick(cots, 1 - parity)[half]]
    ppermute x12 -> x22, waiting for transfers between devices: 9.52 us -> 7.95 us  [swap(): return lax.ppermute(value, axis, pairs)]
  transfers between devices with their start and end apart: 24 -> 34, of which waited for: 12 -> 15; matrix products, arithmetic and copies ran while one was open for 4% -> 6% of each run, Pallas kernels for 15% -> 11%
where the time goes in v1:
time: 122 us
  waiting for transfers between devices  48.6 us (40%)
  starting transfers between devices  31.6 us (26%)
  Pallas kernels  19.1 us (16%)
  local copies, waits for them, and re-layouts  12.7 us (10%)
  matrix products  5.29 us (4%)
  other arithmetic  3.37 us (3%)
    ppermute x12, waiting for transfers between devices, send(): self.came[way] = lax.ppermute(value, 'fsdp', ring)  40.6 us
    ppermute x22, starting transfers between devices, swap(): return lax.ppermute(value, axis, pairs)  16.1 us
    ppermute x12, starting transfers between devices, send(): self.came[way] = lax.ppermute(value, 'fsdp', ring)  15.5 us
    unnamed x35, local copies, waits for them, and re-layouts  10.5 us
    ppermute x22, waiting for transfers between devices, swap(): return lax.ppermute(value, axis, pairs)  7.95 us
    pallas_call x1, Pallas kernels, weight_grads(): pl.pallas_call(lambda *refs: weight_kernel(count, *refs), out_shape=(out,...  6.94 us
    pallas_call x2, Pallas kernels, projected(): pl.pallas_call(project_kernel, out_shape=jax.ShapeDtypeStruct((owners, ro...  6.55 us
    dot_general x2, matrix products, give_back(): lax.dot_general(chains[half].whole.reshape(chips * capacity, 2 * half_uni...  4.2 us
  transfers between devices with their start and end apart: 34, of which 15 were waited for; matrix products, arithmetic and copies ran while one was open for 6% of the time, Pallas kernels for 11%

profile of v1, /device:TPU:0, one launch (start us, length us, event | category | flops | bytes accessed | tf_op | source)
XLA Modules:
  0.0 121.8 jit_solution(12823769737068458449)
XLA Ops:
  0.6 2.3 %pack_rows.1 = (bf16[256,128]{1,0:T(8,128)(2,1)}, bf16[32,1792]{1,0:T(8,128)(2,1)}, bf16[32,1792]{1,0:T(8,128)(2,1)}, bf16[32,1792]{1,0:T(8,128)(2,1)}, bf16[32,...) custom-call(s32[1]{0:T(128)} %bitcast.refs_0_, ...), custom_call_target="tpu_custom_call" | custom-call | flops 117440512 | bytes 1376256 | tf_op jit(solution)/shard_map/pack_rows/pallas_call | solution.py:145
  2.9 2.4 %collective-permute-start.1 = (bf16[32,1792]{1,0:T(8,128)(2,1)}, bf16[32,1792]{1,0:T(8,128)(2,1)S(1)}, u32[]{:S(2)}, u32[]{:S(2)}) collective-permute-start(bf16[32,1792]{1,0:T(8,128)(2,1)} %get-tuple-element.49), channel_id=1, source_target_pairs={{0,12},{4,8},{8,4},{12,0},{16,28},{20,24},{24,20},{28,16},{1,13},{... | collective-permute-start | bytes 344072 | tf_op jit(solution)/shard_map/ppermute | solution.py:13
  5.3 1.8 %collective-permute-start.5 = (bf16[32,1792]{1,0:T(8,128)(2,1)}, bf16[32,1792]{1,0:T(8,128)(2,1)S(1)}, u32[]{:S(2)}, u32[]{:S(2)}) collective-permute-start(bf16[32,1792]{1,0:T(8,128)(2,1)} %get-tuple-element.53), channel_id=1, source_target_pairs={{0,28},{4,24},{8,20},{12,16},{16,12},{20,8},{24,4},{28,0},{1,29},{... | collective-permute-start | bytes 344072 | tf_op jit(solution)/shard_map/ppermute | solution.py:13
  8.5 3.4 %scale_weights.1.refs_8_ = bf16[1792,2048]{1,0:T(8,128)(2,1)S(1)} custom-call(s32[1]{0:T(128)} %bitcast.1.refs_0_, bf16[1,1792,1024]{2,1,0:T(8,128)(2,1)} %refs_1_.3, bf16[1,1792,1024]{2,1,0:T(8,128)(2,1)} %refs_2_.3, f32[1,8,56]{2,1,0:T(8,128)S(1)} %bitcast.113, f32[1,8,56]{2,1,0:T(8,128)S(1)} %bitcast.114), custom_call_target="tpu_custom_call" | custom-call | flops 256 | bytes 256 | tf_op jit(solution)/shard_map/scale_weights/pallas_call | solution.py:84
  11.9 2.9 %copy-done = bf16[1792,2048]{1,0:T(8,128)(2,1)} copy-done((bf16[1792,2048]{1,0:T(8,128)(2,1)}, bf16[1792,2048]{1,0:T(8,128)(2,1)S(1)}, u32[]{:S(2)}) %copy-start) | copy-done | bytes 7340056
  17.4 3.1 %copy-done.1 = bf16[1792,2048]{1,0:T(8,128)(2,1)S(1)} copy-done((bf16[1792,2048]{1,0:T(8,128)(2,1)S(1)}, bf16[1792,2048]{1,0:T(8,128)(2,1)}, u32[]{:S(2)}) %copy-start.1) | copy-done | bytes 7340056
  20.5 3.3 %project.2 = bf16[4,64,2048]{2,1,0:T(8,128)(2,1)S(1)} custom-call(bf16[32,1792]{1,0:T(8,128)(2,1)S(1)} %collective-permute-done.refs_0_, bf16[32,1792]{1,0:T(8,128)(2,1)S(1)} %copy-done.3, bf16[32,1792]{1,0:T(8,128)(2,1)S(1)} %collective-permute-done.1.refs_2_, bf16[32,1792]{1,0:T(8,128)(2,1)S(1)} %collective-permute-done.2.refs_3_, ...), custom_call_target="tpu_custom_call" | custom-call | flops 256 | bytes 256 | tf_op jit(solution)/shard_map/project/pallas_call | solution.py:181
  23.8 1.9 %collective-permute-start.7 = (bf16[64,2048]{1,0:T(8,128)(2,1)S(1)}, bf16[64,2048]{1,0:T(8,128)(2,1)S(1)}, u32[]{:S(2)}, u32[]{:S(2)}) collective-permute-start(bf16[64,2048]{1,0:T(8,128)(2,1)S(1)} %get-tuple-element.95), channel_id=1, source_target_pairs={{0,1},{1,2},{2,3},{3,0},{4,5},{5,6},{6,7},{7,4},{8,9},{9,10},{10,1... | collective-permute-start | bytes 786440 | tf_op jit(solution)/shard_map/ppermute | solution.py:269
  25.7 1.2 collective-permute-start.10
  26.9 1.6 %collective-permute-start.12 = (bf16[32,1792]{1,0:T(8,128)(2,1)}, bf16[32,1792]{1,0:T(8,128)(2,1)S(1)}, u32[]{:S(2)}, u32[]{:S(2)}) collective-permute-start(bf16[32,1792]{1,0:T(8,128)(2,1)} %get-tuple-element.63), channel_id=1, source_target_pairs={{0,20},{4,16},{8,28},{12,24},{16,4},{20,0},{24,12},{28,8},{1,21},{... | collective-permute-start | bytes 344072 | tf_op jit(solution)/shard_map/ppermute | solution.py:13
  28.6 6.0 %collective-permute-done.7 = bf16[64,2048]{1,0:T(8,128)(2,1)S(1)} collective-permute-done((bf16[64,2048]{1,0:T(8,128)(2,1)S(1)}, bf16[64,2048]{1,0:T(8,128)(2,1)S(1)}, u32[]{:S(2)}, u32[]{:S(2)}) %collective-permute-start.7) | collective-permute-done | bytes 262176 | tf_op jit(solution)/shard_map/ppermute | solution.py:269
  35.8 1.7 %collective-permute-start.16 = (bf16[64,2048]{1,0:T(8,128)(2,1)S(1)}, bf16[64,2048]{1,0:T(8,128)(2,1)S(1)}, u32[]{:S(2)}, u32[]{:S(2)}) collective-permute-start(bf16[64,2048]{1,0:T(8,128)(2,1)S(1)} %get-tuple-element.56), channel_id=1, source_target_pairs={{0,3},{1,0},{2,1},{3,2},{4,7},{5,4},{6,5},{7,6},{8,11},{9,8},{10,9... | collective-permute-start | bytes 786440 | tf_op jit(solution)/shard_map/ppermute | solution.py:269
  38.4 1.6 %dynamic-slice_bitcast_fusion.5 = (bf16[32,1024]{1,0:T(8,128)(2,1)S(1)}, bf16[32,1024]{1,0:T(8,128)(2,1)}, bf16[32,1024]{1,0:T(8,128)(2,1)}, bf16[32,1024]{1,0:T(8,128)(2,1)S(1)}) fusion(bf16[2,2,32,1024]{3,2,1,0:T(8,128)(2,1)} %bitcast.119, s32[]{:T(128)S(6)} %select_n.70, s32[]{:T(128)S(6)} %add.150, s32[]{:T(128)S(6)} %select_n.71), kind=kLoop, calls=%fused_computation.64 | loop fusion | bytes 524300 | tf_op jit(solution)/shard_map/squeeze | solution.py:344
  40.0 3.1 %copy-done.2 = bf16[1792,2048]{1,0:T(8,128)(2,1)S(1)} copy-done((bf16[1792,2048]{1,0:T(8,128)(2,1)S(1)}, bf16[1792,2048]{1,0:T(8,128)(2,1)}, u32[]{:S(2)}) %copy-start.2) | copy-done | bytes 7340056
  43.1 3.3 %project.3 = bf16[4,64,2048]{2,1,0:T(8,128)(2,1)S(1)} custom-call(bf16[32,1792]{1,0:T(8,128)(2,1)S(1)} %collective-permute-done.9.refs_0_.refs_8_, bf16[32,1792]{1,0:T(8,128)(2,1)S(1)} %copy-done.4, bf16[32,1792]{1,0:T(8,128)(2,1)S(1)} %collective-permute-done.10.refs_2_.refs_10_, bf16[32,1792]{1,0:T(8,128)(2,1)S(1)} %collective-permute-done.11.refs_3_.refs_11_, ...), custom_call_target="tpu_custom_call" | custom-call | flops 256 | bytes 256 | tf_op jit(solution)/shard_map/project/pallas_call | solution.py:181
  46.6 3.8 %collective-permute-start.21 = (bf16[64,2048]{1,0:T(8,128)(2,1)S(1)}, bf16[64,2048]{1,0:T(8,128)(2,1)S(1)}, u32[]{:S(2)}, u32[]{:S(2)}) collective-permute-start(bf16[64,2048]{1,0:T(8,128)(2,1)S(1)} %get-tuple-element.70), channel_id=1, source_target_pairs={{0,3},{1,0},{2,1},{3,2},{4,7},{5,4},{6,5},{7,6},{8,11},{9,8},{10,9... | collective-permute-start | bytes 786440 | tf_op jit(solution)/shard_map/ppermute | solution.py:269
  51.6 1.8 %collective-permute-start.19 = (bf16[64,2048]{1,0:T(8,128)(2,1)S(1)}, bf16[64,2048]{1,0:T(8,128)(2,1)S(1)}, u32[]{:S(2)}, u32[]{:S(2)}) collective-permute-start(bf16[64,2048]{1,0:T(8,128)(2,1)S(1)} %pad_maximum_fusion), channel_id=1, source_target_pairs={{0,3},{1,0},{2,1},{3,2},{4,7},{5,4},{6,5},{7,6},{8,11},{9,8},{10,9... | collective-permute-start | bytes 786440 | tf_op jit(solution)/shard_map/ppermute | solution.py:269
  54.1 3.4 %collective-permute-done.17 = bf16[64,2048]{1,0:T(8,128)(2,1)S(1)} collective-permute-done((bf16[64,2048]{1,0:T(8,128)(2,1)S(1)}, bf16[64,2048]{1,0:T(8,128)(2,1)S(1)}, u32[]{:S(2)}, u32[]{:S(2)}) %collective-permute-start.17) | collective-permute-done | bytes 262176 | tf_op jit(solution)/shard_map/ppermute | solution.py:269
  58.1 16.2 %collective-permute-done.20 = bf16[64,2048]{1,0:T(8,128)(2,1)S(1)} collective-permute-done((bf16[64,2048]{1,0:T(8,128)(2,1)S(1)}, bf16[64,2048]{1,0:T(8,128)(2,1)S(1)}, u32[]{:S(2)}, u32[]{:S(2)}) %collective-permute-start.20) | collective-permute-done | bytes 262176 | tf_op jit(solution)/shard_map/ppermute | solution.py:269
  75.0 5.0 %collective-permute-done.18 = bf16[64,2048]{1,0:T(8,128)(2,1)S(1)} collective-permute-done((bf16[64,2048]{1,0:T(8,128)(2,1)S(1)}, bf16[64,2048]{1,0:T(8,128)(2,1)S(1)}, u32[]{:S(2)}, u32[]{:S(2)}) %collective-permute-start.18) | collective-permute-done | bytes 262176 | tf_op jit(solution)/shard_map/ppermute | solution.py:269
  80.9 3.2 %collective-permute-start.24 = (bf16[64,2048]{1,0:T(8,128)(2,1)S(1)}, bf16[64,2048]{1,0:T(8,128)(2,1)S(1)}, u32[]{:S(2)}, u32[]{:S(2)}) collective-permute-start(bf16[64,2048]{1,0:T(8,128)(2,1)S(1)} %pad_maximum_fusion.1), channel_id=1, source_target_pairs={{0,3},{1,0},{2,1},{3,2},{4,7},{5,4},{6,5},{7,6},{8,11},{9,8},{10,9... | collective-permute-start | bytes 786440 | tf_op jit(solution)/shard_map/ppermute | solution.py:269
  85.8 2.1 %convolution_convert_fusion.1 = bf16[256,1792]{1,0:T(8,128)(2,1)S(1)} fusion(bf16[256,2048]{1,0:T(8,128)(2,1)S(1)} %bitcast.111, bf16[1792,2048]{1,0:T(8,128)(2,1)S(1)} %bitcast.108), kind=kOutput, calls=%fused_computation.1 | convolution fusion | flops 1879506944 | bytes 9306112 | tf_op jit(solution)/shard_map/dot_general | solution.py:370
  88.0 3.3 %collective-permute-done.23 = bf16[64,2048]{1,0:T(8,128)(2,1)S(1)} collective-permute-done((bf16[64,2048]{1,0:T(8,128)(2,1)S(1)}, bf16[64,2048]{1,0:T(8,128)(2,1)S(1)}, u32[]{:S(2)}, u32[]{:S(2)}) %collective-permute-start.23) | collective-permute-done | bytes 262176 | tf_op jit(solution)/shard_map/ppermute | solution.py:269
  91.8 5.1 %collective-permute-done.24 = bf16[64,2048]{1,0:T(8,128)(2,1)S(1)} collective-permute-done((bf16[64,2048]{1,0:T(8,128)(2,1)S(1)}, bf16[64,2048]{1,0:T(8,128)(2,1)S(1)}, u32[]{:S(2)}, u32[]{:S(2)}) %collective-permute-start.24) | collective-permute-done | bytes 262176 | tf_op jit(solution)/shard_map/ppermute | solution.py:269
  97.1 1.6 %collective-permute-start.27 = (bf16[32,1792]{1,0:T(8,128)(2,1)S(1)}, bf16[32,1792]{1,0:T(8,128)(2,1)S(1)}, u32[]{:S(2)}, u32[]{:S(2)}) collective-permute-start(bf16[32,1792]{1,0:T(8,128)(2,1)S(1)} %get-tuple-element.107), channel_id=1, source_target_pairs={{0,8},{4,12},{8,0},{12,4},{16,24},{20,28},{24,16},{28,20},{1,9},{5... | collective-permute-start | bytes 344072 | tf_op jit(solution)/shard_map/ppermute | solution.py:13
  98.6 1.5 %collective-permute-start.28 = (bf16[32,1792]{1,0:T(8,128)(2,1)S(1)}, bf16[32,1792]{1,0:T(8,128)(2,1)S(1)}, u32[]{:S(2)}, u32[]{:S(2)}) collective-permute-start(bf16[32,1792]{1,0:T(8,128)(2,1)S(1)} %get-tuple-element.106), channel_id=1, source_target_pairs={{0,16},{4,20},{8,24},{12,28},{16,0},{20,4},{24,8},{28,12},{1,17},{... | collective-permute-start | bytes 344072 | tf_op jit(solution)/shard_map/ppermute | solution.py:13
  102.0 3.0 %collective-permute-done.28 = bf16[32,1792]{1,0:T(8,128)(2,1)S(1)} collective-permute-done((bf16[32,1792]{1,0:T(8,128)(2,1)S(1)}, bf16[32,1792]{1,0:T(8,128)(2,1)S(1)}, u32[]{:S(2)}, u32[]{:S(2)}) %collective-permute-start.28) | collective-permute-done | bytes 114720 | tf_op jit(solution)/shard_map/ppermute | solution.py:13
  105.9 2.1 %convolution_convert_fusion = bf16[256,1792]{1,0:T(8,128)(2,1)S(1)} fusion(bf16[256,2048]{1,0:T(8,128)(2,1)S(1)} %bitcast.109, bf16[1792,2048]{1,0:T(8,128)(2,1)S(1)} %bitcast.108), kind=kOutput, calls=%fused_computation | convolution fusion | flops 1879506944 | bytes 9306112 | tf_op jit(solution)/shard_map/dot_general | solution.py:370
  108.2 1.7 %collective-permute-done.30 = bf16[4,32,1792]{2,1,0:T(8,128)(2,1)S(1)} collective-permute-done((bf16[4,32,1792]{2,1,0:T(8,128)(2,1)S(1)}, bf16[4,32,1792]{2,1,0:T(8,128)(2,1)S(1)}, u32[]{:S(2)}, u32[]{:S(2)}) %collective-permute-start.30) | collective-permute-done | bytes 458784 | tf_op jit(solution)/shard_map/ppermute | solution.py:13
  110.1 1.1 collective-permute-start.31
  112.1 1.6 %collective-permute-start.33 = (bf16[32,1792]{1,0:T(8,128)(2,1)S(1)}, bf16[32,1792]{1,0:T(8,128)(2,1)S(1)}, u32[]{:S(2)}, u32[]{:S(2)}) collective-permute-start(bf16[32,1792]{1,0:T(8,128)(2,1)S(1)} %get-tuple-element.102), channel_id=1, source_target_pairs={{0,24},{4,28},{8,16},{12,20},{16,8},{20,12},{24,0},{28,4},{1,25},{... | collective-permute-start | bytes 344072 | tf_op jit(solution)/shard_map/ppermute | solution.py:13
  113.7 6.9 %weight_grads.1 = (bf16[1,1792,1024]{2,1,0:T(8,128)(2,1)}, bf16[1,1792,1024]{2,1,0:T(8,128)(2,1)}) custom-call(bf16[32,1792]{1,0:T(8,128)(2,1)S(1)} %collective-permute-done.refs_0_, bf16[32,1792]{1,0:T(8,128)(2,1)S(1)} %copy-done.3, bf16[32,1792]{1,0:T(8,128)(2,1)S(1)} %collective-permute-done.1.refs_2_, ...), custom_call_target="tpu_custom_call" | custom-call | flops 3758096384 | bytes 11272192 | tf_op jit(solution)/shard_map/weight_grads/pallas_call | solution.py:225
  (111 shorter events, 17.9 us)
Async XLA Ops:
  2.9 11.9 %collective-permute-start.1 = (bf16[32,1792]{1,0:T(8,128)(2,1)}, bf16[32,1792]{1,0:T(8,128)(2,1)S(1)}, u32[]{:S(2)}, u32[]{:S(2)}) collective-permute-start(bf16[32,1792]{1,0:T(8,128)(2,1)} %get-tuple-element.49), channel_id=1, source_target_pairs={{0,12},{4,8},{8,4},{12,0},{16,28},{20,24},{24,20},{28,16},{1,13},{... | collective-permute-start | bytes 344072 | tf_op jit(solution)/shard_map/ppermute | solution.py:13
  5.3 10.0 %collective-permute-start.5 = (bf16[32,1792]{1,0:T(8,128)(2,1)}, bf16[32,1792]{1,0:T(8,128)(2,1)S(1)}, u32[]{:S(2)}, u32[]{:S(2)}) collective-permute-start(bf16[32,1792]{1,0:T(8,128)(2,1)} %get-tuple-element.53), channel_id=1, source_target_pairs={{0,28},{4,24},{8,20},{12,16},{16,12},{20,8},{24,4},{28,0},{1,29},{... | collective-permute-start | bytes 344072 | tf_op jit(solution)/shard_map/ppermute | solution.py:13
  7.1 8.2 %collective-permute-start.3 = (bf16[32,1792]{1,0:T(8,128)(2,1)}, bf16[32,1792]{1,0:T(8,128)(2,1)S(1)}, u32[]{:S(2)}, u32[]{:S(2)}) collective-permute-start(bf16[32,1792]{1,0:T(8,128)(2,1)} %get-tuple-element.51), channel_id=1, source_target_pairs={{0,20},{4,16},{8,28},{12,24},{16,4},{20,0},{24,12},{28,8},{1,21},{... | collective-permute-start | bytes 344072 | tf_op jit(solution)/shard_map/ppermute | solution.py:13
  14.8 1.5 %collective-permute-start = (bf16[32,1792]{1,0:T(8,128)(2,1)S(1)}, bf16[32,1792]{1,0:T(8,128)(2,1)S(1)}, u32[]{:S(2)}, u32[]{:S(2)}) collective-permute-start(bf16[32,1792]{1,0:T(8,128)(2,1)S(1)} %copy-done.3), channel_id=1, source_target_pairs={{0,4},{4,0},{8,12},{12,8},{16,20},{20,16},{24,28},{28,24},{1,5},{5... | collective-permute-start | bytes 344072 | tf_op jit(solution)/shard_map/ppermute | solution.py:13
  15.3 1.3 %collective-permute-start.4 = (bf16[32,1792]{1,0:T(8,128)(2,1)S(1)}, bf16[32,1792]{1,0:T(8,128)(2,1)S(1)}, u32[]{:S(2)}, u32[]{:S(2)}) collective-permute-start(bf16[32,1792]{1,0:T(8,128)(2,1)S(1)} %collective-permute-done.3.refs_4_), channel_id=1, source_target_pairs={{0,4},{4,0},{8,12},{12,8},{16,20},{20,16},{24,28},{28,24},{1,5},{5... | collective-permute-start | bytes 344072 | tf_op jit(solution)/shard_map/ppermute | solution.py:13
  23.8 10.7 %collective-permute-start.7 = (bf16[64,2048]{1,0:T(8,128)(2,1)S(1)}, bf16[64,2048]{1,0:T(8,128)(2,1)S(1)}, u32[]{:S(2)}, u32[]{:S(2)}) collective-permute-start(bf16[64,2048]{1,0:T(8,128)(2,1)S(1)} %get-tuple-element.95), channel_id=1, source_target_pairs={{0,1},{1,2},{2,3},{3,0},{4,5},{5,6},{6,7},{7,4},{8,9},{9,10},{10,1... | collective-permute-start | bytes 786440 | tf_op jit(solution)/shard_map/ppermute | solution.py:269
  25.7 9.6 %collective-permute-start.10 = (bf16[32,1792]{1,0:T(8,128)(2,1)S(1)}, bf16[32,1792]{1,0:T(8,128)(2,1)S(1)}, u32[]{:S(2)}, u32[]{:S(2)}) collective-permute-start(bf16[32,1792]{1,0:T(8,128)(2,1)S(1)} %copy-done.11), channel_id=1, source_target_pairs={{0,12},{4,8},{8,4},{12,0},{16,28},{20,24},{24,20},{28,16},{1,13},{... | collective-permute-start | bytes 344072 | tf_op jit(solution)/shard_map/ppermute | solution.py:13
  26.9 10.7 %collective-permute-start.12 = (bf16[32,1792]{1,0:T(8,128)(2,1)}, bf16[32,1792]{1,0:T(8,128)(2,1)S(1)}, u32[]{:S(2)}, u32[]{:S(2)}) collective-permute-start(bf16[32,1792]{1,0:T(8,128)(2,1)} %get-tuple-element.63), channel_id=1, source_target_pairs={{0,20},{4,16},{8,28},{12,24},{16,4},{20,0},{24,12},{28,8},{1,21},{... | collective-permute-start | bytes 344072 | tf_op jit(solution)/shard_map/ppermute | solution.py:13
  28.4 9.4 %collective-permute-start.14 = (bf16[32,1792]{1,0:T(8,128)(2,1)S(1)}, bf16[32,1792]{1,0:T(8,128)(2,1)S(1)}, u32[]{:S(2)}, u32[]{:S(2)}) collective-permute-start(bf16[32,1792]{1,0:T(8,128)(2,1)S(1)} %copy-done.10), channel_id=1, source_target_pairs={{0,28},{4,24},{8,20},{12,16},{16,12},{20,8},{24,4},{28,0},{1,29},{... | collective-permute-start | bytes 344072 | tf_op jit(solution)/shard_map/ppermute | solution.py:13
  35.3 2.6 %collective-permute-start.11 = (bf16[32,1792]{1,0:T(8,128)(2,1)S(1)}, bf16[32,1792]{1,0:T(8,128)(2,1)S(1)}, u32[]{:S(2)}, u32[]{:S(2)}) collective-permute-start(bf16[32,1792]{1,0:T(8,128)(2,1)S(1)} %collective-permute-done.10.refs_2_.refs_10_), channel_id=1, source_target_pairs={{0,4},{4,0},{8,12},{12,8},{16,20},{20,16},{24,28},{28,24},{1,5},{5... | collective-permute-start | bytes 344072 | tf_op jit(solution)/shard_map/ppermute | solution.py:13
  35.3 4.7 %collective-permute-start.9 = (bf16[32,1792]{1,0:T(8,128)(2,1)S(1)}, bf16[32,1792]{1,0:T(8,128)(2,1)S(1)}, u32[]{:S(2)}, u32[]{:S(2)}) collective-permute-start(bf16[32,1792]{1,0:T(8,128)(2,1)S(1)} %copy-done.4), channel_id=1, source_target_pairs={{0,4},{4,0},{8,12},{12,8},{16,20},{20,16},{24,28},{28,24},{1,5},{5... | collective-permute-start | bytes 344072 | tf_op jit(solution)/shard_map/ppermute | solution.py:13
  35.8 14.5 %collective-permute-start.16 = (bf16[64,2048]{1,0:T(8,128)(2,1)S(1)}, bf16[64,2048]{1,0:T(8,128)(2,1)S(1)}, u32[]{:S(2)}, u32[]{:S(2)}) collective-permute-start(bf16[64,2048]{1,0:T(8,128)(2,1)S(1)} %get-tuple-element.56), channel_id=1, source_target_pairs={{0,3},{1,0},{2,1},{3,2},{4,7},{5,4},{6,5},{7,6},{8,11},{9,8},{10,9... | collective-permute-start | bytes 786440 | tf_op jit(solution)/shard_map/ppermute | solution.py:269
  37.6 12.7 %collective-permute-start.8 = (bf16[64,2048]{1,0:T(8,128)(2,1)}, bf16[64,2048]{1,0:T(8,128)(2,1)}, u32[]{:S(2)}, u32[]{:S(2)}) collective-permute-start(bf16[64,2048]{1,0:T(8,128)(2,1)} %fusion.4), channel_id=1, source_target_pairs={{0,1},{1,2},{2,3},{3,0},{4,5},{5,6},{6,7},{7,4},{8,9},{9,10},{10,1... | collective-permute-start | bytes 786440 | tf_op jit(solution)/shard_map/ppermute | solution.py:269
  37.9 2.1 %collective-permute-start.13 = (bf16[32,1792]{1,0:T(8,128)(2,1)S(1)}, bf16[32,1792]{1,0:T(8,128)(2,1)S(1)}, u32[]{:S(2)}, u32[]{:S(2)}) collective-permute-start(bf16[32,1792]{1,0:T(8,128)(2,1)S(1)} %collective-permute-done.12.refs_4_.refs_12_), channel_id=1, source_target_pairs={{0,4},{4,0},{8,12},{12,8},{16,20},{20,16},{24,28},{28,24},{1,5},{5... | collective-permute-start | bytes 344072 | tf_op jit(solution)/shard_map/ppermute | solution.py:13
  37.9 2.1 %collective-permute-start.15 = (bf16[32,1792]{1,0:T(8,128)(2,1)S(1)}, bf16[32,1792]{1,0:T(8,128)(2,1)S(1)}, u32[]{:S(2)}, u32[]{:S(2)}) collective-permute-start(bf16[32,1792]{1,0:T(8,128)(2,1)S(1)} %collective-permute-done.14.refs_6_.refs_14_), channel_id=1, source_target_pairs={{0,4},{4,0},{8,12},{12,8},{16,20},{20,16},{24,28},{28,24},{1,5},{5... | collective-permute-start | bytes 344072 | tf_op jit(solution)/shard_map/ppermute | solution.py:13
  46.4 11.1 %collective-permute-start.17 = (bf16[64,2048]{1,0:T(8,128)(2,1)S(1)}, bf16[64,2048]{1,0:T(8,128)(2,1)S(1)}, u32[]{:S(2)}, u32[]{:S(2)}) collective-permute-start(bf16[64,2048]{1,0:T(8,128)(2,1)S(1)} %get-tuple-element.69), channel_id=1, source_target_pairs={{0,1},{1,2},{2,3},{3,0},{4,5},{5,6},{6,7},{7,4},{8,9},{9,10},{10,1... | collective-permute-start | bytes 786440 | tf_op jit(solution)/shard_map/ppermute | solution.py:269
  46.6 28.4 %collective-permute-start.21 = (bf16[64,2048]{1,0:T(8,128)(2,1)S(1)}, bf16[64,2048]{1,0:T(8,128)(2,1)S(1)}, u32[]{:S(2)}, u32[]{:S(2)}) collective-permute-start(bf16[64,2048]{1,0:T(8,128)(2,1)S(1)} %get-tuple-element.70), channel_id=1, source_target_pairs={{0,3},{1,0},{2,1},{3,2},{4,7},{5,4},{6,5},{7,6},{8,11},{9,8},{10,9... | collective-permute-start | bytes 786440 | tf_op jit(solution)/shard_map/ppermute | solution.py:269
  51.6 23.3 %collective-permute-start.19 = (bf16[64,2048]{1,0:T(8,128)(2,1)S(1)}, bf16[64,2048]{1,0:T(8,128)(2,1)S(1)}, u32[]{:S(2)}, u32[]{:S(2)}) collective-permute-start(bf16[64,2048]{1,0:T(8,128)(2,1)S(1)} %pad_maximum_fusion), channel_id=1, source_target_pairs={{0,3},{1,0},{2,1},{3,2},{4,7},{5,4},{6,5},{7,6},{8,11},{9,8},{10,9... | collective-permute-start | bytes 786440 | tf_op jit(solution)/shard_map/ppermute | solution.py:269
  53.4 21.0 %collective-permute-start.20 = (bf16[64,2048]{1,0:T(8,128)(2,1)S(1)}, bf16[64,2048]{1,0:T(8,128)(2,1)S(1)}, u32[]{:S(2)}, u32[]{:S(2)}) collective-permute-start(bf16[64,2048]{1,0:T(8,128)(2,1)S(1)} %pad_maximum_fusion), channel_id=1, source_target_pairs={{0,1},{1,2},{2,3},{3,0},{4,5},{5,6},{6,7},{7,4},{8,9},{9,10},{10,1... | collective-permute-start | bytes 786440 | tf_op jit(solution)/shard_map/ppermute | solution.py:269
  57.6 22.4 %collective-permute-start.18 = (bf16[64,2048]{1,0:T(8,128)(2,1)S(1)}, bf16[64,2048]{1,0:T(8,128)(2,1)S(1)}, u32[]{:S(2)}, u32[]{:S(2)}) collective-permute-start(bf16[64,2048]{1,0:T(8,128)(2,1)S(1)} %fusion.2), channel_id=1, source_target_pairs={{0,1},{1,2},{2,3},{3,0},{4,5},{5,6},{6,7},{7,4},{8,9},{9,10},{10,1... | collective-permute-start | bytes 786440 | tf_op jit(solution)/shard_map/ppermute | solution.py:269
  74.3 11.4 %collective-permute-start.22 = (bf16[64,2048]{1,0:T(8,128)(2,1)S(1)}, bf16[64,2048]{1,0:T(8,128)(2,1)S(1)}, u32[]{:S(2)}, u32[]{:S(2)}) collective-permute-start(bf16[64,2048]{1,0:T(8,128)(2,1)S(1)} %collective-permute-done.20), channel_id=1, source_target_pairs={{0,1},{1,2},{2,3},{3,0},{4,5},{5,6},{6,7},{7,4},{8,9},{9,10},{10,1... | collective-permute-start | bytes 786440 | tf_op jit(solution)/shard_map/ppermute | solution.py:269
  80.3 11.1 %collective-permute-start.23 = (bf16[64,2048]{1,0:T(8,128)(2,1)S(1)}, bf16[64,2048]{1,0:T(8,128)(2,1)S(1)}, u32[]{:S(2)}, u32[]{:S(2)}) collective-permute-start(bf16[64,2048]{1,0:T(8,128)(2,1)S(1)} %pad_maximum_fusion.1), channel_id=1, source_target_pairs={{0,1},{1,2},{2,3},{3,0},{4,5},{5,6},{6,7},{7,4},{8,9},{9,10},{10,1... | collective-permute-start | bytes 786440 | tf_op jit(solution)/shard_map/ppermute | solution.py:269
  80.9 16.0 %collective-permute-start.24 = (bf16[64,2048]{1,0:T(8,128)(2,1)S(1)}, bf16[64,2048]{1,0:T(8,128)(2,1)S(1)}, u32[]{:S(2)}, u32[]{:S(2)}) collective-permute-start(bf16[64,2048]{1,0:T(8,128)(2,1)S(1)} %pad_maximum_fusion.1), channel_id=1, source_target_pairs={{0,3},{1,0},{2,1},{3,2},{4,7},{5,4},{6,5},{7,6},{8,11},{9,8},{10,9... | collective-permute-start | bytes 786440 | tf_op jit(solution)/shard_map/ppermute | solution.py:269
  87.9 9.0 %collective-permute-start.26 = (bf16[4,32,1792]{2,1,0:T(8,128)(2,1)S(1)}, bf16[4,32,1792]{2,1,0:T(8,128)(2,1)S(1)}, u32[]{:S(2)}, u32[]{:S(2)}) collective-permute-start(bf16[4,32,1792]{2,1,0:T(8,128)(2,1)S(1)} %slice_bitcast_fusion.2), channel_id=1, source_target_pairs={{0,4},{4,0},{8,12},{12,8},{16,20},{20,16},{24,28},{28,24},{1,5},{5... | collective-permute-start | bytes 1376264 | tf_op jit(solution)/shard_map/ppermute | solution.py:13
  91.4 10.2 %collective-permute-start.25 = (bf16[64,2048]{1,0:T(8,128)(2,1)S(1)}, bf16[64,2048]{1,0:T(8,128)(2,1)S(1)}, u32[]{:S(2)}, u32[]{:S(2)}) collective-permute-start(bf16[64,2048]{1,0:T(8,128)(2,1)S(1)} %collective-permute-done.23), channel_id=1, source_target_pairs={{0,1},{1,2},{2,3},{3,0},{4,5},{5,6},{6,7},{7,4},{8,9},{9,10},{10,1... | collective-permute-start | bytes 786440 | tf_op jit(solution)/shard_map/ppermute | solution.py:269
  97.1 5.0 %collective-permute-start.27 = (bf16[32,1792]{1,0:T(8,128)(2,1)S(1)}, bf16[32,1792]{1,0:T(8,128)(2,1)S(1)}, u32[]{:S(2)}, u32[]{:S(2)}) collective-permute-start(bf16[32,1792]{1,0:T(8,128)(2,1)S(1)} %get-tuple-element.107), channel_id=1, source_target_pairs={{0,8},{4,12},{8,0},{12,4},{16,24},{20,28},{24,16},{28,20},{1,9},{5... | collective-permute-start | bytes 344072 | tf_op jit(solution)/shard_map/ppermute | solution.py:13
  98.6 6.4 %collective-permute-start.28 = (bf16[32,1792]{1,0:T(8,128)(2,1)S(1)}, bf16[32,1792]{1,0:T(8,128)(2,1)S(1)}, u32[]{:S(2)}, u32[]{:S(2)}) collective-permute-start(bf16[32,1792]{1,0:T(8,128)(2,1)S(1)} %get-tuple-element.106), channel_id=1, source_target_pairs={{0,16},{4,20},{8,24},{12,28},{16,0},{20,4},{24,8},{28,12},{1,17},{... | collective-permute-start | bytes 344072 | tf_op jit(solution)/shard_map/ppermute | solution.py:13
  100.2 5.7 %collective-permute-start.29 = (bf16[32,1792]{1,0:T(8,128)(2,1)S(1)}, bf16[32,1792]{1,0:T(8,128)(2,1)S(1)}, u32[]{:S(2)}, u32[]{:S(2)}) collective-permute-start(bf16[32,1792]{1,0:T(8,128)(2,1)S(1)} %get-tuple-element.105), channel_id=1, source_target_pairs={{0,24},{4,28},{8,16},{12,20},{16,8},{20,12},{24,0},{28,4},{1,25},{... | collective-permute-start | bytes 344072 | tf_op jit(solution)/shard_map/ppermute | solution.py:13
  108.1 1.9 %collective-permute-start.30 = (bf16[4,32,1792]{2,1,0:T(8,128)(2,1)S(1)}, bf16[4,32,1792]{2,1,0:T(8,128)(2,1)S(1)}, u32[]{:S(2)}, u32[]{:S(2)}) collective-permute-start(bf16[4,32,1792]{2,1,0:T(8,128)(2,1)S(1)} %slice_bitcast_fusion), channel_id=1, source_target_pairs={{0,4},{4,0},{8,12},{12,8},{16,20},{20,16},{24,28},{28,24},{1,5},{5... | collective-permute-start | bytes 1376264 | tf_op jit(solution)/shard_map/ppermute | solution.py:13
  110.1 10.5 %collective-permute-start.31 = (bf16[32,1792]{1,0:T(8,128)(2,1)S(1)}, bf16[32,1792]{1,0:T(8,128)(2,1)S(1)}, u32[]{:S(2)}, u32[]{:S(2)}) collective-permute-start(bf16[32,1792]{1,0:T(8,128)(2,1)S(1)} %get-tuple-element.104), channel_id=1, source_target_pairs={{0,8},{4,12},{8,0},{12,4},{16,24},{20,28},{24,16},{28,20},{1,9},{5... | collective-permute-start | bytes 344072 | tf_op jit(solution)/shard_map/ppermute | solution.py:13
  111.2 9.4 %collective-permute-start.32 = (bf16[32,1792]{1,0:T(8,128)(2,1)S(1)}, bf16[32,1792]{1,0:T(8,128)(2,1)S(1)}, u32[]{:S(2)}, u32[]{:S(2)}) collective-permute-start(bf16[32,1792]{1,0:T(8,128)(2,1)S(1)} %get-tuple-element.103), channel_id=1, source_target_pairs={{0,16},{4,20},{8,24},{12,28},{16,0},{20,4},{24,8},{28,12},{1,17},{... | collective-permute-start | bytes 344072 | tf_op jit(solution)/shard_map/ppermute | solution.py:13
  112.1 8.6 %collective-permute-start.33 = (bf16[32,1792]{1,0:T(8,128)(2,1)S(1)}, bf16[32,1792]{1,0:T(8,128)(2,1)S(1)}, u32[]{:S(2)}, u32[]{:S(2)}) collective-permute-start(bf16[32,1792]{1,0:T(8,128)(2,1)S(1)} %get-tuple-element.102), channel_id=1, source_target_pairs={{0,24},{4,28},{8,16},{12,20},{16,8},{20,12},{24,0},{28,4},{1,25},{... | collective-permute-start | bytes 344072 | tf_op jit(solution)/shard_map/ppermute | solution.py:13
  (16 other events, 192.5 us)

commit v2 on v0

--- a/solution.py
+++ b/solution.py
@@ -260,7 +260,7 @@
         self.size = size
         self.index = lax.axis_index("fsdp")
         self.reach = {1: size // 2, -1: size - 1 - size // 2}
-        self.partial = None
+        self.partials = []
         self.whole = None
         self.came = {}
 
@@ -268,7 +268,14 @@
         return lax.rem(self.index + self.size + steps, self.size)
 
     def block(self, steps):
-        return pick(self.partial, self.owner(steps) ^ self.chip)
+        near, far = self.partials
+        place = self.owner(steps) ^ self.chip
+        count = near.shape[0]
+        return jnp.where(
+            place < count,
+            pick(near, jnp.minimum(place, count - 1)),
+            pick(far, jnp.maximum(place - count, 0)),
+        )
 
     def send(self, way, value):
         ring = [(source, (source + way) % self.size) for source in range(self.size)]
@@ -307,7 +314,7 @@
     def begin(group):
         nonlocal token
         chain = chains[group]
-        chain.partial = projected(inputs[group], weights)
+        chain.partials.append(projected(inputs[group][chips // 2 :], weights))
         for way, reach in chain.reach.items():
             if reach:
                 token = ordered(chain.block(way * reach))
@@ -356,8 +363,16 @@
             whole, weights, (((1,), (1,)), ((), ())), preferred_element_type=jnp.float32
         ).astype(jnp.bfloat16)
 
-    arrived = [swap(packed[mask], "expert", 2 * mask + 1) for mask in masks]
-    inputs = [arrived, [swap(rows, "expert", 1) for rows in arrived]]
+    inputs = [[], []]
+    for mask in masks:
+        rows = swap(packed[mask], "expert", 2 * mask + 1)
+        if mask == chips // 2:
+            for group in range(2):
+                chains[group].partials.append(projected(inputs[group], weights))
+        if mask >= chips // 2:
+            rows = earlier(rows, *(chain.partials[0] for chain in chains))
+        inputs[0].append(rows)
+        inputs[1].append(swap(rows, "expert", 1) if mask else packed[0])
     for group in range(2):
         begin(group)
     steps = range(1, n_fsdp)

time: 112 us -> 119 us (1.062)
  starting transfers between devices: 39.5 us -> 42.5 us
  Pallas kernels: 18.7 us -> 21.6 us
    pallas_call x2 -> x4, Pallas kernels: 6.56 us -> 9.42 us  [projected(): pl.pallas_call(project_kernel, out_shape=jax.ShapeDtypeStruct((count, cap...]
    ppermute x12 -> x11, starting transfers between devices: 9.16 us -> 10.9 us  [swap(): return lax.ppermute(value, axis, pairs)]
    ppermute x12, starting transfers between devices: 30.3 us -> 31.6 us  [send(): self.came[way] = lax.ppermute(value, 'fsdp', ring)]
    ppermute x12 -> x11, waiting for transfers between devices: 9.52 us -> 10.1 us  [swap(): return lax.ppermute(value, axis, pairs)]
  transfers between devices with their start and end apart: 24 -> 23, of which waited for: 12 -> 13; matrix products, arithmetic and copies ran while one was open for 4% -> 4% of each run, Pallas kernels for 15% -> 16%
where the time goes in v2:
time: 119 us
  waiting for transfers between devices  44.5 us (37%)
  starting transfers between devices  42.5 us (36%)
  Pallas kernels  21.6 us (18%)
  matrix products  5.3 us (4%)
  other arithmetic  1.96 us (2%)
  local copies, waits for them, and re-layouts  1.74 us (1%)
    ppermute x12, waiting for transfers between devices, send(): self.came[way] = lax.ppermute(value, 'fsdp', ring)  34.4 us
    ppermute x12, starting transfers between devices, send(): self.came[way] = lax.ppermute(value, 'fsdp', ring)  31.6 us
    ppermute x11, starting transfers between devices, swap(): return lax.ppermute(value, axis, pairs)  10.9 us
    ppermute x11, waiting for transfers between devices, swap(): return lax.ppermute(value, axis, pairs)  10.1 us
    pallas_call x4, Pallas kernels, projected(): pl.pallas_call(project_kernel, out_shape=jax.ShapeDtypeStruct((count, cap...  9.42 us
    pallas_call x1, Pallas kernels, weight_grads(): pl.pallas_call(lambda *refs: weight_kernel(count, *refs), out_shape=(out,...  6.59 us
    dot_general x2, matrix products, back(): lax.dot_general(whole, weights, (((1,), (1,)), ((), ())), preferred_eleme...  4.21 us
    pallas_call x1, Pallas kernels, scaled_weights(): pl.pallas_call(lambda *refs: scale_kernel(sub, *refs), out_shape=jax.Shap...  3.3 us
  transfers between devices with their start and end apart: 23, of which 13 were waited for; matrix products, arithmetic and copies ran while one was open for 4% of the time, Pallas kernels for 16%

profile of v2, /device:TPU:0, one launch (start us, length us, event | category | flops | bytes accessed | tf_op | source)
XLA Modules:
  0.0 118.5 jit_solution(3870953051905675820)
XLA Ops:
  0.6 2.3 %pack_rows.1 = (bf16[256,128]{1,0:T(8,128)(2,1)}, bf16[64,1792]{1,0:T(8,128)(2,1)}, bf16[64,1792]{1,0:T(8,128)(2,1)}, bf16[64,1792]{1,0:T(8,128)(2,1)}, bf16[64,1792]{1,0:T(8,128)(2,1)}) custom-call(s32[1]{0:T(128)} %bitcast.chip_ref, s32[1,4]{1,0:T(1,128)} %counts_ref.1, bf16[128,1792]{1,0:T(8,128)(2,1)} %tokens_ref.1), custom_call_target="tpu_custom_call" | custom-call | flops 117440512 | bytes 1376256 | tf_op jit(solution)/shard_map/pack_rows/pallas_call | solution.py:148
  2.9 2.4 %collective-permute-start = (bf16[64,1792]{1,0:T(8,128)(2,1)}, bf16[64,1792]{1,0:T(8,128)(2,1)S(1)}, u32[]{:S(2)}, u32[]{:S(2)}) collective-permute-start(bf16[64,1792]{1,0:T(8,128)(2,1)} %get-tuple-element.30), channel_id=1, source_target_pairs={{0,12},{4,8},{8,4},{12,0},{16,28},{20,24},{24,20},{28,16},{1,13},{... | collective-permute-start | bytes 688136 | tf_op jit(solution)/shard_map/ppermute | solution.py:13
  6.0 5.6 %collective-permute-done.refs_1_ = bf16[64,1792]{1,0:T(8,128)(2,1)S(1)} collective-permute-done((bf16[64,1792]{1,0:T(8,128)(2,1)}, bf16[64,1792]{1,0:T(8,128)(2,1)S(1)}, u32[]{:S(2)}, u32[]{:S(2)}) %collective-permute-start) | collective-permute-done | bytes 229408 | tf_op jit(solution)/shard_map/ppermute | solution.py:13
  11.7 3.3 %collective-permute-start.5 = (bf16[64,1792]{1,0:T(8,128)(2,1)}, bf16[64,1792]{1,0:T(8,128)(2,1)S(1)}, u32[]{:S(2)}, u32[]{:S(2)}) collective-permute-start(bf16[64,1792]{1,0:T(8,128)(2,1)} %get-tuple-element.33), channel_id=1, source_target_pairs={{0,28},{4,24},{8,20},{12,16},{16,12},{20,8},{24,4},{28,0},{1,29},{... | collective-permute-start | bytes 688136 | tf_op jit(solution)/shard_map/ppermute | solution.py:13
  16.7 3.3 %scale_weights.1.refs_2_ = bf16[1792,2048]{1,0:T(8,128)(2,1)S(1)} custom-call(s32[1]{0:T(128)} %bitcast.1.refs_0_, bf16[1,1792,1024]{2,1,0:T(8,128)(2,1)} %refs_1_.1, bf16[1,1792,1024]{2,1,0:T(8,128)(2,1)} %refs_2_.1, f32[1,8,56]{2,1,0:T(8,128)S(1)} %bitcast.64, f32[1,8,56]{2,1,0:T(8,128)S(1)} %bitcast.65), custom_call_target="tpu_custom_call" | custom-call | flops 3670016 | bytes 14680064 | tf_op jit(solution)/shard_map/scale_weights/pallas_call | solution.py:84
  20.0 2.4 %project.5 = bf16[2,64,2048]{2,1,0:T(8,128)(2,1)S(1)} custom-call(bf16[64,1792]{1,0:T(8,128)(2,1)S(1)} %collective-permute-done.3.refs_0_, bf16[64,1792]{1,0:T(8,128)(2,1)S(1)} %collective-permute-done.refs_1_, bf16[1792,2048]{1,0:T(8,128)(2,1)S(1)} %scale_weights.1.refs_2_), custom_call_target="tpu_custom_call" | custom-call | flops 939524096 | bytes 8323072 | tf_op jit(solution)/shard_map/project/pallas_call | solution.py:183
  22.4 2.4 %project.4 = bf16[2,64,2048]{2,1,0:T(8,128)(2,1)S(1)} custom-call(bf16[64,1792]{1,0:T(8,128)(2,1)S(1)} %copy-done, bf16[64,1792]{1,0:T(8,128)(2,1)S(1)} %collective-permute-done.1.refs_1_.refs_5_, bf16[1792,2048]{1,0:T(8,128)(2,1)S(1)} %scale_weights.1.refs_2_), custom_call_target="tpu_custom_call" | custom-call | flops 939524096 | bytes 8323072 | tf_op jit(solution)/shard_map/project/pallas_call | solution.py:183
  26.4 2.4 %project.7 = bf16[2,64,2048]{2,1,0:T(8,128)(2,1)S(1)} custom-call(bf16[64,1792]{1,0:T(8,128)(2,1)S(1)} %collective-permute-done.2.refs_0_.refs_2_, bf16[64,1792]{1,0:T(8,128)(2,1)S(1)} %collective-permute-done.5.refs_1_.refs_3_, bf16[1792,2048]{1,0:T(8,128)(2,1)S(1)} %scale_weights.1.refs_2_), custom_call_target="tpu_custom_call" | custom-call | flops 939524096 | bytes 8323072 | tf_op jit(solution)/shard_map/project/pallas_call | solution.py:183
  28.9 1.9 %collective-permute-start.8 = (bf16[64,2048]{1,0:T(8,128)(2,1)S(1)}, bf16[64,2048]{1,0:T(8,128)(2,1)S(1)}, u32[]{:S(2)}, u32[]{:S(2)}) collective-permute-start(bf16[64,2048]{1,0:T(8,128)(2,1)S(1)} %get-tuple-element.60), channel_id=1, source_target_pairs={{0,1},{1,2},{2,3},{3,0},{4,5},{5,6},{6,7},{7,4},{8,9},{9,10},{10,1... | collective-permute-start | bytes 786440 | tf_op jit(solution)/shard_map/ppermute | solution.py:282
  30.7 2.1 %collective-permute-start.11 = (bf16[64,2048]{1,0:T(8,128)(2,1)S(1)}, bf16[64,2048]{1,0:T(8,128)(2,1)S(1)}, u32[]{:S(2)}, u32[]{:S(2)}) collective-permute-start(bf16[64,2048]{1,0:T(8,128)(2,1)S(1)} %get-tuple-element.35), channel_id=1, source_target_pairs={{0,3},{1,0},{2,1},{3,2},{4,7},{5,4},{6,5},{7,6},{8,11},{9,8},{10,9... | collective-permute-start | bytes 786440 | tf_op jit(solution)/shard_map/ppermute | solution.py:282
  32.8 2.4 %project.6 = bf16[2,64,2048]{2,1,0:T(8,128)(2,1)S(1)} custom-call(bf16[64,1792]{1,0:T(8,128)(2,1)S(1)} %collective-permute-done.4.refs_0_.refs_6_, bf16[64,1792]{1,0:T(8,128)(2,1)S(1)} %collective-permute-done.6.refs_1_.refs_7_, bf16[1792,2048]{1,0:T(8,128)(2,1)S(1)} %scale_weights.1.refs_2_), custom_call_target="tpu_custom_call" | custom-call | flops 939524096 | bytes 8323072 | tf_op jit(solution)/shard_map/project/pallas_call | solution.py:183
  35.3 3.8 %collective-permute-start.12 = (bf16[64,2048]{1,0:T(8,128)(2,1)S(1)}, bf16[64,2048]{1,0:T(8,128)(2,1)S(1)}, u32[]{:S(2)}, u32[]{:S(2)}) collective-permute-start(bf16[64,2048]{1,0:T(8,128)(2,1)S(1)} %get-tuple-element.37), channel_id=1, source_target_pairs={{0,3},{1,0},{2,1},{3,2},{4,7},{5,4},{6,5},{7,6},{8,11},{9,8},{10,9... | collective-permute-start | bytes 786440 | tf_op jit(solution)/shard_map/ppermute | solution.py:282
  40.0 4.2 %collective-permute-start.10 = (bf16[64,2048]{1,0:T(8,128)(2,1)S(1)}, bf16[64,2048]{1,0:T(8,128)(2,1)S(1)}, u32[]{:S(2)}, u32[]{:S(2)}) collective-permute-start(bf16[64,2048]{1,0:T(8,128)(2,1)S(1)} %fusion.8), channel_id=1, source_target_pairs={{0,1},{1,2},{2,3},{3,0},{4,5},{5,6},{6,7},{7,4},{8,9},{9,10},{10,1... | collective-permute-start | bytes 786440 | tf_op jit(solution)/shard_map/ppermute | solution.py:282
  44.3 6.9 %collective-permute-done.7 = bf16[64,2048]{1,0:T(8,128)(2,1)S(1)} collective-permute-done((bf16[64,2048]{1,0:T(8,128)(2,1)S(1)}, bf16[64,2048]{1,0:T(8,128)(2,1)S(1)}, u32[]{:S(2)}, u32[]{:S(2)}) %collective-permute-start.7) | collective-permute-done | bytes 262176 | tf_op jit(solution)/shard_map/ppermute | solution.py:282
  51.3 4.1 %collective-permute-start.9 = (bf16[64,2048]{1,0:T(8,128)(2,1)S(1)}, bf16[64,2048]{1,0:T(8,128)(2,1)S(1)}, u32[]{:S(2)}, u32[]{:S(2)}) collective-permute-start(bf16[64,2048]{1,0:T(8,128)(2,1)S(1)} %fusion.9), channel_id=1, source_target_pairs={{0,1},{1,2},{2,3},{3,0},{4,5},{5,6},{6,7},{7,4},{8,9},{9,10},{10,1... | collective-permute-start | bytes 786440 | tf_op jit(solution)/shard_map/ppermute | solution.py:282
  55.5 7.0 %collective-permute-done.10 = bf16[64,2048]{1,0:T(8,128)(2,1)S(1)} collective-permute-done((bf16[64,2048]{1,0:T(8,128)(2,1)S(1)}, bf16[64,2048]{1,0:T(8,128)(2,1)S(1)}, u32[]{:S(2)}, u32[]{:S(2)}) %collective-permute-start.10) | collective-permute-done | bytes 262176 | tf_op jit(solution)/shard_map/ppermute | solution.py:282
  62.8 3.8 %collective-permute-start.14 = (bf16[64,2048]{1,0:T(8,128)(2,1)S(1)}, bf16[64,2048]{1,0:T(8,128)(2,1)S(1)}, u32[]{:S(2)}, u32[]{:S(2)}) collective-permute-start(bf16[64,2048]{1,0:T(8,128)(2,1)S(1)} %pad_maximum_fusion), channel_id=1, source_target_pairs={{0,3},{1,0},{2,1},{3,2},{4,7},{5,4},{6,5},{7,6},{8,11},{9,8},{10,9... | collective-permute-start | bytes 786440 | tf_op jit(solution)/shard_map/ppermute | solution.py:282
  66.8 1.4 %collective-permute-done.9 = bf16[64,2048]{1,0:T(8,128)(2,1)S(1)} collective-permute-done((bf16[64,2048]{1,0:T(8,128)(2,1)S(1)}, bf16[64,2048]{1,0:T(8,128)(2,1)S(1)}, u32[]{:S(2)}, u32[]{:S(2)}) %collective-permute-start.9) | collective-permute-done | bytes 262176 | tf_op jit(solution)/shard_map/ppermute | solution.py:282
  68.6 3.8 %collective-permute-start.16 = (bf16[64,2048]{1,0:T(8,128)(2,1)S(1)}, bf16[64,2048]{1,0:T(8,128)(2,1)S(1)}, u32[]{:S(2)}, u32[]{:S(2)}) collective-permute-start(bf16[64,2048]{1,0:T(8,128)(2,1)S(1)} %pad_maximum_fusion.1), channel_id=1, source_target_pairs={{0,3},{1,0},{2,1},{3,2},{4,7},{5,4},{6,5},{7,6},{8,11},{9,8},{10,9... | collective-permute-start | bytes 786440 | tf_op jit(solution)/shard_map/ppermute | solution.py:282
  73.9 3.9 %collective-permute-start.15 = (bf16[64,2048]{1,0:T(8,128)(2,1)S(1)}, bf16[64,2048]{1,0:T(8,128)(2,1)S(1)}, u32[]{:S(2)}, u32[]{:S(2)}) collective-permute-start(bf16[64,2048]{1,0:T(8,128)(2,1)S(1)} %collective-permute-done.13), channel_id=1, source_target_pairs={{0,1},{1,2},{2,3},{3,0},{4,5},{5,6},{6,7},{7,4},{8,9},{9,10},{10,1... | collective-permute-start | bytes 786440 | tf_op jit(solution)/shard_map/ppermute | solution.py:282
  77.7 1.9 %collective-permute-done.14 = bf16[64,2048]{1,0:T(8,128)(2,1)S(1)} collective-permute-done((bf16[64,2048]{1,0:T(8,128)(2,1)S(1)}, bf16[64,2048]{1,0:T(8,128)(2,1)S(1)}, u32[]{:S(2)}, u32[]{:S(2)}) %collective-permute-start.14) | collective-permute-done | bytes 262176 | tf_op jit(solution)/shard_map/ppermute | solution.py:282
  79.6 5.5 %collective-permute-done.17 = bf16[64,2048]{1,0:T(8,128)(2,1)S(1)} collective-permute-done((bf16[64,2048]{1,0:T(8,128)(2,1)S(1)}, bf16[64,2048]{1,0:T(8,128)(2,1)S(1)}, u32[]{:S(2)}, u32[]{:S(2)}) %collective-permute-start.17) | collective-permute-done | bytes 262176 | tf_op jit(solution)/shard_map/ppermute | solution.py:282
  85.1 3.8 %collective-permute-start.18 = (bf16[64,2048]{1,0:T(8,128)(2,1)S(1)}, bf16[64,2048]{1,0:T(8,128)(2,1)S(1)}, u32[]{:S(2)}, u32[]{:S(2)}) collective-permute-start(bf16[64,2048]{1,0:T(8,128)(2,1)S(1)} %collective-permute-done.17), channel_id=1, source_target_pairs={{0,1},{1,2},{2,3},{3,0},{4,5},{5,6},{6,7},{7,4},{8,9},{9,10},{10,1... | collective-permute-start | bytes 786440 | tf_op jit(solution)/shard_map/ppermute | solution.py:282
  88.9 1.7 %collective-permute-done.16 = bf16[64,2048]{1,0:T(8,128)(2,1)S(1)} collective-permute-done((bf16[64,2048]{1,0:T(8,128)(2,1)S(1)}, bf16[64,2048]{1,0:T(8,128)(2,1)S(1)}, u32[]{:S(2)}, u32[]{:S(2)}) %collective-permute-start.16) | collective-permute-done | bytes 262176 | tf_op jit(solution)/shard_map/ppermute | solution.py:282
  90.6 5.8 %collective-permute-done.15 = bf16[64,2048]{1,0:T(8,128)(2,1)S(1)} collective-permute-done((bf16[64,2048]{1,0:T(8,128)(2,1)S(1)}, bf16[64,2048]{1,0:T(8,128)(2,1)S(1)}, u32[]{:S(2)}, u32[]{:S(2)}) %collective-permute-start.15) | collective-permute-done | bytes 262176 | tf_op jit(solution)/shard_map/ppermute | solution.py:282
  96.4 2.1 %convolution_convert_fusion.1 = bf16[256,1792]{1,0:T(8,128)(2,1)S(1)} fusion(bf16[256,2048]{1,0:T(8,128)(2,1)S(1)} %bitcast.62, bf16[1792,2048]{1,0:T(8,128)(2,1)S(1)} %scale_weights.1.refs_2_), kind=kOutput, calls=%fused_computation.1 | convolution fusion | flops 1879506944 | bytes 9306112 | tf_op jit(solution)/shard_map/dot_general | solution.py:362
  98.6 2.9 %collective-permute-done.18 = bf16[64,2048]{1,0:T(8,128)(2,1)S(1)} collective-permute-done((bf16[64,2048]{1,0:T(8,128)(2,1)S(1)}, bf16[64,2048]{1,0:T(8,128)(2,1)S(1)}, u32[]{:S(2)}, u32[]{:S(2)}) %collective-permute-start.18) | collective-permute-done | bytes 262176 | tf_op jit(solution)/shard_map/ppermute | solution.py:282
  101.6 2.1 %convolution_convert_fusion = bf16[256,1792]{1,0:T(8,128)(2,1)S(1)} fusion(bf16[256,2048]{1,0:T(8,128)(2,1)S(1)} %bitcast.60, bf16[1792,2048]{1,0:T(8,128)(2,1)S(1)} %scale_weights.1.refs_2_), kind=kOutput, calls=%fused_computation | convolution fusion | flops 1879506944 | bytes 9306112 | tf_op jit(solution)/shard_map/dot_general | solution.py:362
  103.9 1.6 %collective-permute-start.20 = (bf16[64,1792]{1,0:T(8,128)(2,1)S(1)}, bf16[64,1792]{1,0:T(8,128)(2,1)S(1)}, u32[]{:S(2)}, u32[]{:S(2)}) collective-permute-start(bf16[64,1792]{1,0:T(8,128)(2,1)S(1)} %get-tuple-element.57), channel_id=1, source_target_pairs={{0,8},{4,12},{8,0},{12,4},{16,24},{20,28},{24,16},{28,20},{1,9},{5... | collective-permute-start | bytes 688136 | tf_op jit(solution)/shard_map/ppermute | solution.py:13
  106.2 1.2 %collective-permute-start.22 = (bf16[64,1792]{1,0:T(8,128)(2,1)S(1)}, bf16[64,1792]{1,0:T(8,128)(2,1)S(1)}, u32[]{:S(2)}, u32[]{:S(2)}) collective-permute-start(bf16[64,1792]{1,0:T(8,128)(2,1)S(1)} %get-tuple-element.55), channel_id=1, source_target_pairs={{0,24},{4,28},{8,16},{12,20},{16,8},{20,12},{24,0},{28,4},{1,25},{... | collective-permute-start | bytes 688136 | tf_op jit(solution)/shard_map/ppermute | solution.py:13
  107.5 6.6 %weight_grads.1 = (bf16[1,1792,1024]{2,1,0:T(8,128)(2,1)}, bf16[1,1792,1024]{2,1,0:T(8,128)(2,1)}) custom-call(bf16[64,1792]{1,0:T(8,128)(2,1)S(1)} %collective-permute-done.3.refs_0_, bf16[64,1792]{1,0:T(8,128)(2,1)S(1)} %collective-permute-done.refs_1_, bf16[64,1792]{1,0:T(8,128)(2,1)S(1)} %collective-permute-done.2.refs_0_.refs_2_, ...), custom_call_target="tpu_custom_call" | custom-call | flops 3758096384 | bytes 11272192 | tf_op jit(solution)/shard_map/weight_grads/pallas_call | solution.py:231
  114.1 3.4 %collective-permute-done.21 = bf16[64,1792]{1,0:T(8,128)(2,1)S(1)} collective-permute-done((bf16[64,1792]{1,0:T(8,128)(2,1)S(1)}, bf16[64,1792]{1,0:T(8,128)(2,1)S(1)}, u32[]{:S(2)}, u32[]{:S(2)}) %collective-permute-start.21) | collective-permute-done | bytes 229408 | tf_op jit(solution)/shard_map/ppermute | solution.py:13
  (56 shorter events, 9.8 us)
Async XLA Ops:
  2.9 8.7 %collective-permute-start = (bf16[64,1792]{1,0:T(8,128)(2,1)}, bf16[64,1792]{1,0:T(8,128)(2,1)S(1)}, u32[]{:S(2)}, u32[]{:S(2)}) collective-permute-start(bf16[64,1792]{1,0:T(8,128)(2,1)} %get-tuple-element.30), channel_id=1, source_target_pairs={{0,12},{4,8},{8,4},{12,0},{16,28},{20,24},{24,20},{28,16},{1,13},{... | collective-permute-start | bytes 688136 | tf_op jit(solution)/shard_map/ppermute | solution.py:13
  5.3 14.7 %collective-permute-start.3 = (bf16[64,1792]{1,0:T(8,128)(2,1)}, bf16[64,1792]{1,0:T(8,128)(2,1)S(1)}, u32[]{:S(2)}, u32[]{:S(2)}) collective-permute-start(bf16[64,1792]{1,0:T(8,128)(2,1)} %get-tuple-element.29.refs_0_.refs_4_), channel_id=1, source_target_pairs={{0,4},{4,0},{8,12},{12,8},{16,20},{20,16},{24,28},{28,24},{1,5},{5... | collective-permute-start | bytes 688136 | tf_op jit(solution)/shard_map/ppermute | solution.py:13
  11.6 10.8 %collective-permute-start.1 = (bf16[64,1792]{1,0:T(8,128)(2,1)S(1)}, bf16[64,1792]{1,0:T(8,128)(2,1)S(1)}, u32[]{:S(2)}, u32[]{:S(2)}) collective-permute-start(bf16[64,1792]{1,0:T(8,128)(2,1)S(1)} %collective-permute-done.refs_1_), channel_id=1, source_target_pairs={{0,4},{4,0},{8,12},{12,8},{16,20},{20,16},{24,28},{28,24},{1,5},{5... | collective-permute-start | bytes 688136 | tf_op jit(solution)/shard_map/ppermute | solution.py:13
  11.7 13.1 %collective-permute-start.5 = (bf16[64,1792]{1,0:T(8,128)(2,1)}, bf16[64,1792]{1,0:T(8,128)(2,1)S(1)}, u32[]{:S(2)}, u32[]{:S(2)}) collective-permute-start(bf16[64,1792]{1,0:T(8,128)(2,1)} %get-tuple-element.33), channel_id=1, source_target_pairs={{0,28},{4,24},{8,20},{12,16},{16,12},{20,8},{24,4},{28,0},{1,29},{... | collective-permute-start | bytes 688136 | tf_op jit(solution)/shard_map/ppermute | solution.py:13
  15.0 11.3 %collective-permute-start.2 = (bf16[64,1792]{1,0:T(8,128)(2,1)}, bf16[64,1792]{1,0:T(8,128)(2,1)S(1)}, u32[]{:S(2)}, u32[]{:S(2)}) collective-permute-start(bf16[64,1792]{1,0:T(8,128)(2,1)} %get-tuple-element.31), channel_id=1, source_target_pairs={{0,20},{4,16},{8,28},{12,24},{16,4},{20,0},{24,12},{28,8},{1,21},{... | collective-permute-start | bytes 688136 | tf_op jit(solution)/shard_map/ppermute | solution.py:13
  15.3 0.7 copy-start.1
  16.0 0.7 copy-start.2
  20.0 2.4 %copy-start = (bf16[64,1792]{1,0:T(8,128)(2,1)S(1)}, bf16[64,1792]{1,0:T(8,128)(2,1)}, u32[]{:S(2)}) copy-start(bf16[64,1792]{1,0:T(8,128)(2,1)} %get-tuple-element.29.refs_0_.refs_4_) | copy-start | bytes 688132
  24.8 8.0 %collective-permute-start.6 = (bf16[64,1792]{1,0:T(8,128)(2,1)S(1)}, bf16[64,1792]{1,0:T(8,128)(2,1)S(1)}, u32[]{:S(2)}, u32[]{:S(2)}) collective-permute-start(bf16[64,1792]{1,0:T(8,128)(2,1)S(1)} %collective-permute-done.5.refs_1_.refs_3_), channel_id=1, source_target_pairs={{0,4},{4,0},{8,12},{12,8},{16,20},{20,16},{24,28},{28,24},{1,5},{5... | collective-permute-start | bytes 688136 | tf_op jit(solution)/shard_map/ppermute | solution.py:13
  26.3 6.5 %collective-permute-start.4 = (bf16[64,1792]{1,0:T(8,128)(2,1)S(1)}, bf16[64,1792]{1,0:T(8,128)(2,1)S(1)}, u32[]{:S(2)}, u32[]{:S(2)}) collective-permute-start(bf16[64,1792]{1,0:T(8,128)(2,1)S(1)} %collective-permute-done.2.refs_0_.refs_2_), channel_id=1, source_target_pairs={{0,4},{4,0},{8,12},{12,8},{16,20},{20,16},{24,28},{28,24},{1,5},{5... | collective-permute-start | bytes 688136 | tf_op jit(solution)/shard_map/ppermute | solution.py:13
  28.9 11.1 %collective-permute-start.8 = (bf16[64,2048]{1,0:T(8,128)(2,1)S(1)}, bf16[64,2048]{1,0:T(8,128)(2,1)S(1)}, u32[]{:S(2)}, u32[]{:S(2)}) collective-permute-start(bf16[64,2048]{1,0:T(8,128)(2,1)S(1)} %get-tuple-element.60), channel_id=1, source_target_pairs={{0,1},{1,2},{2,3},{3,0},{4,5},{5,6},{6,7},{7,4},{8,9},{9,10},{10,1... | collective-permute-start | bytes 786440 | tf_op jit(solution)/shard_map/ppermute | solution.py:282
  30.7 24.7 %collective-permute-start.11 = (bf16[64,2048]{1,0:T(8,128)(2,1)S(1)}, bf16[64,2048]{1,0:T(8,128)(2,1)S(1)}, u32[]{:S(2)}, u32[]{:S(2)}) collective-permute-start(bf16[64,2048]{1,0:T(8,128)(2,1)S(1)} %get-tuple-element.35), channel_id=1, source_target_pairs={{0,3},{1,0},{2,1},{3,2},{4,7},{5,4},{6,5},{7,6},{8,11},{9,8},{10,9... | collective-permute-start | bytes 786440 | tf_op jit(solution)/shard_map/ppermute | solution.py:282
  35.2 27.4 %copy-start.3 = (bf16[1,128,1024]{2,1,0:T(8,128)(2,1)S(1)}, bf16[1,128,1024]{2,1,0:T(8,128)(2,1)}, u32[]{:S(2)}) copy-start(bf16[1,128,1024]{2,1,0:T(8,128)(2,1)} %param.13) | copy-start | bytes 786436
  35.3 15.9 %collective-permute-start.7 = (bf16[64,2048]{1,0:T(8,128)(2,1)S(1)}, bf16[64,2048]{1,0:T(8,128)(2,1)S(1)}, u32[]{:S(2)}, u32[]{:S(2)}) collective-permute-start(bf16[64,2048]{1,0:T(8,128)(2,1)S(1)} %get-tuple-element.36), channel_id=1, source_target_pairs={{0,1},{1,2},{2,3},{3,0},{4,5},{5,6},{6,7},{7,4},{8,9},{9,10},{10,1... | collective-permute-start | bytes 786440 | tf_op jit(solution)/shard_map/ppermute | solution.py:282
  35.3 31.3 %collective-permute-start.12 = (bf16[64,2048]{1,0:T(8,128)(2,1)S(1)}, bf16[64,2048]{1,0:T(8,128)(2,1)S(1)}, u32[]{:S(2)}, u32[]{:S(2)}) collective-permute-start(bf16[64,2048]{1,0:T(8,128)(2,1)S(1)} %get-tuple-element.37), channel_id=1, source_target_pairs={{0,3},{1,0},{2,1},{3,2},{4,7},{5,4},{6,5},{7,6},{8,11},{9,8},{10,9... | collective-permute-start | bytes 786440 | tf_op jit(solution)/shard_map/ppermute | solution.py:282
  40.0 22.4 %collective-permute-start.10 = (bf16[64,2048]{1,0:T(8,128)(2,1)S(1)}, bf16[64,2048]{1,0:T(8,128)(2,1)S(1)}, u32[]{:S(2)}, u32[]{:S(2)}) collective-permute-start(bf16[64,2048]{1,0:T(8,128)(2,1)S(1)} %fusion.8), channel_id=1, source_target_pairs={{0,1},{1,2},{2,3},{3,0},{4,5},{5,6},{6,7},{7,4},{8,9},{9,10},{10,1... | collective-permute-start | bytes 786440 | tf_op jit(solution)/shard_map/ppermute | solution.py:282
  51.3 16.9 %collective-permute-start.9 = (bf16[64,2048]{1,0:T(8,128)(2,1)S(1)}, bf16[64,2048]{1,0:T(8,128)(2,1)S(1)}, u32[]{:S(2)}, u32[]{:S(2)}) collective-permute-start(bf16[64,2048]{1,0:T(8,128)(2,1)S(1)} %fusion.9), channel_id=1, source_target_pairs={{0,1},{1,2},{2,3},{3,0},{4,5},{5,6},{6,7},{7,4},{8,9},{9,10},{10,1... | collective-permute-start | bytes 786440 | tf_op jit(solution)/shard_map/ppermute | solution.py:282
  62.8 11.1 %collective-permute-start.13 = (bf16[64,2048]{1,0:T(8,128)(2,1)S(1)}, bf16[64,2048]{1,0:T(8,128)(2,1)S(1)}, u32[]{:S(2)}, u32[]{:S(2)}) collective-permute-start(bf16[64,2048]{1,0:T(8,128)(2,1)S(1)} %pad_maximum_fusion), channel_id=1, source_target_pairs={{0,1},{1,2},{2,3},{3,0},{4,5},{5,6},{6,7},{7,4},{8,9},{9,10},{10,1... | collective-permute-start | bytes 786440 | tf_op jit(solution)/shard_map/ppermute | solution.py:282
  62.8 16.8 %collective-permute-start.14 = (bf16[64,2048]{1,0:T(8,128)(2,1)S(1)}, bf16[64,2048]{1,0:T(8,128)(2,1)S(1)}, u32[]{:S(2)}, u32[]{:S(2)}) collective-permute-start(bf16[64,2048]{1,0:T(8,128)(2,1)S(1)} %pad_maximum_fusion), channel_id=1, source_target_pairs={{0,3},{1,0},{2,1},{3,2},{4,7},{5,4},{6,5},{7,6},{8,11},{9,8},{10,9... | collective-permute-start | bytes 786440 | tf_op jit(solution)/shard_map/ppermute | solution.py:282
  68.5 16.6 %collective-permute-start.17 = (bf16[64,2048]{1,0:T(8,128)(2,1)S(1)}, bf16[64,2048]{1,0:T(8,128)(2,1)S(1)}, u32[]{:S(2)}, u32[]{:S(2)}) collective-permute-start(bf16[64,2048]{1,0:T(8,128)(2,1)S(1)} %pad_maximum_fusion.1), channel_id=1, source_target_pairs={{0,1},{1,2},{2,3},{3,0},{4,5},{5,6},{6,7},{7,4},{8,9},{9,10},{10,1... | collective-permute-start | bytes 786440 | tf_op jit(solution)/shard_map/ppermute | solution.py:282
  68.6 22.0 %collective-permute-start.16 = (bf16[64,2048]{1,0:T(8,128)(2,1)S(1)}, bf16[64,2048]{1,0:T(8,128)(2,1)S(1)}, u32[]{:S(2)}, u32[]{:S(2)}) collective-permute-start(bf16[64,2048]{1,0:T(8,128)(2,1)S(1)} %pad_maximum_fusion.1), channel_id=1, source_target_pairs={{0,3},{1,0},{2,1},{3,2},{4,7},{5,4},{6,5},{7,6},{8,11},{9,8},{10,9... | collective-permute-start | bytes 786440 | tf_op jit(solution)/shard_map/ppermute | solution.py:282
  73.9 22.5 %collective-permute-start.15 = (bf16[64,2048]{1,0:T(8,128)(2,1)S(1)}, bf16[64,2048]{1,0:T(8,128)(2,1)S(1)}, u32[]{:S(2)}, u32[]{:S(2)}) collective-permute-start(bf16[64,2048]{1,0:T(8,128)(2,1)S(1)} %collective-permute-done.13), channel_id=1, source_target_pairs={{0,1},{1,2},{2,3},{3,0},{4,5},{5,6},{6,7},{7,4},{8,9},{9,10},{10,1... | collective-permute-start | bytes 786440 | tf_op jit(solution)/shard_map/ppermute | solution.py:282
  85.1 16.4 %collective-permute-start.18 = (bf16[64,2048]{1,0:T(8,128)(2,1)S(1)}, bf16[64,2048]{1,0:T(8,128)(2,1)S(1)}, u32[]{:S(2)}, u32[]{:S(2)}) collective-permute-start(bf16[64,2048]{1,0:T(8,128)(2,1)S(1)} %collective-permute-done.17), channel_id=1, source_target_pairs={{0,1},{1,2},{2,3},{3,0},{4,5},{5,6},{6,7},{7,4},{8,9},{9,10},{10,1... | collective-permute-start | bytes 786440 | tf_op jit(solution)/shard_map/ppermute | solution.py:282
  98.5 3.1 %collective-permute-start.19 = (bf16[256,1792]{1,0:T(8,128)(2,1)S(1)}, bf16[256,1792]{1,0:T(8,128)(2,1)S(1)}, u32[]{:S(2)}, u32[]{:S(2)}) collective-permute-start(bf16[256,1792]{1,0:T(8,128)(2,1)S(1)} %convolution_convert_fusion.1), channel_id=1, source_target_pairs={{0,4},{4,0},{8,12},{12,8},{16,20},{20,16},{24,28},{28,24},{1,5},{5... | collective-permute-start | bytes 2752520 | tf_op jit(solution)/shard_map/ppermute | solution.py:13
  103.9 10.2 %collective-permute-start.20 = (bf16[64,1792]{1,0:T(8,128)(2,1)S(1)}, bf16[64,1792]{1,0:T(8,128)(2,1)S(1)}, u32[]{:S(2)}, u32[]{:S(2)}) collective-permute-start(bf16[64,1792]{1,0:T(8,128)(2,1)S(1)} %get-tuple-element.57), channel_id=1, source_target_pairs={{0,8},{4,12},{8,0},{12,4},{16,24},{20,28},{24,16},{28,20},{1,9},{5... | collective-permute-start | bytes 688136 | tf_op jit(solution)/shard_map/ppermute | solution.py:13
  105.5 11.9 %collective-permute-start.21 = (bf16[64,1792]{1,0:T(8,128)(2,1)S(1)}, bf16[64,1792]{1,0:T(8,128)(2,1)S(1)}, u32[]{:S(2)}, u32[]{:S(2)}) collective-permute-start(bf16[64,1792]{1,0:T(8,128)(2,1)S(1)} %get-tuple-element.56), channel_id=1, source_target_pairs={{0,16},{4,20},{8,24},{12,28},{16,0},{20,4},{24,8},{28,12},{1,17},{... | collective-permute-start | bytes 688136 | tf_op jit(solution)/shard_map/ppermute | solution.py:13
  106.2 11.2 %copy-start.4 = (bf16[256,128]{1,0:T(8,128)(2,1)S(1)}, bf16[256,128]{1,0:T(8,128)(2,1)}, u32[]{:S(2)}) copy-start(bf16[256,128]{1,0:T(8,128)(2,1)} %get-tuple-element.52) | copy-start | bytes 196612
  106.2 11.2 %collective-permute-start.22 = (bf16[64,1792]{1,0:T(8,128)(2,1)S(1)}, bf16[64,1792]{1,0:T(8,128)(2,1)S(1)}, u32[]{:S(2)}, u32[]{:S(2)}) collective-permute-start(bf16[64,1792]{1,0:T(8,128)(2,1)S(1)} %get-tuple-element.55), channel_id=1, source_target_pairs={{0,24},{4,28},{8,16},{12,20},{16,8},{20,12},{24,0},{28,4},{1,25},{... | collective-permute-start | bytes 688136 | tf_op jit(solution)/shard_map/ppermute | solution.py:13

commit v3 on v0

--- a/solution.py
+++ b/solution.py
@@ -351,13 +351,19 @@
         if step < chain.reach[way]:
             chain.send(way, token)
 
-    def back(whole):
+    def back(whole, columns):
         return lax.dot_general(
-            whole, weights, (((1,), (1,)), ((), ())), preferred_element_type=jnp.float32
+            whole,
+            weights[columns],
+            (((1,), (1,)), ((), ())),
+            preferred_element_type=jnp.float32,
         ).astype(jnp.bfloat16)
 
-    arrived = [swap(packed[mask], "expert", 2 * mask + 1) for mask in masks]
-    inputs = [arrived, [swap(rows, "expert", 1) for rows in arrived]]
+    arrived = {mask: swap(packed[mask], "expert", 2 * mask + 1) for mask in reversed(masks)}
+    inputs = [
+        [arrived[mask] for mask in masks],
+        [swap(arrived[mask], "expert", 1) if mask else packed[0] for mask in masks],
+    ]
     for group in range(2):
         begin(group)
     steps = range(1, n_fsdp)
@@ -375,24 +381,34 @@
                     gather(group, way, step)
     wholes = [chain.whole.reshape(chips * capacity, 2 * half_units) for chain in chains]
 
-    taken = swap(back(wholes[0]), "expert", 1)
-    kept = back(earlier(wholes[1], taken))
-    pieces = []
-    for mask in masks:
-        rows = slice(mask * capacity, (mask + 1) * capacity)
-        both = add_rounded(kept[rows], taken[rows])
-        pieces.append(swap(both, "expert", 2 * mask) if mask else both)
+    taken = swap(back(wholes[0], slice(None)), "expert", 1)
+    returned = []
+    sums = wholes[1]
+    for start in (0, feat_cols // 2):
+        columns = slice(start, start + feat_cols // 2)
+        sums = add_rounded(back(earlier(wholes[1], sums), columns), taken[:, columns])
+        pieces = {}
+        for mask in reversed(masks):
+            rows = sums[mask * capacity : (mask + 1) * capacity]
+            pieces[mask] = swap(rows, "expert", 2 * mask) if mask else rows
+        returned.append([pieces[mask] for mask in masks])
 
     hidden = jnp.where(
         parity == 0, jnp.concatenate([hiddens[1], hiddens[0]], 0), jnp.concatenate(hiddens, 0)
     )
     grad_gate, grad_up = weight_grads(inputs[0] + inputs[1], wholes)
-    grad_tokens = lax.dot_general(
-        chooser,
-        jnp.concatenate(pieces, 0),
-        (((0,), (0,)), ((), ())),
-        preferred_element_type=jnp.float32,
-    ).astype(jnp.bfloat16)
+    grad_tokens = jnp.concatenate(
+        [
+            lax.dot_general(
+                chooser,
+                jnp.concatenate(pieces, 0),
+                (((0,), (0,)), ((), ())),
+                preferred_element_type=jnp.float32,
+            ).astype(jnp.bfloat16)
+            for pieces in returned
+        ],
+        1,
+    )
     return (hidden[None], grad_gate, grad_up, grad_tokens)
 
 

time: 112 us -> 117 us (1.045)
  waiting for transfers between devices: 43.9 us -> 48.4 us
    ppermute x12, waiting for transfers between devices: 34.4 us -> 37.9 us  [send(): self.came[way] = lax.ppermute(value, 'fsdp', ring)]
    ppermute x12, starting transfers between devices: 30.3 us -> 27.1 us  [send(): self.came[way] = lax.ppermute(value, 'fsdp', ring)]
    ppermute x12 -> x14, starting transfers between devices: 9.16 us -> 12.2 us  [swap(): return lax.ppermute(value, axis, pairs)]
    ppermute x12 -> x14, waiting for transfers between devices: 9.52 us -> 10.5 us  [swap(): return lax.ppermute(value, axis, pairs)]
    dot_general x2 -> x3, matrix products: 4.21 us -> 4.68 us  [back(): lax.dot_general(whole, weights[columns], (((1,), (1,)), ((), ())), prefer...]
  transfers between devices with their start and end apart: 24 -> 26, of which waited for: 12 -> 15; matrix products, arithmetic and copies ran while one was open for 4% -> 5% of each run, Pallas kernels for 15% -> 14%
where the time goes in v3:
time: 117 us
  waiting for transfers between devices  48.4 us (41%)
  starting transfers between devices  39.4 us (34%)
  Pallas kernels  18.8 us (16%)
  matrix products  5.19 us (4%)
  other arithmetic  2.27 us (2%)
  local copies, waits for them, and re-layouts  1.91 us (2%)
    ppermute x12, waiting for transfers between devices, send(): self.came[way] = lax.ppermute(value, 'fsdp', ring)  37.9 us
    ppermute x12, starting transfers between devices, send(): self.came[way] = lax.ppermute(value, 'fsdp', ring)  27.1 us
    ppermute x14, starting transfers between devices, swap(): return lax.ppermute(value, axis, pairs)  12.2 us
    ppermute x14, waiting for transfers between devices, swap(): return lax.ppermute(value, axis, pairs)  10.5 us
    pallas_call x1, Pallas kernels, weight_grads(): pl.pallas_call(lambda *refs: weight_kernel(count, *refs), out_shape=(out,...  6.62 us
    pallas_call x2, Pallas kernels, projected(): pl.pallas_call(project_kernel, out_shape=jax.ShapeDtypeStruct((count, cap...  6.56 us
    dot_general x3, matrix products, back(): lax.dot_general(whole, weights[columns], (((1,), (1,)), ((), ())), prefer...  4.68 us
    pallas_call x1, Pallas kernels, scaled_weights(): pl.pallas_call(lambda *refs: scale_kernel(sub, *refs), out_shape=jax.Shap...  3.3 us
  transfers between devices with their start and end apart: 26, of which 15 were waited for; matrix products, arithmetic and copies ran while one was open for 5% of the time, Pallas kernels for 14%

profile of v3, /device:TPU:0, one launch (start us, length us, event | category | flops | bytes accessed | tf_op | source)
XLA Modules:
  0.0 116.9 jit_solution(1948990665862835870)
XLA Ops:
  0.6 2.3 %pack_rows.1 = (bf16[256,128]{1,0:T(8,128)(2,1)}, bf16[64,1792]{1,0:T(8,128)(2,1)}, bf16[64,1792]{1,0:T(8,128)(2,1)}, bf16[64,1792]{1,0:T(8,128)(2,1)}, bf16[64,1792]{1,0:T(8,128)(2,1)}) custom-call(s32[1]{0:T(128)} %bitcast.chip_ref, s32[1,4]{1,0:T(1,128)} %counts_ref.1, bf16[128,1792]{1,0:T(8,128)(2,1)} %tokens_ref.1), custom_call_target="tpu_custom_call" | custom-call | flops 117440512 | bytes 1376256 | tf_op jit(solution)/shard_map/pack_rows/pallas_call | solution.py:148
  2.9 2.4 %collective-permute-start = (bf16[64,1792]{1,0:T(8,128)(2,1)}, bf16[64,1792]{1,0:T(8,128)(2,1)S(1)}, u32[]{:S(2)}, u32[]{:S(2)}) collective-permute-start(bf16[64,1792]{1,0:T(8,128)(2,1)} %get-tuple-element.29), channel_id=1, source_target_pairs={{0,12},{4,8},{8,4},{12,0},{16,28},{20,24},{24,20},{28,16},{1,13},{... | collective-permute-start | bytes 688136 | tf_op jit(solution)/shard_map/ppermute | solution.py:13
  5.3 1.8 %collective-permute-start.2 = (bf16[64,1792]{1,0:T(8,128)(2,1)}, bf16[64,1792]{1,0:T(8,128)(2,1)S(1)}, u32[]{:S(2)}, u32[]{:S(2)}) collective-permute-start(bf16[64,1792]{1,0:T(8,128)(2,1)} %get-tuple-element.30), channel_id=1, source_target_pairs={{0,20},{4,16},{8,28},{12,24},{16,4},{20,0},{24,12},{28,8},{1,21},{... | collective-permute-start | bytes 688136 | tf_op jit(solution)/shard_map/ppermute | solution.py:13
  8.5 3.3 %scale_weights.1.refs_4_ = bf16[1792,2048]{1,0:T(8,128)(2,1)S(1)} custom-call(s32[1]{0:T(128)} %bitcast.1.refs_0_, bf16[1,1792,1024]{2,1,0:T(8,128)(2,1)} %refs_1_.1, bf16[1,1792,1024]{2,1,0:T(8,128)(2,1)} %refs_2_.1, f32[1,8,56]{2,1,0:T(8,128)S(1)} %bitcast.66, f32[1,8,56]{2,1,0:T(8,128)S(1)} %bitcast.67), custom_call_target="tpu_custom_call" | custom-call | flops 3670016 | bytes 14680064 | tf_op jit(solution)/shard_map/scale_weights/pallas_call | solution.py:84
  12.6 4.9 %collective-permute-done.2.refs_2_ = bf16[64,1792]{1,0:T(8,128)(2,1)S(1)} collective-permute-done((bf16[64,1792]{1,0:T(8,128)(2,1)}, bf16[64,1792]{1,0:T(8,128)(2,1)S(1)}, u32[]{:S(2)}, u32[]{:S(2)}) %collective-permute-start.2) | collective-permute-done | bytes 229408 | tf_op jit(solution)/shard_map/ppermute | solution.py:13
  18.4 3.3 %project.3 = bf16[4,64,2048]{2,1,0:T(8,128)(2,1)S(1)} custom-call(bf16[64,1792]{1,0:T(8,128)(2,1)S(1)} %collective-permute-done.6.refs_0_, bf16[64,1792]{1,0:T(8,128)(2,1)S(1)} %collective-permute-done.refs_1_, bf16[64,1792]{1,0:T(8,128)(2,1)S(1)} %collective-permute-done.2.refs_2_, bf16[64,1792]{1,0:T(8,128)(2,1)S(1)} %collective-permute-done.4.refs_3_, ...), custom_call_target="tpu_custom_call" | custom-call | flops 1879048192 | bytes 9306112 | tf_op jit(solution)/shard_map/project/pallas_call | solution.py:183
  21.8 1.6 %collective-permute-start.8 = (bf16[64,2048]{1,0:T(8,128)(2,1)S(1)}, bf16[64,2048]{1,0:T(8,128)(2,1)S(1)}, u32[]{:S(2)}, u32[]{:S(2)}) collective-permute-start(bf16[64,2048]{1,0:T(8,128)(2,1)S(1)} %get-tuple-element.54), channel_id=1, source_target_pairs={{0,1},{1,2},{2,3},{3,0},{4,5},{5,6},{6,7},{7,4},{8,9},{9,10},{10,1... | collective-permute-start | bytes 786440 | tf_op jit(solution)/shard_map/ppermute | solution.py:275
  23.4 2.2 %collective-permute-start.11 = (bf16[64,2048]{1,0:T(8,128)(2,1)S(1)}, bf16[64,2048]{1,0:T(8,128)(2,1)S(1)}, u32[]{:S(2)}, u32[]{:S(2)}) collective-permute-start(bf16[64,2048]{1,0:T(8,128)(2,1)S(1)} %get-tuple-element.32), channel_id=1, source_target_pairs={{0,3},{1,0},{2,1},{3,2},{4,7},{5,4},{6,5},{7,6},{8,11},{9,8},{10,9... | collective-permute-start | bytes 786440 | tf_op jit(solution)/shard_map/ppermute | solution.py:275
  25.7 3.3 %project.2 = bf16[4,64,2048]{2,1,0:T(8,128)(2,1)S(1)} custom-call(bf16[64,1792]{1,0:T(8,128)(2,1)S(1)} %copy-done, bf16[64,1792]{1,0:T(8,128)(2,1)S(1)} %collective-permute-done.1.refs_1_.refs_5_, bf16[64,1792]{1,0:T(8,128)(2,1)S(1)} %collective-permute-done.3.refs_2_.refs_6_, bf16[64,1792]{1,0:T(8,128)(2,1)S(1)} %collective-permute-done.5.refs_3_.refs_7_, ...), custom_call_target="tpu_custom_call" | custom-call | flops 1879048192 | bytes 9306112 | tf_op jit(solution)/shard_map/project/pallas_call | solution.py:183
  29.1 3.8 %collective-permute-start.12 = (bf16[64,2048]{1,0:T(8,128)(2,1)S(1)}, bf16[64,2048]{1,0:T(8,128)(2,1)S(1)}, u32[]{:S(2)}, u32[]{:S(2)}) collective-permute-start(bf16[64,2048]{1,0:T(8,128)(2,1)S(1)} %get-tuple-element.34), channel_id=1, source_target_pairs={{0,3},{1,0},{2,1},{3,2},{4,7},{5,4},{6,5},{7,6},{8,11},{9,8},{10,9... | collective-permute-start | bytes 786440 | tf_op jit(solution)/shard_map/ppermute | solution.py:275
  33.0 3.9 %collective-permute-start.10 = (bf16[64,2048]{1,0:T(8,128)(2,1)S(1)}, bf16[64,2048]{1,0:T(8,128)(2,1)S(1)}, u32[]{:S(2)}, u32[]{:S(2)}) collective-permute-start(bf16[64,2048]{1,0:T(8,128)(2,1)S(1)} %fusion.17), channel_id=1, source_target_pairs={{0,1},{1,2},{2,3},{3,0},{4,5},{5,6},{6,7},{7,4},{8,9},{9,10},{10,1... | collective-permute-start | bytes 786440 | tf_op jit(solution)/shard_map/ppermute | solution.py:275
  36.9 7.1 %collective-permute-done.7 = bf16[64,2048]{1,0:T(8,128)(2,1)S(1)} collective-permute-done((bf16[64,2048]{1,0:T(8,128)(2,1)S(1)}, bf16[64,2048]{1,0:T(8,128)(2,1)S(1)}, u32[]{:S(2)}, u32[]{:S(2)}) %collective-permute-start.7) | collective-permute-done | bytes 262176 | tf_op jit(solution)/shard_map/ppermute | solution.py:275
  44.1 4.0 %collective-permute-start.9 = (bf16[64,2048]{1,0:T(8,128)(2,1)S(1)}, bf16[64,2048]{1,0:T(8,128)(2,1)S(1)}, u32[]{:S(2)}, u32[]{:S(2)}) collective-permute-start(bf16[64,2048]{1,0:T(8,128)(2,1)S(1)} %fusion.18), channel_id=1, source_target_pairs={{0,1},{1,2},{2,3},{3,0},{4,5},{5,6},{6,7},{7,4},{8,9},{9,10},{10,1... | collective-permute-start | bytes 786440 | tf_op jit(solution)/shard_map/ppermute | solution.py:275
  48.1 7.2 %collective-permute-done.10 = bf16[64,2048]{1,0:T(8,128)(2,1)S(1)} collective-permute-done((bf16[64,2048]{1,0:T(8,128)(2,1)S(1)}, bf16[64,2048]{1,0:T(8,128)(2,1)S(1)}, u32[]{:S(2)}, u32[]{:S(2)}) %collective-permute-start.10) | collective-permute-done | bytes 262176 | tf_op jit(solution)/shard_map/ppermute | solution.py:275
  55.7 3.8 %collective-permute-start.14 = (bf16[64,2048]{1,0:T(8,128)(2,1)S(1)}, bf16[64,2048]{1,0:T(8,128)(2,1)S(1)}, u32[]{:S(2)}, u32[]{:S(2)}) collective-permute-start(bf16[64,2048]{1,0:T(8,128)(2,1)S(1)} %pad_maximum_fusion.1), channel_id=1, source_target_pairs={{0,3},{1,0},{2,1},{3,2},{4,7},{5,4},{6,5},{7,6},{8,11},{9,8},{10,9... | collective-permute-start | bytes 786440 | tf_op jit(solution)/shard_map/ppermute | solution.py:275
  59.6 1.4 %collective-permute-done.9 = bf16[64,2048]{1,0:T(8,128)(2,1)S(1)} collective-permute-done((bf16[64,2048]{1,0:T(8,128)(2,1)S(1)}, bf16[64,2048]{1,0:T(8,128)(2,1)S(1)}, u32[]{:S(2)}, u32[]{:S(2)}) %collective-permute-start.9) | collective-permute-done | bytes 262176 | tf_op jit(solution)/shard_map/ppermute | solution.py:275
  61.4 3.8 %collective-permute-start.16 = (bf16[64,2048]{1,0:T(8,128)(2,1)S(1)}, bf16[64,2048]{1,0:T(8,128)(2,1)S(1)}, u32[]{:S(2)}, u32[]{:S(2)}) collective-permute-start(bf16[64,2048]{1,0:T(8,128)(2,1)S(1)} %pad_maximum_fusion.2), channel_id=1, source_target_pairs={{0,3},{1,0},{2,1},{3,2},{4,7},{5,4},{6,5},{7,6},{8,11},{9,8},{10,9... | collective-permute-start | bytes 786440 | tf_op jit(solution)/shard_map/ppermute | solution.py:275
  66.7 3.7 %collective-permute-start.15 = (bf16[64,2048]{1,0:T(8,128)(2,1)S(1)}, bf16[64,2048]{1,0:T(8,128)(2,1)S(1)}, u32[]{:S(2)}, u32[]{:S(2)}) collective-permute-start(bf16[64,2048]{1,0:T(8,128)(2,1)S(1)} %collective-permute-done.13), channel_id=1, source_target_pairs={{0,1},{1,2},{2,3},{3,0},{4,5},{5,6},{6,7},{7,4},{8,9},{9,10},{10,1... | collective-permute-start | bytes 786440 | tf_op jit(solution)/shard_map/ppermute | solution.py:275
  70.4 2.0 %collective-permute-done.14 = bf16[64,2048]{1,0:T(8,128)(2,1)S(1)} collective-permute-done((bf16[64,2048]{1,0:T(8,128)(2,1)S(1)}, bf16[64,2048]{1,0:T(8,128)(2,1)S(1)}, u32[]{:S(2)}, u32[]{:S(2)}) %collective-permute-start.14) | collective-permute-done | bytes 262176 | tf_op jit(solution)/shard_map/ppermute | solution.py:275
  72.5 5.4 %collective-permute-done.17 = bf16[64,2048]{1,0:T(8,128)(2,1)S(1)} collective-permute-done((bf16[64,2048]{1,0:T(8,128)(2,1)S(1)}, bf16[64,2048]{1,0:T(8,128)(2,1)S(1)}, u32[]{:S(2)}, u32[]{:S(2)}) %collective-permute-start.17) | collective-permute-done | bytes 262176 | tf_op jit(solution)/shard_map/ppermute | solution.py:275
  78.0 5.4 %collective-permute-done.16 = bf16[64,2048]{1,0:T(8,128)(2,1)S(1)} collective-permute-done((bf16[64,2048]{1,0:T(8,128)(2,1)S(1)}, bf16[64,2048]{1,0:T(8,128)(2,1)S(1)}, u32[]{:S(2)}, u32[]{:S(2)}) %collective-permute-start.16) | collective-permute-done | bytes 262176 | tf_op jit(solution)/shard_map/ppermute | solution.py:275
  83.4 5.8 %collective-permute-done.15 = bf16[64,2048]{1,0:T(8,128)(2,1)S(1)} collective-permute-done((bf16[64,2048]{1,0:T(8,128)(2,1)S(1)}, bf16[64,2048]{1,0:T(8,128)(2,1)S(1)}, u32[]{:S(2)}, u32[]{:S(2)}) %collective-permute-start.15) | collective-permute-done | bytes 262176 | tf_op jit(solution)/shard_map/ppermute | solution.py:275
  89.2 2.1 %convolution_convert_fusion = bf16[256,1792]{1,0:T(8,128)(2,1)S(1)} fusion(bf16[256,2048]{1,0:T(8,128)(2,1)S(1)} %bitcast.64, bf16[1792,2048]{1,0:T(8,128)(2,1)S(1)} %scale_weights.1.refs_4_), kind=kOutput, calls=%fused_computation.4 | convolution fusion | flops 1879506944 | bytes 9306112 | tf_op jit(solution)/shard_map/dot_general | solution.py:355
  91.4 2.9 %collective-permute-done.18 = bf16[64,2048]{1,0:T(8,128)(2,1)S(1)} collective-permute-done((bf16[64,2048]{1,0:T(8,128)(2,1)S(1)}, bf16[64,2048]{1,0:T(8,128)(2,1)S(1)}, u32[]{:S(2)}, u32[]{:S(2)}) %collective-permute-start.18) | collective-permute-done | bytes 262176 | tf_op jit(solution)/shard_map/ppermute | solution.py:275
  94.3 6.6 %weight_grads.1 = (bf16[1,1792,1024]{2,1,0:T(8,128)(2,1)}, bf16[1,1792,1024]{2,1,0:T(8,128)(2,1)}) custom-call(bf16[64,1792]{1,0:T(8,128)(2,1)S(1)} %collective-permute-done.6.refs_0_, bf16[64,1792]{1,0:T(8,128)(2,1)S(1)} %collective-permute-done.refs_1_, bf16[64,1792]{1,0:T(8,128)(2,1)S(1)} %collective-permute-done.2.refs_2_, ...), custom_call_target="tpu_custom_call" | custom-call | flops 3758096384 | bytes 11272192 | tf_op jit(solution)/shard_map/weight_grads/pallas_call | solution.py:231
  102.3 1.6 %collective-permute-start.20 = (bf16[64,896]{1,0:T(8,128)(2,1)S(1)}, bf16[64,896]{1,0:T(8,128)(2,1)S(1)}, u32[]{:S(2)}, u32[]{:S(2)}) collective-permute-start(bf16[64,896]{1,0:T(8,128)(2,1)S(1)} %get-tuple-element.65), channel_id=1, source_target_pairs={{0,8},{4,12},{8,0},{12,4},{16,24},{20,28},{24,16},{28,20},{1,9},{5... | collective-permute-start | bytes 344072 | tf_op jit(solution)/shard_map/ppermute | solution.py:13
  104.4 1.4 %collective-permute-start.22 = (bf16[64,896]{1,0:T(8,128)(2,1)S(1)}, bf16[64,896]{1,0:T(8,128)(2,1)S(1)}, u32[]{:S(2)}, u32[]{:S(2)}) collective-permute-start(bf16[64,896]{1,0:T(8,128)(2,1)S(1)} %get-tuple-element.63), channel_id=1, source_target_pairs={{0,24},{4,28},{8,16},{12,20},{16,8},{20,12},{24,0},{28,4},{1,25},{... | collective-permute-start | bytes 344072 | tf_op jit(solution)/shard_map/ppermute | solution.py:13
  105.9 1.3 %add_convert_fusion = bf16[256,896]{1,0:T(8,128)(2,1)S(1)} fusion(bf16[256,1792]{1,0:T(8,128)(2,1)S(1)} %collective-permute-done.19, bf16[256,2048]{1,0:T(8,128)(2,1)S(1)} %bitcast.63, bf16[1792,2048]{1,0:T(8,128)(2,1)S(1)} %scale_weights.1.refs_4_), kind=kOutput, calls=%fused_computation.11 | convolution fusion | flops 940670976 | bytes 5636096 | tf_op jit(solution)/shard_map/dot_general | solution.py:355
  107.2 1.6 %collective-permute-start.23 = (bf16[64,896]{1,0:T(8,128)(2,1)S(1)}, bf16[64,896]{1,0:T(8,128)(2,1)S(1)}, u32[]{:S(2)}, u32[]{:S(2)}) collective-permute-start(bf16[64,896]{1,0:T(8,128)(2,1)S(1)} %get-tuple-element.69), channel_id=1, source_target_pairs={{0,8},{4,12},{8,0},{12,4},{16,24},{20,28},{24,16},{28,20},{1,9},{5... | collective-permute-start | bytes 344072 | tf_op jit(solution)/shard_map/ppermute | solution.py:13
  109.3 1.4 %collective-permute-start.25 = (bf16[64,896]{1,0:T(8,128)(2,1)S(1)}, bf16[64,896]{1,0:T(8,128)(2,1)S(1)}, u32[]{:S(2)}, u32[]{:S(2)}) collective-permute-start(bf16[64,896]{1,0:T(8,128)(2,1)S(1)} %get-tuple-element.67), channel_id=1, source_target_pairs={{0,24},{4,28},{8,16},{12,20},{16,8},{20,12},{24,0},{28,4},{1,25},{... | collective-permute-start | bytes 344072 | tf_op jit(solution)/shard_map/ppermute | solution.py:13
  111.6 2.0 %collective-permute-done.23 = bf16[64,896]{1,0:T(8,128)(2,1)S(1)} collective-permute-done((bf16[64,896]{1,0:T(8,128)(2,1)S(1)}, bf16[64,896]{1,0:T(8,128)(2,1)S(1)}, u32[]{:S(2)}, u32[]{:S(2)}) %collective-permute-start.23) | collective-permute-done | bytes 114720 | tf_op jit(solution)/shard_map/ppermute | solution.py:13
  113.5 2.3 %collective-permute-done.24 = bf16[64,896]{1,0:T(8,128)(2,1)S(1)} collective-permute-done((bf16[64,896]{1,0:T(8,128)(2,1)S(1)}, bf16[64,896]{1,0:T(8,128)(2,1)S(1)}, u32[]{:S(2)}, u32[]{:S(2)}) %collective-permute-start.24) | collective-permute-done | bytes 114720 | tf_op jit(solution)/shard_map/ppermute | solution.py:13
  (64 shorter events, 10.3 us)
Async XLA Ops:
  2.9 8.9 %collective-permute-start = (bf16[64,1792]{1,0:T(8,128)(2,1)}, bf16[64,1792]{1,0:T(8,128)(2,1)S(1)}, u32[]{:S(2)}, u32[]{:S(2)}) collective-permute-start(bf16[64,1792]{1,0:T(8,128)(2,1)} %get-tuple-element.29), channel_id=1, source_target_pairs={{0,12},{4,8},{8,4},{12,0},{16,28},{20,24},{24,20},{28,16},{1,13},{... | collective-permute-start | bytes 688136 | tf_op jit(solution)/shard_map/ppermute | solution.py:13
  5.3 12.2 %collective-permute-start.2 = (bf16[64,1792]{1,0:T(8,128)(2,1)}, bf16[64,1792]{1,0:T(8,128)(2,1)S(1)}, u32[]{:S(2)}, u32[]{:S(2)}) collective-permute-start(bf16[64,1792]{1,0:T(8,128)(2,1)} %get-tuple-element.30), channel_id=1, source_target_pairs={{0,20},{4,16},{8,28},{12,24},{16,4},{20,0},{24,12},{28,8},{1,21},{... | collective-permute-start | bytes 688136 | tf_op jit(solution)/shard_map/ppermute | solution.py:13
  7.1 11.2 %collective-permute-start.4 = (bf16[64,1792]{1,0:T(8,128)(2,1)}, bf16[64,1792]{1,0:T(8,128)(2,1)S(1)}, u32[]{:S(2)}, u32[]{:S(2)}) collective-permute-start(bf16[64,1792]{1,0:T(8,128)(2,1)} %get-tuple-element.31), channel_id=1, source_target_pairs={{0,28},{4,24},{8,20},{12,16},{16,12},{20,8},{24,4},{28,0},{1,29},{... | collective-permute-start | bytes 688136 | tf_op jit(solution)/shard_map/ppermute | solution.py:13
  7.1 11.3 %collective-permute-start.6 = (bf16[64,1792]{1,0:T(8,128)(2,1)}, bf16[64,1792]{1,0:T(8,128)(2,1)S(1)}, u32[]{:S(2)}, u32[]{:S(2)}) collective-permute-start(bf16[64,1792]{1,0:T(8,128)(2,1)} %get-tuple-element.28.refs_0_.refs_4_), channel_id=1, source_target_pairs={{0,4},{4,0},{8,12},{12,8},{16,20},{20,16},{24,28},{28,24},{1,5},{5... | collective-permute-start | bytes 688136 | tf_op jit(solution)/shard_map/ppermute | solution.py:13
  7.1 0.7 copy-start.1
  7.8 0.7 copy-start.2
  11.8 13.9 %copy-start = (bf16[64,1792]{1,0:T(8,128)(2,1)S(1)}, bf16[64,1792]{1,0:T(8,128)(2,1)}, u32[]{:S(2)}) copy-start(bf16[64,1792]{1,0:T(8,128)(2,1)} %get-tuple-element.28.refs_0_.refs_4_) | copy-start | bytes 688132
  11.8 13.8 %collective-permute-start.1 = (bf16[64,1792]{1,0:T(8,128)(2,1)S(1)}, bf16[64,1792]{1,0:T(8,128)(2,1)S(1)}, u32[]{:S(2)}, u32[]{:S(2)}) collective-permute-start(bf16[64,1792]{1,0:T(8,128)(2,1)S(1)} %collective-permute-done.refs_1_), channel_id=1, source_target_pairs={{0,4},{4,0},{8,12},{12,8},{16,20},{20,16},{24,28},{28,24},{1,5},{5... | collective-permute-start | bytes 688136 | tf_op jit(solution)/shard_map/ppermute | solution.py:13
  17.5 8.2 %collective-permute-start.3 = (bf16[64,1792]{1,0:T(8,128)(2,1)S(1)}, bf16[64,1792]{1,0:T(8,128)(2,1)S(1)}, u32[]{:S(2)}, u32[]{:S(2)}) collective-permute-start(bf16[64,1792]{1,0:T(8,128)(2,1)S(1)} %collective-permute-done.2.refs_2_), channel_id=1, source_target_pairs={{0,4},{4,0},{8,12},{12,8},{16,20},{20,16},{24,28},{28,24},{1,5},{5... | collective-permute-start | bytes 688136 | tf_op jit(solution)/shard_map/ppermute | solution.py:13
  18.4 7.3 %collective-permute-start.5 = (bf16[64,1792]{1,0:T(8,128)(2,1)S(1)}, bf16[64,1792]{1,0:T(8,128)(2,1)S(1)}, u32[]{:S(2)}, u32[]{:S(2)}) collective-permute-start(bf16[64,1792]{1,0:T(8,128)(2,1)S(1)} %collective-permute-done.4.refs_3_), channel_id=1, source_target_pairs={{0,4},{4,0},{8,12},{12,8},{16,20},{20,16},{24,28},{28,24},{1,5},{5... | collective-permute-start | bytes 688136 | tf_op jit(solution)/shard_map/ppermute | solution.py:13
  21.8 11.1 %collective-permute-start.8 = (bf16[64,2048]{1,0:T(8,128)(2,1)S(1)}, bf16[64,2048]{1,0:T(8,128)(2,1)S(1)}, u32[]{:S(2)}, u32[]{:S(2)}) collective-permute-start(bf16[64,2048]{1,0:T(8,128)(2,1)S(1)} %get-tuple-element.54), channel_id=1, source_target_pairs={{0,1},{1,2},{2,3},{3,0},{4,5},{5,6},{6,7},{7,4},{8,9},{9,10},{10,1... | collective-permute-start | bytes 786440 | tf_op jit(solution)/shard_map/ppermute | solution.py:275
  23.4 24.7 %collective-permute-start.11 = (bf16[64,2048]{1,0:T(8,128)(2,1)S(1)}, bf16[64,2048]{1,0:T(8,128)(2,1)S(1)}, u32[]{:S(2)}, u32[]{:S(2)}) collective-permute-start(bf16[64,2048]{1,0:T(8,128)(2,1)S(1)} %get-tuple-element.32), channel_id=1, source_target_pairs={{0,3},{1,0},{2,1},{3,2},{4,7},{5,4},{6,5},{7,6},{8,11},{9,8},{10,9... | collective-permute-start | bytes 786440 | tf_op jit(solution)/shard_map/ppermute | solution.py:275
  29.0 26.4 %copy-start.3 = (bf16[1,128,1024]{2,1,0:T(8,128)(2,1)S(1)}, bf16[1,128,1024]{2,1,0:T(8,128)(2,1)}, u32[]{:S(2)}) copy-start(bf16[1,128,1024]{2,1,0:T(8,128)(2,1)} %param.13) | copy-start | bytes 786436
  29.1 15.0 %collective-permute-start.7 = (bf16[64,2048]{1,0:T(8,128)(2,1)S(1)}, bf16[64,2048]{1,0:T(8,128)(2,1)S(1)}, u32[]{:S(2)}, u32[]{:S(2)}) collective-permute-start(bf16[64,2048]{1,0:T(8,128)(2,1)S(1)} %get-tuple-element.33), channel_id=1, source_target_pairs={{0,1},{1,2},{2,3},{3,0},{4,5},{5,6},{6,7},{7,4},{8,9},{9,10},{10,1... | collective-permute-start | bytes 786440 | tf_op jit(solution)/shard_map/ppermute | solution.py:275
  29.1 30.4 %collective-permute-start.12 = (bf16[64,2048]{1,0:T(8,128)(2,1)S(1)}, bf16[64,2048]{1,0:T(8,128)(2,1)S(1)}, u32[]{:S(2)}, u32[]{:S(2)}) collective-permute-start(bf16[64,2048]{1,0:T(8,128)(2,1)S(1)} %get-tuple-element.34), channel_id=1, source_target_pairs={{0,3},{1,0},{2,1},{3,2},{4,7},{5,4},{6,5},{7,6},{8,11},{9,8},{10,9... | collective-permute-start | bytes 786440 | tf_op jit(solution)/shard_map/ppermute | solution.py:275
  33.0 22.3 %collective-permute-start.10 = (bf16[64,2048]{1,0:T(8,128)(2,1)S(1)}, bf16[64,2048]{1,0:T(8,128)(2,1)S(1)}, u32[]{:S(2)}, u32[]{:S(2)}) collective-permute-start(bf16[64,2048]{1,0:T(8,128)(2,1)S(1)} %fusion.17), channel_id=1, source_target_pairs={{0,1},{1,2},{2,3},{3,0},{4,5},{5,6},{6,7},{7,4},{8,9},{9,10},{10,1... | collective-permute-start | bytes 786440 | tf_op jit(solution)/shard_map/ppermute | solution.py:275
  44.1 16.9 %collective-permute-start.9 = (bf16[64,2048]{1,0:T(8,128)(2,1)S(1)}, bf16[64,2048]{1,0:T(8,128)(2,1)S(1)}, u32[]{:S(2)}, u32[]{:S(2)}) collective-permute-start(bf16[64,2048]{1,0:T(8,128)(2,1)S(1)} %fusion.18), channel_id=1, source_target_pairs={{0,1},{1,2},{2,3},{3,0},{4,5},{5,6},{6,7},{7,4},{8,9},{9,10},{10,1... | collective-permute-start | bytes 786440 | tf_op jit(solution)/shard_map/ppermute | solution.py:275
  55.6 11.1 %collective-permute-start.13 = (bf16[64,2048]{1,0:T(8,128)(2,1)S(1)}, bf16[64,2048]{1,0:T(8,128)(2,1)S(1)}, u32[]{:S(2)}, u32[]{:S(2)}) collective-permute-start(bf16[64,2048]{1,0:T(8,128)(2,1)S(1)} %pad_maximum_fusion.1), channel_id=1, source_target_pairs={{0,1},{1,2},{2,3},{3,0},{4,5},{5,6},{6,7},{7,4},{8,9},{9,10},{10,1... | collective-permute-start | bytes 786440 | tf_op jit(solution)/shard_map/ppermute | solution.py:275
  55.7 16.8 %collective-permute-start.14 = (bf16[64,2048]{1,0:T(8,128)(2,1)S(1)}, bf16[64,2048]{1,0:T(8,128)(2,1)S(1)}, u32[]{:S(2)}, u32[]{:S(2)}) collective-permute-start(bf16[64,2048]{1,0:T(8,128)(2,1)S(1)} %pad_maximum_fusion.1), channel_id=1, source_target_pairs={{0,3},{1,0},{2,1},{3,2},{4,7},{5,4},{6,5},{7,6},{8,11},{9,8},{10,9... | collective-permute-start | bytes 786440 | tf_op jit(solution)/shard_map/ppermute | solution.py:275
  61.4 16.6 %collective-permute-start.17 = (bf16[64,2048]{1,0:T(8,128)(2,1)S(1)}, bf16[64,2048]{1,0:T(8,128)(2,1)S(1)}, u32[]{:S(2)}, u32[]{:S(2)}) collective-permute-start(bf16[64,2048]{1,0:T(8,128)(2,1)S(1)} %pad_maximum_fusion.2), channel_id=1, source_target_pairs={{0,1},{1,2},{2,3},{3,0},{4,5},{5,6},{6,7},{7,4},{8,9},{9,10},{10,1... | collective-permute-start | bytes 786440 | tf_op jit(solution)/shard_map/ppermute | solution.py:275
  61.4 22.0 %collective-permute-start.16 = (bf16[64,2048]{1,0:T(8,128)(2,1)S(1)}, bf16[64,2048]{1,0:T(8,128)(2,1)S(1)}, u32[]{:S(2)}, u32[]{:S(2)}) collective-permute-start(bf16[64,2048]{1,0:T(8,128)(2,1)S(1)} %pad_maximum_fusion.2), channel_id=1, source_target_pairs={{0,3},{1,0},{2,1},{3,2},{4,7},{5,4},{6,5},{7,6},{8,11},{9,8},{10,9... | collective-permute-start | bytes 786440 | tf_op jit(solution)/shard_map/ppermute | solution.py:275
  66.7 22.5 %collective-permute-start.15 = (bf16[64,2048]{1,0:T(8,128)(2,1)S(1)}, bf16[64,2048]{1,0:T(8,128)(2,1)S(1)}, u32[]{:S(2)}, u32[]{:S(2)}) collective-permute-start(bf16[64,2048]{1,0:T(8,128)(2,1)S(1)} %collective-permute-done.13), channel_id=1, source_target_pairs={{0,1},{1,2},{2,3},{3,0},{4,5},{5,6},{6,7},{7,4},{8,9},{9,10},{10,1... | collective-permute-start | bytes 786440 | tf_op jit(solution)/shard_map/ppermute | solution.py:275
  78.0 16.3 %collective-permute-start.18 = (bf16[64,2048]{1,0:T(8,128)(2,1)S(1)}, bf16[64,2048]{1,0:T(8,128)(2,1)S(1)}, u32[]{:S(2)}, u32[]{:S(2)}) collective-permute-start(bf16[64,2048]{1,0:T(8,128)(2,1)S(1)} %collective-permute-done.17), channel_id=1, source_target_pairs={{0,1},{1,2},{2,3},{3,0},{4,5},{5,6},{6,7},{7,4},{8,9},{9,10},{10,1... | collective-permute-start | bytes 786440 | tf_op jit(solution)/shard_map/ppermute | solution.py:275
  91.3 9.6 %collective-permute-start.19 = (bf16[256,1792]{1,0:T(8,128)(2,1)S(1)}, bf16[256,1792]{1,0:T(8,128)(2,1)S(1)}, u32[]{:S(2)}, u32[]{:S(2)}) collective-permute-start(bf16[256,1792]{1,0:T(8,128)(2,1)S(1)} %convolution_convert_fusion), channel_id=1, source_target_pairs={{0,4},{4,0},{8,12},{12,8},{16,20},{20,16},{24,28},{28,24},{1,5},{5... | collective-permute-start | bytes 2752520 | tf_op jit(solution)/shard_map/ppermute | solution.py:13
  102.3 7.0 %collective-permute-start.20 = (bf16[64,896]{1,0:T(8,128)(2,1)S(1)}, bf16[64,896]{1,0:T(8,128)(2,1)S(1)}, u32[]{:S(2)}, u32[]{:S(2)}) collective-permute-start(bf16[64,896]{1,0:T(8,128)(2,1)S(1)} %get-tuple-element.65), channel_id=1, source_target_pairs={{0,8},{4,12},{8,0},{12,4},{16,24},{20,28},{24,16},{28,20},{1,9},{5... | collective-permute-start | bytes 344072 | tf_op jit(solution)/shard_map/ppermute | solution.py:13
  103.9 7.2 %collective-permute-start.21 = (bf16[64,896]{1,0:T(8,128)(2,1)S(1)}, bf16[64,896]{1,0:T(8,128)(2,1)S(1)}, u32[]{:S(2)}, u32[]{:S(2)}) collective-permute-start(bf16[64,896]{1,0:T(8,128)(2,1)S(1)} %get-tuple-element.64), channel_id=1, source_target_pairs={{0,16},{4,20},{8,24},{12,28},{16,0},{20,4},{24,8},{28,12},{1,17},{... | collective-permute-start | bytes 344072 | tf_op jit(solution)/shard_map/ppermute | solution.py:13
  104.4 6.9 %copy-start.4 = (bf16[256,128]{1,0:T(8,128)(2,1)S(1)}, bf16[256,128]{1,0:T(8,128)(2,1)}, u32[]{:S(2)}) copy-start(bf16[256,128]{1,0:T(8,128)(2,1)} %get-tuple-element.49) | copy-start | bytes 196612
  104.4 6.9 %collective-permute-start.22 = (bf16[64,896]{1,0:T(8,128)(2,1)S(1)}, bf16[64,896]{1,0:T(8,128)(2,1)S(1)}, u32[]{:S(2)}, u32[]{:S(2)}) collective-permute-start(bf16[64,896]{1,0:T(8,128)(2,1)S(1)} %get-tuple-element.63), channel_id=1, source_target_pairs={{0,24},{4,28},{8,16},{12,20},{16,8},{20,12},{24,0},{28,4},{1,25},{... | collective-permute-start | bytes 344072 | tf_op jit(solution)/shard_map/ppermute | solution.py:13
  107.2 6.3 %collective-permute-start.23 = (bf16[64,896]{1,0:T(8,128)(2,1)S(1)}, bf16[64,896]{1,0:T(8,128)(2,1)S(1)}, u32[]{:S(2)}, u32[]{:S(2)}) collective-permute-start(bf16[64,896]{1,0:T(8,128)(2,1)S(1)} %get-tuple-element.69), channel_id=1, source_target_pairs={{0,8},{4,12},{8,0},{12,4},{16,24},{20,28},{24,16},{28,20},{1,9},{5... | collective-permute-start | bytes 344072 | tf_op jit(solution)/shard_map/ppermute | solution.py:13
  108.8 7.0 %collective-permute-start.24 = (bf16[64,896]{1,0:T(8,128)(2,1)S(1)}, bf16[64,896]{1,0:T(8,128)(2,1)S(1)}, u32[]{:S(2)}, u32[]{:S(2)}) collective-permute-start(bf16[64,896]{1,0:T(8,128)(2,1)S(1)} %get-tuple-element.68), channel_id=1, source_target_pairs={{0,16},{4,20},{8,24},{12,28},{16,0},{20,4},{24,8},{28,12},{1,17},{... | collective-permute-start | bytes 344072 | tf_op jit(solution)/shard_map/ppermute | solution.py:13
  109.3 6.5 %collective-permute-start.25 = (bf16[64,896]{1,0:T(8,128)(2,1)S(1)}, bf16[64,896]{1,0:T(8,128)(2,1)S(1)}, u32[]{:S(2)}, u32[]{:S(2)}) collective-permute-start(bf16[64,896]{1,0:T(8,128)(2,1)S(1)} %get-tuple-element.67), channel_id=1, source_target_pairs={{0,24},{4,28},{8,16},{12,20},{16,8},{20,12},{24,0},{28,4},{1,25},{... | collective-permute-start | bytes 344072 | tf_op jit(solution)/shard_map/ppermute | solution.py:13

commit v4 on v0

--- a/solution.py
+++ b/solution.py
@@ -179,7 +179,7 @@
     count = len(blocks)
     capacity, feat_cols = blocks[0].shape
     units = weights.shape[1]
-    tile = math.gcd(units, 512)
+    tile = math.gcd(units, 1024)
     return pl.pallas_call(
         project_kernel,
         out_shape=jax.ShapeDtypeStruct((count, capacity, units), jnp.bfloat16),
@@ -188,7 +188,7 @@
         + [pl.BlockSpec((feat_cols, tile), lambda i: (0, i))],
         out_specs=pl.BlockSpec((count, capacity, tile), lambda i: (0, 0, i)),
         scratch_shapes=[pltpu.VMEM((count * capacity, feat_cols), jnp.bfloat16)],
-        compiler_params=pltpu.CompilerParams(vmem_limit_bytes=16 * 2**20),
+        compiler_params=pltpu.CompilerParams(vmem_limit_bytes=24 * 2**20),
         cost_estimate=pl.CostEstimate(
             flops=2 * count * capacity * feat_cols * units,
             bytes_accessed=2 * (count * capacity * (feat_cols + units) + feat_cols * units),
@@ -356,8 +356,11 @@
             whole, weights, (((1,), (1,)), ((), ())), preferred_element_type=jnp.float32
         ).astype(jnp.bfloat16)
 
-    arrived = [swap(packed[mask], "expert", 2 * mask + 1) for mask in masks]
-    inputs = [arrived, [swap(rows, "expert", 1) for rows in arrived]]
+    arrived = {mask: swap(packed[mask], "expert", 2 * mask + 1) for mask in reversed(masks)}
+    inputs = [
+        [arrived[mask] for mask in masks],
+        [swap(arrived[mask], "expert", 1) if mask else packed[0] for mask in masks],
+    ]
     for group in range(2):
         begin(group)
     steps = range(1, n_fsdp)

time: 112 us -> 111 us (level)
  starting transfers between devices: 39.5 us -> 36 us
  waiting for transfers between devices: 43.9 us -> 47.1 us
    ppermute x12, waiting for transfers between devices: 34.4 us -> 38.1 us  [send(): self.came[way] = lax.ppermute(value, 'fsdp', ring)]
    ppermute x12, starting transfers between devices: 30.3 us -> 27.3 us  [send(): self.came[way] = lax.ppermute(value, 'fsdp', ring)]
    ppermute x12 -> x11, waiting for transfers between devices: 9.52 us -> 9 us  [swap(): return lax.ppermute(value, axis, pairs)]
    ppermute x12 -> x11, starting transfers between devices: 9.16 us -> 8.7 us  [swap(): return lax.ppermute(value, axis, pairs)]
  transfers between devices with their start and end apart: 24 -> 23, of which waited for: 12 -> 13; matrix products, arithmetic and copies ran while one was open for 4% -> 4% of each run, Pallas kernels for 15% -> 14%
where the time goes in v4:
time: 111 us
  waiting for transfers between devices  47.1 us (42%)
  starting transfers between devices  36 us (32%)
  Pallas kernels  17.9 us (16%)
  matrix products  5.29 us (5%)
  local copies, waits for them, and re-layouts  1.84 us (2%)
  other arithmetic  1.69 us (2%)
    ppermute x12, waiting for transfers between devices, send(): self.came[way] = lax.ppermute(value, 'fsdp', ring)  38.1 us
    ppermute x12, starting transfers between devices, send(): self.came[way] = lax.ppermute(value, 'fsdp', ring)  27.3 us
    ppermute x11, waiting for transfers between devices, swap(): return lax.ppermute(value, axis, pairs)  9 us
    ppermute x11, starting transfers between devices, swap(): return lax.ppermute(value, axis, pairs)  8.7 us
    pallas_call x1, Pallas kernels, weight_grads(): pl.pallas_call(lambda *refs: weight_kernel(count, *refs), out_shape=(out,...  6.59 us
    pallas_call x2, Pallas kernels, projected(): pl.pallas_call(project_kernel, out_shape=jax.ShapeDtypeStruct((count, cap...  5.72 us
    dot_general x2, matrix products, back(): lax.dot_general(whole, weights, (((1,), (1,)), ((), ())), preferred_eleme...  4.21 us
    pallas_call x1, Pallas kernels, scaled_weights(): pl.pallas_call(lambda *refs: scale_kernel(sub, *refs), out_shape=jax.Shap...  3.3 us
  transfers between devices with their start and end apart: 23, of which 13 were waited for; matrix products, arithmetic and copies ran while one was open for 4% of the time, Pallas kernels for 14%

profile of v4, /device:TPU:0, one launch (start us, length us, event | category | flops | bytes accessed | tf_op | source)
XLA Modules:
  0.0 110.7 jit_solution(4357455398124645425)
XLA Ops:
  0.6 2.3 %pack_rows.1 = (bf16[256,128]{1,0:T(8,128)(2,1)}, bf16[64,1792]{1,0:T(8,128)(2,1)}, bf16[64,1792]{1,0:T(8,128)(2,1)}, bf16[64,1792]{1,0:T(8,128)(2,1)}, bf16[64,1792]{1,0:T(8,128)(2,1)}) custom-call(s32[1]{0:T(128)} %bitcast.chip_ref, s32[1,4]{1,0:T(1,128)} %counts_ref.1, bf16[128,1792]{1,0:T(8,128)(2,1)} %tokens_ref.1), custom_call_target="tpu_custom_call" | custom-call | flops 117440512 | bytes 1376256 | tf_op jit(solution)/shard_map/pack_rows/pallas_call | solution.py:148
  2.9 2.4 %collective-permute-start = (bf16[64,1792]{1,0:T(8,128)(2,1)}, bf16[64,1792]{1,0:T(8,128)(2,1)S(1)}, u32[]{:S(2)}, u32[]{:S(2)}) collective-permute-start(bf16[64,1792]{1,0:T(8,128)(2,1)} %get-tuple-element.28), channel_id=1, source_target_pairs={{0,12},{4,8},{8,4},{12,0},{16,28},{20,24},{24,20},{28,16},{1,13},{... | collective-permute-start | bytes 688136 | tf_op jit(solution)/shard_map/ppermute | solution.py:13
  5.3 1.8 %collective-permute-start.2 = (bf16[64,1792]{1,0:T(8,128)(2,1)}, bf16[64,1792]{1,0:T(8,128)(2,1)S(1)}, u32[]{:S(2)}, u32[]{:S(2)}) collective-permute-start(bf16[64,1792]{1,0:T(8,128)(2,1)} %get-tuple-element.29), channel_id=1, source_target_pairs={{0,20},{4,16},{8,28},{12,24},{16,4},{20,0},{24,12},{28,8},{1,21},{... | collective-permute-start | bytes 688136 | tf_op jit(solution)/shard_map/ppermute | solution.py:13
  8.5 3.3 %scale_weights.1.refs_4_ = bf16[1792,2048]{1,0:T(8,128)(2,1)S(1)} custom-call(s32[1]{0:T(128)} %bitcast.1.refs_0_, bf16[1,1792,1024]{2,1,0:T(8,128)(2,1)} %refs_1_.1, bf16[1,1792,1024]{2,1,0:T(8,128)(2,1)} %refs_2_.1, f32[1,8,56]{2,1,0:T(8,128)S(1)} %bitcast.64, f32[1,8,56]{2,1,0:T(8,128)S(1)} %bitcast.65), custom_call_target="tpu_custom_call" | custom-call | flops 3670016 | bytes 14680064 | tf_op jit(solution)/shard_map/scale_weights/pallas_call | solution.py:84
  11.8 0.8 collective-permute-start.1
  12.6 4.9 %collective-permute-done.2.refs_2_ = bf16[64,1792]{1,0:T(8,128)(2,1)S(1)} collective-permute-done((bf16[64,1792]{1,0:T(8,128)(2,1)}, bf16[64,1792]{1,0:T(8,128)(2,1)S(1)}, u32[]{:S(2)}, u32[]{:S(2)}) %collective-permute-start.2) | collective-permute-done | bytes 229408 | tf_op jit(solution)/shard_map/ppermute | solution.py:13
  17.5 0.9 collective-permute-done.4.refs_3_
  18.4 2.9 %project.3 = bf16[4,64,2048]{2,1,0:T(8,128)(2,1)S(1)} custom-call(bf16[64,1792]{1,0:T(8,128)(2,1)S(1)} %collective-permute-done.6.refs_0_, bf16[64,1792]{1,0:T(8,128)(2,1)S(1)} %collective-permute-done.refs_1_, bf16[64,1792]{1,0:T(8,128)(2,1)S(1)} %collective-permute-done.2.refs_2_, bf16[64,1792]{1,0:T(8,128)(2,1)S(1)} %collective-permute-done.4.refs_3_, ...), custom_call_target="tpu_custom_call" | custom-call | flops 1879048192 | bytes 9306112 | tf_op jit(solution)/shard_map/project/pallas_call | solution.py:183
  21.4 1.6 %collective-permute-start.8 = (bf16[64,2048]{1,0:T(8,128)(2,1)S(1)}, bf16[64,2048]{1,0:T(8,128)(2,1)S(1)}, u32[]{:S(2)}, u32[]{:S(2)}) collective-permute-start(bf16[64,2048]{1,0:T(8,128)(2,1)S(1)} %get-tuple-element.56), channel_id=1, source_target_pairs={{0,1},{1,2},{2,3},{3,0},{4,5},{5,6},{6,7},{7,4},{8,9},{9,10},{10,1... | collective-permute-start | bytes 786440 | tf_op jit(solution)/shard_map/ppermute | solution.py:275
  23.0 2.2 %collective-permute-start.11 = (bf16[64,2048]{1,0:T(8,128)(2,1)S(1)}, bf16[64,2048]{1,0:T(8,128)(2,1)S(1)}, u32[]{:S(2)}, u32[]{:S(2)}) collective-permute-start(bf16[64,2048]{1,0:T(8,128)(2,1)S(1)} %get-tuple-element.31), channel_id=1, source_target_pairs={{0,3},{1,0},{2,1},{3,2},{4,7},{5,4},{6,5},{7,6},{8,11},{9,8},{10,9... | collective-permute-start | bytes 786440 | tf_op jit(solution)/shard_map/ppermute | solution.py:275
  25.3 2.9 %project.2 = bf16[4,64,2048]{2,1,0:T(8,128)(2,1)S(1)} custom-call(bf16[64,1792]{1,0:T(8,128)(2,1)S(1)} %copy-done, bf16[64,1792]{1,0:T(8,128)(2,1)S(1)} %collective-permute-done.1.refs_1_.refs_5_, bf16[64,1792]{1,0:T(8,128)(2,1)S(1)} %collective-permute-done.3.refs_2_.refs_6_, bf16[64,1792]{1,0:T(8,128)(2,1)S(1)} %collective-permute-done.5.refs_3_.refs_7_, ...), custom_call_target="tpu_custom_call" | custom-call | flops 1879048192 | bytes 9306112 | tf_op jit(solution)/shard_map/project/pallas_call | solution.py:183
  28.3 3.8 %collective-permute-start.12 = (bf16[64,2048]{1,0:T(8,128)(2,1)S(1)}, bf16[64,2048]{1,0:T(8,128)(2,1)S(1)}, u32[]{:S(2)}, u32[]{:S(2)}) collective-permute-start(bf16[64,2048]{1,0:T(8,128)(2,1)S(1)} %get-tuple-element.33), channel_id=1, source_target_pairs={{0,3},{1,0},{2,1},{3,2},{4,7},{5,4},{6,5},{7,6},{8,11},{9,8},{10,9... | collective-permute-start | bytes 786440 | tf_op jit(solution)/shard_map/ppermute | solution.py:275
  32.4 4.1 %collective-permute-start.10 = (bf16[64,2048]{1,0:T(8,128)(2,1)S(1)}, bf16[64,2048]{1,0:T(8,128)(2,1)S(1)}, u32[]{:S(2)}, u32[]{:S(2)}) collective-permute-start(bf16[64,2048]{1,0:T(8,128)(2,1)S(1)} %fusion.8), channel_id=1, source_target_pairs={{0,1},{1,2},{2,3},{3,0},{4,5},{5,6},{6,7},{7,4},{8,9},{9,10},{10,1... | collective-permute-start | bytes 786440 | tf_op jit(solution)/shard_map/ppermute | solution.py:275
  36.5 7.1 %collective-permute-done.7 = bf16[64,2048]{1,0:T(8,128)(2,1)S(1)} collective-permute-done((bf16[64,2048]{1,0:T(8,128)(2,1)S(1)}, bf16[64,2048]{1,0:T(8,128)(2,1)S(1)}, u32[]{:S(2)}, u32[]{:S(2)}) %collective-permute-start.7) | collective-permute-done | bytes 262176 | tf_op jit(solution)/shard_map/ppermute | solution.py:275
  43.7 4.0 %collective-permute-start.9 = (bf16[64,2048]{1,0:T(8,128)(2,1)S(1)}, bf16[64,2048]{1,0:T(8,128)(2,1)S(1)}, u32[]{:S(2)}, u32[]{:S(2)}) collective-permute-start(bf16[64,2048]{1,0:T(8,128)(2,1)S(1)} %fusion.9), channel_id=1, source_target_pairs={{0,1},{1,2},{2,3},{3,0},{4,5},{5,6},{6,7},{7,4},{8,9},{9,10},{10,1... | collective-permute-start | bytes 786440 | tf_op jit(solution)/shard_map/ppermute | solution.py:275
  47.7 7.2 %collective-permute-done.10 = bf16[64,2048]{1,0:T(8,128)(2,1)S(1)} collective-permute-done((bf16[64,2048]{1,0:T(8,128)(2,1)S(1)}, bf16[64,2048]{1,0:T(8,128)(2,1)S(1)}, u32[]{:S(2)}, u32[]{:S(2)}) %collective-permute-start.10) | collective-permute-done | bytes 262176 | tf_op jit(solution)/shard_map/ppermute | solution.py:275
  55.2 3.8 %collective-permute-start.14 = (bf16[64,2048]{1,0:T(8,128)(2,1)S(1)}, bf16[64,2048]{1,0:T(8,128)(2,1)S(1)}, u32[]{:S(2)}, u32[]{:S(2)}) collective-permute-start(bf16[64,2048]{1,0:T(8,128)(2,1)S(1)} %pad_maximum_fusion), channel_id=1, source_target_pairs={{0,3},{1,0},{2,1},{3,2},{4,7},{5,4},{6,5},{7,6},{8,11},{9,8},{10,9... | collective-permute-start | bytes 786440 | tf_op jit(solution)/shard_map/ppermute | solution.py:275
  59.2 1.4 %collective-permute-done.9 = bf16[64,2048]{1,0:T(8,128)(2,1)S(1)} collective-permute-done((bf16[64,2048]{1,0:T(8,128)(2,1)S(1)}, bf16[64,2048]{1,0:T(8,128)(2,1)S(1)}, u32[]{:S(2)}, u32[]{:S(2)}) %collective-permute-start.9) | collective-permute-done | bytes 262176 | tf_op jit(solution)/shard_map/ppermute | solution.py:275
  61.0 3.8 %collective-permute-start.16 = (bf16[64,2048]{1,0:T(8,128)(2,1)S(1)}, bf16[64,2048]{1,0:T(8,128)(2,1)S(1)}, u32[]{:S(2)}, u32[]{:S(2)}) collective-permute-start(bf16[64,2048]{1,0:T(8,128)(2,1)S(1)} %pad_maximum_fusion.1), channel_id=1, source_target_pairs={{0,3},{1,0},{2,1},{3,2},{4,7},{5,4},{6,5},{7,6},{8,11},{9,8},{10,9... | collective-permute-start | bytes 786440 | tf_op jit(solution)/shard_map/ppermute | solution.py:275
  66.3 3.7 %collective-permute-start.15 = (bf16[64,2048]{1,0:T(8,128)(2,1)S(1)}, bf16[64,2048]{1,0:T(8,128)(2,1)S(1)}, u32[]{:S(2)}, u32[]{:S(2)}) collective-permute-start(bf16[64,2048]{1,0:T(8,128)(2,1)S(1)} %collective-permute-done.13), channel_id=1, source_target_pairs={{0,1},{1,2},{2,3},{3,0},{4,5},{5,6},{6,7},{7,4},{8,9},{9,10},{10,1... | collective-permute-start | bytes 786440 | tf_op jit(solution)/shard_map/ppermute | solution.py:275
  70.0 2.0 %collective-permute-done.14 = bf16[64,2048]{1,0:T(8,128)(2,1)S(1)} collective-permute-done((bf16[64,2048]{1,0:T(8,128)(2,1)S(1)}, bf16[64,2048]{1,0:T(8,128)(2,1)S(1)}, u32[]{:S(2)}, u32[]{:S(2)}) %collective-permute-start.14) | collective-permute-done | bytes 262176 | tf_op jit(solution)/shard_map/ppermute | solution.py:275
  72.1 5.4 %collective-permute-done.17 = bf16[64,2048]{1,0:T(8,128)(2,1)S(1)} collective-permute-done((bf16[64,2048]{1,0:T(8,128)(2,1)S(1)}, bf16[64,2048]{1,0:T(8,128)(2,1)S(1)}, u32[]{:S(2)}, u32[]{:S(2)}) %collective-permute-start.17) | collective-permute-done | bytes 262176 | tf_op jit(solution)/shard_map/ppermute | solution.py:275
  77.6 5.4 %collective-permute-done.16 = bf16[64,2048]{1,0:T(8,128)(2,1)S(1)} collective-permute-done((bf16[64,2048]{1,0:T(8,128)(2,1)S(1)}, bf16[64,2048]{1,0:T(8,128)(2,1)S(1)}, u32[]{:S(2)}, u32[]{:S(2)}) %collective-permute-start.16) | collective-permute-done | bytes 262176 | tf_op jit(solution)/shard_map/ppermute | solution.py:275
  83.0 5.8 %collective-permute-done.15 = bf16[64,2048]{1,0:T(8,128)(2,1)S(1)} collective-permute-done((bf16[64,2048]{1,0:T(8,128)(2,1)S(1)}, bf16[64,2048]{1,0:T(8,128)(2,1)S(1)}, u32[]{:S(2)}, u32[]{:S(2)}) %collective-permute-start.15) | collective-permute-done | bytes 262176 | tf_op jit(solution)/shard_map/ppermute | solution.py:275
  88.8 2.1 %convolution_convert_fusion.1 = bf16[256,1792]{1,0:T(8,128)(2,1)S(1)} fusion(bf16[256,2048]{1,0:T(8,128)(2,1)S(1)} %bitcast.62, bf16[1792,2048]{1,0:T(8,128)(2,1)S(1)} %scale_weights.1.refs_4_), kind=kOutput, calls=%fused_computation.1 | convolution fusion | flops 1879506944 | bytes 9306112 | tf_op jit(solution)/shard_map/dot_general | solution.py:355
  91.0 2.8 %collective-permute-done.18 = bf16[64,2048]{1,0:T(8,128)(2,1)S(1)} collective-permute-done((bf16[64,2048]{1,0:T(8,128)(2,1)S(1)}, bf16[64,2048]{1,0:T(8,128)(2,1)S(1)}, u32[]{:S(2)}, u32[]{:S(2)}) %collective-permute-start.18) | collective-permute-done | bytes 262176 | tf_op jit(solution)/shard_map/ppermute | solution.py:275
  93.9 2.1 %convolution_convert_fusion = bf16[256,1792]{1,0:T(8,128)(2,1)S(1)} fusion(bf16[256,2048]{1,0:T(8,128)(2,1)S(1)} %bitcast.60, bf16[1792,2048]{1,0:T(8,128)(2,1)S(1)} %scale_weights.1.refs_4_), kind=kOutput, calls=%fused_computation | convolution fusion | flops 1879506944 | bytes 9306112 | tf_op jit(solution)/shard_map/dot_general | solution.py:355
  96.2 1.6 %collective-permute-start.20 = (bf16[64,1792]{1,0:T(8,128)(2,1)S(1)}, bf16[64,1792]{1,0:T(8,128)(2,1)S(1)}, u32[]{:S(2)}, u32[]{:S(2)}) collective-permute-start(bf16[64,1792]{1,0:T(8,128)(2,1)S(1)} %get-tuple-element.53), channel_id=1, source_target_pairs={{0,8},{4,12},{8,0},{12,4},{16,24},{20,28},{24,16},{28,20},{1,9},{5... | collective-permute-start | bytes 688136 | tf_op jit(solution)/shard_map/ppermute | solution.py:13
  98.4 1.4 %collective-permute-start.22 = (bf16[64,1792]{1,0:T(8,128)(2,1)S(1)}, bf16[64,1792]{1,0:T(8,128)(2,1)S(1)}, u32[]{:S(2)}, u32[]{:S(2)}) collective-permute-start(bf16[64,1792]{1,0:T(8,128)(2,1)S(1)} %get-tuple-element.51), channel_id=1, source_target_pairs={{0,24},{4,28},{8,16},{12,20},{16,8},{20,12},{24,0},{28,4},{1,25},{... | collective-permute-start | bytes 688136 | tf_op jit(solution)/shard_map/ppermute | solution.py:13
  99.8 6.6 %weight_grads.1 = (bf16[1,1792,1024]{2,1,0:T(8,128)(2,1)}, bf16[1,1792,1024]{2,1,0:T(8,128)(2,1)}) custom-call(bf16[64,1792]{1,0:T(8,128)(2,1)S(1)} %collective-permute-done.6.refs_0_, bf16[64,1792]{1,0:T(8,128)(2,1)S(1)} %collective-permute-done.refs_1_, bf16[64,1792]{1,0:T(8,128)(2,1)S(1)} %collective-permute-done.2.refs_2_, ...), custom_call_target="tpu_custom_call" | custom-call | flops 3758096384 | bytes 11272192 | tf_op jit(solution)/shard_map/weight_grads/pallas_call | solution.py:231
  106.4 3.3 %collective-permute-done.21 = bf16[64,1792]{1,0:T(8,128)(2,1)S(1)} collective-permute-done((bf16[64,1792]{1,0:T(8,128)(2,1)S(1)}, bf16[64,1792]{1,0:T(8,128)(2,1)S(1)}, u32[]{:S(2)}, u32[]{:S(2)}) %collective-permute-start.21) | collective-permute-done | bytes 229408 | tf_op jit(solution)/shard_map/ppermute | solution.py:13
  109.7 1.1 convolution_convert_fusion.2
  (54 shorter events, 5.3 us)
Async XLA Ops:
  2.9 8.9 %collective-permute-start = (bf16[64,1792]{1,0:T(8,128)(2,1)}, bf16[64,1792]{1,0:T(8,128)(2,1)S(1)}, u32[]{:S(2)}, u32[]{:S(2)}) collective-permute-start(bf16[64,1792]{1,0:T(8,128)(2,1)} %get-tuple-element.28), channel_id=1, source_target_pairs={{0,12},{4,8},{8,4},{12,0},{16,28},{20,24},{24,20},{28,16},{1,13},{... | collective-permute-start | bytes 688136 | tf_op jit(solution)/shard_map/ppermute | solution.py:13
  5.3 12.2 %collective-permute-start.2 = (bf16[64,1792]{1,0:T(8,128)(2,1)}, bf16[64,1792]{1,0:T(8,128)(2,1)S(1)}, u32[]{:S(2)}, u32[]{:S(2)}) collective-permute-start(bf16[64,1792]{1,0:T(8,128)(2,1)} %get-tuple-element.29), channel_id=1, source_target_pairs={{0,20},{4,16},{8,28},{12,24},{16,4},{20,0},{24,12},{28,8},{1,21},{... | collective-permute-start | bytes 688136 | tf_op jit(solution)/shard_map/ppermute | solution.py:13
  7.1 11.2 %collective-permute-start.4 = (bf16[64,1792]{1,0:T(8,128)(2,1)}, bf16[64,1792]{1,0:T(8,128)(2,1)S(1)}, u32[]{:S(2)}, u32[]{:S(2)}) collective-permute-start(bf16[64,1792]{1,0:T(8,128)(2,1)} %get-tuple-element.30), channel_id=1, source_target_pairs={{0,28},{4,24},{8,20},{12,16},{16,12},{20,8},{24,4},{28,0},{1,29},{... | collective-permute-start | bytes 688136 | tf_op jit(solution)/shard_map/ppermute | solution.py:13
  7.1 11.3 %collective-permute-start.6 = (bf16[64,1792]{1,0:T(8,128)(2,1)}, bf16[64,1792]{1,0:T(8,128)(2,1)S(1)}, u32[]{:S(2)}, u32[]{:S(2)}) collective-permute-start(bf16[64,1792]{1,0:T(8,128)(2,1)} %get-tuple-element.27.refs_0_.refs_4_), channel_id=1, source_target_pairs={{0,4},{4,0},{8,12},{12,8},{16,20},{20,16},{24,28},{28,24},{1,5},{5... | collective-permute-start | bytes 688136 | tf_op jit(solution)/shard_map/ppermute | solution.py:13
  7.1 0.7 copy-start.1
  7.8 0.7 copy-start.2
  11.8 13.5 %copy-start = (bf16[64,1792]{1,0:T(8,128)(2,1)S(1)}, bf16[64,1792]{1,0:T(8,128)(2,1)}, u32[]{:S(2)}) copy-start(bf16[64,1792]{1,0:T(8,128)(2,1)} %get-tuple-element.27.refs_0_.refs_4_) | copy-start | bytes 688132
  11.8 13.4 %collective-permute-start.1 = (bf16[64,1792]{1,0:T(8,128)(2,1)S(1)}, bf16[64,1792]{1,0:T(8,128)(2,1)S(1)}, u32[]{:S(2)}, u32[]{:S(2)}) collective-permute-start(bf16[64,1792]{1,0:T(8,128)(2,1)S(1)} %collective-permute-done.refs_1_), channel_id=1, source_target_pairs={{0,4},{4,0},{8,12},{12,8},{16,20},{20,16},{24,28},{28,24},{1,5},{5... | collective-permute-start | bytes 688136 | tf_op jit(solution)/shard_map/ppermute | solution.py:13
  17.5 7.8 %collective-permute-start.3 = (bf16[64,1792]{1,0:T(8,128)(2,1)S(1)}, bf16[64,1792]{1,0:T(8,128)(2,1)S(1)}, u32[]{:S(2)}, u32[]{:S(2)}) collective-permute-start(bf16[64,1792]{1,0:T(8,128)(2,1)S(1)} %collective-permute-done.2.refs_2_), channel_id=1, source_target_pairs={{0,4},{4,0},{8,12},{12,8},{16,20},{20,16},{24,28},{28,24},{1,5},{5... | collective-permute-start | bytes 688136 | tf_op jit(solution)/shard_map/ppermute | solution.py:13
  18.4 6.9 %collective-permute-start.5 = (bf16[64,1792]{1,0:T(8,128)(2,1)S(1)}, bf16[64,1792]{1,0:T(8,128)(2,1)S(1)}, u32[]{:S(2)}, u32[]{:S(2)}) collective-permute-start(bf16[64,1792]{1,0:T(8,128)(2,1)S(1)} %collective-permute-done.4.refs_3_), channel_id=1, source_target_pairs={{0,4},{4,0},{8,12},{12,8},{16,20},{20,16},{24,28},{28,24},{1,5},{5... | collective-permute-start | bytes 688136 | tf_op jit(solution)/shard_map/ppermute | solution.py:13
  21.4 11.0 %collective-permute-start.8 = (bf16[64,2048]{1,0:T(8,128)(2,1)S(1)}, bf16[64,2048]{1,0:T(8,128)(2,1)S(1)}, u32[]{:S(2)}, u32[]{:S(2)}) collective-permute-start(bf16[64,2048]{1,0:T(8,128)(2,1)S(1)} %get-tuple-element.56), channel_id=1, source_target_pairs={{0,1},{1,2},{2,3},{3,0},{4,5},{5,6},{6,7},{7,4},{8,9},{9,10},{10,1... | collective-permute-start | bytes 786440 | tf_op jit(solution)/shard_map/ppermute | solution.py:275
  23.0 24.7 %collective-permute-start.11 = (bf16[64,2048]{1,0:T(8,128)(2,1)S(1)}, bf16[64,2048]{1,0:T(8,128)(2,1)S(1)}, u32[]{:S(2)}, u32[]{:S(2)}) collective-permute-start(bf16[64,2048]{1,0:T(8,128)(2,1)S(1)} %get-tuple-element.31), channel_id=1, source_target_pairs={{0,3},{1,0},{2,1},{3,2},{4,7},{5,4},{6,5},{7,6},{8,11},{9,8},{10,9... | collective-permute-start | bytes 786440 | tf_op jit(solution)/shard_map/ppermute | solution.py:275
  28.1 26.8 %copy-start.3 = (bf16[1,128,1024]{2,1,0:T(8,128)(2,1)S(1)}, bf16[1,128,1024]{2,1,0:T(8,128)(2,1)}, u32[]{:S(2)}) copy-start(bf16[1,128,1024]{2,1,0:T(8,128)(2,1)} %param.13) | copy-start | bytes 786436
  28.2 15.4 %collective-permute-start.7 = (bf16[64,2048]{1,0:T(8,128)(2,1)S(1)}, bf16[64,2048]{1,0:T(8,128)(2,1)S(1)}, u32[]{:S(2)}, u32[]{:S(2)}) collective-permute-start(bf16[64,2048]{1,0:T(8,128)(2,1)S(1)} %get-tuple-element.32), channel_id=1, source_target_pairs={{0,1},{1,2},{2,3},{3,0},{4,5},{5,6},{6,7},{7,4},{8,9},{9,10},{10,1... | collective-permute-start | bytes 786440 | tf_op jit(solution)/shard_map/ppermute | solution.py:275
  28.3 30.8 %collective-permute-start.12 = (bf16[64,2048]{1,0:T(8,128)(2,1)S(1)}, bf16[64,2048]{1,0:T(8,128)(2,1)S(1)}, u32[]{:S(2)}, u32[]{:S(2)}) collective-permute-start(bf16[64,2048]{1,0:T(8,128)(2,1)S(1)} %get-tuple-element.33), channel_id=1, source_target_pairs={{0,3},{1,0},{2,1},{3,2},{4,7},{5,4},{6,5},{7,6},{8,11},{9,8},{10,9... | collective-permute-start | bytes 786440 | tf_op jit(solution)/shard_map/ppermute | solution.py:275
  32.4 22.4 %collective-permute-start.10 = (bf16[64,2048]{1,0:T(8,128)(2,1)S(1)}, bf16[64,2048]{1,0:T(8,128)(2,1)S(1)}, u32[]{:S(2)}, u32[]{:S(2)}) collective-permute-start(bf16[64,2048]{1,0:T(8,128)(2,1)S(1)} %fusion.8), channel_id=1, source_target_pairs={{0,1},{1,2},{2,3},{3,0},{4,5},{5,6},{6,7},{7,4},{8,9},{9,10},{10,1... | collective-permute-start | bytes 786440 | tf_op jit(solution)/shard_map/ppermute | solution.py:275
  43.7 16.9 %collective-permute-start.9 = (bf16[64,2048]{1,0:T(8,128)(2,1)S(1)}, bf16[64,2048]{1,0:T(8,128)(2,1)S(1)}, u32[]{:S(2)}, u32[]{:S(2)}) collective-permute-start(bf16[64,2048]{1,0:T(8,128)(2,1)S(1)} %fusion.9), channel_id=1, source_target_pairs={{0,1},{1,2},{2,3},{3,0},{4,5},{5,6},{6,7},{7,4},{8,9},{9,10},{10,1... | collective-permute-start | bytes 786440 | tf_op jit(solution)/shard_map/ppermute | solution.py:275
  55.2 11.1 %collective-permute-start.13 = (bf16[64,2048]{1,0:T(8,128)(2,1)S(1)}, bf16[64,2048]{1,0:T(8,128)(2,1)S(1)}, u32[]{:S(2)}, u32[]{:S(2)}) collective-permute-start(bf16[64,2048]{1,0:T(8,128)(2,1)S(1)} %pad_maximum_fusion), channel_id=1, source_target_pairs={{0,1},{1,2},{2,3},{3,0},{4,5},{5,6},{6,7},{7,4},{8,9},{9,10},{10,1... | collective-permute-start | bytes 786440 | tf_op jit(solution)/shard_map/ppermute | solution.py:275
  55.2 16.8 %collective-permute-start.14 = (bf16[64,2048]{1,0:T(8,128)(2,1)S(1)}, bf16[64,2048]{1,0:T(8,128)(2,1)S(1)}, u32[]{:S(2)}, u32[]{:S(2)}) collective-permute-start(bf16[64,2048]{1,0:T(8,128)(2,1)S(1)} %pad_maximum_fusion), channel_id=1, source_target_pairs={{0,3},{1,0},{2,1},{3,2},{4,7},{5,4},{6,5},{7,6},{8,11},{9,8},{10,9... | collective-permute-start | bytes 786440 | tf_op jit(solution)/shard_map/ppermute | solution.py:275
  60.9 16.6 %collective-permute-start.17 = (bf16[64,2048]{1,0:T(8,128)(2,1)S(1)}, bf16[64,2048]{1,0:T(8,128)(2,1)S(1)}, u32[]{:S(2)}, u32[]{:S(2)}) collective-permute-start(bf16[64,2048]{1,0:T(8,128)(2,1)S(1)} %pad_maximum_fusion.1), channel_id=1, source_target_pairs={{0,1},{1,2},{2,3},{3,0},{4,5},{5,6},{6,7},{7,4},{8,9},{9,10},{10,1... | collective-permute-start | bytes 786440 | tf_op jit(solution)/shard_map/ppermute | solution.py:275
  61.0 22.0 %collective-permute-start.16 = (bf16[64,2048]{1,0:T(8,128)(2,1)S(1)}, bf16[64,2048]{1,0:T(8,128)(2,1)S(1)}, u32[]{:S(2)}, u32[]{:S(2)}) collective-permute-start(bf16[64,2048]{1,0:T(8,128)(2,1)S(1)} %pad_maximum_fusion.1), channel_id=1, source_target_pairs={{0,3},{1,0},{2,1},{3,2},{4,7},{5,4},{6,5},{7,6},{8,11},{9,8},{10,9... | collective-permute-start | bytes 786440 | tf_op jit(solution)/shard_map/ppermute | solution.py:275
  66.3 22.5 %collective-permute-start.15 = (bf16[64,2048]{1,0:T(8,128)(2,1)S(1)}, bf16[64,2048]{1,0:T(8,128)(2,1)S(1)}, u32[]{:S(2)}, u32[]{:S(2)}) collective-permute-start(bf16[64,2048]{1,0:T(8,128)(2,1)S(1)} %collective-permute-done.13), channel_id=1, source_target_pairs={{0,1},{1,2},{2,3},{3,0},{4,5},{5,6},{6,7},{7,4},{8,9},{9,10},{10,1... | collective-permute-start | bytes 786440 | tf_op jit(solution)/shard_map/ppermute | solution.py:275
  77.5 16.3 %collective-permute-start.18 = (bf16[64,2048]{1,0:T(8,128)(2,1)S(1)}, bf16[64,2048]{1,0:T(8,128)(2,1)S(1)}, u32[]{:S(2)}, u32[]{:S(2)}) collective-permute-start(bf16[64,2048]{1,0:T(8,128)(2,1)S(1)} %collective-permute-done.17), channel_id=1, source_target_pairs={{0,1},{1,2},{2,3},{3,0},{4,5},{5,6},{6,7},{7,4},{8,9},{9,10},{10,1... | collective-permute-start | bytes 786440 | tf_op jit(solution)/shard_map/ppermute | solution.py:275
  90.9 3.0 %collective-permute-start.19 = (bf16[256,1792]{1,0:T(8,128)(2,1)S(1)}, bf16[256,1792]{1,0:T(8,128)(2,1)S(1)}, u32[]{:S(2)}, u32[]{:S(2)}) collective-permute-start(bf16[256,1792]{1,0:T(8,128)(2,1)S(1)} %convolution_convert_fusion.1), channel_id=1, source_target_pairs={{0,4},{4,0},{8,12},{12,8},{16,20},{20,16},{24,28},{28,24},{1,5},{5... | collective-permute-start | bytes 2752520 | tf_op jit(solution)/shard_map/ppermute | solution.py:13
  96.2 10.2 %collective-permute-start.20 = (bf16[64,1792]{1,0:T(8,128)(2,1)S(1)}, bf16[64,1792]{1,0:T(8,128)(2,1)S(1)}, u32[]{:S(2)}, u32[]{:S(2)}) collective-permute-start(bf16[64,1792]{1,0:T(8,128)(2,1)S(1)} %get-tuple-element.53), channel_id=1, source_target_pairs={{0,8},{4,12},{8,0},{12,4},{16,24},{20,28},{24,16},{28,20},{1,9},{5... | collective-permute-start | bytes 688136 | tf_op jit(solution)/shard_map/ppermute | solution.py:13
  97.8 11.8 %collective-permute-start.21 = (bf16[64,1792]{1,0:T(8,128)(2,1)S(1)}, bf16[64,1792]{1,0:T(8,128)(2,1)S(1)}, u32[]{:S(2)}, u32[]{:S(2)}) collective-permute-start(bf16[64,1792]{1,0:T(8,128)(2,1)S(1)} %get-tuple-element.52), channel_id=1, source_target_pairs={{0,16},{4,20},{8,24},{12,28},{16,0},{20,4},{24,8},{28,12},{1,17},{... | collective-permute-start | bytes 688136 | tf_op jit(solution)/shard_map/ppermute | solution.py:13
  98.4 11.3 %copy-start.4 = (bf16[256,128]{1,0:T(8,128)(2,1)S(1)}, bf16[256,128]{1,0:T(8,128)(2,1)}, u32[]{:S(2)}) copy-start(bf16[256,128]{1,0:T(8,128)(2,1)} %get-tuple-element.48) | copy-start | bytes 196612
  98.4 11.3 %collective-permute-start.22 = (bf16[64,1792]{1,0:T(8,128)(2,1)S(1)}, bf16[64,1792]{1,0:T(8,128)(2,1)S(1)}, u32[]{:S(2)}, u32[]{:S(2)}) collective-permute-start(bf16[64,1792]{1,0:T(8,128)(2,1)S(1)} %get-tuple-element.51), channel_id=1, source_target_pairs={{0,24},{4,28},{8,16},{12,20},{16,8},{20,12},{24,0},{28,4},{1,25},{... | collective-permute-start | bytes 688136 | tf_op jit(solution)/shard_map/ppermute | solution.py:13

commit v5 on v4

--- a/solution.py
+++ b/solution.py
@@ -163,35 +163,37 @@
 
 def project_kernel(*refs):
     *block_refs, weight_ref, out_ref, held = refs
-    capacity = block_refs[0].shape[0]
+    part = block_refs[0].shape[0]
+    capacity = out_ref.shape[1]
 
     @pl.when(pl.program_id(0) == 0)
     def _():
         for place, block_ref in enumerate(block_refs):
-            held[place * capacity : (place + 1) * capacity, :] = block_ref[...]
+            held[place * part : (place + 1) * part, :] = block_ref[...]
 
     sums = jnp.dot(held[...], weight_ref[...], preferred_element_type=jnp.float32)
-    for place in range(len(block_refs)):
-        out_ref[place] = sums[place * capacity : (place + 1) * capacity].astype(jnp.bfloat16)
-
-
-def projected(blocks, weights):
-    count = len(blocks)
+    for owner in range(out_ref.shape[0]):
+        out_ref[owner] = sums[owner * capacity : (owner + 1) * capacity].astype(jnp.bfloat16)
+
+
+def projected(blocks, half, owners, weights):
     capacity, feat_cols = blocks[0].shape
+    part = capacity // 2
+    rows = len(blocks) * part
     units = weights.shape[1]
     tile = math.gcd(units, 1024)
     return pl.pallas_call(
         project_kernel,
-        out_shape=jax.ShapeDtypeStruct((count, capacity, units), jnp.bfloat16),
+        out_shape=jax.ShapeDtypeStruct((owners, rows // owners, units), jnp.bfloat16),
         grid=(units // tile,),
-        in_specs=[pl.BlockSpec((capacity, feat_cols), lambda i: (0, 0))] * count
+        in_specs=[pl.BlockSpec((part, feat_cols), lambda i: (half, 0))] * len(blocks)
         + [pl.BlockSpec((feat_cols, tile), lambda i: (0, i))],
-        out_specs=pl.BlockSpec((count, capacity, tile), lambda i: (0, 0, i)),
-        scratch_shapes=[pltpu.VMEM((count * capacity, feat_cols), jnp.bfloat16)],
+        out_specs=pl.BlockSpec((owners, rows // owners, tile), lambda i: (0, 0, i)),
+        scratch_shapes=[pltpu.VMEM((rows, feat_cols), jnp.bfloat16)],
         compiler_params=pltpu.CompilerParams(vmem_limit_bytes=24 * 2**20),
         cost_estimate=pl.CostEstimate(
-            flops=2 * count * capacity * feat_cols * units,
-            bytes_accessed=2 * (count * capacity * (feat_cols + units) + feat_cols * units),
+            flops=2 * rows * feat_cols * units,
+            bytes_accessed=2 * (rows * (feat_cols + units) + feat_cols * units),
             transcendentals=0,
         ),
         name="project",
@@ -199,32 +201,25 @@
 
 
 def weight_kernel(count, *refs):
-    input_refs, grad_refs = refs[:count], refs[count:-3]
-    gate_ref, up_ref, held = refs[-3:]
-    half_units = gate_ref.shape[2]
-
-    @pl.when(pl.program_id(0) == 0)
-    def _():
-        place = 0
-        for grad_ref in grad_refs:
-            held[place : place + grad_ref.shape[0], :] = grad_ref[...]
-            place += grad_ref.shape[0]
-
-    inputs = jnp.concatenate([input_ref[...] for input_ref in input_refs], 0)
-    for out_ref, offset in ((gate_ref, 0), (up_ref, half_units)):
-        out_ref[0] = lax.dot_general(
+    block_refs, grad_ref, before_refs = refs[:count], refs[count], refs[count + 1 : -2]
+    half_units = refs[-1].shape[2]
+    inputs = jnp.concatenate([block_ref[...] for block_ref in block_refs], 0)
+    for place, out_ref in enumerate(refs[-2:]):
+        sums = lax.dot_general(
             inputs,
-            held[:, offset : offset + half_units],
+            grad_ref[:, place * half_units : (place + 1) * half_units],
             (((0,), (0,)), ((), ())),
             preferred_element_type=jnp.float32,
-        ).astype(jnp.bfloat16)
-
-
-def weight_grads(inputs, grads):
-    count = len(inputs)
-    rows = sum(value.shape[0] for value in inputs)
-    feat_cols = inputs[0].shape[1]
-    units = grads[0].shape[1]
+        )
+        if before_refs:
+            sums = sums + before_refs[place][0].astype(jnp.float32)
+        out_ref[0] = sums.astype(jnp.bfloat16)
+
+
+def weight_grads(blocks, half, grads, before=()):
+    count = len(blocks)
+    rows, units = grads.shape
+    capacity, feat_cols = blocks[0].shape
     tile = 256 if feat_cols % 256 == 0 else feat_cols
     out = jax.ShapeDtypeStruct((1, feat_cols, units // 2), jnp.bfloat16)
     out_spec = pl.BlockSpec((1, tile, units // 2), lambda i: (0, i, 0))
@@ -232,10 +227,10 @@
         lambda *refs: weight_kernel(count, *refs),
         out_shape=(out, out),
         grid=(feat_cols // tile,),
-        in_specs=[pl.BlockSpec((value.shape[0], tile), lambda i: (0, i)) for value in inputs]
-        + [pl.BlockSpec(value.shape, lambda i: (0, 0)) for value in grads],
+        in_specs=[pl.BlockSpec((capacity // 2, tile), lambda i: (half, i))] * count
+        + [pl.BlockSpec((rows, units), lambda i: (0, 0))]
+        + [out_spec] * len(before),
         out_specs=(out_spec, out_spec),
-        scratch_shapes=[pltpu.VMEM((rows, units), jnp.bfloat16)],
         compiler_params=pltpu.CompilerParams(vmem_limit_bytes=16 * 2**20),
         cost_estimate=pl.CostEstimate(
             flops=2 * rows * feat_cols * units,
@@ -243,7 +238,7 @@
             transcendentals=0,
         ),
         name="weight_grads",
-    )(*inputs, *grads)
+    )(*blocks, grads, *before)
 
 
 def earlier(value, *needed):
@@ -284,6 +279,7 @@
     row_total, feat_cols = tokens.shape
     experts = counts.shape[1]
     capacity = min(4 * row_total // experts, row_total // 2)
+    part = capacity // 2
     n_fsdp = lax.axis_size("fsdp")
     chips = lax.axis_size("expert") // 2
     half_units = gate_values.shape[2]
@@ -296,7 +292,7 @@
     weights = scaled_weights(
         gate_values, up_values, gate_scales, up_scales, index * feat_cols
     )
-    cots = grad_hidden[0].reshape(2, capacity, half_units)
+    cots = grad_hidden[0].reshape(2, 2, part, half_units)
     chains = [Chain(chip, n_fsdp) for _ in range(2)]
     hiddens = [None, None]
     token = None
@@ -304,34 +300,35 @@
     def ordered(value):
         return value if token is None else earlier(value, token)
 
-    def begin(group):
+    def begin(half):
         nonlocal token
-        chain = chains[group]
-        chain.partial = projected(inputs[group], weights)
+        chain = chains[half]
+        chain.partial = projected(inputs, half, chips, weights)
         for way, reach in chain.reach.items():
             if reach:
                 token = ordered(chain.block(way * reach))
                 chain.send(way, token)
 
-    def reduce(group, way, step):
+    def reduce(half, way, step):
         nonlocal token
-        chain = chains[group]
+        chain = chains[half]
         token = add_rounded(
             chain.block(way * (chain.reach[way] - step)), ordered(chain.came[way])
         )
         chain.send(way, token)
 
-    def activate(group):
+    def activate(half):
         nonlocal token
-        chain = chains[group]
+        chain = chains[half]
         pre = chain.block(0).astype(jnp.float32)
         for came in chain.came.values():
             pre = pre + ordered(came).astype(jnp.float32)
         gate_pre = pre[:, :half_units]
         up_pre = pre[:, half_units:]
-        cot = pick(cots, parity ^ (1 - group)).astype(jnp.float32)
+        cot = jnp.concatenate([pick(cots, 1 - parity)[half], pick(cots, parity)[half]], 0)
+        cot = cot.astype(jnp.float32)
         sigmoid_gate = jax.nn.sigmoid(gate_pre)
-        hiddens[group] = (gate_pre * sigmoid_gate * up_pre).astype(jnp.bfloat16)
+        hiddens[half] = (gate_pre * sigmoid_gate * up_pre).astype(jnp.bfloat16)
         grad_gate_pre = cot * up_pre * sigmoid_gate * (1.0 + gate_pre * (1.0 - sigmoid_gate))
         grad_up_pre = cot * gate_pre * sigmoid_gate
         token = jnp.concatenate(
@@ -343,56 +340,63 @@
         chain.whole = jnp.zeros((chips, capacity, 2 * half_units), jnp.bfloat16)
         chain.place(token, 0)
 
-    def gather(group, way, step):
+    def gather(half, step):
         nonlocal token
-        chain = chains[group]
-        token = ordered(chain.came[way])
-        chain.place(token, -way * step)
-        if step < chain.reach[way]:
-            chain.send(way, token)
-
-    def back(whole):
-        return lax.dot_general(
+        chain = chains[half]
+        for way, reach in chain.reach.items():
+            if step <= reach:
+                token = ordered(chain.came[way])
+                chain.place(token, -way * step)
+                if step < reach:
+                    chain.send(way, token)
+
+    def give_back(whole):
+        back = lax.dot_general(
             whole, weights, (((1,), (1,)), ((), ())), preferred_element_type=jnp.float32
         ).astype(jnp.bfloat16)
+        back = back.reshape(chips, 2, part, feat_cols)
+        sums = add_rounded(back[:, 1], swap(back[:, 0], "expert", 1))
+        return sums, [swap(sums[mask], "expert", 2 * mask) if mask else sums[0] for mask in masks]
 
     arrived = {mask: swap(packed[mask], "expert", 2 * mask + 1) for mask in reversed(masks)}
-    inputs = [
-        [arrived[mask] for mask in masks],
-        [swap(arrived[mask], "expert", 1) if mask else packed[0] for mask in masks],
-    ]
-    for group in range(2):
-        begin(group)
-    steps = range(1, n_fsdp)
-    for step in steps:
-        for group in range(2):
-            for way, reach in chains[group].reach.items():
-                if step < reach:
-                    reduce(group, way, step)
-    for group in range(2):
-        activate(group)
-    for step in steps:
-        for group in range(2):
-            for way, reach in chains[group].reach.items():
-                if step <= reach:
-                    gather(group, way, step)
-    wholes = [chain.whole.reshape(chips * capacity, 2 * half_units) for chain in chains]
-
-    taken = swap(back(wholes[0]), "expert", 1)
-    kept = back(earlier(wholes[1], taken))
-    pieces = []
+    inputs = []
     for mask in masks:
-        rows = slice(mask * capacity, (mask + 1) * capacity)
-        both = add_rounded(kept[rows], taken[rows])
-        pieces.append(swap(both, "expert", 2 * mask) if mask else both)
-
+        inputs += [arrived[mask], swap(arrived[mask], "expert", 1) if mask else packed[0]]
+    for half in range(2):
+        begin(half)
+    reach = chains[0].reach[1]
+    for step in range(1, reach):
+        for half in range(2):
+            for way in chains[half].reach:
+                if step < chains[half].reach[way]:
+                    reduce(half, way, step)
+    activate(0)
+    for step in range(1, reach):
+        gather(0, step)
+    activate(1)
+    gather(0, reach)
+    whole = chains[0].whole.reshape(chips * capacity, 2 * half_units)
+    token, low = give_back(whole)
+    partly = weight_grads(inputs, 0, whole)
+    for step in range(1, reach):
+        gather(1, step)
+    came, *kept = lax.optimization_barrier((chains[1].came[1], *low, *partly))
+    chains[1].came[1], low, partly = came, kept[:chips], kept[chips:]
+    gather(1, reach)
+    whole = chains[1].whole.reshape(chips * capacity, 2 * half_units)
+    sums, high = give_back(whole)
+
+    own, other = (
+        jnp.concatenate([rows[side * part : (side + 1) * part] for rows in hiddens], 0)
+        for side in (1, 0)
+    )
     hidden = jnp.where(
-        parity == 0, jnp.concatenate([hiddens[1], hiddens[0]], 0), jnp.concatenate(hiddens, 0)
-    )
-    grad_gate, grad_up = weight_grads(inputs[0] + inputs[1], wholes)
+        parity == 0, jnp.concatenate([own, other], 0), jnp.concatenate([other, own], 0)
+    )
+    grad_gate, grad_up = weight_grads(inputs, 1, earlier(whole, sums), partly)
     grad_tokens = lax.dot_general(
         chooser,
-        jnp.concatenate(pieces, 0),
+        jnp.concatenate([pieces[mask] for mask in masks for pieces in (low, high)], 0),
         (((0,), (0,)), ((), ())),
         preferred_element_type=jnp.float32,
     ).astype(jnp.bfloat16)

time: 111 us -> 131 us (1.18)
  waiting for transfers between devices: 47.1 us -> 54.8 us
  matrix products: 5.29 us -> 8.47 us
  local copies, waits for them, and re-layouts: 1.84 us -> 4.76 us
  Pallas kernels: 17.9 us -> 20.3 us
  starting transfers between devices: 36 us -> 37.7 us
  other arithmetic: 1.69 us -> 3.12 us
    ppermute x11 -> x15, waiting for transfers between devices: 9 us -> 15.9 us  [swap(): return lax.ppermute(value, axis, pairs)]
    ppermute x11 -> x15, starting transfers between devices: 8.7 us -> 12.5 us  [swap(): return lax.ppermute(value, axis, pairs)]
    dot_general x3, matrix products: 5.29 us -> 8.47 us  [the longest x2 7.39 us: give_back(): lax.dot_general(whole, weights, (((1,), (1,)), ((), ())), preferred_eleme...]
    pallas_call x1 -> x2, Pallas kernels: 6.59 us -> 8.9 us  [weight_grads(): pl.pallas_call(lambda *refs: weight_kernel(count, *refs), out_shape=(out,...]
    ppermute x12, starting transfers between devices: 27.3 us -> 25.3 us  [send(): self.came[way] = lax.ppermute(value, 'fsdp', ring)]
    dynamic_update_slice x6, local copies, waits for them, and re-layouts: 0.13 us -> 2.05 us  [place(): lax.dynamic_update_index_in_dim(self.whole, value, self.owner(steps) ^ se...]
  transfers between devices with their start and end apart: 23 -> 27, of which waited for: 13 -> 14; matrix products, arithmetic and copies ran while one was open for 4% -> 4% of each run, Pallas kernels for 14% -> 12%
where the time goes in v5:
time: 131 us; the launch traced here: 130 us
  waiting for transfers between devices  54.8 us (42%)
  starting transfers between devices  37.7 us (29%)
  Pallas kernels  20.3 us (15%)
  matrix products  8.47 us (6%)
  local copies, waits for them, and re-layouts  4.76 us (4%)
  other arithmetic  3.12 us (2%)
    ppermute x12, waiting for transfers between devices, send(): self.came[way] = lax.ppermute(value, 'fsdp', ring)  38.9 us
    ppermute x12, starting transfers between devices, send(): self.came[way] = lax.ppermute(value, 'fsdp', ring)  25.3 us
    ppermute x15, waiting for transfers between devices, swap(): return lax.ppermute(value, axis, pairs)  15.9 us
    ppermute x15, starting transfers between devices, swap(): return lax.ppermute(value, axis, pairs)  12.5 us
    pallas_call x2, Pallas kernels, weight_grads(): pl.pallas_call(lambda *refs: weight_kernel(count, *refs), out_shape=(out,...  8.9 us
    dot_general x2, matrix products, give_back(): lax.dot_general(whole, weights, (((1,), (1,)), ((), ())), preferred_eleme...  7.39 us
    pallas_call x2, Pallas kernels, projected(): pl.pallas_call(project_kernel, out_shape=jax.ShapeDtypeStruct((owners, ro...  5.72 us
    pallas_call x1, Pallas kernels, scaled_weights(): pl.pallas_call(lambda *refs: scale_kernel(sub, *refs), out_shape=jax.Shap...  3.35 us
  transfers between devices with their start and end apart: 27, of which 14 were waited for; matrix products, arithmetic and copies ran while one was open for 4% of the time, Pallas kernels for 12%

profile of v5, /device:TPU:0, one launch (start us, length us, event | category | flops | bytes accessed | tf_op | source)
XLA Modules:
  0.0 130.2 jit_solution(10041925778913125575)
XLA Ops:
  0.6 2.3 %pack_rows.1 = (bf16[256,128]{1,0:T(8,128)(2,1)}, bf16[64,1792]{1,0:T(8,128)(2,1)}, bf16[64,1792]{1,0:T(8,128)(2,1)}, bf16[64,1792]{1,0:T(8,128)(2,1)}, bf16[64,1792]{1,0:T(8,128)(2,1)}) custom-call(s32[1]{0:T(128)} %bitcast.chip_ref, s32[1,4]{1,0:T(1,128)} %counts_ref.1, bf16[128,1792]{1,0:T(8,128)(2,1)} %tokens_ref.1), custom_call_target="tpu_custom_call" | custom-call | flops 117440512 | bytes 1376256 | tf_op jit(solution)/shard_map/pack_rows/pallas_call | solution.py:148
  2.9 2.4 %collective-permute-start.1 = (bf16[64,1792]{1,0:T(8,128)(2,1)}, bf16[64,1792]{1,0:T(8,128)(2,1)S(1)}, u32[]{:S(2)}, u32[]{:S(2)}) collective-permute-start(bf16[64,1792]{1,0:T(8,128)(2,1)} %get-tuple-element.37), channel_id=1, source_target_pairs={{0,12},{4,8},{8,4},{12,0},{16,28},{20,24},{24,20},{28,16},{1,13},{... | collective-permute-start | bytes 688136 | tf_op jit(solution)/shard_map/ppermute | solution.py:13
  5.3 1.8 %collective-permute-start.3 = (bf16[64,1792]{1,0:T(8,128)(2,1)}, bf16[64,1792]{1,0:T(8,128)(2,1)S(1)}, u32[]{:S(2)}, u32[]{:S(2)}) collective-permute-start(bf16[64,1792]{1,0:T(8,128)(2,1)} %get-tuple-element.38), channel_id=1, source_target_pairs={{0,20},{4,16},{8,28},{12,24},{16,4},{20,0},{24,12},{28,8},{1,21},{... | collective-permute-start | bytes 688136 | tf_op jit(solution)/shard_map/ppermute | solution.py:13
  7.1 4.5 %collective-permute-done.1.refs_2_ = bf16[64,1792]{1,0:T(8,128)(2,1)S(1)} collective-permute-done((bf16[64,1792]{1,0:T(8,128)(2,1)}, bf16[64,1792]{1,0:T(8,128)(2,1)S(1)}, u32[]{:S(2)}, u32[]{:S(2)}) %collective-permute-start.1) | collective-permute-done | bytes 229408 | tf_op jit(solution)/shard_map/ppermute | solution.py:13
  12.6 4.9 %collective-permute-done.3.refs_4_ = bf16[64,1792]{1,0:T(8,128)(2,1)S(1)} collective-permute-done((bf16[64,1792]{1,0:T(8,128)(2,1)}, bf16[64,1792]{1,0:T(8,128)(2,1)S(1)}, u32[]{:S(2)}, u32[]{:S(2)}) %collective-permute-start.3) | collective-permute-done | bytes 229408 | tf_op jit(solution)/shard_map/ppermute | solution.py:13
  19.8 3.4 %scale_weights.1.refs_8_ = bf16[1792,2048]{1,0:T(8,128)(2,1)S(1)} custom-call(s32[1]{0:T(128)} %bitcast.1.refs_0_, bf16[1,1792,1024]{2,1,0:T(8,128)(2,1)} %refs_1_.1, bf16[1,1792,1024]{2,1,0:T(8,128)(2,1)} %refs_2_.1, f32[1,8,56]{2,1,0:T(8,128)S(1)} %bitcast.111, f32[1,8,56]{2,1,0:T(8,128)S(1)} %bitcast.112), custom_call_target="tpu_custom_call" | custom-call | flops 3670016 | bytes 14680064 | tf_op jit(solution)/shard_map/scale_weights/pallas_call | solution.py:84
  24.0 2.9 %project.2 = bf16[4,64,2048]{2,1,0:T(8,128)(2,1)S(1)} custom-call(bf16[64,1792]{1,0:T(8,128)(2,1)S(1)} %collective-permute-done.refs_0_, bf16[64,1792]{1,0:T(8,128)(2,1)S(1)} %copy-done.1, bf16[64,1792]{1,0:T(8,128)(2,1)S(1)} %collective-permute-done.1.refs_2_, bf16[64,1792]{1,0:T(8,128)(2,1)S(1)} %collective-permute-done.2.refs_3_, ...), custom_call_target="tpu_custom_call" | custom-call | flops 1879048192 | bytes 9306112 | tf_op jit(solution)/shard_map/project/pallas_call | solution.py:185
  26.9 1.6 %collective-permute-start.7 = (bf16[64,2048]{1,0:T(8,128)(2,1)S(1)}, bf16[64,2048]{1,0:T(8,128)(2,1)S(1)}, u32[]{:S(2)}, u32[]{:S(2)}) collective-permute-start(bf16[64,2048]{1,0:T(8,128)(2,1)S(1)} %get-tuple-element.68), channel_id=1, source_target_pairs={{0,1},{1,2},{2,3},{3,0},{4,5},{5,6},{6,7},{7,4},{8,9},{9,10},{10,1... | collective-permute-start | bytes 786440 | tf_op jit(solution)/shard_map/ppermute | solution.py:270
  28.6 2.2 %collective-permute-start.10 = (bf16[64,2048]{1,0:T(8,128)(2,1)S(1)}, bf16[64,2048]{1,0:T(8,128)(2,1)S(1)}, u32[]{:S(2)}, u32[]{:S(2)}) collective-permute-start(bf16[64,2048]{1,0:T(8,128)(2,1)S(1)} %get-tuple-element.40), channel_id=1, source_target_pairs={{0,3},{1,0},{2,1},{3,2},{4,7},{5,4},{6,5},{7,6},{8,11},{9,8},{10,9... | collective-permute-start | bytes 786440 | tf_op jit(solution)/shard_map/ppermute | solution.py:270
  30.8 2.9 %project.3 = bf16[4,64,2048]{2,1,0:T(8,128)(2,1)S(1)} custom-call(bf16[64,1792]{1,0:T(8,128)(2,1)S(1)} %collective-permute-done.refs_0_, bf16[64,1792]{1,0:T(8,128)(2,1)S(1)} %copy-done.1, bf16[64,1792]{1,0:T(8,128)(2,1)S(1)} %collective-permute-done.1.refs_2_, bf16[64,1792]{1,0:T(8,128)(2,1)S(1)} %collective-permute-done.2.refs_3_, ...), custom_call_target="tpu_custom_call" | custom-call | flops 1879048192 | bytes 9306112 | tf_op jit(solution)/shard_map/project/pallas_call | solution.py:185
  33.8 4.1 %collective-permute-done.7 = bf16[64,2048]{1,0:T(8,128)(2,1)S(1)} collective-permute-done((bf16[64,2048]{1,0:T(8,128)(2,1)S(1)}, bf16[64,2048]{1,0:T(8,128)(2,1)S(1)}, u32[]{:S(2)}, u32[]{:S(2)}) %collective-permute-start.7) | collective-permute-done | bytes 262176 | tf_op jit(solution)/shard_map/ppermute | solution.py:270
  38.0 4.1 %collective-permute-start.8 = (bf16[64,2048]{1,0:T(8,128)(2,1)S(1)}, bf16[64,2048]{1,0:T(8,128)(2,1)S(1)}, u32[]{:S(2)}, u32[]{:S(2)}) collective-permute-start(bf16[64,2048]{1,0:T(8,128)(2,1)S(1)} %fusion.4), channel_id=1, source_target_pairs={{0,1},{1,2},{2,3},{3,0},{4,5},{5,6},{6,7},{7,4},{8,9},{9,10},{10,1... | collective-permute-start | bytes 786440 | tf_op jit(solution)/shard_map/ppermute | solution.py:270
  42.1 7.1 %collective-permute-done.9 = bf16[64,2048]{1,0:T(8,128)(2,1)S(1)} collective-permute-done((bf16[64,2048]{1,0:T(8,128)(2,1)S(1)}, bf16[64,2048]{1,0:T(8,128)(2,1)S(1)}, u32[]{:S(2)}, u32[]{:S(2)}) %collective-permute-start.9) | collective-permute-done | bytes 262176 | tf_op jit(solution)/shard_map/ppermute | solution.py:270
  49.9 4.4 %collective-permute-done.8 = bf16[64,2048]{1,0:T(8,128)(2,1)S(1)} collective-permute-done((bf16[64,2048]{1,0:T(8,128)(2,1)S(1)}, bf16[64,2048]{1,0:T(8,128)(2,1)S(1)}, u32[]{:S(2)}, u32[]{:S(2)}) %collective-permute-start.8) | collective-permute-done | bytes 262176 | tf_op jit(solution)/shard_map/ppermute | solution.py:270
  55.4 3.8 %collective-permute-start.12 = (bf16[64,2048]{1,0:T(8,128)(2,1)}, bf16[64,2048]{1,0:T(8,128)(2,1)}, u32[]{:S(2)}, u32[]{:S(2)}) collective-permute-start(bf16[64,2048]{1,0:T(8,128)(2,1)} %pad_maximum_fusion), channel_id=1, source_target_pairs={{0,3},{1,0},{2,1},{3,2},{4,7},{5,4},{6,5},{7,6},{8,11},{9,8},{10,9... | collective-permute-start | bytes 786440 | tf_op jit(solution)/shard_map/ppermute | solution.py:270
  59.2 2.0 %collective-permute-start.11 = (bf16[64,2048]{1,0:T(8,128)(2,1)}, bf16[64,2048]{1,0:T(8,128)(2,1)S(1)}, u32[]{:S(2)}, u32[]{:S(2)}) collective-permute-start(bf16[64,2048]{1,0:T(8,128)(2,1)} %fusion.3), channel_id=1, source_target_pairs={{0,1},{1,2},{2,3},{3,0},{4,5},{5,6},{6,7},{7,4},{8,9},{9,10},{10,1... | collective-permute-start | bytes 786440 | tf_op jit(solution)/shard_map/ppermute | solution.py:270
  61.4 5.3 %collective-permute-done.13 = bf16[64,2048]{1,0:T(8,128)(2,1)} collective-permute-done((bf16[64,2048]{1,0:T(8,128)(2,1)}, bf16[64,2048]{1,0:T(8,128)(2,1)}, u32[]{:S(2)}, u32[]{:S(2)}) %collective-permute-start.13) | collective-permute-done | bytes 262176 | tf_op jit(solution)/shard_map/ppermute | solution.py:270
  66.7 7.5 %collective-permute-start.16 = (bf16[64,2048]{1,0:T(8,128)(2,1)}, bf16[64,2048]{1,0:T(8,128)(2,1)S(1)}, u32[]{:S(2)}, u32[]{:S(2)}) collective-permute-start(bf16[64,2048]{1,0:T(8,128)(2,1)} %collective-permute-done.13), channel_id=1, source_target_pairs={{0,1},{1,2},{2,3},{3,0},{4,5},{5,6},{6,7},{7,4},{8,9},{9,10},{10,1... | collective-permute-start | bytes 786440 | tf_op jit(solution)/shard_map/ppermute | solution.py:270
  76.2 7.2 %collective-permute-done.11 = bf16[64,2048]{1,0:T(8,128)(2,1)S(1)} collective-permute-done((bf16[64,2048]{1,0:T(8,128)(2,1)}, bf16[64,2048]{1,0:T(8,128)(2,1)S(1)}, u32[]{:S(2)}, u32[]{:S(2)}) %collective-permute-start.11) | collective-permute-done | bytes 262176 | tf_op jit(solution)/shard_map/ppermute | solution.py:270
  83.8 4.1 %collective-permute-done.16 = bf16[64,2048]{1,0:T(8,128)(2,1)S(1)} collective-permute-done((bf16[64,2048]{1,0:T(8,128)(2,1)}, bf16[64,2048]{1,0:T(8,128)(2,1)S(1)}, u32[]{:S(2)}, u32[]{:S(2)}) %collective-permute-start.16) | collective-permute-done | bytes 262176 | tf_op jit(solution)/shard_map/ppermute | solution.py:270
  87.8 5.3 %convolution_convert_fusion.1 = bf16[256,1792]{1,0:T(8,128)(2,1)S(1)} fusion(bf16[256,2048]{1,0:T(8,128)(2,1)S(1)} %bitcast.109, bf16[1792,2048]{1,0:T(8,128)(2,1)} %copy-done), kind=kOutput, calls=%fused_computation.1 | convolution fusion | flops 1879506944 | bytes 9306112 | tf_op jit(solution)/shard_map/dot_general | solution.py:354
  93.4 3.8 %collective-permute-start.18 = (bf16[64,2048]{1,0:T(8,128)(2,1)S(1)}, bf16[64,2048]{1,0:T(8,128)(2,1)S(1)}, u32[]{:S(2)}, u32[]{:S(2)}) collective-permute-start(bf16[64,2048]{1,0:T(8,128)(2,1)S(1)} %pad_maximum_fusion.1), channel_id=1, source_target_pairs={{0,3},{1,0},{2,1},{3,2},{4,7},{5,4},{6,5},{7,6},{8,11},{9,8},{10,9... | collective-permute-start | bytes 786440 | tf_op jit(solution)/shard_map/ppermute | solution.py:270
  97.3 3.6 %weight_grads.2 = (bf16[1,1792,1024]{2,1,0:T(8,128)(2,1)S(1)}, bf16[1,1792,1024]{2,1,0:T(8,128)(2,1)S(1)}) custom-call(bf16[64,1792]{1,0:T(8,128)(2,1)S(1)} %collective-permute-done.refs_0_, bf16[64,1792]{1,0:T(8,128)(2,1)S(1)} %copy-done.1, bf16[64,1792]{1,0:T(8,128)(2,1)S(1)} %collective-permute-done.1.refs_2_, ...), custom_call_target="tpu_custom_call" | custom-call | flops 1879048192 | bytes 9306112 | tf_op jit(solution)/shard_map/weight_grads/pallas_call | solution.py:226
  101.1 3.2 %collective-permute-done.15 = bf16[64,2048]{1,0:T(8,128)(2,1)S(1)} collective-permute-done((bf16[64,2048]{1,0:T(8,128)(2,1)S(1)}, bf16[64,2048]{1,0:T(8,128)(2,1)S(1)}, u32[]{:S(2)}, u32[]{:S(2)}) %collective-permute-start.15) | collective-permute-done | bytes 262176 | tf_op jit(solution)/shard_map/ppermute | solution.py:270
  104.3 3.4 %collective-permute-done.18 = bf16[64,2048]{1,0:T(8,128)(2,1)S(1)} collective-permute-done((bf16[64,2048]{1,0:T(8,128)(2,1)S(1)}, bf16[64,2048]{1,0:T(8,128)(2,1)S(1)}, u32[]{:S(2)}, u32[]{:S(2)}) %collective-permute-start.18) | collective-permute-done | bytes 262176 | tf_op jit(solution)/shard_map/ppermute | solution.py:270
  107.7 1.5 %collective-permute-start.22 = (bf16[32,1792]{1,0:T(8,128)(2,1)S(1)}, bf16[32,1792]{1,0:T(8,128)(2,1)S(1)}, u32[]{:S(2)}, u32[]{:S(2)}) collective-permute-start(bf16[32,1792]{1,0:T(8,128)(2,1)S(1)} %get-tuple-element.81), channel_id=1, source_target_pairs={{0,24},{4,28},{8,16},{12,20},{16,8},{20,12},{24,0},{28,4},{1,25},{... | collective-permute-start | bytes 344072 | tf_op jit(solution)/shard_map/ppermute | solution.py:13
  109.2 1.4 %collective-permute-start.21 = (bf16[32,1792]{1,0:T(8,128)(2,1)S(1)}, bf16[32,1792]{1,0:T(8,128)(2,1)S(1)}, u32[]{:S(2)}, u32[]{:S(2)}) collective-permute-start(bf16[32,1792]{1,0:T(8,128)(2,1)S(1)} %get-tuple-element.82), channel_id=1, source_target_pairs={{0,16},{4,20},{8,24},{12,28},{16,0},{20,4},{24,8},{28,12},{1,17},{... | collective-permute-start | bytes 344072 | tf_op jit(solution)/shard_map/ppermute | solution.py:13
  111.2 3.1 %collective-permute-done.22 = bf16[32,1792]{1,0:T(8,128)(2,1)S(1)} collective-permute-done((bf16[32,1792]{1,0:T(8,128)(2,1)S(1)}, bf16[32,1792]{1,0:T(8,128)(2,1)S(1)}, u32[]{:S(2)}, u32[]{:S(2)}) %collective-permute-start.22) | collective-permute-done | bytes 114720 | tf_op jit(solution)/shard_map/ppermute | solution.py:13
  114.4 1.5 %collective-permute-done.21 = bf16[32,1792]{1,0:T(8,128)(2,1)S(1)} collective-permute-done((bf16[32,1792]{1,0:T(8,128)(2,1)S(1)}, bf16[32,1792]{1,0:T(8,128)(2,1)S(1)}, u32[]{:S(2)}, u32[]{:S(2)}) %collective-permute-start.21) | collective-permute-done | bytes 114720 | tf_op jit(solution)/shard_map/ppermute | solution.py:13
  115.9 2.1 %convolution_convert_fusion = bf16[256,1792]{1,0:T(8,128)(2,1)S(1)} fusion(bf16[256,2048]{1,0:T(8,128)(2,1)S(1)} %bitcast.107, bf16[1792,2048]{1,0:T(8,128)(2,1)S(1)} %bitcast.106), kind=kOutput, calls=%fused_computation | convolution fusion | flops 1879506944 | bytes 9306112 | tf_op jit(solution)/shard_map/dot_general | solution.py:354
  120.1 1.6 %collective-permute-start.26 = (bf16[32,1792]{1,0:T(8,128)(2,1)S(1)}, bf16[32,1792]{1,0:T(8,128)(2,1)S(1)}, u32[]{:S(2)}, u32[]{:S(2)}) collective-permute-start(bf16[32,1792]{1,0:T(8,128)(2,1)S(1)} %get-tuple-element.78), channel_id=1, source_target_pairs={{0,24},{4,28},{8,16},{12,20},{16,8},{20,12},{24,0},{28,4},{1,25},{... | collective-permute-start | bytes 344072 | tf_op jit(solution)/shard_map/ppermute | solution.py:13
  123.7 5.3 %weight_grads.3 = (bf16[1,1792,1024]{2,1,0:T(8,128)(2,1)}, bf16[1,1792,1024]{2,1,0:T(8,128)(2,1)}) custom-call(bf16[64,1792]{1,0:T(8,128)(2,1)S(1)} %collective-permute-done.refs_0_, bf16[64,1792]{1,0:T(8,128)(2,1)S(1)} %copy-done.1, bf16[64,1792]{1,0:T(8,128)(2,1)S(1)} %collective-permute-done.1.refs_2_, ...), custom_call_target="tpu_custom_call" | custom-call | flops 1879048192 | bytes 9306112 | tf_op jit(solution)/shard_map/weight_grads/pallas_call | solution.py:226
  (90 shorter events, 14.8 us)
Async XLA Ops:
  2.9 8.7 %collective-permute-start.1 = (bf16[64,1792]{1,0:T(8,128)(2,1)}, bf16[64,1792]{1,0:T(8,128)(2,1)S(1)}, u32[]{:S(2)}, u32[]{:S(2)}) collective-permute-start(bf16[64,1792]{1,0:T(8,128)(2,1)} %get-tuple-element.37), channel_id=1, source_target_pairs={{0,12},{4,8},{8,4},{12,0},{16,28},{20,24},{24,20},{28,16},{1,13},{... | collective-permute-start | bytes 688136 | tf_op jit(solution)/shard_map/ppermute | solution.py:13
  5.3 12.2 %collective-permute-start.3 = (bf16[64,1792]{1,0:T(8,128)(2,1)}, bf16[64,1792]{1,0:T(8,128)(2,1)S(1)}, u32[]{:S(2)}, u32[]{:S(2)}) collective-permute-start(bf16[64,1792]{1,0:T(8,128)(2,1)} %get-tuple-element.38), channel_id=1, source_target_pairs={{0,20},{4,16},{8,28},{12,24},{16,4},{20,0},{24,12},{28,8},{1,21},{... | collective-permute-start | bytes 688136 | tf_op jit(solution)/shard_map/ppermute | solution.py:13
  7.1 11.2 %collective-permute-start.5 = (bf16[64,1792]{1,0:T(8,128)(2,1)}, bf16[64,1792]{1,0:T(8,128)(2,1)S(1)}, u32[]{:S(2)}, u32[]{:S(2)}) collective-permute-start(bf16[64,1792]{1,0:T(8,128)(2,1)} %get-tuple-element.39), channel_id=1, source_target_pairs={{0,28},{4,24},{8,20},{12,16},{16,12},{20,8},{24,4},{28,0},{1,29},{... | collective-permute-start | bytes 688136 | tf_op jit(solution)/shard_map/ppermute | solution.py:13
  7.1 16.9 %collective-permute-start = (bf16[64,1792]{1,0:T(8,128)(2,1)}, bf16[64,1792]{1,0:T(8,128)(2,1)S(1)}, u32[]{:S(2)}, u32[]{:S(2)}) collective-permute-start(bf16[64,1792]{1,0:T(8,128)(2,1)} %get-tuple-element.36.refs_1_), channel_id=1, source_target_pairs={{0,4},{4,0},{8,12},{12,8},{16,20},{20,16},{24,28},{28,24},{1,5},{5... | collective-permute-start | bytes 688136 | tf_op jit(solution)/shard_map/ppermute | solution.py:13
  11.6 12.3 %collective-permute-start.2 = (bf16[64,1792]{1,0:T(8,128)(2,1)S(1)}, bf16[64,1792]{1,0:T(8,128)(2,1)S(1)}, u32[]{:S(2)}, u32[]{:S(2)}) collective-permute-start(bf16[64,1792]{1,0:T(8,128)(2,1)S(1)} %collective-permute-done.1.refs_2_), channel_id=1, source_target_pairs={{0,4},{4,0},{8,12},{12,8},{16,20},{20,16},{24,28},{28,24},{1,5},{5... | collective-permute-start | bytes 688136 | tf_op jit(solution)/shard_map/ppermute | solution.py:13
  17.5 6.5 %collective-permute-start.4 = (bf16[64,1792]{1,0:T(8,128)(2,1)S(1)}, bf16[64,1792]{1,0:T(8,128)(2,1)S(1)}, u32[]{:S(2)}, u32[]{:S(2)}) collective-permute-start(bf16[64,1792]{1,0:T(8,128)(2,1)S(1)} %collective-permute-done.3.refs_4_), channel_id=1, source_target_pairs={{0,4},{4,0},{8,12},{12,8},{16,20},{20,16},{24,28},{28,24},{1,5},{5... | collective-permute-start | bytes 688136 | tf_op jit(solution)/shard_map/ppermute | solution.py:13
  18.4 5.6 %collective-permute-start.6 = (bf16[64,1792]{1,0:T(8,128)(2,1)S(1)}, bf16[64,1792]{1,0:T(8,128)(2,1)S(1)}, u32[]{:S(2)}, u32[]{:S(2)}) collective-permute-start(bf16[64,1792]{1,0:T(8,128)(2,1)S(1)} %collective-permute-done.5.refs_6_), channel_id=1, source_target_pairs={{0,4},{4,0},{8,12},{12,8},{16,20},{20,16},{24,28},{28,24},{1,5},{5... | collective-permute-start | bytes 688136 | tf_op jit(solution)/shard_map/ppermute | solution.py:13
  23.2 7.6 %copy-start = (bf16[1792,2048]{1,0:T(8,128)(2,1)}, bf16[1792,2048]{1,0:T(8,128)(2,1)S(1)}, u32[]{:S(2)}) copy-start(bf16[1792,2048]{1,0:T(8,128)(2,1)S(1)} %scale_weights.1.refs_8_) | copy-start | bytes 22020100
  26.9 11.0 %collective-permute-start.7 = (bf16[64,2048]{1,0:T(8,128)(2,1)S(1)}, bf16[64,2048]{1,0:T(8,128)(2,1)S(1)}, u32[]{:S(2)}, u32[]{:S(2)}) collective-permute-start(bf16[64,2048]{1,0:T(8,128)(2,1)S(1)} %get-tuple-element.68), channel_id=1, source_target_pairs={{0,1},{1,2},{2,3},{3,0},{4,5},{5,6},{6,7},{7,4},{8,9},{9,10},{10,1... | collective-permute-start | bytes 786440 | tf_op jit(solution)/shard_map/ppermute | solution.py:270
  28.6 21.4 %collective-permute-start.10 = (bf16[64,2048]{1,0:T(8,128)(2,1)S(1)}, bf16[64,2048]{1,0:T(8,128)(2,1)S(1)}, u32[]{:S(2)}, u32[]{:S(2)}) collective-permute-start(bf16[64,2048]{1,0:T(8,128)(2,1)S(1)} %get-tuple-element.40), channel_id=1, source_target_pairs={{0,3},{1,0},{2,1},{3,2},{4,7},{5,4},{6,5},{7,6},{8,11},{9,8},{10,9... | collective-permute-start | bytes 786440 | tf_op jit(solution)/shard_map/ppermute | solution.py:270
  33.7 15.4 %collective-permute-start.9 = (bf16[64,2048]{1,0:T(8,128)(2,1)S(1)}, bf16[64,2048]{1,0:T(8,128)(2,1)S(1)}, u32[]{:S(2)}, u32[]{:S(2)}) collective-permute-start(bf16[64,2048]{1,0:T(8,128)(2,1)S(1)} %get-tuple-element.41), channel_id=1, source_target_pairs={{0,1},{1,2},{2,3},{3,0},{4,5},{5,6},{6,7},{7,4},{8,9},{9,10},{10,1... | collective-permute-start | bytes 786440 | tf_op jit(solution)/shard_map/ppermute | solution.py:270
  38.0 16.4 %collective-permute-start.8 = (bf16[64,2048]{1,0:T(8,128)(2,1)S(1)}, bf16[64,2048]{1,0:T(8,128)(2,1)S(1)}, u32[]{:S(2)}, u32[]{:S(2)}) collective-permute-start(bf16[64,2048]{1,0:T(8,128)(2,1)S(1)} %fusion.4), channel_id=1, source_target_pairs={{0,1},{1,2},{2,3},{3,0},{4,5},{5,6},{6,7},{7,4},{8,9},{9,10},{10,1... | collective-permute-start | bytes 786440 | tf_op jit(solution)/shard_map/ppermute | solution.py:270
  55.4 11.3 %collective-permute-start.13 = (bf16[64,2048]{1,0:T(8,128)(2,1)}, bf16[64,2048]{1,0:T(8,128)(2,1)}, u32[]{:S(2)}, u32[]{:S(2)}) collective-permute-start(bf16[64,2048]{1,0:T(8,128)(2,1)} %pad_maximum_fusion), channel_id=1, source_target_pairs={{0,1},{1,2},{2,3},{3,0},{4,5},{5,6},{6,7},{7,4},{8,9},{9,10},{10,1... | collective-permute-start | bytes 786440 | tf_op jit(solution)/shard_map/ppermute | solution.py:270
  55.4 18.9 %collective-permute-start.12 = (bf16[64,2048]{1,0:T(8,128)(2,1)}, bf16[64,2048]{1,0:T(8,128)(2,1)}, u32[]{:S(2)}, u32[]{:S(2)}) collective-permute-start(bf16[64,2048]{1,0:T(8,128)(2,1)} %pad_maximum_fusion), channel_id=1, source_target_pairs={{0,3},{1,0},{2,1},{3,2},{4,7},{5,4},{6,5},{7,6},{8,11},{9,8},{10,9... | collective-permute-start | bytes 786440 | tf_op jit(solution)/shard_map/ppermute | solution.py:270
  59.2 24.3 %copy-start.4 = (bf16[32,1024]{1,0:T(8,128)(2,1)S(1)}, bf16[32,1024]{1,0:T(8,128)(2,1)}, u32[]{:S(2)}) copy-start(bf16[32,1024]{1,0:T(8,128)(2,1)} %get-tuple-element.85) | copy-start | bytes 196612
  59.2 24.4 %copy-start.5 = (bf16[32,1024]{1,0:T(8,128)(2,1)S(1)}, bf16[32,1024]{1,0:T(8,128)(2,1)}, u32[]{:S(2)}) copy-start(bf16[32,1024]{1,0:T(8,128)(2,1)} %get-tuple-element.88) | copy-start | bytes 196612
  59.2 16.0 %collective-permute-start.14 = (bf16[64,2048]{1,0:T(8,128)(2,1)S(1)}, bf16[64,2048]{1,0:T(8,128)(2,1)S(1)}, u32[]{:S(2)}, u32[]{:S(2)}) collective-permute-start(bf16[64,2048]{1,0:T(8,128)(2,1)S(1)} %get-tuple-element.42), channel_id=1, source_target_pairs={{0,3},{1,0},{2,1},{3,2},{4,7},{5,4},{6,5},{7,6},{8,11},{9,8},{10,9... | collective-permute-start | bytes 786440 | tf_op jit(solution)/shard_map/ppermute | solution.py:270
  59.2 24.2 %collective-permute-start.11 = (bf16[64,2048]{1,0:T(8,128)(2,1)}, bf16[64,2048]{1,0:T(8,128)(2,1)S(1)}, u32[]{:S(2)}, u32[]{:S(2)}) collective-permute-start(bf16[64,2048]{1,0:T(8,128)(2,1)} %fusion.3), channel_id=1, source_target_pairs={{0,1},{1,2},{2,3},{3,0},{4,5},{5,6},{6,7},{7,4},{8,9},{9,10},{10,1... | collective-permute-start | bytes 786440 | tf_op jit(solution)/shard_map/ppermute | solution.py:270
  66.7 21.1 %collective-permute-start.16 = (bf16[64,2048]{1,0:T(8,128)(2,1)}, bf16[64,2048]{1,0:T(8,128)(2,1)S(1)}, u32[]{:S(2)}, u32[]{:S(2)}) collective-permute-start(bf16[64,2048]{1,0:T(8,128)(2,1)} %collective-permute-done.13), channel_id=1, source_target_pairs={{0,1},{1,2},{2,3},{3,0},{4,5},{5,6},{6,7},{7,4},{8,9},{9,10},{10,1... | collective-permute-start | bytes 786440 | tf_op jit(solution)/shard_map/ppermute | solution.py:270
  93.1 22.7 %slice-start = ((s8[7340032]{0:T(1024)(128)(4,1)}), s8[4194304]{0:T(1024)(128)(4,1)S(1)}, s32[]{:S(2)}) async-start(s8[7340032]{0:T(1024)(128)(4,1)} %bitcast.105), calls=%async_computation | async-start | bytes 8388608
  93.2 7.7 %collective-permute-start.17 = (bf16[4,32,1792]{2,1,0:T(8,128)(2,1)S(1)}, bf16[4,32,1792]{2,1,0:T(8,128)(2,1)S(1)}, u32[]{:S(2)}, u32[]{:S(2)}) collective-permute-start(bf16[4,32,1792]{2,1,0:T(8,128)(2,1)S(1)} %slice_bitcast_fusion.2), channel_id=1, source_target_pairs={{0,4},{4,0},{8,12},{12,8},{16,20},{20,16},{24,28},{28,24},{1,5},{5... | collective-permute-start | bytes 1376264 | tf_op jit(solution)/shard_map/ppermute | solution.py:13
  93.3 11.0 %collective-permute-start.15 = (bf16[64,2048]{1,0:T(8,128)(2,1)S(1)}, bf16[64,2048]{1,0:T(8,128)(2,1)S(1)}, u32[]{:S(2)}, u32[]{:S(2)}) collective-permute-start(bf16[64,2048]{1,0:T(8,128)(2,1)S(1)} %pad_maximum_fusion.1), channel_id=1, source_target_pairs={{0,1},{1,2},{2,3},{3,0},{4,5},{5,6},{6,7},{7,4},{8,9},{9,10},{10,1... | collective-permute-start | bytes 786440 | tf_op jit(solution)/shard_map/ppermute | solution.py:270
  93.4 14.4 %collective-permute-start.18 = (bf16[64,2048]{1,0:T(8,128)(2,1)S(1)}, bf16[64,2048]{1,0:T(8,128)(2,1)S(1)}, u32[]{:S(2)}, u32[]{:S(2)}) collective-permute-start(bf16[64,2048]{1,0:T(8,128)(2,1)S(1)} %pad_maximum_fusion.1), channel_id=1, source_target_pairs={{0,3},{1,0},{2,1},{3,2},{4,7},{5,4},{6,5},{7,6},{8,11},{9,8},{10,9... | collective-permute-start | bytes 786440 | tf_op jit(solution)/shard_map/ppermute | solution.py:270
  97.3 18.6 %slice-start.1 = ((s8[7340032]{0:T(1024)(128)(4,1)}), s8[3145728]{0:T(1024)(128)(4,1)S(1)}, s32[]{:S(2)}) async-start(s8[7340032]{0:T(1024)(128)(4,1)} %bitcast.105), calls=%async_computation.1 | async-start | bytes 6291456
  104.3 11.6 %collective-permute-start.19 = (bf16[64,2048]{1,0:T(8,128)(2,1)S(1)}, bf16[64,2048]{1,0:T(8,128)(2,1)S(1)}, u32[]{:S(2)}, u32[]{:S(2)}) collective-permute-start(bf16[64,2048]{1,0:T(8,128)(2,1)S(1)} %collective-permute-done.15), channel_id=1, source_target_pairs={{0,1},{1,2},{2,3},{3,0},{4,5},{5,6},{6,7},{7,4},{8,9},{9,10},{10,1... | collective-permute-start | bytes 786440 | tf_op jit(solution)/shard_map/ppermute | solution.py:270
  107.7 6.7 %collective-permute-start.22 = (bf16[32,1792]{1,0:T(8,128)(2,1)S(1)}, bf16[32,1792]{1,0:T(8,128)(2,1)S(1)}, u32[]{:S(2)}, u32[]{:S(2)}) collective-permute-start(bf16[32,1792]{1,0:T(8,128)(2,1)S(1)} %get-tuple-element.81), channel_id=1, source_target_pairs={{0,24},{4,28},{8,16},{12,20},{16,8},{20,12},{24,0},{28,4},{1,25},{... | collective-permute-start | bytes 344072 | tf_op jit(solution)/shard_map/ppermute | solution.py:13
  109.2 6.6 %collective-permute-start.21 = (bf16[32,1792]{1,0:T(8,128)(2,1)S(1)}, bf16[32,1792]{1,0:T(8,128)(2,1)S(1)}, u32[]{:S(2)}, u32[]{:S(2)}) collective-permute-start(bf16[32,1792]{1,0:T(8,128)(2,1)S(1)} %get-tuple-element.82), channel_id=1, source_target_pairs={{0,16},{4,20},{8,24},{12,28},{16,0},{20,4},{24,8},{28,12},{1,17},{... | collective-permute-start | bytes 344072 | tf_op jit(solution)/shard_map/ppermute | solution.py:13
  110.6 5.2 %collective-permute-start.20 = (bf16[32,1792]{1,0:T(8,128)(2,1)S(1)}, bf16[32,1792]{1,0:T(8,128)(2,1)S(1)}, u32[]{:S(2)}, u32[]{:S(2)}) collective-permute-start(bf16[32,1792]{1,0:T(8,128)(2,1)S(1)} %get-tuple-element.83), channel_id=1, source_target_pairs={{0,8},{4,12},{8,0},{12,4},{16,24},{20,28},{24,16},{28,20},{1,9},{5... | collective-permute-start | bytes 344072 | tf_op jit(solution)/shard_map/ppermute | solution.py:13
  118.1 1.9 %collective-permute-start.23 = (bf16[4,32,1792]{2,1,0:T(8,128)(2,1)S(1)}, bf16[4,32,1792]{2,1,0:T(8,128)(2,1)S(1)}, u32[]{:S(2)}, u32[]{:S(2)}) collective-permute-start(bf16[4,32,1792]{2,1,0:T(8,128)(2,1)S(1)} %slice_bitcast_fusion), channel_id=1, source_target_pairs={{0,4},{4,0},{8,12},{12,8},{16,20},{20,16},{24,28},{28,24},{1,5},{5... | collective-permute-start | bytes 1376264 | tf_op jit(solution)/shard_map/ppermute | solution.py:13
  120.1 9.0 %collective-permute-start.26 = (bf16[32,1792]{1,0:T(8,128)(2,1)S(1)}, bf16[32,1792]{1,0:T(8,128)(2,1)S(1)}, u32[]{:S(2)}, u32[]{:S(2)}) collective-permute-start(bf16[32,1792]{1,0:T(8,128)(2,1)S(1)} %get-tuple-element.78), channel_id=1, source_target_pairs={{0,24},{4,28},{8,16},{12,20},{16,8},{20,12},{24,0},{28,4},{1,25},{... | collective-permute-start | bytes 344072 | tf_op jit(solution)/shard_map/ppermute | solution.py:13
  121.7 7.4 %collective-permute-start.25 = (bf16[32,1792]{1,0:T(8,128)(2,1)S(1)}, bf16[32,1792]{1,0:T(8,128)(2,1)S(1)}, u32[]{:S(2)}, u32[]{:S(2)}) collective-permute-start(bf16[32,1792]{1,0:T(8,128)(2,1)S(1)} %get-tuple-element.79), channel_id=1, source_target_pairs={{0,16},{4,20},{8,24},{12,28},{16,0},{20,4},{24,8},{28,12},{1,17},{... | collective-permute-start | bytes 344072 | tf_op jit(solution)/shard_map/ppermute | solution.py:13
  123.0 6.0 %collective-permute-start.24 = (bf16[32,1792]{1,0:T(8,128)(2,1)S(1)}, bf16[32,1792]{1,0:T(8,128)(2,1)S(1)}, u32[]{:S(2)}, u32[]{:S(2)}) collective-permute-start(bf16[32,1792]{1,0:T(8,128)(2,1)S(1)} %get-tuple-element.80), channel_id=1, source_target_pairs={{0,8},{4,12},{8,0},{12,4},{16,24},{20,28},{24,16},{28,20},{1,9},{5... | collective-permute-start | bytes 344072 | tf_op jit(solution)/shard_map/ppermute | solution.py:13
  (5 other events, 14.4 us)

commit v6 on v4

--- a/solution.py
+++ b/solution.py
@@ -123,14 +123,15 @@
     return first, live
 
 
-def pack_kernel(chip_ref, counts_ref, tokens_ref, chooser_ref, *out_refs):
+def pack_kernel(counts_ref, tokens_ref, chooser_ref, *out_refs):
+    chip = lax.axis_index("expert") // 2
     row_total = tokens_ref.shape[0]
     capacity = out_refs[0].shape[0]
     row = lax.broadcasted_iota(jnp.int32, (capacity, row_total), 1)
     slot = lax.broadcasted_iota(jnp.int32, (capacity, row_total), 0)
     hits = []
     for mask in range(len(out_refs)):
-        first, live = rows_of(counts_ref, chip_ref[0] ^ mask)
+        first, live = rows_of(counts_ref, chip ^ mask)
         hits.append(((row == first + slot) & (slot < live)).astype(jnp.float32))
     chooser = jnp.concatenate(hits, 0).astype(jnp.bfloat16)
     chooser_ref[...] = chooser
@@ -139,25 +140,29 @@
         out_ref[...] = chosen[mask * capacity : (mask + 1) * capacity].astype(jnp.bfloat16)
 
 
-def packed_rows(tokens, counts, chip, capacity):
+def packed_rows(tokens, counts, capacity):
     row_total, feat_cols = tokens.shape
     experts = counts.shape[1]
-    smem = pl.BlockSpec(memory_space=pltpu.SMEM)
-    vmem = pl.BlockSpec(memory_space=pltpu.VMEM)
+    tile = feat_cols // 2 if feat_cols % 256 == 0 else feat_cols
     block = jax.ShapeDtypeStruct((capacity, feat_cols), jnp.bfloat16)
     chooser, *packed = pl.pallas_call(
         pack_kernel,
         out_shape=(jax.ShapeDtypeStruct((experts * capacity, row_total), jnp.bfloat16),)
         + (block,) * experts,
-        in_specs=[smem, smem, vmem],
-        out_specs=(vmem,) * (experts + 1),
+        grid=(feat_cols // tile,),
+        in_specs=[
+            pl.BlockSpec(memory_space=pltpu.SMEM),
+            pl.BlockSpec((row_total, tile), lambda i: (0, i)),
+        ],
+        out_specs=(pl.BlockSpec((experts * capacity, row_total), lambda i: (0, 0)),)
+        + (pl.BlockSpec((capacity, tile), lambda i: (0, i)),) * experts,
         cost_estimate=pl.CostEstimate(
             flops=2 * experts * capacity * row_total * feat_cols,
             bytes_accessed=2 * (row_total + experts * capacity) * feat_cols,
             transcendentals=0,
         ),
         name="pack_rows",
-    )(chip[None], counts, tokens)
+    )(counts, pltpu.with_memory_space_constraint(tokens, pltpu.HBM))
     return chooser, packed
 
 
@@ -179,7 +184,7 @@
     count = len(blocks)
     capacity, feat_cols = blocks[0].shape
     units = weights.shape[1]
-    tile = math.gcd(units, 1024)
+    tile = units
     return pl.pallas_call(
         project_kernel,
         out_shape=jax.ShapeDtypeStruct((count, capacity, units), jnp.bfloat16),
@@ -292,7 +297,7 @@
     index = lax.axis_index("fsdp")
     masks = range(chips)
 
-    chooser, packed = packed_rows(tokens, counts, chip, capacity)
+    chooser, packed = packed_rows(tokens, counts, capacity)
     weights = scaled_weights(
         gate_values, up_values, gate_scales, up_scales, index * feat_cols
     )

time: 111 us -> 110 us (level)
  Pallas kernels: 17.9 us -> 16.4 us
    pallas_call x2, Pallas kernels: 5.72 us -> 4.16 us  [projected(): pl.pallas_call(project_kernel, out_shape=jax.ShapeDtypeStruct((count, cap...]
  transfers between devices with their start and end apart: 23 -> 23, of which waited for: 13 -> 13; matrix products, arithmetic and copies ran while one was open for 4% -> 4% of each run, Pallas kernels for 14% -> 13%
where the time goes in v6:
time: 110 us
  waiting for transfers between devices  48 us (44%)
  starting transfers between devices  36 us (33%)
  Pallas kernels  16.4 us (15%)
  matrix products  5.28 us (5%)
  local copies, waits for them, and re-layouts  1.84 us (2%)
  other arithmetic  1.69 us (2%)
    ppermute x12, waiting for transfers between devices, send(): self.came[way] = lax.ppermute(value, 'fsdp', ring)  38.9 us
    ppermute x12, starting transfers between devices, send(): self.came[way] = lax.ppermute(value, 'fsdp', ring)  27.3 us
    ppermute x11, waiting for transfers between devices, swap(): return lax.ppermute(value, axis, pairs)  9.05 us
    ppermute x11, starting transfers between devices, swap(): return lax.ppermute(value, axis, pairs)  8.69 us
    pallas_call x1, Pallas kernels, weight_grads(): pl.pallas_call(lambda *refs: weight_kernel(count, *refs), out_shape=(out,...  6.59 us
    dot_general x2, matrix products, back(): lax.dot_general(whole, weights, (((1,), (1,)), ((), ())), preferred_eleme...  4.2 us
    pallas_call x2, Pallas kernels, projected(): pl.pallas_call(project_kernel, out_shape=jax.ShapeDtypeStruct((count, cap...  4.16 us
    pallas_call x1, Pallas kernels, scaled_weights(): pl.pallas_call(lambda *refs: scale_kernel(sub, *refs), out_shape=jax.Shap...  3.3 us
  transfers between devices with their start and end apart: 23, of which 13 were waited for; matrix products, arithmetic and copies ran while one was open for 4% of the time, Pallas kernels for 13%

profile of v6, /device:TPU:0, one launch (start us, length us, event | category | flops | bytes accessed | tf_op | source)
XLA Modules:
  0.0 110.1 jit_solution(14029646029457465333)
XLA Ops:
  0.6 2.3 %pack_rows.1 = (bf16[256,128]{1,0:T(8,128)(2,1)}, bf16[64,1792]{1,0:T(8,128)(2,1)}, bf16[64,1792]{1,0:T(8,128)(2,1)}, bf16[64,1792]{1,0:T(8,128)(2,1)}, bf16[64,1792]{1,0:T(8,128)(2,1)}) custom-call(s32[1,4]{1,0:T(1,128)} %counts_ref.1, bf16[128,1792]{1,0:T(8,128)(2,1)} %tokens_ref.1), custom_call_target="tpu_custom_call" | custom-call | flops 117440512 | bytes 1376256 | tf_op jit(solution)/shard_map/pack_rows/pallas_call | solution.py:148
  2.9 2.4 %collective-permute-start = (bf16[64,1792]{1,0:T(8,128)(2,1)}, bf16[64,1792]{1,0:T(8,128)(2,1)S(1)}, u32[]{:S(2)}, u32[]{:S(2)}) collective-permute-start(bf16[64,1792]{1,0:T(8,128)(2,1)} %get-tuple-element.28), channel_id=1, source_target_pairs={{0,12},{4,8},{8,4},{12,0},{16,28},{20,24},{24,20},{28,16},{1,13},{... | collective-permute-start | bytes 688136 | tf_op jit(solution)/shard_map/ppermute | solution.py:13
  5.3 1.8 %collective-permute-start.2 = (bf16[64,1792]{1,0:T(8,128)(2,1)}, bf16[64,1792]{1,0:T(8,128)(2,1)S(1)}, u32[]{:S(2)}, u32[]{:S(2)}) collective-permute-start(bf16[64,1792]{1,0:T(8,128)(2,1)} %get-tuple-element.29), channel_id=1, source_target_pairs={{0,20},{4,16},{8,28},{12,24},{16,4},{20,0},{24,12},{28,8},{1,21},{... | collective-permute-start | bytes 688136 | tf_op jit(solution)/shard_map/ppermute | solution.py:13
  8.5 3.3 %scale_weights.1.refs_4_ = bf16[1792,2048]{1,0:T(8,128)(2,1)S(1)} custom-call(s32[1]{0:T(128)} %bitcast.refs_0_, bf16[1,1792,1024]{2,1,0:T(8,128)(2,1)} %refs_1_.1, bf16[1,1792,1024]{2,1,0:T(8,128)(2,1)} %refs_2_.1, f32[1,8,56]{2,1,0:T(8,128)S(1)} %bitcast.63, f32[1,8,56]{2,1,0:T(8,128)S(1)} %bitcast.64), custom_call_target="tpu_custom_call" | custom-call | flops 3670016 | bytes 14680064 | tf_op jit(solution)/shard_map/scale_weights/pallas_call | solution.py:84
  12.6 4.9 %collective-permute-done.2.refs_2_ = bf16[64,1792]{1,0:T(8,128)(2,1)S(1)} collective-permute-done((bf16[64,1792]{1,0:T(8,128)(2,1)}, bf16[64,1792]{1,0:T(8,128)(2,1)S(1)}, u32[]{:S(2)}, u32[]{:S(2)}) %collective-permute-start.2) | collective-permute-done | bytes 229408 | tf_op jit(solution)/shard_map/ppermute | solution.py:13
  17.5 0.9 collective-permute-done.4.refs_3_
  18.4 2.1 %project.3 = bf16[4,64,2048]{2,1,0:T(8,128)(2,1)S(1)} custom-call(bf16[64,1792]{1,0:T(8,128)(2,1)S(1)} %collective-permute-done.6.refs_0_, bf16[64,1792]{1,0:T(8,128)(2,1)S(1)} %collective-permute-done.refs_1_, bf16[64,1792]{1,0:T(8,128)(2,1)S(1)} %collective-permute-done.2.refs_2_, bf16[64,1792]{1,0:T(8,128)(2,1)S(1)} %collective-permute-done.4.refs_3_, ...), custom_call_target="tpu_custom_call" | custom-call | flops 1879048192 | bytes 9306112 | tf_op jit(solution)/shard_map/project/pallas_call | solution.py:188
  20.6 1.7 %collective-permute-start.8 = (bf16[64,2048]{1,0:T(8,128)(2,1)S(1)}, bf16[64,2048]{1,0:T(8,128)(2,1)S(1)}, u32[]{:S(2)}, u32[]{:S(2)}) collective-permute-start(bf16[64,2048]{1,0:T(8,128)(2,1)S(1)} %get-tuple-element.56), channel_id=1, source_target_pairs={{0,1},{1,2},{2,3},{3,0},{4,5},{5,6},{6,7},{7,4},{8,9},{9,10},{10,1... | collective-permute-start | bytes 786440 | tf_op jit(solution)/shard_map/ppermute | solution.py:280
  22.3 2.2 %collective-permute-start.11 = (bf16[64,2048]{1,0:T(8,128)(2,1)S(1)}, bf16[64,2048]{1,0:T(8,128)(2,1)S(1)}, u32[]{:S(2)}, u32[]{:S(2)}) collective-permute-start(bf16[64,2048]{1,0:T(8,128)(2,1)S(1)} %get-tuple-element.31), channel_id=1, source_target_pairs={{0,3},{1,0},{2,1},{3,2},{4,7},{5,4},{6,5},{7,6},{8,11},{9,8},{10,9... | collective-permute-start | bytes 786440 | tf_op jit(solution)/shard_map/ppermute | solution.py:280
  24.5 2.1 %project.2 = bf16[4,64,2048]{2,1,0:T(8,128)(2,1)S(1)} custom-call(bf16[64,1792]{1,0:T(8,128)(2,1)S(1)} %copy-done, bf16[64,1792]{1,0:T(8,128)(2,1)S(1)} %collective-permute-done.1.refs_1_.refs_5_, bf16[64,1792]{1,0:T(8,128)(2,1)S(1)} %collective-permute-done.3.refs_2_.refs_6_, bf16[64,1792]{1,0:T(8,128)(2,1)S(1)} %collective-permute-done.5.refs_3_.refs_7_, ...), custom_call_target="tpu_custom_call" | custom-call | flops 1879048192 | bytes 9306112 | tf_op jit(solution)/shard_map/project/pallas_call | solution.py:188
  26.7 3.8 %collective-permute-start.12 = (bf16[64,2048]{1,0:T(8,128)(2,1)S(1)}, bf16[64,2048]{1,0:T(8,128)(2,1)S(1)}, u32[]{:S(2)}, u32[]{:S(2)}) collective-permute-start(bf16[64,2048]{1,0:T(8,128)(2,1)S(1)} %get-tuple-element.33), channel_id=1, source_target_pairs={{0,3},{1,0},{2,1},{3,2},{4,7},{5,4},{6,5},{7,6},{8,11},{9,8},{10,9... | collective-permute-start | bytes 786440 | tf_op jit(solution)/shard_map/ppermute | solution.py:280
  30.5 1.1 collective-permute-done.8
  31.7 4.1 %collective-permute-start.10 = (bf16[64,2048]{1,0:T(8,128)(2,1)S(1)}, bf16[64,2048]{1,0:T(8,128)(2,1)S(1)}, u32[]{:S(2)}, u32[]{:S(2)}) collective-permute-start(bf16[64,2048]{1,0:T(8,128)(2,1)S(1)} %fusion.8), channel_id=1, source_target_pairs={{0,1},{1,2},{2,3},{3,0},{4,5},{5,6},{6,7},{7,4},{8,9},{9,10},{10,1... | collective-permute-start | bytes 786440 | tf_op jit(solution)/shard_map/ppermute | solution.py:280
  35.8 7.1 %collective-permute-done.7 = bf16[64,2048]{1,0:T(8,128)(2,1)S(1)} collective-permute-done((bf16[64,2048]{1,0:T(8,128)(2,1)S(1)}, bf16[64,2048]{1,0:T(8,128)(2,1)S(1)}, u32[]{:S(2)}, u32[]{:S(2)}) %collective-permute-start.7) | collective-permute-done | bytes 262176 | tf_op jit(solution)/shard_map/ppermute | solution.py:280
  43.0 4.0 %collective-permute-start.9 = (bf16[64,2048]{1,0:T(8,128)(2,1)S(1)}, bf16[64,2048]{1,0:T(8,128)(2,1)S(1)}, u32[]{:S(2)}, u32[]{:S(2)}) collective-permute-start(bf16[64,2048]{1,0:T(8,128)(2,1)S(1)} %fusion.9), channel_id=1, source_target_pairs={{0,1},{1,2},{2,3},{3,0},{4,5},{5,6},{6,7},{7,4},{8,9},{9,10},{10,1... | collective-permute-start | bytes 786440 | tf_op jit(solution)/shard_map/ppermute | solution.py:280
  47.0 7.2 %collective-permute-done.10 = bf16[64,2048]{1,0:T(8,128)(2,1)S(1)} collective-permute-done((bf16[64,2048]{1,0:T(8,128)(2,1)S(1)}, bf16[64,2048]{1,0:T(8,128)(2,1)S(1)}, u32[]{:S(2)}, u32[]{:S(2)}) %collective-permute-start.10) | collective-permute-done | bytes 262176 | tf_op jit(solution)/shard_map/ppermute | solution.py:280
  54.5 3.8 %collective-permute-start.14 = (bf16[64,2048]{1,0:T(8,128)(2,1)S(1)}, bf16[64,2048]{1,0:T(8,128)(2,1)S(1)}, u32[]{:S(2)}, u32[]{:S(2)}) collective-permute-start(bf16[64,2048]{1,0:T(8,128)(2,1)S(1)} %pad_maximum_fusion), channel_id=1, source_target_pairs={{0,3},{1,0},{2,1},{3,2},{4,7},{5,4},{6,5},{7,6},{8,11},{9,8},{10,9... | collective-permute-start | bytes 786440 | tf_op jit(solution)/shard_map/ppermute | solution.py:280
  58.4 1.4 %collective-permute-done.9 = bf16[64,2048]{1,0:T(8,128)(2,1)S(1)} collective-permute-done((bf16[64,2048]{1,0:T(8,128)(2,1)S(1)}, bf16[64,2048]{1,0:T(8,128)(2,1)S(1)}, u32[]{:S(2)}, u32[]{:S(2)}) %collective-permute-start.9) | collective-permute-done | bytes 262176 | tf_op jit(solution)/shard_map/ppermute | solution.py:280
  60.2 3.8 %collective-permute-start.16 = (bf16[64,2048]{1,0:T(8,128)(2,1)S(1)}, bf16[64,2048]{1,0:T(8,128)(2,1)S(1)}, u32[]{:S(2)}, u32[]{:S(2)}) collective-permute-start(bf16[64,2048]{1,0:T(8,128)(2,1)S(1)} %pad_maximum_fusion.1), channel_id=1, source_target_pairs={{0,3},{1,0},{2,1},{3,2},{4,7},{5,4},{6,5},{7,6},{8,11},{9,8},{10,9... | collective-permute-start | bytes 786440 | tf_op jit(solution)/shard_map/ppermute | solution.py:280
  65.5 3.8 %collective-permute-start.15 = (bf16[64,2048]{1,0:T(8,128)(2,1)S(1)}, bf16[64,2048]{1,0:T(8,128)(2,1)S(1)}, u32[]{:S(2)}, u32[]{:S(2)}) collective-permute-start(bf16[64,2048]{1,0:T(8,128)(2,1)S(1)} %collective-permute-done.13), channel_id=1, source_target_pairs={{0,1},{1,2},{2,3},{3,0},{4,5},{5,6},{6,7},{7,4},{8,9},{9,10},{10,1... | collective-permute-start | bytes 786440 | tf_op jit(solution)/shard_map/ppermute | solution.py:280
  69.3 2.0 %collective-permute-done.14 = bf16[64,2048]{1,0:T(8,128)(2,1)S(1)} collective-permute-done((bf16[64,2048]{1,0:T(8,128)(2,1)S(1)}, bf16[64,2048]{1,0:T(8,128)(2,1)S(1)}, u32[]{:S(2)}, u32[]{:S(2)}) %collective-permute-start.14) | collective-permute-done | bytes 262176 | tf_op jit(solution)/shard_map/ppermute | solution.py:280
  71.3 5.4 %collective-permute-done.17 = bf16[64,2048]{1,0:T(8,128)(2,1)S(1)} collective-permute-done((bf16[64,2048]{1,0:T(8,128)(2,1)S(1)}, bf16[64,2048]{1,0:T(8,128)(2,1)S(1)}, u32[]{:S(2)}, u32[]{:S(2)}) %collective-permute-start.17) | collective-permute-done | bytes 262176 | tf_op jit(solution)/shard_map/ppermute | solution.py:280
  76.8 5.4 %collective-permute-done.16 = bf16[64,2048]{1,0:T(8,128)(2,1)S(1)} collective-permute-done((bf16[64,2048]{1,0:T(8,128)(2,1)S(1)}, bf16[64,2048]{1,0:T(8,128)(2,1)S(1)}, u32[]{:S(2)}, u32[]{:S(2)}) %collective-permute-start.16) | collective-permute-done | bytes 262176 | tf_op jit(solution)/shard_map/ppermute | solution.py:280
  82.3 5.8 %collective-permute-done.15 = bf16[64,2048]{1,0:T(8,128)(2,1)S(1)} collective-permute-done((bf16[64,2048]{1,0:T(8,128)(2,1)S(1)}, bf16[64,2048]{1,0:T(8,128)(2,1)S(1)}, u32[]{:S(2)}, u32[]{:S(2)}) %collective-permute-start.15) | collective-permute-done | bytes 262176 | tf_op jit(solution)/shard_map/ppermute | solution.py:280
  88.0 2.1 %convolution_convert_fusion.1 = bf16[256,1792]{1,0:T(8,128)(2,1)S(1)} fusion(bf16[256,2048]{1,0:T(8,128)(2,1)S(1)} %bitcast.61, bf16[1792,2048]{1,0:T(8,128)(2,1)S(1)} %scale_weights.1.refs_4_), kind=kOutput, calls=%fused_computation.1 | convolution fusion | flops 1879506944 | bytes 9306112 | tf_op jit(solution)/shard_map/dot_general | solution.py:360
  90.3 2.9 %collective-permute-done.18 = bf16[64,2048]{1,0:T(8,128)(2,1)S(1)} collective-permute-done((bf16[64,2048]{1,0:T(8,128)(2,1)S(1)}, bf16[64,2048]{1,0:T(8,128)(2,1)S(1)}, u32[]{:S(2)}, u32[]{:S(2)}) %collective-permute-start.18) | collective-permute-done | bytes 262176 | tf_op jit(solution)/shard_map/ppermute | solution.py:280
  93.2 2.1 %convolution_convert_fusion = bf16[256,1792]{1,0:T(8,128)(2,1)S(1)} fusion(bf16[256,2048]{1,0:T(8,128)(2,1)S(1)} %bitcast.59, bf16[1792,2048]{1,0:T(8,128)(2,1)S(1)} %scale_weights.1.refs_4_), kind=kOutput, calls=%fused_computation | convolution fusion | flops 1879506944 | bytes 9306112 | tf_op jit(solution)/shard_map/dot_general | solution.py:360
  95.5 1.6 %collective-permute-start.20 = (bf16[64,1792]{1,0:T(8,128)(2,1)S(1)}, bf16[64,1792]{1,0:T(8,128)(2,1)S(1)}, u32[]{:S(2)}, u32[]{:S(2)}) collective-permute-start(bf16[64,1792]{1,0:T(8,128)(2,1)S(1)} %get-tuple-element.53), channel_id=1, source_target_pairs={{0,8},{4,12},{8,0},{12,4},{16,24},{20,28},{24,16},{28,20},{1,9},{5... | collective-permute-start | bytes 688136 | tf_op jit(solution)/shard_map/ppermute | solution.py:13
  97.7 1.3 %collective-permute-start.22 = (bf16[64,1792]{1,0:T(8,128)(2,1)S(1)}, bf16[64,1792]{1,0:T(8,128)(2,1)S(1)}, u32[]{:S(2)}, u32[]{:S(2)}) collective-permute-start(bf16[64,1792]{1,0:T(8,128)(2,1)S(1)} %get-tuple-element.51), channel_id=1, source_target_pairs={{0,24},{4,28},{8,16},{12,20},{16,8},{20,12},{24,0},{28,4},{1,25},{... | collective-permute-start | bytes 688136 | tf_op jit(solution)/shard_map/ppermute | solution.py:13
  99.1 6.6 %weight_grads.1 = (bf16[1,1792,1024]{2,1,0:T(8,128)(2,1)}, bf16[1,1792,1024]{2,1,0:T(8,128)(2,1)}) custom-call(bf16[64,1792]{1,0:T(8,128)(2,1)S(1)} %collective-permute-done.6.refs_0_, bf16[64,1792]{1,0:T(8,128)(2,1)S(1)} %collective-permute-done.refs_1_, bf16[64,1792]{1,0:T(8,128)(2,1)S(1)} %collective-permute-done.2.refs_2_, ...), custom_call_target="tpu_custom_call" | custom-call | flops 3758096384 | bytes 11272192 | tf_op jit(solution)/shard_map/weight_grads/pallas_call | solution.py:236
  105.7 3.3 %collective-permute-done.21 = bf16[64,1792]{1,0:T(8,128)(2,1)S(1)} collective-permute-done((bf16[64,1792]{1,0:T(8,128)(2,1)S(1)}, bf16[64,1792]{1,0:T(8,128)(2,1)S(1)}, u32[]{:S(2)}, u32[]{:S(2)}) %collective-permute-start.21) | collective-permute-done | bytes 229408 | tf_op jit(solution)/shard_map/ppermute | solution.py:13
  109.0 1.1 convolution_convert_fusion.2
  (54 shorter events, 5.9 us)
Async XLA Ops:
  2.9 8.9 %collective-permute-start = (bf16[64,1792]{1,0:T(8,128)(2,1)}, bf16[64,1792]{1,0:T(8,128)(2,1)S(1)}, u32[]{:S(2)}, u32[]{:S(2)}) collective-permute-start(bf16[64,1792]{1,0:T(8,128)(2,1)} %get-tuple-element.28), channel_id=1, source_target_pairs={{0,12},{4,8},{8,4},{12,0},{16,28},{20,24},{24,20},{28,16},{1,13},{... | collective-permute-start | bytes 688136 | tf_op jit(solution)/shard_map/ppermute | solution.py:13
  5.3 12.2 %collective-permute-start.2 = (bf16[64,1792]{1,0:T(8,128)(2,1)}, bf16[64,1792]{1,0:T(8,128)(2,1)S(1)}, u32[]{:S(2)}, u32[]{:S(2)}) collective-permute-start(bf16[64,1792]{1,0:T(8,128)(2,1)} %get-tuple-element.29), channel_id=1, source_target_pairs={{0,20},{4,16},{8,28},{12,24},{16,4},{20,0},{24,12},{28,8},{1,21},{... | collective-permute-start | bytes 688136 | tf_op jit(solution)/shard_map/ppermute | solution.py:13
  7.1 11.2 %collective-permute-start.4 = (bf16[64,1792]{1,0:T(8,128)(2,1)}, bf16[64,1792]{1,0:T(8,128)(2,1)S(1)}, u32[]{:S(2)}, u32[]{:S(2)}) collective-permute-start(bf16[64,1792]{1,0:T(8,128)(2,1)} %get-tuple-element.30), channel_id=1, source_target_pairs={{0,28},{4,24},{8,20},{12,16},{16,12},{20,8},{24,4},{28,0},{1,29},{... | collective-permute-start | bytes 688136 | tf_op jit(solution)/shard_map/ppermute | solution.py:13
  7.1 11.3 %collective-permute-start.6 = (bf16[64,1792]{1,0:T(8,128)(2,1)}, bf16[64,1792]{1,0:T(8,128)(2,1)S(1)}, u32[]{:S(2)}, u32[]{:S(2)}) collective-permute-start(bf16[64,1792]{1,0:T(8,128)(2,1)} %get-tuple-element.27.refs_0_.refs_4_), channel_id=1, source_target_pairs={{0,4},{4,0},{8,12},{12,8},{16,20},{20,16},{24,28},{28,24},{1,5},{5... | collective-permute-start | bytes 688136 | tf_op jit(solution)/shard_map/ppermute | solution.py:13
  7.1 0.7 copy-start.1
  7.8 0.7 copy-start.2
  11.8 12.7 %copy-start = (bf16[64,1792]{1,0:T(8,128)(2,1)S(1)}, bf16[64,1792]{1,0:T(8,128)(2,1)}, u32[]{:S(2)}) copy-start(bf16[64,1792]{1,0:T(8,128)(2,1)} %get-tuple-element.27.refs_0_.refs_4_) | copy-start | bytes 688132
  11.8 12.7 %collective-permute-start.1 = (bf16[64,1792]{1,0:T(8,128)(2,1)S(1)}, bf16[64,1792]{1,0:T(8,128)(2,1)S(1)}, u32[]{:S(2)}, u32[]{:S(2)}) collective-permute-start(bf16[64,1792]{1,0:T(8,128)(2,1)S(1)} %collective-permute-done.refs_1_), channel_id=1, source_target_pairs={{0,4},{4,0},{8,12},{12,8},{16,20},{20,16},{24,28},{28,24},{1,5},{5... | collective-permute-start | bytes 688136 | tf_op jit(solution)/shard_map/ppermute | solution.py:13
  17.5 7.0 %collective-permute-start.3 = (bf16[64,1792]{1,0:T(8,128)(2,1)S(1)}, bf16[64,1792]{1,0:T(8,128)(2,1)S(1)}, u32[]{:S(2)}, u32[]{:S(2)}) collective-permute-start(bf16[64,1792]{1,0:T(8,128)(2,1)S(1)} %collective-permute-done.2.refs_2_), channel_id=1, source_target_pairs={{0,4},{4,0},{8,12},{12,8},{16,20},{20,16},{24,28},{28,24},{1,5},{5... | collective-permute-start | bytes 688136 | tf_op jit(solution)/shard_map/ppermute | solution.py:13
  18.3 6.1 %collective-permute-start.5 = (bf16[64,1792]{1,0:T(8,128)(2,1)S(1)}, bf16[64,1792]{1,0:T(8,128)(2,1)S(1)}, u32[]{:S(2)}, u32[]{:S(2)}) collective-permute-start(bf16[64,1792]{1,0:T(8,128)(2,1)S(1)} %collective-permute-done.4.refs_3_), channel_id=1, source_target_pairs={{0,4},{4,0},{8,12},{12,8},{16,20},{20,16},{24,28},{28,24},{1,5},{5... | collective-permute-start | bytes 688136 | tf_op jit(solution)/shard_map/ppermute | solution.py:13
  20.6 11.0 %collective-permute-start.8 = (bf16[64,2048]{1,0:T(8,128)(2,1)S(1)}, bf16[64,2048]{1,0:T(8,128)(2,1)S(1)}, u32[]{:S(2)}, u32[]{:S(2)}) collective-permute-start(bf16[64,2048]{1,0:T(8,128)(2,1)S(1)} %get-tuple-element.56), channel_id=1, source_target_pairs={{0,1},{1,2},{2,3},{3,0},{4,5},{5,6},{6,7},{7,4},{8,9},{9,10},{10,1... | collective-permute-start | bytes 786440 | tf_op jit(solution)/shard_map/ppermute | solution.py:280
  22.3 24.7 %collective-permute-start.11 = (bf16[64,2048]{1,0:T(8,128)(2,1)S(1)}, bf16[64,2048]{1,0:T(8,128)(2,1)S(1)}, u32[]{:S(2)}, u32[]{:S(2)}) collective-permute-start(bf16[64,2048]{1,0:T(8,128)(2,1)S(1)} %get-tuple-element.31), channel_id=1, source_target_pairs={{0,3},{1,0},{2,1},{3,2},{4,7},{5,4},{6,5},{7,6},{8,11},{9,8},{10,9... | collective-permute-start | bytes 786440 | tf_op jit(solution)/shard_map/ppermute | solution.py:280
  26.6 27.6 %copy-start.3 = (bf16[1,128,1024]{2,1,0:T(8,128)(2,1)S(1)}, bf16[1,128,1024]{2,1,0:T(8,128)(2,1)}, u32[]{:S(2)}) copy-start(bf16[1,128,1024]{2,1,0:T(8,128)(2,1)} %param.13) | copy-start | bytes 786436
  26.6 16.2 %collective-permute-start.7 = (bf16[64,2048]{1,0:T(8,128)(2,1)S(1)}, bf16[64,2048]{1,0:T(8,128)(2,1)S(1)}, u32[]{:S(2)}, u32[]{:S(2)}) collective-permute-start(bf16[64,2048]{1,0:T(8,128)(2,1)S(1)} %get-tuple-element.32), channel_id=1, source_target_pairs={{0,1},{1,2},{2,3},{3,0},{4,5},{5,6},{6,7},{7,4},{8,9},{9,10},{10,1... | collective-permute-start | bytes 786440 | tf_op jit(solution)/shard_map/ppermute | solution.py:280
  26.7 31.6 %collective-permute-start.12 = (bf16[64,2048]{1,0:T(8,128)(2,1)S(1)}, bf16[64,2048]{1,0:T(8,128)(2,1)S(1)}, u32[]{:S(2)}, u32[]{:S(2)}) collective-permute-start(bf16[64,2048]{1,0:T(8,128)(2,1)S(1)} %get-tuple-element.33), channel_id=1, source_target_pairs={{0,3},{1,0},{2,1},{3,2},{4,7},{5,4},{6,5},{7,6},{8,11},{9,8},{10,9... | collective-permute-start | bytes 786440 | tf_op jit(solution)/shard_map/ppermute | solution.py:280
  31.7 22.4 %collective-permute-start.10 = (bf16[64,2048]{1,0:T(8,128)(2,1)S(1)}, bf16[64,2048]{1,0:T(8,128)(2,1)S(1)}, u32[]{:S(2)}, u32[]{:S(2)}) collective-permute-start(bf16[64,2048]{1,0:T(8,128)(2,1)S(1)} %fusion.8), channel_id=1, source_target_pairs={{0,1},{1,2},{2,3},{3,0},{4,5},{5,6},{6,7},{7,4},{8,9},{9,10},{10,1... | collective-permute-start | bytes 786440 | tf_op jit(solution)/shard_map/ppermute | solution.py:280
  43.0 16.9 %collective-permute-start.9 = (bf16[64,2048]{1,0:T(8,128)(2,1)S(1)}, bf16[64,2048]{1,0:T(8,128)(2,1)S(1)}, u32[]{:S(2)}, u32[]{:S(2)}) collective-permute-start(bf16[64,2048]{1,0:T(8,128)(2,1)S(1)} %fusion.9), channel_id=1, source_target_pairs={{0,1},{1,2},{2,3},{3,0},{4,5},{5,6},{6,7},{7,4},{8,9},{9,10},{10,1... | collective-permute-start | bytes 786440 | tf_op jit(solution)/shard_map/ppermute | solution.py:280
  54.4 11.1 %collective-permute-start.13 = (bf16[64,2048]{1,0:T(8,128)(2,1)S(1)}, bf16[64,2048]{1,0:T(8,128)(2,1)S(1)}, u32[]{:S(2)}, u32[]{:S(2)}) collective-permute-start(bf16[64,2048]{1,0:T(8,128)(2,1)S(1)} %pad_maximum_fusion), channel_id=1, source_target_pairs={{0,1},{1,2},{2,3},{3,0},{4,5},{5,6},{6,7},{7,4},{8,9},{9,10},{10,1... | collective-permute-start | bytes 786440 | tf_op jit(solution)/shard_map/ppermute | solution.py:280
  54.5 16.8 %collective-permute-start.14 = (bf16[64,2048]{1,0:T(8,128)(2,1)S(1)}, bf16[64,2048]{1,0:T(8,128)(2,1)S(1)}, u32[]{:S(2)}, u32[]{:S(2)}) collective-permute-start(bf16[64,2048]{1,0:T(8,128)(2,1)S(1)} %pad_maximum_fusion), channel_id=1, source_target_pairs={{0,3},{1,0},{2,1},{3,2},{4,7},{5,4},{6,5},{7,6},{8,11},{9,8},{10,9... | collective-permute-start | bytes 786440 | tf_op jit(solution)/shard_map/ppermute | solution.py:280
  60.2 16.6 %collective-permute-start.17 = (bf16[64,2048]{1,0:T(8,128)(2,1)S(1)}, bf16[64,2048]{1,0:T(8,128)(2,1)S(1)}, u32[]{:S(2)}, u32[]{:S(2)}) collective-permute-start(bf16[64,2048]{1,0:T(8,128)(2,1)S(1)} %pad_maximum_fusion.1), channel_id=1, source_target_pairs={{0,1},{1,2},{2,3},{3,0},{4,5},{5,6},{6,7},{7,4},{8,9},{9,10},{10,1... | collective-permute-start | bytes 786440 | tf_op jit(solution)/shard_map/ppermute | solution.py:280
  60.2 22.0 %collective-permute-start.16 = (bf16[64,2048]{1,0:T(8,128)(2,1)S(1)}, bf16[64,2048]{1,0:T(8,128)(2,1)S(1)}, u32[]{:S(2)}, u32[]{:S(2)}) collective-permute-start(bf16[64,2048]{1,0:T(8,128)(2,1)S(1)} %pad_maximum_fusion.1), channel_id=1, source_target_pairs={{0,3},{1,0},{2,1},{3,2},{4,7},{5,4},{6,5},{7,6},{8,11},{9,8},{10,9... | collective-permute-start | bytes 786440 | tf_op jit(solution)/shard_map/ppermute | solution.py:280
  65.5 22.5 %collective-permute-start.15 = (bf16[64,2048]{1,0:T(8,128)(2,1)S(1)}, bf16[64,2048]{1,0:T(8,128)(2,1)S(1)}, u32[]{:S(2)}, u32[]{:S(2)}) collective-permute-start(bf16[64,2048]{1,0:T(8,128)(2,1)S(1)} %collective-permute-done.13), channel_id=1, source_target_pairs={{0,1},{1,2},{2,3},{3,0},{4,5},{5,6},{6,7},{7,4},{8,9},{9,10},{10,1... | collective-permute-start | bytes 786440 | tf_op jit(solution)/shard_map/ppermute | solution.py:280
  76.8 16.4 %collective-permute-start.18 = (bf16[64,2048]{1,0:T(8,128)(2,1)S(1)}, bf16[64,2048]{1,0:T(8,128)(2,1)S(1)}, u32[]{:S(2)}, u32[]{:S(2)}) collective-permute-start(bf16[64,2048]{1,0:T(8,128)(2,1)S(1)} %collective-permute-done.17), channel_id=1, source_target_pairs={{0,1},{1,2},{2,3},{3,0},{4,5},{5,6},{6,7},{7,4},{8,9},{9,10},{10,1... | collective-permute-start | bytes 786440 | tf_op jit(solution)/shard_map/ppermute | solution.py:280
  90.2 3.0 %collective-permute-start.19 = (bf16[256,1792]{1,0:T(8,128)(2,1)S(1)}, bf16[256,1792]{1,0:T(8,128)(2,1)S(1)}, u32[]{:S(2)}, u32[]{:S(2)}) collective-permute-start(bf16[256,1792]{1,0:T(8,128)(2,1)S(1)} %convolution_convert_fusion.1), channel_id=1, source_target_pairs={{0,4},{4,0},{8,12},{12,8},{16,20},{20,16},{24,28},{28,24},{1,5},{5... | collective-permute-start | bytes 2752520 | tf_op jit(solution)/shard_map/ppermute | solution.py:13
  95.5 10.2 %collective-permute-start.20 = (bf16[64,1792]{1,0:T(8,128)(2,1)S(1)}, bf16[64,1792]{1,0:T(8,128)(2,1)S(1)}, u32[]{:S(2)}, u32[]{:S(2)}) collective-permute-start(bf16[64,1792]{1,0:T(8,128)(2,1)S(1)} %get-tuple-element.53), channel_id=1, source_target_pairs={{0,8},{4,12},{8,0},{12,4},{16,24},{20,28},{24,16},{28,20},{1,9},{5... | collective-permute-start | bytes 688136 | tf_op jit(solution)/shard_map/ppermute | solution.py:13
  97.1 11.9 %collective-permute-start.21 = (bf16[64,1792]{1,0:T(8,128)(2,1)S(1)}, bf16[64,1792]{1,0:T(8,128)(2,1)S(1)}, u32[]{:S(2)}, u32[]{:S(2)}) collective-permute-start(bf16[64,1792]{1,0:T(8,128)(2,1)S(1)} %get-tuple-element.52), channel_id=1, source_target_pairs={{0,16},{4,20},{8,24},{12,28},{16,0},{20,4},{24,8},{28,12},{1,17},{... | collective-permute-start | bytes 688136 | tf_op jit(solution)/shard_map/ppermute | solution.py:13
  97.7 11.2 %copy-start.4 = (bf16[256,128]{1,0:T(8,128)(2,1)S(1)}, bf16[256,128]{1,0:T(8,128)(2,1)}, u32[]{:S(2)}) copy-start(bf16[256,128]{1,0:T(8,128)(2,1)} %get-tuple-element.48) | copy-start | bytes 196612
  97.7 11.2 %collective-permute-start.22 = (bf16[64,1792]{1,0:T(8,128)(2,1)S(1)}, bf16[64,1792]{1,0:T(8,128)(2,1)S(1)}, u32[]{:S(2)}, u32[]{:S(2)}) collective-permute-start(bf16[64,1792]{1,0:T(8,128)(2,1)S(1)} %get-tuple-element.51), channel_id=1, source_target_pairs={{0,24},{4,28},{8,16},{12,20},{16,8},{20,12},{24,0},{28,4},{1,25},{... | collective-permute-start | bytes 688136 | tf_op jit(solution)/shard_map/ppermute | solution.py:13

commit v7 on v6

--- a/solution.py
+++ b/solution.py
@@ -113,25 +113,18 @@
     )
 
 
-def rows_of(counts_ref, expert):
-    first = jnp.int32(0)
-    live = jnp.int32(0)
-    for other in range(counts_ref.shape[1]):
-        count = counts_ref[0, other]
-        first = first + jnp.where(other < expert, count, 0)
-        live = jnp.where(other == expert, count, live)
-    return first, live
-
-
 def pack_kernel(counts_ref, tokens_ref, chooser_ref, *out_refs):
     chip = lax.axis_index("expert") // 2
     row_total = tokens_ref.shape[0]
     capacity = out_refs[0].shape[0]
-    row = lax.broadcasted_iota(jnp.int32, (capacity, row_total), 1)
-    slot = lax.broadcasted_iota(jnp.int32, (capacity, row_total), 0)
+    counts = counts_ref[...].astype(jnp.float32)
+    expert = lax.broadcasted_iota(jnp.int32, counts.shape, 1)
+    row = lax.broadcasted_iota(jnp.int32, (capacity, row_total), 1).astype(jnp.float32)
+    slot = lax.broadcasted_iota(jnp.int32, (capacity, row_total), 0).astype(jnp.float32)
     hits = []
     for mask in range(len(out_refs)):
-        first, live = rows_of(counts_ref, chip ^ mask)
+        first = jnp.sum(jnp.where(expert < (chip ^ mask), counts, 0.0), 1, keepdims=True)
+        live = jnp.sum(jnp.where(expert == (chip ^ mask), counts, 0.0), 1, keepdims=True)
         hits.append(((row == first + slot) & (slot < live)).astype(jnp.float32))
     chooser = jnp.concatenate(hits, 0).astype(jnp.bfloat16)
     chooser_ref[...] = chooser
@@ -151,7 +144,7 @@
         + (block,) * experts,
         grid=(feat_cols // tile,),
         in_specs=[
-            pl.BlockSpec(memory_space=pltpu.SMEM),
+            pl.BlockSpec(counts.shape, lambda i: (0, 0)),
             pl.BlockSpec((row_total, tile), lambda i: (0, i)),
         ],
         out_specs=(pl.BlockSpec((experts * capacity, row_total), lambda i: (0, 0)),)
@@ -385,11 +378,11 @@
 
     taken = swap(back(wholes[0]), "expert", 1)
     kept = back(earlier(wholes[1], taken))
-    pieces = []
-    for mask in masks:
+    pieces = {}
+    for mask in reversed(masks):
         rows = slice(mask * capacity, (mask + 1) * capacity)
         both = add_rounded(kept[rows], taken[rows])
-        pieces.append(swap(both, "expert", 2 * mask) if mask else both)
+        pieces[mask] = swap(both, "expert", 2 * mask) if mask else both
 
     hidden = jnp.where(
         parity == 0, jnp.concatenate([hiddens[1], hiddens[0]], 0), jnp.concatenate(hiddens, 0)
@@ -397,7 +390,7 @@
     grad_gate, grad_up = weight_grads(inputs[0] + inputs[1], wholes)
     grad_tokens = lax.dot_general(
         chooser,
-        jnp.concatenate(pieces, 0),
+        jnp.concatenate([pieces[mask] for mask in masks], 0),
         (((0,), (0,)), ((), ())),
         preferred_element_type=jnp.float32,
     ).astype(jnp.bfloat16)

time: 110 us -> 110 us (level)
  starting transfers between devices: 36 us -> 39.8 us
  waiting for transfers between devices: 48 us -> 44.2 us
    ppermute x12, waiting for transfers between devices: 38.9 us -> 35.2 us  [send(): self.came[way] = lax.ppermute(value, 'fsdp', ring)]
    ppermute x12, starting transfers between devices: 27.3 us -> 31.1 us  [send(): self.came[way] = lax.ppermute(value, 'fsdp', ring)]
where the time goes in v7:
time: 110 us
  waiting for transfers between devices  44.2 us (40%)
  starting transfers between devices  39.8 us (36%)
  Pallas kernels  16.5 us (15%)
  matrix products  5.29 us (5%)
  local copies, waits for them, and re-layouts  1.84 us (2%)
  other arithmetic  1.69 us (2%)
    ppermute x12, waiting for transfers between devices, send(): self.came[way] = lax.ppermute(value, 'fsdp', ring)  35.2 us
    ppermute x12, starting transfers between devices, send(): self.came[way] = lax.ppermute(value, 'fsdp', ring)  31.1 us
    ppermute x11, waiting for transfers between devices, swap(): return lax.ppermute(value, axis, pairs)  9.03 us
    ppermute x11, starting transfers between devices, swap(): return lax.ppermute(value, axis, pairs)  8.7 us
    pallas_call x1, Pallas kernels, weight_grads(): pl.pallas_call(lambda *refs: weight_kernel(count, *refs), out_shape=(out,...  6.59 us
    dot_general x2, matrix products, back(): lax.dot_general(whole, weights, (((1,), (1,)), ((), ())), preferred_eleme...  4.21 us
    pallas_call x2, Pallas kernels, projected(): pl.pallas_call(project_kernel, out_shape=jax.ShapeDtypeStruct((count, cap...  4.16 us
    pallas_call x1, Pallas kernels, scaled_weights(): pl.pallas_call(lambda *refs: scale_kernel(sub, *refs), out_shape=jax.Shap...  3.3 us
  transfers between devices with their start and end apart: 23, of which 13 were waited for; matrix products, arithmetic and copies ran while one was open for 4% of the time, Pallas kernels for 13%

profile of v7, /device:TPU:0, one launch (start us, length us, event | category | flops | bytes accessed | tf_op | source)
XLA Modules:
  0.0 110.2 jit_solution(7799053100273298068)
XLA Ops:
  0.6 2.4 %pack_rows.1 = (bf16[256,128]{1,0:T(8,128)(2,1)}, bf16[64,1792]{1,0:T(8,128)(2,1)}, bf16[64,1792]{1,0:T(8,128)(2,1)}, bf16[64,1792]{1,0:T(8,128)(2,1)}, bf16[64,1792]{1,0:T(8,128)(2,1)}) custom-call(s32[1,4]{1,0:T(1,128)} %counts_ref.1, bf16[128,1792]{1,0:T(8,128)(2,1)} %tokens_ref.1), custom_call_target="tpu_custom_call" | custom-call | flops 117440512 | bytes 1376256 | tf_op jit(solution)/shard_map/pack_rows/pallas_call | solution.py:141
  3.0 2.4 %collective-permute-start = (bf16[64,1792]{1,0:T(8,128)(2,1)}, bf16[64,1792]{1,0:T(8,128)(2,1)S(1)}, u32[]{:S(2)}, u32[]{:S(2)}) collective-permute-start(bf16[64,1792]{1,0:T(8,128)(2,1)} %get-tuple-element.28), channel_id=1, source_target_pairs={{0,12},{4,8},{8,4},{12,0},{16,28},{20,24},{24,20},{28,16},{1,13},{... | collective-permute-start | bytes 688136 | tf_op jit(solution)/shard_map/ppermute | solution.py:13
  5.4 1.8 %collective-permute-start.2 = (bf16[64,1792]{1,0:T(8,128)(2,1)}, bf16[64,1792]{1,0:T(8,128)(2,1)S(1)}, u32[]{:S(2)}, u32[]{:S(2)}) collective-permute-start(bf16[64,1792]{1,0:T(8,128)(2,1)} %get-tuple-element.29), channel_id=1, source_target_pairs={{0,20},{4,16},{8,28},{12,24},{16,4},{20,0},{24,12},{28,8},{1,21},{... | collective-permute-start | bytes 688136 | tf_op jit(solution)/shard_map/ppermute | solution.py:13
  8.6 3.3 %scale_weights.1.refs_4_ = bf16[1792,2048]{1,0:T(8,128)(2,1)S(1)} custom-call(s32[1]{0:T(128)} %bitcast.refs_0_, bf16[1,1792,1024]{2,1,0:T(8,128)(2,1)} %refs_1_.1, bf16[1,1792,1024]{2,1,0:T(8,128)(2,1)} %refs_2_.1, f32[1,8,56]{2,1,0:T(8,128)S(1)} %bitcast.63, f32[1,8,56]{2,1,0:T(8,128)S(1)} %bitcast.64), custom_call_target="tpu_custom_call" | custom-call | flops 3670016 | bytes 14680064 | tf_op jit(solution)/shard_map/scale_weights/pallas_call | solution.py:84
  12.8 4.9 %collective-permute-done.2.refs_2_ = bf16[64,1792]{1,0:T(8,128)(2,1)S(1)} collective-permute-done((bf16[64,1792]{1,0:T(8,128)(2,1)}, bf16[64,1792]{1,0:T(8,128)(2,1)S(1)}, u32[]{:S(2)}, u32[]{:S(2)}) %collective-permute-start.2) | collective-permute-done | bytes 229408 | tf_op jit(solution)/shard_map/ppermute | solution.py:13
  18.5 2.1 %project.3 = bf16[4,64,2048]{2,1,0:T(8,128)(2,1)S(1)} custom-call(bf16[64,1792]{1,0:T(8,128)(2,1)S(1)} %collective-permute-done.6.refs_0_, bf16[64,1792]{1,0:T(8,128)(2,1)S(1)} %collective-permute-done.refs_1_, bf16[64,1792]{1,0:T(8,128)(2,1)S(1)} %collective-permute-done.2.refs_2_, bf16[64,1792]{1,0:T(8,128)(2,1)S(1)} %collective-permute-done.4.refs_3_, ...), custom_call_target="tpu_custom_call" | custom-call | flops 1879048192 | bytes 9306112 | tf_op jit(solution)/shard_map/project/pallas_call | solution.py:181
  20.7 1.6 %collective-permute-start.8 = (bf16[64,2048]{1,0:T(8,128)(2,1)S(1)}, bf16[64,2048]{1,0:T(8,128)(2,1)S(1)}, u32[]{:S(2)}, u32[]{:S(2)}) collective-permute-start(bf16[64,2048]{1,0:T(8,128)(2,1)S(1)} %get-tuple-element.56), channel_id=1, source_target_pairs={{0,1},{1,2},{2,3},{3,0},{4,5},{5,6},{6,7},{7,4},{8,9},{9,10},{10,1... | collective-permute-start | bytes 786440 | tf_op jit(solution)/shard_map/ppermute | solution.py:273
  22.4 2.2 %collective-permute-start.11 = (bf16[64,2048]{1,0:T(8,128)(2,1)S(1)}, bf16[64,2048]{1,0:T(8,128)(2,1)S(1)}, u32[]{:S(2)}, u32[]{:S(2)}) collective-permute-start(bf16[64,2048]{1,0:T(8,128)(2,1)S(1)} %get-tuple-element.31), channel_id=1, source_target_pairs={{0,3},{1,0},{2,1},{3,2},{4,7},{5,4},{6,5},{7,6},{8,11},{9,8},{10,9... | collective-permute-start | bytes 786440 | tf_op jit(solution)/shard_map/ppermute | solution.py:273
  24.6 2.1 %project.2 = bf16[4,64,2048]{2,1,0:T(8,128)(2,1)S(1)} custom-call(bf16[64,1792]{1,0:T(8,128)(2,1)S(1)} %copy-done, bf16[64,1792]{1,0:T(8,128)(2,1)S(1)} %collective-permute-done.1.refs_1_.refs_5_, bf16[64,1792]{1,0:T(8,128)(2,1)S(1)} %collective-permute-done.3.refs_2_.refs_6_, bf16[64,1792]{1,0:T(8,128)(2,1)S(1)} %collective-permute-done.5.refs_3_.refs_7_, ...), custom_call_target="tpu_custom_call" | custom-call | flops 1879048192 | bytes 9306112 | tf_op jit(solution)/shard_map/project/pallas_call | solution.py:181
  26.8 3.8 %collective-permute-start.12 = (bf16[64,2048]{1,0:T(8,128)(2,1)S(1)}, bf16[64,2048]{1,0:T(8,128)(2,1)S(1)}, u32[]{:S(2)}, u32[]{:S(2)}) collective-permute-start(bf16[64,2048]{1,0:T(8,128)(2,1)S(1)} %get-tuple-element.33), channel_id=1, source_target_pairs={{0,3},{1,0},{2,1},{3,2},{4,7},{5,4},{6,5},{7,6},{8,11},{9,8},{10,9... | collective-permute-start | bytes 786440 | tf_op jit(solution)/shard_map/ppermute | solution.py:273
  30.6 1.1 collective-permute-done.8
  31.8 4.1 %collective-permute-start.10 = (bf16[64,2048]{1,0:T(8,128)(2,1)S(1)}, bf16[64,2048]{1,0:T(8,128)(2,1)S(1)}, u32[]{:S(2)}, u32[]{:S(2)}) collective-permute-start(bf16[64,2048]{1,0:T(8,128)(2,1)S(1)} %fusion.8), channel_id=1, source_target_pairs={{0,1},{1,2},{2,3},{3,0},{4,5},{5,6},{6,7},{7,4},{8,9},{9,10},{10,1... | collective-permute-start | bytes 786440 | tf_op jit(solution)/shard_map/ppermute | solution.py:273
  35.9 7.1 %collective-permute-done.7 = bf16[64,2048]{1,0:T(8,128)(2,1)S(1)} collective-permute-done((bf16[64,2048]{1,0:T(8,128)(2,1)S(1)}, bf16[64,2048]{1,0:T(8,128)(2,1)S(1)}, u32[]{:S(2)}, u32[]{:S(2)}) %collective-permute-start.7) | collective-permute-done | bytes 262176 | tf_op jit(solution)/shard_map/ppermute | solution.py:273
  43.1 4.0 %collective-permute-start.9 = (bf16[64,2048]{1,0:T(8,128)(2,1)S(1)}, bf16[64,2048]{1,0:T(8,128)(2,1)S(1)}, u32[]{:S(2)}, u32[]{:S(2)}) collective-permute-start(bf16[64,2048]{1,0:T(8,128)(2,1)S(1)} %fusion.9), channel_id=1, source_target_pairs={{0,1},{1,2},{2,3},{3,0},{4,5},{5,6},{6,7},{7,4},{8,9},{9,10},{10,1... | collective-permute-start | bytes 786440 | tf_op jit(solution)/shard_map/ppermute | solution.py:273
  47.1 7.1 %collective-permute-done.10 = bf16[64,2048]{1,0:T(8,128)(2,1)S(1)} collective-permute-done((bf16[64,2048]{1,0:T(8,128)(2,1)S(1)}, bf16[64,2048]{1,0:T(8,128)(2,1)S(1)}, u32[]{:S(2)}, u32[]{:S(2)}) %collective-permute-start.10) | collective-permute-done | bytes 262176 | tf_op jit(solution)/shard_map/ppermute | solution.py:273
  54.6 3.8 %collective-permute-start.14 = (bf16[64,2048]{1,0:T(8,128)(2,1)S(1)}, bf16[64,2048]{1,0:T(8,128)(2,1)S(1)}, u32[]{:S(2)}, u32[]{:S(2)}) collective-permute-start(bf16[64,2048]{1,0:T(8,128)(2,1)S(1)} %pad_maximum_fusion), channel_id=1, source_target_pairs={{0,3},{1,0},{2,1},{3,2},{4,7},{5,4},{6,5},{7,6},{8,11},{9,8},{10,9... | collective-permute-start | bytes 786440 | tf_op jit(solution)/shard_map/ppermute | solution.py:273
  58.6 1.4 %collective-permute-done.9 = bf16[64,2048]{1,0:T(8,128)(2,1)S(1)} collective-permute-done((bf16[64,2048]{1,0:T(8,128)(2,1)S(1)}, bf16[64,2048]{1,0:T(8,128)(2,1)S(1)}, u32[]{:S(2)}, u32[]{:S(2)}) %collective-permute-start.9) | collective-permute-done | bytes 262176 | tf_op jit(solution)/shard_map/ppermute | solution.py:273
  60.4 3.8 %collective-permute-start.16 = (bf16[64,2048]{1,0:T(8,128)(2,1)S(1)}, bf16[64,2048]{1,0:T(8,128)(2,1)S(1)}, u32[]{:S(2)}, u32[]{:S(2)}) collective-permute-start(bf16[64,2048]{1,0:T(8,128)(2,1)S(1)} %pad_maximum_fusion.1), channel_id=1, source_target_pairs={{0,3},{1,0},{2,1},{3,2},{4,7},{5,4},{6,5},{7,6},{8,11},{9,8},{10,9... | collective-permute-start | bytes 786440 | tf_op jit(solution)/shard_map/ppermute | solution.py:273
  65.6 3.8 %collective-permute-start.15 = (bf16[64,2048]{1,0:T(8,128)(2,1)S(1)}, bf16[64,2048]{1,0:T(8,128)(2,1)S(1)}, u32[]{:S(2)}, u32[]{:S(2)}) collective-permute-start(bf16[64,2048]{1,0:T(8,128)(2,1)S(1)} %collective-permute-done.13), channel_id=1, source_target_pairs={{0,1},{1,2},{2,3},{3,0},{4,5},{5,6},{6,7},{7,4},{8,9},{9,10},{10,1... | collective-permute-start | bytes 786440 | tf_op jit(solution)/shard_map/ppermute | solution.py:273
  69.4 2.0 %collective-permute-done.14 = bf16[64,2048]{1,0:T(8,128)(2,1)S(1)} collective-permute-done((bf16[64,2048]{1,0:T(8,128)(2,1)S(1)}, bf16[64,2048]{1,0:T(8,128)(2,1)S(1)}, u32[]{:S(2)}, u32[]{:S(2)}) %collective-permute-start.14) | collective-permute-done | bytes 262176 | tf_op jit(solution)/shard_map/ppermute | solution.py:273
  71.5 5.4 %collective-permute-done.17 = bf16[64,2048]{1,0:T(8,128)(2,1)S(1)} collective-permute-done((bf16[64,2048]{1,0:T(8,128)(2,1)S(1)}, bf16[64,2048]{1,0:T(8,128)(2,1)S(1)}, u32[]{:S(2)}, u32[]{:S(2)}) %collective-permute-start.17) | collective-permute-done | bytes 262176 | tf_op jit(solution)/shard_map/ppermute | solution.py:273
  76.9 3.6 %collective-permute-start.18 = (bf16[64,2048]{1,0:T(8,128)(2,1)S(1)}, bf16[64,2048]{1,0:T(8,128)(2,1)S(1)}, u32[]{:S(2)}, u32[]{:S(2)}) collective-permute-start(bf16[64,2048]{1,0:T(8,128)(2,1)S(1)} %collective-permute-done.17), channel_id=1, source_target_pairs={{0,1},{1,2},{2,3},{3,0},{4,5},{5,6},{6,7},{7,4},{8,9},{9,10},{10,1... | collective-permute-start | bytes 786440 | tf_op jit(solution)/shard_map/ppermute | solution.py:273
  80.6 1.8 %collective-permute-done.16 = bf16[64,2048]{1,0:T(8,128)(2,1)S(1)} collective-permute-done((bf16[64,2048]{1,0:T(8,128)(2,1)S(1)}, bf16[64,2048]{1,0:T(8,128)(2,1)S(1)}, u32[]{:S(2)}, u32[]{:S(2)}) %collective-permute-start.16) | collective-permute-done | bytes 262176 | tf_op jit(solution)/shard_map/ppermute | solution.py:273
  82.4 5.8 %collective-permute-done.15 = bf16[64,2048]{1,0:T(8,128)(2,1)S(1)} collective-permute-done((bf16[64,2048]{1,0:T(8,128)(2,1)S(1)}, bf16[64,2048]{1,0:T(8,128)(2,1)S(1)}, u32[]{:S(2)}, u32[]{:S(2)}) %collective-permute-start.15) | collective-permute-done | bytes 262176 | tf_op jit(solution)/shard_map/ppermute | solution.py:273
  88.2 2.1 %convolution_convert_fusion.1 = bf16[256,1792]{1,0:T(8,128)(2,1)S(1)} fusion(bf16[256,2048]{1,0:T(8,128)(2,1)S(1)} %bitcast.61, bf16[1792,2048]{1,0:T(8,128)(2,1)S(1)} %scale_weights.1.refs_4_), kind=kOutput, calls=%fused_computation.1 | convolution fusion | flops 1879506944 | bytes 9306112 | tf_op jit(solution)/shard_map/dot_general | solution.py:353
  90.4 2.9 %collective-permute-done.18 = bf16[64,2048]{1,0:T(8,128)(2,1)S(1)} collective-permute-done((bf16[64,2048]{1,0:T(8,128)(2,1)S(1)}, bf16[64,2048]{1,0:T(8,128)(2,1)S(1)}, u32[]{:S(2)}, u32[]{:S(2)}) %collective-permute-start.18) | collective-permute-done | bytes 262176 | tf_op jit(solution)/shard_map/ppermute | solution.py:273
  93.3 2.1 %convolution_convert_fusion = bf16[256,1792]{1,0:T(8,128)(2,1)S(1)} fusion(bf16[256,2048]{1,0:T(8,128)(2,1)S(1)} %bitcast.59, bf16[1792,2048]{1,0:T(8,128)(2,1)S(1)} %scale_weights.1.refs_4_), kind=kOutput, calls=%fused_computation | convolution fusion | flops 1879506944 | bytes 9306112 | tf_op jit(solution)/shard_map/dot_general | solution.py:353
  95.6 1.6 %collective-permute-start.20 = (bf16[64,1792]{1,0:T(8,128)(2,1)S(1)}, bf16[64,1792]{1,0:T(8,128)(2,1)S(1)}, u32[]{:S(2)}, u32[]{:S(2)}) collective-permute-start(bf16[64,1792]{1,0:T(8,128)(2,1)S(1)} %get-tuple-element.53), channel_id=1, source_target_pairs={{0,8},{4,12},{8,0},{12,4},{16,24},{20,28},{24,16},{28,20},{1,9},{5... | collective-permute-start | bytes 688136 | tf_op jit(solution)/shard_map/ppermute | solution.py:13
  97.9 1.3 %collective-permute-start.22 = (bf16[64,1792]{1,0:T(8,128)(2,1)S(1)}, bf16[64,1792]{1,0:T(8,128)(2,1)S(1)}, u32[]{:S(2)}, u32[]{:S(2)}) collective-permute-start(bf16[64,1792]{1,0:T(8,128)(2,1)S(1)} %get-tuple-element.51), channel_id=1, source_target_pairs={{0,24},{4,28},{8,16},{12,20},{16,8},{20,12},{24,0},{28,4},{1,25},{... | collective-permute-start | bytes 688136 | tf_op jit(solution)/shard_map/ppermute | solution.py:13
  99.2 6.6 %weight_grads.1 = (bf16[1,1792,1024]{2,1,0:T(8,128)(2,1)}, bf16[1,1792,1024]{2,1,0:T(8,128)(2,1)}) custom-call(bf16[64,1792]{1,0:T(8,128)(2,1)S(1)} %collective-permute-done.6.refs_0_, bf16[64,1792]{1,0:T(8,128)(2,1)S(1)} %collective-permute-done.refs_1_, bf16[64,1792]{1,0:T(8,128)(2,1)S(1)} %collective-permute-done.2.refs_2_, ...), custom_call_target="tpu_custom_call" | custom-call | flops 3758096384 | bytes 11272192 | tf_op jit(solution)/shard_map/weight_grads/pallas_call | solution.py:229
  105.8 3.3 %collective-permute-done.21 = bf16[64,1792]{1,0:T(8,128)(2,1)S(1)} collective-permute-done((bf16[64,1792]{1,0:T(8,128)(2,1)S(1)}, bf16[64,1792]{1,0:T(8,128)(2,1)S(1)}, u32[]{:S(2)}, u32[]{:S(2)}) %collective-permute-start.21) | collective-permute-done | bytes 229408 | tf_op jit(solution)/shard_map/ppermute | solution.py:13
  109.1 1.1 convolution_convert_fusion.2
  (54 shorter events, 6.8 us)
Async XLA Ops:
  3.0 8.9 %collective-permute-start = (bf16[64,1792]{1,0:T(8,128)(2,1)}, bf16[64,1792]{1,0:T(8,128)(2,1)S(1)}, u32[]{:S(2)}, u32[]{:S(2)}) collective-permute-start(bf16[64,1792]{1,0:T(8,128)(2,1)} %get-tuple-element.28), channel_id=1, source_target_pairs={{0,12},{4,8},{8,4},{12,0},{16,28},{20,24},{24,20},{28,16},{1,13},{... | collective-permute-start | bytes 688136 | tf_op jit(solution)/shard_map/ppermute | solution.py:13
  5.4 12.2 %collective-permute-start.2 = (bf16[64,1792]{1,0:T(8,128)(2,1)}, bf16[64,1792]{1,0:T(8,128)(2,1)S(1)}, u32[]{:S(2)}, u32[]{:S(2)}) collective-permute-start(bf16[64,1792]{1,0:T(8,128)(2,1)} %get-tuple-element.29), channel_id=1, source_target_pairs={{0,20},{4,16},{8,28},{12,24},{16,4},{20,0},{24,12},{28,8},{1,21},{... | collective-permute-start | bytes 688136 | tf_op jit(solution)/shard_map/ppermute | solution.py:13
  7.2 11.2 %collective-permute-start.4 = (bf16[64,1792]{1,0:T(8,128)(2,1)}, bf16[64,1792]{1,0:T(8,128)(2,1)S(1)}, u32[]{:S(2)}, u32[]{:S(2)}) collective-permute-start(bf16[64,1792]{1,0:T(8,128)(2,1)} %get-tuple-element.30), channel_id=1, source_target_pairs={{0,28},{4,24},{8,20},{12,16},{16,12},{20,8},{24,4},{28,0},{1,29},{... | collective-permute-start | bytes 688136 | tf_op jit(solution)/shard_map/ppermute | solution.py:13
  7.2 11.3 %collective-permute-start.6 = (bf16[64,1792]{1,0:T(8,128)(2,1)}, bf16[64,1792]{1,0:T(8,128)(2,1)S(1)}, u32[]{:S(2)}, u32[]{:S(2)}) collective-permute-start(bf16[64,1792]{1,0:T(8,128)(2,1)} %get-tuple-element.27.refs_0_.refs_4_), channel_id=1, source_target_pairs={{0,4},{4,0},{8,12},{12,8},{16,20},{20,16},{24,28},{28,24},{1,5},{5... | collective-permute-start | bytes 688136 | tf_op jit(solution)/shard_map/ppermute | solution.py:13
  7.2 0.7 copy-start.1
  7.9 0.7 copy-start.2
  11.9 12.7 %copy-start = (bf16[64,1792]{1,0:T(8,128)(2,1)S(1)}, bf16[64,1792]{1,0:T(8,128)(2,1)}, u32[]{:S(2)}) copy-start(bf16[64,1792]{1,0:T(8,128)(2,1)} %get-tuple-element.27.refs_0_.refs_4_) | copy-start | bytes 688132
  12.0 12.6 %collective-permute-start.1 = (bf16[64,1792]{1,0:T(8,128)(2,1)S(1)}, bf16[64,1792]{1,0:T(8,128)(2,1)S(1)}, u32[]{:S(2)}, u32[]{:S(2)}) collective-permute-start(bf16[64,1792]{1,0:T(8,128)(2,1)S(1)} %collective-permute-done.refs_1_), channel_id=1, source_target_pairs={{0,4},{4,0},{8,12},{12,8},{16,20},{20,16},{24,28},{28,24},{1,5},{5... | collective-permute-start | bytes 688136 | tf_op jit(solution)/shard_map/ppermute | solution.py:13
  17.6 7.0 %collective-permute-start.3 = (bf16[64,1792]{1,0:T(8,128)(2,1)S(1)}, bf16[64,1792]{1,0:T(8,128)(2,1)S(1)}, u32[]{:S(2)}, u32[]{:S(2)}) collective-permute-start(bf16[64,1792]{1,0:T(8,128)(2,1)S(1)} %collective-permute-done.2.refs_2_), channel_id=1, source_target_pairs={{0,4},{4,0},{8,12},{12,8},{16,20},{20,16},{24,28},{28,24},{1,5},{5... | collective-permute-start | bytes 688136 | tf_op jit(solution)/shard_map/ppermute | solution.py:13
  18.5 6.1 %collective-permute-start.5 = (bf16[64,1792]{1,0:T(8,128)(2,1)S(1)}, bf16[64,1792]{1,0:T(8,128)(2,1)S(1)}, u32[]{:S(2)}, u32[]{:S(2)}) collective-permute-start(bf16[64,1792]{1,0:T(8,128)(2,1)S(1)} %collective-permute-done.4.refs_3_), channel_id=1, source_target_pairs={{0,4},{4,0},{8,12},{12,8},{16,20},{20,16},{24,28},{28,24},{1,5},{5... | collective-permute-start | bytes 688136 | tf_op jit(solution)/shard_map/ppermute | solution.py:13
  20.7 11.0 %collective-permute-start.8 = (bf16[64,2048]{1,0:T(8,128)(2,1)S(1)}, bf16[64,2048]{1,0:T(8,128)(2,1)S(1)}, u32[]{:S(2)}, u32[]{:S(2)}) collective-permute-start(bf16[64,2048]{1,0:T(8,128)(2,1)S(1)} %get-tuple-element.56), channel_id=1, source_target_pairs={{0,1},{1,2},{2,3},{3,0},{4,5},{5,6},{6,7},{7,4},{8,9},{9,10},{10,1... | collective-permute-start | bytes 786440 | tf_op jit(solution)/shard_map/ppermute | solution.py:273
  22.4 24.8 %collective-permute-start.11 = (bf16[64,2048]{1,0:T(8,128)(2,1)S(1)}, bf16[64,2048]{1,0:T(8,128)(2,1)S(1)}, u32[]{:S(2)}, u32[]{:S(2)}) collective-permute-start(bf16[64,2048]{1,0:T(8,128)(2,1)S(1)} %get-tuple-element.31), channel_id=1, source_target_pairs={{0,3},{1,0},{2,1},{3,2},{4,7},{5,4},{6,5},{7,6},{8,11},{9,8},{10,9... | collective-permute-start | bytes 786440 | tf_op jit(solution)/shard_map/ppermute | solution.py:273
  26.7 27.6 %copy-start.3 = (bf16[1,128,1024]{2,1,0:T(8,128)(2,1)S(1)}, bf16[1,128,1024]{2,1,0:T(8,128)(2,1)}, u32[]{:S(2)}) copy-start(bf16[1,128,1024]{2,1,0:T(8,128)(2,1)} %param.13) | copy-start | bytes 786436
  26.8 16.2 %collective-permute-start.7 = (bf16[64,2048]{1,0:T(8,128)(2,1)S(1)}, bf16[64,2048]{1,0:T(8,128)(2,1)S(1)}, u32[]{:S(2)}, u32[]{:S(2)}) collective-permute-start(bf16[64,2048]{1,0:T(8,128)(2,1)S(1)} %get-tuple-element.32), channel_id=1, source_target_pairs={{0,1},{1,2},{2,3},{3,0},{4,5},{5,6},{6,7},{7,4},{8,9},{9,10},{10,1... | collective-permute-start | bytes 786440 | tf_op jit(solution)/shard_map/ppermute | solution.py:273
  26.8 31.6 %collective-permute-start.12 = (bf16[64,2048]{1,0:T(8,128)(2,1)S(1)}, bf16[64,2048]{1,0:T(8,128)(2,1)S(1)}, u32[]{:S(2)}, u32[]{:S(2)}) collective-permute-start(bf16[64,2048]{1,0:T(8,128)(2,1)S(1)} %get-tuple-element.33), channel_id=1, source_target_pairs={{0,3},{1,0},{2,1},{3,2},{4,7},{5,4},{6,5},{7,6},{8,11},{9,8},{10,9... | collective-permute-start | bytes 786440 | tf_op jit(solution)/shard_map/ppermute | solution.py:273
  31.8 22.4 %collective-permute-start.10 = (bf16[64,2048]{1,0:T(8,128)(2,1)S(1)}, bf16[64,2048]{1,0:T(8,128)(2,1)S(1)}, u32[]{:S(2)}, u32[]{:S(2)}) collective-permute-start(bf16[64,2048]{1,0:T(8,128)(2,1)S(1)} %fusion.8), channel_id=1, source_target_pairs={{0,1},{1,2},{2,3},{3,0},{4,5},{5,6},{6,7},{7,4},{8,9},{9,10},{10,1... | collective-permute-start | bytes 786440 | tf_op jit(solution)/shard_map/ppermute | solution.py:273
  43.1 16.9 %collective-permute-start.9 = (bf16[64,2048]{1,0:T(8,128)(2,1)S(1)}, bf16[64,2048]{1,0:T(8,128)(2,1)S(1)}, u32[]{:S(2)}, u32[]{:S(2)}) collective-permute-start(bf16[64,2048]{1,0:T(8,128)(2,1)S(1)} %fusion.9), channel_id=1, source_target_pairs={{0,1},{1,2},{2,3},{3,0},{4,5},{5,6},{6,7},{7,4},{8,9},{9,10},{10,1... | collective-permute-start | bytes 786440 | tf_op jit(solution)/shard_map/ppermute | solution.py:273
  54.5 11.1 %collective-permute-start.13 = (bf16[64,2048]{1,0:T(8,128)(2,1)S(1)}, bf16[64,2048]{1,0:T(8,128)(2,1)S(1)}, u32[]{:S(2)}, u32[]{:S(2)}) collective-permute-start(bf16[64,2048]{1,0:T(8,128)(2,1)S(1)} %pad_maximum_fusion), channel_id=1, source_target_pairs={{0,1},{1,2},{2,3},{3,0},{4,5},{5,6},{6,7},{7,4},{8,9},{9,10},{10,1... | collective-permute-start | bytes 786440 | tf_op jit(solution)/shard_map/ppermute | solution.py:273
  54.6 16.8 %collective-permute-start.14 = (bf16[64,2048]{1,0:T(8,128)(2,1)S(1)}, bf16[64,2048]{1,0:T(8,128)(2,1)S(1)}, u32[]{:S(2)}, u32[]{:S(2)}) collective-permute-start(bf16[64,2048]{1,0:T(8,128)(2,1)S(1)} %pad_maximum_fusion), channel_id=1, source_target_pairs={{0,3},{1,0},{2,1},{3,2},{4,7},{5,4},{6,5},{7,6},{8,11},{9,8},{10,9... | collective-permute-start | bytes 786440 | tf_op jit(solution)/shard_map/ppermute | solution.py:273
  60.3 16.6 %collective-permute-start.17 = (bf16[64,2048]{1,0:T(8,128)(2,1)S(1)}, bf16[64,2048]{1,0:T(8,128)(2,1)S(1)}, u32[]{:S(2)}, u32[]{:S(2)}) collective-permute-start(bf16[64,2048]{1,0:T(8,128)(2,1)S(1)} %pad_maximum_fusion.1), channel_id=1, source_target_pairs={{0,1},{1,2},{2,3},{3,0},{4,5},{5,6},{6,7},{7,4},{8,9},{9,10},{10,1... | collective-permute-start | bytes 786440 | tf_op jit(solution)/shard_map/ppermute | solution.py:273
  60.4 22.0 %collective-permute-start.16 = (bf16[64,2048]{1,0:T(8,128)(2,1)S(1)}, bf16[64,2048]{1,0:T(8,128)(2,1)S(1)}, u32[]{:S(2)}, u32[]{:S(2)}) collective-permute-start(bf16[64,2048]{1,0:T(8,128)(2,1)S(1)} %pad_maximum_fusion.1), channel_id=1, source_target_pairs={{0,3},{1,0},{2,1},{3,2},{4,7},{5,4},{6,5},{7,6},{8,11},{9,8},{10,9... | collective-permute-start | bytes 786440 | tf_op jit(solution)/shard_map/ppermute | solution.py:273
  65.6 22.5 %collective-permute-start.15 = (bf16[64,2048]{1,0:T(8,128)(2,1)S(1)}, bf16[64,2048]{1,0:T(8,128)(2,1)S(1)}, u32[]{:S(2)}, u32[]{:S(2)}) collective-permute-start(bf16[64,2048]{1,0:T(8,128)(2,1)S(1)} %collective-permute-done.13), channel_id=1, source_target_pairs={{0,1},{1,2},{2,3},{3,0},{4,5},{5,6},{6,7},{7,4},{8,9},{9,10},{10,1... | collective-permute-start | bytes 786440 | tf_op jit(solution)/shard_map/ppermute | solution.py:273
  76.9 16.4 %collective-permute-start.18 = (bf16[64,2048]{1,0:T(8,128)(2,1)S(1)}, bf16[64,2048]{1,0:T(8,128)(2,1)S(1)}, u32[]{:S(2)}, u32[]{:S(2)}) collective-permute-start(bf16[64,2048]{1,0:T(8,128)(2,1)S(1)} %collective-permute-done.17), channel_id=1, source_target_pairs={{0,1},{1,2},{2,3},{3,0},{4,5},{5,6},{6,7},{7,4},{8,9},{9,10},{10,1... | collective-permute-start | bytes 786440 | tf_op jit(solution)/shard_map/ppermute | solution.py:273
  90.3 3.0 %collective-permute-start.19 = (bf16[256,1792]{1,0:T(8,128)(2,1)S(1)}, bf16[256,1792]{1,0:T(8,128)(2,1)S(1)}, u32[]{:S(2)}, u32[]{:S(2)}) collective-permute-start(bf16[256,1792]{1,0:T(8,128)(2,1)S(1)} %convolution_convert_fusion.1), channel_id=1, source_target_pairs={{0,4},{4,0},{8,12},{12,8},{16,20},{20,16},{24,28},{28,24},{1,5},{5... | collective-permute-start | bytes 2752520 | tf_op jit(solution)/shard_map/ppermute | solution.py:13
  95.6 10.1 %collective-permute-start.20 = (bf16[64,1792]{1,0:T(8,128)(2,1)S(1)}, bf16[64,1792]{1,0:T(8,128)(2,1)S(1)}, u32[]{:S(2)}, u32[]{:S(2)}) collective-permute-start(bf16[64,1792]{1,0:T(8,128)(2,1)S(1)} %get-tuple-element.53), channel_id=1, source_target_pairs={{0,8},{4,12},{8,0},{12,4},{16,24},{20,28},{24,16},{28,20},{1,9},{5... | collective-permute-start | bytes 688136 | tf_op jit(solution)/shard_map/ppermute | solution.py:13
  97.2 11.9 %collective-permute-start.21 = (bf16[64,1792]{1,0:T(8,128)(2,1)S(1)}, bf16[64,1792]{1,0:T(8,128)(2,1)S(1)}, u32[]{:S(2)}, u32[]{:S(2)}) collective-permute-start(bf16[64,1792]{1,0:T(8,128)(2,1)S(1)} %get-tuple-element.52), channel_id=1, source_target_pairs={{0,16},{4,20},{8,24},{12,28},{16,0},{20,4},{24,8},{28,12},{1,17},{... | collective-permute-start | bytes 688136 | tf_op jit(solution)/shard_map/ppermute | solution.py:13
  97.9 11.2 %copy-start.4 = (bf16[256,128]{1,0:T(8,128)(2,1)S(1)}, bf16[256,128]{1,0:T(8,128)(2,1)}, u32[]{:S(2)}) copy-start(bf16[256,128]{1,0:T(8,128)(2,1)} %get-tuple-element.48) | copy-start | bytes 196612
  97.9 11.2 %collective-permute-start.22 = (bf16[64,1792]{1,0:T(8,128)(2,1)S(1)}, bf16[64,1792]{1,0:T(8,128)(2,1)S(1)}, u32[]{:S(2)}, u32[]{:S(2)}) collective-permute-start(bf16[64,1792]{1,0:T(8,128)(2,1)S(1)} %get-tuple-element.51), channel_id=1, source_target_pairs={{0,24},{4,28},{8,16},{12,20},{16,8},{20,12},{24,0},{28,4},{1,25},{... | collective-permute-start | bytes 688136 | tf_op jit(solution)/shard_map/ppermute | solution.py:13

commit v8 on v7

--- a/solution.py
+++ b/solution.py
@@ -122,15 +122,15 @@
     row = lax.broadcasted_iota(jnp.int32, (capacity, row_total), 1).astype(jnp.float32)
     slot = lax.broadcasted_iota(jnp.int32, (capacity, row_total), 0).astype(jnp.float32)
     hits = []
-    for mask in range(len(out_refs)):
+    for mask in reversed(range(len(out_refs))):
         first = jnp.sum(jnp.where(expert < (chip ^ mask), counts, 0.0), 1, keepdims=True)
         live = jnp.sum(jnp.where(expert == (chip ^ mask), counts, 0.0), 1, keepdims=True)
         hits.append(((row == first + slot) & (slot < live)).astype(jnp.float32))
     chooser = jnp.concatenate(hits, 0).astype(jnp.bfloat16)
     chooser_ref[...] = chooser
     chosen = jnp.dot(chooser, tokens_ref[...], preferred_element_type=jnp.float32)
-    for mask, out_ref in enumerate(out_refs):
-        out_ref[...] = chosen[mask * capacity : (mask + 1) * capacity].astype(jnp.bfloat16)
+    for place, out_ref in enumerate(reversed(out_refs)):
+        out_ref[...] = chosen[place * capacity : (place + 1) * capacity].astype(jnp.bfloat16)
 
 
 def packed_rows(tokens, counts, capacity):
@@ -165,7 +165,7 @@
 
     @pl.when(pl.program_id(0) == 0)
     def _():
-        for place, block_ref in enumerate(block_refs):
+        for place, block_ref in enumerate(reversed(block_refs)):
             held[place * capacity : (place + 1) * capacity, :] = block_ref[...]
 
     sums = jnp.dot(held[...], weight_ref[...], preferred_element_type=jnp.float32)
@@ -193,7 +193,7 @@
             transcendentals=0,
         ),
         name="project",
-    )(*blocks, pltpu.with_memory_space_constraint(weights, pltpu.VMEM))
+    )(*reversed(blocks), pltpu.with_memory_space_constraint(weights, pltpu.VMEM))
 
 
 def weight_kernel(count, *refs):
@@ -355,9 +355,10 @@
         ).astype(jnp.bfloat16)
 
     arrived = {mask: swap(packed[mask], "expert", 2 * mask + 1) for mask in reversed(masks)}
+    passed = {mask: swap(arrived[mask], "expert", 1) for mask in reversed(masks[1:])}
     inputs = [
         [arrived[mask] for mask in masks],
-        [swap(arrived[mask], "expert", 1) if mask else packed[0] for mask in masks],
+        [passed[mask] if mask else packed[0] for mask in masks],
     ]
     for group in range(2):
         begin(group)
@@ -390,7 +391,7 @@
     grad_gate, grad_up = weight_grads(inputs[0] + inputs[1], wholes)
     grad_tokens = lax.dot_general(
         chooser,
-        jnp.concatenate([pieces[mask] for mask in masks], 0),
+        jnp.concatenate([pieces[mask] for mask in reversed(masks)], 0),
         (((0,), (0,)), ((), ())),
         preferred_element_type=jnp.float32,
     ).astype(jnp.bfloat16)

time: 110 us -> 111 us (level)
  transfers between devices with their start and end apart: 23 -> 23, of which waited for: 13 -> 15; matrix products, arithmetic and copies ran while one was open for 4% -> 4% of each run, Pallas kernels for 13% -> 13%
where the time goes in v8:
time: 111 us; the launch traced here: 110 us
  waiting for transfers between devices  43.2 us (39%)
  starting transfers between devices  40.9 us (37%)
  Pallas kernels  16.5 us (15%)
  matrix products  5.3 us (5%)
  local copies, waits for them, and re-layouts  1.84 us (2%)
  other arithmetic  1.69 us (2%)
    ppermute x12, waiting for transfers between devices, send(): self.came[way] = lax.ppermute(value, 'fsdp', ring)  34.3 us
    ppermute x12, starting transfers between devices, send(): self.came[way] = lax.ppermute(value, 'fsdp', ring)  31.9 us
    ppermute x11, starting transfers between devices, swap(): return lax.ppermute(value, axis, pairs)  8.96 us
    ppermute x11, waiting for transfers between devices, swap(): return lax.ppermute(value, axis, pairs)  8.91 us
    pallas_call x1, Pallas kernels, weight_grads(): pl.pallas_call(lambda *refs: weight_kernel(count, *refs), out_shape=(out,...  6.59 us
    dot_general x2, matrix products, back(): lax.dot_general(whole, weights, (((1,), (1,)), ((), ())), preferred_eleme...  4.22 us
    pallas_call x2, Pallas kernels, projected(): pl.pallas_call(project_kernel, out_shape=jax.ShapeDtypeStruct((count, cap...  4.18 us
    pallas_call x1, Pallas kernels, scaled_weights(): pl.pallas_call(lambda *refs: scale_kernel(sub, *refs), out_shape=jax.Shap...  3.3 us
  transfers between devices with their start and end apart: 23, of which 15 were waited for; matrix products, arithmetic and copies ran while one was open for 4% of the time, Pallas kernels for 13%

profile of v8, /device:TPU:0, one launch (start us, length us, event | category | flops | bytes accessed | tf_op | source)
XLA Modules:
  0.0 110.3 jit_solution(6554098223979350878)
XLA Ops:
  0.6 2.4 %pack_rows.1 = (bf16[256,128]{1,0:T(8,128)(2,1)}, bf16[64,1792]{1,0:T(8,128)(2,1)}, bf16[64,1792]{1,0:T(8,128)(2,1)}, bf16[64,1792]{1,0:T(8,128)(2,1)}, bf16[64,1792]{1,0:T(8,128)(2,1)}) custom-call(s32[1,4]{1,0:T(1,128)} %counts_ref.1, bf16[128,1792]{1,0:T(8,128)(2,1)} %tokens_ref.1), custom_call_target="tpu_custom_call" | custom-call | flops 117440512 | bytes 1376256 | tf_op jit(solution)/shard_map/pack_rows/pallas_call | solution.py:141
  3.1 3.4 %collective-permute-start = (bf16[64,1792]{1,0:T(8,128)(2,1)}, bf16[64,1792]{1,0:T(8,128)(2,1)S(1)}, u32[]{:S(2)}, u32[]{:S(2)}) collective-permute-start(bf16[64,1792]{1,0:T(8,128)(2,1)} %get-tuple-element.27), channel_id=1, source_target_pairs={{0,28},{4,24},{8,20},{12,16},{16,12},{20,8},{24,4},{28,0},{1,29},{... | collective-permute-start | bytes 688136 | tf_op jit(solution)/shard_map/ppermute | solution.py:13
  6.4 0.8 collective-permute-start.2
  8.7 3.3 %scale_weights.1.refs_4_ = bf16[1792,2048]{1,0:T(8,128)(2,1)S(1)} custom-call(s32[1]{0:T(128)} %bitcast.refs_0_, bf16[1,1792,1024]{2,1,0:T(8,128)(2,1)} %refs_1_.1, bf16[1,1792,1024]{2,1,0:T(8,128)(2,1)} %refs_2_.1, f32[1,8,56]{2,1,0:T(8,128)S(1)} %bitcast.63, f32[1,8,56]{2,1,0:T(8,128)S(1)} %bitcast.64), custom_call_target="tpu_custom_call" | custom-call | flops 3670016 | bytes 14680064 | tf_op jit(solution)/shard_map/scale_weights/pallas_call | solution.py:84
  13.5 4.1 %collective-permute-done.2.refs_1_.refs_2_ = bf16[64,1792]{1,0:T(8,128)(2,1)S(1)} collective-permute-done((bf16[64,1792]{1,0:T(8,128)(2,1)}, bf16[64,1792]{1,0:T(8,128)(2,1)S(1)}, u32[]{:S(2)}, u32[]{:S(2)}) %collective-permute-start.2) | collective-permute-done | bytes 229408 | tf_op jit(solution)/shard_map/ppermute | solution.py:13
  18.7 2.1 %project.3 = bf16[4,64,2048]{2,1,0:T(8,128)(2,1)S(1)} custom-call(bf16[64,1792]{1,0:T(8,128)(2,1)S(1)} %collective-permute-done.refs_0_.refs_3_, bf16[64,1792]{1,0:T(8,128)(2,1)S(1)} %collective-permute-done.2.refs_1_.refs_2_, bf16[64,1792]{1,0:T(8,128)(2,1)S(1)} %collective-permute-done.4.refs_2_.refs_1_, ...), custom_call_target="tpu_custom_call" | custom-call | flops 1879048192 | bytes 9306112 | tf_op jit(solution)/shard_map/project/pallas_call | solution.py:181
  20.9 1.8 %collective-permute-start.8 = (bf16[64,2048]{1,0:T(8,128)(2,1)S(1)}, bf16[64,2048]{1,0:T(8,128)(2,1)S(1)}, u32[]{:S(2)}, u32[]{:S(2)}) collective-permute-start(bf16[64,2048]{1,0:T(8,128)(2,1)S(1)} %get-tuple-element.56), channel_id=1, source_target_pairs={{0,1},{1,2},{2,3},{3,0},{4,5},{5,6},{6,7},{7,4},{8,9},{9,10},{10,1... | collective-permute-start | bytes 786440 | tf_op jit(solution)/shard_map/ppermute | solution.py:273
  22.7 2.1 %collective-permute-start.11 = (bf16[64,2048]{1,0:T(8,128)(2,1)S(1)}, bf16[64,2048]{1,0:T(8,128)(2,1)S(1)}, u32[]{:S(2)}, u32[]{:S(2)}) collective-permute-start(bf16[64,2048]{1,0:T(8,128)(2,1)S(1)} %get-tuple-element.31), channel_id=1, source_target_pairs={{0,3},{1,0},{2,1},{3,2},{4,7},{5,4},{6,5},{7,6},{8,11},{9,8},{10,9... | collective-permute-start | bytes 786440 | tf_op jit(solution)/shard_map/ppermute | solution.py:273
  24.8 2.1 %project.2 = bf16[4,64,2048]{2,1,0:T(8,128)(2,1)S(1)} custom-call(bf16[64,1792]{1,0:T(8,128)(2,1)S(1)} %collective-permute-done.1.refs_0_.refs_7_, bf16[64,1792]{1,0:T(8,128)(2,1)S(1)} %collective-permute-done.3.refs_1_.refs_6_, bf16[64,1792]{1,0:T(8,128)(2,1)S(1)} %collective-permute-done.5.refs_2_.refs_5_, bf16[64,1792]{1,0:T(8,128)(2,1)S(1)} %copy-done, ...), custom_call_target="tpu_custom_call" | custom-call | flops 1879048192 | bytes 9306112 | tf_op jit(solution)/shard_map/project/pallas_call | solution.py:181
  27.0 3.8 %collective-permute-start.12 = (bf16[64,2048]{1,0:T(8,128)(2,1)S(1)}, bf16[64,2048]{1,0:T(8,128)(2,1)S(1)}, u32[]{:S(2)}, u32[]{:S(2)}) collective-permute-start(bf16[64,2048]{1,0:T(8,128)(2,1)S(1)} %get-tuple-element.33), channel_id=1, source_target_pairs={{0,3},{1,0},{2,1},{3,2},{4,7},{5,4},{6,5},{7,6},{8,11},{9,8},{10,9... | collective-permute-start | bytes 786440 | tf_op jit(solution)/shard_map/ppermute | solution.py:273
  30.9 1.1 collective-permute-done.8
  32.0 4.3 %collective-permute-start.10 = (bf16[64,2048]{1,0:T(8,128)(2,1)S(1)}, bf16[64,2048]{1,0:T(8,128)(2,1)S(1)}, u32[]{:S(2)}, u32[]{:S(2)}) collective-permute-start(bf16[64,2048]{1,0:T(8,128)(2,1)S(1)} %fusion.8), channel_id=1, source_target_pairs={{0,1},{1,2},{2,3},{3,0},{4,5},{5,6},{6,7},{7,4},{8,9},{9,10},{10,1... | collective-permute-start | bytes 786440 | tf_op jit(solution)/shard_map/ppermute | solution.py:273
  36.3 6.9 %collective-permute-done.7 = bf16[64,2048]{1,0:T(8,128)(2,1)S(1)} collective-permute-done((bf16[64,2048]{1,0:T(8,128)(2,1)S(1)}, bf16[64,2048]{1,0:T(8,128)(2,1)S(1)}, u32[]{:S(2)}, u32[]{:S(2)}) %collective-permute-start.7) | collective-permute-done | bytes 262176 | tf_op jit(solution)/shard_map/ppermute | solution.py:273
  43.3 4.2 %collective-permute-start.9 = (bf16[64,2048]{1,0:T(8,128)(2,1)S(1)}, bf16[64,2048]{1,0:T(8,128)(2,1)S(1)}, u32[]{:S(2)}, u32[]{:S(2)}) collective-permute-start(bf16[64,2048]{1,0:T(8,128)(2,1)S(1)} %fusion.9), channel_id=1, source_target_pairs={{0,1},{1,2},{2,3},{3,0},{4,5},{5,6},{6,7},{7,4},{8,9},{9,10},{10,1... | collective-permute-start | bytes 786440 | tf_op jit(solution)/shard_map/ppermute | solution.py:273
  47.5 6.9 %collective-permute-done.10 = bf16[64,2048]{1,0:T(8,128)(2,1)S(1)} collective-permute-done((bf16[64,2048]{1,0:T(8,128)(2,1)S(1)}, bf16[64,2048]{1,0:T(8,128)(2,1)S(1)}, u32[]{:S(2)}, u32[]{:S(2)}) %collective-permute-start.10) | collective-permute-done | bytes 262176 | tf_op jit(solution)/shard_map/ppermute | solution.py:273
  54.8 3.8 %collective-permute-start.14 = (bf16[64,2048]{1,0:T(8,128)(2,1)S(1)}, bf16[64,2048]{1,0:T(8,128)(2,1)S(1)}, u32[]{:S(2)}, u32[]{:S(2)}) collective-permute-start(bf16[64,2048]{1,0:T(8,128)(2,1)S(1)} %pad_maximum_fusion), channel_id=1, source_target_pairs={{0,3},{1,0},{2,1},{3,2},{4,7},{5,4},{6,5},{7,6},{8,11},{9,8},{10,9... | collective-permute-start | bytes 786440 | tf_op jit(solution)/shard_map/ppermute | solution.py:273
  58.8 1.4 %collective-permute-done.9 = bf16[64,2048]{1,0:T(8,128)(2,1)S(1)} collective-permute-done((bf16[64,2048]{1,0:T(8,128)(2,1)S(1)}, bf16[64,2048]{1,0:T(8,128)(2,1)S(1)}, u32[]{:S(2)}, u32[]{:S(2)}) %collective-permute-start.9) | collective-permute-done | bytes 262176 | tf_op jit(solution)/shard_map/ppermute | solution.py:273
  60.6 3.8 %collective-permute-start.16 = (bf16[64,2048]{1,0:T(8,128)(2,1)S(1)}, bf16[64,2048]{1,0:T(8,128)(2,1)S(1)}, u32[]{:S(2)}, u32[]{:S(2)}) collective-permute-start(bf16[64,2048]{1,0:T(8,128)(2,1)S(1)} %pad_maximum_fusion.1), channel_id=1, source_target_pairs={{0,3},{1,0},{2,1},{3,2},{4,7},{5,4},{6,5},{7,6},{8,11},{9,8},{10,9... | collective-permute-start | bytes 786440 | tf_op jit(solution)/shard_map/ppermute | solution.py:273
  65.8 4.0 %collective-permute-start.15 = (bf16[64,2048]{1,0:T(8,128)(2,1)S(1)}, bf16[64,2048]{1,0:T(8,128)(2,1)S(1)}, u32[]{:S(2)}, u32[]{:S(2)}) collective-permute-start(bf16[64,2048]{1,0:T(8,128)(2,1)S(1)} %collective-permute-done.13), channel_id=1, source_target_pairs={{0,1},{1,2},{2,3},{3,0},{4,5},{5,6},{6,7},{7,4},{8,9},{9,10},{10,1... | collective-permute-start | bytes 786440 | tf_op jit(solution)/shard_map/ppermute | solution.py:273
  69.8 1.8 %collective-permute-done.14 = bf16[64,2048]{1,0:T(8,128)(2,1)S(1)} collective-permute-done((bf16[64,2048]{1,0:T(8,128)(2,1)S(1)}, bf16[64,2048]{1,0:T(8,128)(2,1)S(1)}, u32[]{:S(2)}, u32[]{:S(2)}) %collective-permute-start.14) | collective-permute-done | bytes 262176 | tf_op jit(solution)/shard_map/ppermute | solution.py:273
  71.7 5.4 %collective-permute-done.17 = bf16[64,2048]{1,0:T(8,128)(2,1)S(1)} collective-permute-done((bf16[64,2048]{1,0:T(8,128)(2,1)S(1)}, bf16[64,2048]{1,0:T(8,128)(2,1)S(1)}, u32[]{:S(2)}, u32[]{:S(2)}) %collective-permute-start.17) | collective-permute-done | bytes 262176 | tf_op jit(solution)/shard_map/ppermute | solution.py:273
  77.1 3.9 %collective-permute-start.18 = (bf16[64,2048]{1,0:T(8,128)(2,1)S(1)}, bf16[64,2048]{1,0:T(8,128)(2,1)S(1)}, u32[]{:S(2)}, u32[]{:S(2)}) collective-permute-start(bf16[64,2048]{1,0:T(8,128)(2,1)S(1)} %collective-permute-done.17), channel_id=1, source_target_pairs={{0,1},{1,2},{2,3},{3,0},{4,5},{5,6},{6,7},{7,4},{8,9},{9,10},{10,1... | collective-permute-start | bytes 786440 | tf_op jit(solution)/shard_map/ppermute | solution.py:273
  81.0 1.6 %collective-permute-done.16 = bf16[64,2048]{1,0:T(8,128)(2,1)S(1)} collective-permute-done((bf16[64,2048]{1,0:T(8,128)(2,1)S(1)}, bf16[64,2048]{1,0:T(8,128)(2,1)S(1)}, u32[]{:S(2)}, u32[]{:S(2)}) %collective-permute-start.16) | collective-permute-done | bytes 262176 | tf_op jit(solution)/shard_map/ppermute | solution.py:273
  82.6 5.8 %collective-permute-done.15 = bf16[64,2048]{1,0:T(8,128)(2,1)S(1)} collective-permute-done((bf16[64,2048]{1,0:T(8,128)(2,1)S(1)}, bf16[64,2048]{1,0:T(8,128)(2,1)S(1)}, u32[]{:S(2)}, u32[]{:S(2)}) %collective-permute-start.15) | collective-permute-done | bytes 262176 | tf_op jit(solution)/shard_map/ppermute | solution.py:273
  88.4 2.1 %convolution_convert_fusion.1 = bf16[256,1792]{1,0:T(8,128)(2,1)S(1)} fusion(bf16[256,2048]{1,0:T(8,128)(2,1)S(1)} %bitcast.61, bf16[1792,2048]{1,0:T(8,128)(2,1)S(1)} %scale_weights.1.refs_4_), kind=kOutput, calls=%fused_computation.1 | convolution fusion | flops 1879506944 | bytes 9306112 | tf_op jit(solution)/shard_map/dot_general | solution.py:353
  90.6 2.8 %collective-permute-done.18 = bf16[64,2048]{1,0:T(8,128)(2,1)S(1)} collective-permute-done((bf16[64,2048]{1,0:T(8,128)(2,1)S(1)}, bf16[64,2048]{1,0:T(8,128)(2,1)S(1)}, u32[]{:S(2)}, u32[]{:S(2)}) %collective-permute-start.18) | collective-permute-done | bytes 262176 | tf_op jit(solution)/shard_map/ppermute | solution.py:273
  93.4 2.1 %convolution_convert_fusion = bf16[256,1792]{1,0:T(8,128)(2,1)S(1)} fusion(bf16[256,2048]{1,0:T(8,128)(2,1)S(1)} %bitcast.59, bf16[1792,2048]{1,0:T(8,128)(2,1)S(1)} %scale_weights.1.refs_4_), kind=kOutput, calls=%fused_computation | convolution fusion | flops 1879506944 | bytes 9306112 | tf_op jit(solution)/shard_map/dot_general | solution.py:353
  95.8 1.6 %collective-permute-start.20 = (bf16[64,1792]{1,0:T(8,128)(2,1)S(1)}, bf16[64,1792]{1,0:T(8,128)(2,1)S(1)}, u32[]{:S(2)}, u32[]{:S(2)}) collective-permute-start(bf16[64,1792]{1,0:T(8,128)(2,1)S(1)} %get-tuple-element.50), channel_id=1, source_target_pairs={{0,24},{4,28},{8,16},{12,20},{16,8},{20,12},{24,0},{28,4},{1,25},{... | collective-permute-start | bytes 688136 | tf_op jit(solution)/shard_map/ppermute | solution.py:13
  97.4 1.4 %collective-permute-start.21 = (bf16[64,1792]{1,0:T(8,128)(2,1)S(1)}, bf16[64,1792]{1,0:T(8,128)(2,1)S(1)}, u32[]{:S(2)}, u32[]{:S(2)}) collective-permute-start(bf16[64,1792]{1,0:T(8,128)(2,1)S(1)} %get-tuple-element.53), channel_id=1, source_target_pairs={{0,16},{4,20},{8,24},{12,28},{16,0},{20,4},{24,8},{28,12},{1,17},{... | collective-permute-start | bytes 688136 | tf_op jit(solution)/shard_map/ppermute | solution.py:13
  99.3 6.6 %weight_grads.1 = (bf16[1,1792,1024]{2,1,0:T(8,128)(2,1)}, bf16[1,1792,1024]{2,1,0:T(8,128)(2,1)}) custom-call(bf16[64,1792]{1,0:T(8,128)(2,1)S(1)} %collective-permute-done.6.refs_3_.refs_0_, bf16[64,1792]{1,0:T(8,128)(2,1)S(1)} %collective-permute-done.4.refs_2_.refs_1_, bf16[64,1792]{1,0:T(8,128)(2,1)S(1)} %collective-permute-done.2.refs_1_.refs_2_, ...), custom_call_target="tpu_custom_call" | custom-call | flops 3758096384 | bytes 11272192 | tf_op jit(solution)/shard_map/weight_grads/pallas_call | solution.py:229
  105.9 2.9 %collective-permute-done.21 = bf16[64,1792]{1,0:T(8,128)(2,1)S(1)} collective-permute-done((bf16[64,1792]{1,0:T(8,128)(2,1)S(1)}, bf16[64,1792]{1,0:T(8,128)(2,1)S(1)}, u32[]{:S(2)}, u32[]{:S(2)}) %collective-permute-start.21) | collective-permute-done | bytes 229408 | tf_op jit(solution)/shard_map/ppermute | solution.py:13
  109.2 1.1 convolution_convert_fusion.2
  (54 shorter events, 7.9 us)
Async XLA Ops:
  3.1 9.7 %collective-permute-start = (bf16[64,1792]{1,0:T(8,128)(2,1)}, bf16[64,1792]{1,0:T(8,128)(2,1)S(1)}, u32[]{:S(2)}, u32[]{:S(2)}) collective-permute-start(bf16[64,1792]{1,0:T(8,128)(2,1)} %get-tuple-element.27), channel_id=1, source_target_pairs={{0,28},{4,24},{8,20},{12,16},{16,12},{20,8},{24,4},{28,0},{1,29},{... | collective-permute-start | bytes 688136 | tf_op jit(solution)/shard_map/ppermute | solution.py:13
  6.4 11.2 %collective-permute-start.2 = (bf16[64,1792]{1,0:T(8,128)(2,1)}, bf16[64,1792]{1,0:T(8,128)(2,1)S(1)}, u32[]{:S(2)}, u32[]{:S(2)}) collective-permute-start(bf16[64,1792]{1,0:T(8,128)(2,1)} %get-tuple-element.28), channel_id=1, source_target_pairs={{0,20},{4,16},{8,28},{12,24},{16,4},{20,0},{24,12},{28,8},{1,21},{... | collective-permute-start | bytes 688136 | tf_op jit(solution)/shard_map/ppermute | solution.py:13
  7.2 11.3 %collective-permute-start.4 = (bf16[64,1792]{1,0:T(8,128)(2,1)}, bf16[64,1792]{1,0:T(8,128)(2,1)S(1)}, u32[]{:S(2)}, u32[]{:S(2)}) collective-permute-start(bf16[64,1792]{1,0:T(8,128)(2,1)} %get-tuple-element.29), channel_id=1, source_target_pairs={{0,12},{4,8},{8,4},{12,0},{16,28},{20,24},{24,20},{28,16},{1,13},{... | collective-permute-start | bytes 688136 | tf_op jit(solution)/shard_map/ppermute | solution.py:13
  7.4 11.3 %collective-permute-start.6 = (bf16[64,1792]{1,0:T(8,128)(2,1)}, bf16[64,1792]{1,0:T(8,128)(2,1)S(1)}, u32[]{:S(2)}, u32[]{:S(2)}) collective-permute-start(bf16[64,1792]{1,0:T(8,128)(2,1)} %get-tuple-element.30.refs_3_.refs_4_), channel_id=1, source_target_pairs={{0,4},{4,0},{8,12},{12,8},{16,20},{20,16},{24,28},{28,24},{1,5},{5... | collective-permute-start | bytes 688136 | tf_op jit(solution)/shard_map/ppermute | solution.py:13
  7.4 0.7 copy-start.1
  8.1 0.7 copy-start.2
  12.1 12.8 %copy-start = (bf16[64,1792]{1,0:T(8,128)(2,1)S(1)}, bf16[64,1792]{1,0:T(8,128)(2,1)}, u32[]{:S(2)}) copy-start(bf16[64,1792]{1,0:T(8,128)(2,1)} %get-tuple-element.30.refs_3_.refs_4_) | copy-start | bytes 688132
  12.8 12.0 %collective-permute-start.1 = (bf16[64,1792]{1,0:T(8,128)(2,1)S(1)}, bf16[64,1792]{1,0:T(8,128)(2,1)S(1)}, u32[]{:S(2)}, u32[]{:S(2)}) collective-permute-start(bf16[64,1792]{1,0:T(8,128)(2,1)S(1)} %collective-permute-done.refs_0_.refs_3_), channel_id=1, source_target_pairs={{0,4},{4,0},{8,12},{12,8},{16,20},{20,16},{24,28},{28,24},{1,5},{5... | collective-permute-start | bytes 688136 | tf_op jit(solution)/shard_map/ppermute | solution.py:13
  17.7 7.2 %collective-permute-start.3 = (bf16[64,1792]{1,0:T(8,128)(2,1)S(1)}, bf16[64,1792]{1,0:T(8,128)(2,1)S(1)}, u32[]{:S(2)}, u32[]{:S(2)}) collective-permute-start(bf16[64,1792]{1,0:T(8,128)(2,1)S(1)} %collective-permute-done.2.refs_1_.refs_2_), channel_id=1, source_target_pairs={{0,4},{4,0},{8,12},{12,8},{16,20},{20,16},{24,28},{28,24},{1,5},{5... | collective-permute-start | bytes 688136 | tf_op jit(solution)/shard_map/ppermute | solution.py:13
  18.6 6.3 %collective-permute-start.5 = (bf16[64,1792]{1,0:T(8,128)(2,1)S(1)}, bf16[64,1792]{1,0:T(8,128)(2,1)S(1)}, u32[]{:S(2)}, u32[]{:S(2)}) collective-permute-start(bf16[64,1792]{1,0:T(8,128)(2,1)S(1)} %collective-permute-done.4.refs_2_.refs_1_), channel_id=1, source_target_pairs={{0,4},{4,0},{8,12},{12,8},{16,20},{20,16},{24,28},{28,24},{1,5},{5... | collective-permute-start | bytes 688136 | tf_op jit(solution)/shard_map/ppermute | solution.py:13
  20.9 11.0 %collective-permute-start.8 = (bf16[64,2048]{1,0:T(8,128)(2,1)S(1)}, bf16[64,2048]{1,0:T(8,128)(2,1)S(1)}, u32[]{:S(2)}, u32[]{:S(2)}) collective-permute-start(bf16[64,2048]{1,0:T(8,128)(2,1)S(1)} %get-tuple-element.56), channel_id=1, source_target_pairs={{0,1},{1,2},{2,3},{3,0},{4,5},{5,6},{6,7},{7,4},{8,9},{9,10},{10,1... | collective-permute-start | bytes 786440 | tf_op jit(solution)/shard_map/ppermute | solution.py:273
  22.7 24.8 %collective-permute-start.11 = (bf16[64,2048]{1,0:T(8,128)(2,1)S(1)}, bf16[64,2048]{1,0:T(8,128)(2,1)S(1)}, u32[]{:S(2)}, u32[]{:S(2)}) collective-permute-start(bf16[64,2048]{1,0:T(8,128)(2,1)S(1)} %get-tuple-element.31), channel_id=1, source_target_pairs={{0,3},{1,0},{2,1},{3,2},{4,7},{5,4},{6,5},{7,6},{8,11},{9,8},{10,9... | collective-permute-start | bytes 786440 | tf_op jit(solution)/shard_map/ppermute | solution.py:273
  26.9 27.6 %copy-start.3 = (bf16[1,128,1024]{2,1,0:T(8,128)(2,1)S(1)}, bf16[1,128,1024]{2,1,0:T(8,128)(2,1)}, u32[]{:S(2)}) copy-start(bf16[1,128,1024]{2,1,0:T(8,128)(2,1)} %param.13) | copy-start | bytes 786436
  27.0 16.2 %collective-permute-start.7 = (bf16[64,2048]{1,0:T(8,128)(2,1)S(1)}, bf16[64,2048]{1,0:T(8,128)(2,1)S(1)}, u32[]{:S(2)}, u32[]{:S(2)}) collective-permute-start(bf16[64,2048]{1,0:T(8,128)(2,1)S(1)} %get-tuple-element.32), channel_id=1, source_target_pairs={{0,1},{1,2},{2,3},{3,0},{4,5},{5,6},{6,7},{7,4},{8,9},{9,10},{10,1... | collective-permute-start | bytes 786440 | tf_op jit(solution)/shard_map/ppermute | solution.py:273
  27.0 31.6 %collective-permute-start.12 = (bf16[64,2048]{1,0:T(8,128)(2,1)S(1)}, bf16[64,2048]{1,0:T(8,128)(2,1)S(1)}, u32[]{:S(2)}, u32[]{:S(2)}) collective-permute-start(bf16[64,2048]{1,0:T(8,128)(2,1)S(1)} %get-tuple-element.33), channel_id=1, source_target_pairs={{0,3},{1,0},{2,1},{3,2},{4,7},{5,4},{6,5},{7,6},{8,11},{9,8},{10,9... | collective-permute-start | bytes 786440 | tf_op jit(solution)/shard_map/ppermute | solution.py:273
  32.0 22.4 %collective-permute-start.10 = (bf16[64,2048]{1,0:T(8,128)(2,1)S(1)}, bf16[64,2048]{1,0:T(8,128)(2,1)S(1)}, u32[]{:S(2)}, u32[]{:S(2)}) collective-permute-start(bf16[64,2048]{1,0:T(8,128)(2,1)S(1)} %fusion.8), channel_id=1, source_target_pairs={{0,1},{1,2},{2,3},{3,0},{4,5},{5,6},{6,7},{7,4},{8,9},{9,10},{10,1... | collective-permute-start | bytes 786440 | tf_op jit(solution)/shard_map/ppermute | solution.py:273
  43.3 16.9 %collective-permute-start.9 = (bf16[64,2048]{1,0:T(8,128)(2,1)S(1)}, bf16[64,2048]{1,0:T(8,128)(2,1)S(1)}, u32[]{:S(2)}, u32[]{:S(2)}) collective-permute-start(bf16[64,2048]{1,0:T(8,128)(2,1)S(1)} %fusion.9), channel_id=1, source_target_pairs={{0,1},{1,2},{2,3},{3,0},{4,5},{5,6},{6,7},{7,4},{8,9},{9,10},{10,1... | collective-permute-start | bytes 786440 | tf_op jit(solution)/shard_map/ppermute | solution.py:273
  54.7 11.1 %collective-permute-start.13 = (bf16[64,2048]{1,0:T(8,128)(2,1)S(1)}, bf16[64,2048]{1,0:T(8,128)(2,1)S(1)}, u32[]{:S(2)}, u32[]{:S(2)}) collective-permute-start(bf16[64,2048]{1,0:T(8,128)(2,1)S(1)} %pad_maximum_fusion), channel_id=1, source_target_pairs={{0,1},{1,2},{2,3},{3,0},{4,5},{5,6},{6,7},{7,4},{8,9},{9,10},{10,1... | collective-permute-start | bytes 786440 | tf_op jit(solution)/shard_map/ppermute | solution.py:273
  54.8 16.8 %collective-permute-start.14 = (bf16[64,2048]{1,0:T(8,128)(2,1)S(1)}, bf16[64,2048]{1,0:T(8,128)(2,1)S(1)}, u32[]{:S(2)}, u32[]{:S(2)}) collective-permute-start(bf16[64,2048]{1,0:T(8,128)(2,1)S(1)} %pad_maximum_fusion), channel_id=1, source_target_pairs={{0,3},{1,0},{2,1},{3,2},{4,7},{5,4},{6,5},{7,6},{8,11},{9,8},{10,9... | collective-permute-start | bytes 786440 | tf_op jit(solution)/shard_map/ppermute | solution.py:273
  60.5 16.6 %collective-permute-start.17 = (bf16[64,2048]{1,0:T(8,128)(2,1)S(1)}, bf16[64,2048]{1,0:T(8,128)(2,1)S(1)}, u32[]{:S(2)}, u32[]{:S(2)}) collective-permute-start(bf16[64,2048]{1,0:T(8,128)(2,1)S(1)} %pad_maximum_fusion.1), channel_id=1, source_target_pairs={{0,1},{1,2},{2,3},{3,0},{4,5},{5,6},{6,7},{7,4},{8,9},{9,10},{10,1... | collective-permute-start | bytes 786440 | tf_op jit(solution)/shard_map/ppermute | solution.py:273
  60.6 22.0 %collective-permute-start.16 = (bf16[64,2048]{1,0:T(8,128)(2,1)S(1)}, bf16[64,2048]{1,0:T(8,128)(2,1)S(1)}, u32[]{:S(2)}, u32[]{:S(2)}) collective-permute-start(bf16[64,2048]{1,0:T(8,128)(2,1)S(1)} %pad_maximum_fusion.1), channel_id=1, source_target_pairs={{0,3},{1,0},{2,1},{3,2},{4,7},{5,4},{6,5},{7,6},{8,11},{9,8},{10,9... | collective-permute-start | bytes 786440 | tf_op jit(solution)/shard_map/ppermute | solution.py:273
  65.8 22.5 %collective-permute-start.15 = (bf16[64,2048]{1,0:T(8,128)(2,1)S(1)}, bf16[64,2048]{1,0:T(8,128)(2,1)S(1)}, u32[]{:S(2)}, u32[]{:S(2)}) collective-permute-start(bf16[64,2048]{1,0:T(8,128)(2,1)S(1)} %collective-permute-done.13), channel_id=1, source_target_pairs={{0,1},{1,2},{2,3},{3,0},{4,5},{5,6},{6,7},{7,4},{8,9},{9,10},{10,1... | collective-permute-start | bytes 786440 | tf_op jit(solution)/shard_map/ppermute | solution.py:273
  77.1 16.3 %collective-permute-start.18 = (bf16[64,2048]{1,0:T(8,128)(2,1)S(1)}, bf16[64,2048]{1,0:T(8,128)(2,1)S(1)}, u32[]{:S(2)}, u32[]{:S(2)}) collective-permute-start(bf16[64,2048]{1,0:T(8,128)(2,1)S(1)} %collective-permute-done.17), channel_id=1, source_target_pairs={{0,1},{1,2},{2,3},{3,0},{4,5},{5,6},{6,7},{7,4},{8,9},{9,10},{10,1... | collective-permute-start | bytes 786440 | tf_op jit(solution)/shard_map/ppermute | solution.py:273
  90.5 3.0 %collective-permute-start.19 = (bf16[256,1792]{1,0:T(8,128)(2,1)S(1)}, bf16[256,1792]{1,0:T(8,128)(2,1)S(1)}, u32[]{:S(2)}, u32[]{:S(2)}) collective-permute-start(bf16[256,1792]{1,0:T(8,128)(2,1)S(1)} %convolution_convert_fusion.1), channel_id=1, source_target_pairs={{0,4},{4,0},{8,12},{12,8},{16,20},{20,16},{24,28},{28,24},{1,5},{5... | collective-permute-start | bytes 2752520 | tf_op jit(solution)/shard_map/ppermute | solution.py:13
  95.8 10.2 %collective-permute-start.20 = (bf16[64,1792]{1,0:T(8,128)(2,1)S(1)}, bf16[64,1792]{1,0:T(8,128)(2,1)S(1)}, u32[]{:S(2)}, u32[]{:S(2)}) collective-permute-start(bf16[64,1792]{1,0:T(8,128)(2,1)S(1)} %get-tuple-element.50), channel_id=1, source_target_pairs={{0,24},{4,28},{8,16},{12,20},{16,8},{20,12},{24,0},{28,4},{1,25},{... | collective-permute-start | bytes 688136 | tf_op jit(solution)/shard_map/ppermute | solution.py:13
  97.4 11.5 %collective-permute-start.21 = (bf16[64,1792]{1,0:T(8,128)(2,1)S(1)}, bf16[64,1792]{1,0:T(8,128)(2,1)S(1)}, u32[]{:S(2)}, u32[]{:S(2)}) collective-permute-start(bf16[64,1792]{1,0:T(8,128)(2,1)S(1)} %get-tuple-element.53), channel_id=1, source_target_pairs={{0,16},{4,20},{8,24},{12,28},{16,0},{20,4},{24,8},{28,12},{1,17},{... | collective-permute-start | bytes 688136 | tf_op jit(solution)/shard_map/ppermute | solution.py:13
  98.8 10.4 %copy-start.4 = (bf16[256,128]{1,0:T(8,128)(2,1)S(1)}, bf16[256,128]{1,0:T(8,128)(2,1)}, u32[]{:S(2)}) copy-start(bf16[256,128]{1,0:T(8,128)(2,1)} %get-tuple-element.48) | copy-start | bytes 196612
  98.8 10.4 %collective-permute-start.22 = (bf16[64,1792]{1,0:T(8,128)(2,1)S(1)}, bf16[64,1792]{1,0:T(8,128)(2,1)S(1)}, u32[]{:S(2)}, u32[]{:S(2)}) collective-permute-start(bf16[64,1792]{1,0:T(8,128)(2,1)S(1)} %get-tuple-element.52), channel_id=1, source_target_pairs={{0,8},{4,12},{8,0},{12,4},{16,24},{20,28},{24,16},{28,20},{1,9},{5... | collective-permute-start | bytes 688136 | tf_op jit(solution)/shard_map/ppermute | solution.py:13

commit v9 on v8

--- a/solution.py
+++ b/solution.py
@@ -137,7 +137,7 @@
     row_total, feat_cols = tokens.shape
     experts = counts.shape[1]
     tile = feat_cols // 2 if feat_cols % 256 == 0 else feat_cols
-    block = jax.ShapeDtypeStruct((capacity, feat_cols), jnp.bfloat16)
+    block = pltpu.VMEM((capacity, feat_cols), jnp.bfloat16)
     chooser, *packed = pl.pallas_call(
         pack_kernel,
         out_shape=(jax.ShapeDtypeStruct((experts * capacity, row_total), jnp.bfloat16),)

time: 111 us -> 110 us (level)
  no operation moved by 1% of the time
where the time goes in v9:
time: 110 us
  waiting for transfers between devices  42.9 us (39%)
  starting transfers between devices  41 us (37%)
  Pallas kernels  16.2 us (15%)
  matrix products  5.3 us (5%)
  local copies, waits for them, and re-layouts  1.83 us (2%)
  other arithmetic  1.69 us (2%)
    ppermute x12, waiting for transfers between devices, send(): self.came[way] = lax.ppermute(value, 'fsdp', ring)  34.2 us
    ppermute x12, starting transfers between devices, send(): self.came[way] = lax.ppermute(value, 'fsdp', ring)  32 us
    ppermute x11, starting transfers between devices, swap(): return lax.ppermute(value, axis, pairs)  8.93 us
    ppermute x11, waiting for transfers between devices, swap(): return lax.ppermute(value, axis, pairs)  8.67 us
    pallas_call x1, Pallas kernels, weight_grads(): pl.pallas_call(lambda *refs: weight_kernel(count, *refs), out_shape=(out,...  6.59 us
    dot_general x2, matrix products, back(): lax.dot_general(whole, weights, (((1,), (1,)), ((), ())), preferred_eleme...  4.21 us
    pallas_call x2, Pallas kernels, projected(): pl.pallas_call(project_kernel, out_shape=jax.ShapeDtypeStruct((count, cap...  4.19 us
    pallas_call x1, Pallas kernels, scaled_weights(): pl.pallas_call(lambda *refs: scale_kernel(sub, *refs), out_shape=jax.Shap...  3.3 us
  transfers between devices with their start and end apart: 23, of which 15 were waited for; matrix products, arithmetic and copies ran while one was open for 4% of the time, Pallas kernels for 13%

profile of v9, /device:TPU:0, one launch (start us, length us, event | category | flops | bytes accessed | tf_op | source)
XLA Modules:
  0.0 109.7 jit_solution(2861431334951041890)
XLA Ops:
  0.6 2.1 %pack_rows.1 = (bf16[256,128]{1,0:T(8,128)(2,1)}, bf16[64,1792]{1,0:T(8,128)(2,1)S(1)}, bf16[64,1792]{1,0:T(8,128)(2,1)S(1)}, bf16[64,1792]{1,0:T(8,128)(2,1)S(1)}, bf16[64,1792]{1,0:T(8,128)(2,1)S(1)}) custom-call(s32[1,4]{1,0:T(1,128)} %counts_ref.1, bf16[128,1792]{1,0:T(8,128)(2,1)} %tokens_ref.1), custom_call_target="tpu_custom_call" | custom-call | flops 117440512 | bytes 1376256 | tf_op jit(solution)/shard_map/pack_rows/pallas_call | solution.py:141
  2.8 3.3 %collective-permute-start = (bf16[64,1792]{1,0:T(8,128)(2,1)S(1)}, bf16[64,1792]{1,0:T(8,128)(2,1)S(1)}, u32[]{:S(2)}, u32[]{:S(2)}) collective-permute-start(bf16[64,1792]{1,0:T(8,128)(2,1)S(1)} %get-tuple-element.27), channel_id=1, source_target_pairs={{0,28},{4,24},{8,20},{12,16},{16,12},{20,8},{24,4},{28,0},{1,29},{... | collective-permute-start | bytes 688136 | tf_op jit(solution)/shard_map/ppermute | solution.py:13
  8.3 3.3 %scale_weights.1.refs_4_ = bf16[1792,2048]{1,0:T(8,128)(2,1)S(1)} custom-call(s32[1]{0:T(128)} %bitcast.refs_0_, bf16[1,1792,1024]{2,1,0:T(8,128)(2,1)} %refs_1_.1, bf16[1,1792,1024]{2,1,0:T(8,128)(2,1)} %refs_2_.1, f32[1,8,56]{2,1,0:T(8,128)S(1)} %bitcast.63, f32[1,8,56]{2,1,0:T(8,128)S(1)} %bitcast.64), custom_call_target="tpu_custom_call" | custom-call | flops 3670016 | bytes 14680064 | tf_op jit(solution)/shard_map/scale_weights/pallas_call | solution.py:84
  12.1 0.8 collective-permute-start.1
  12.9 4.1 %collective-permute-done.2.refs_1_.refs_2_ = bf16[64,1792]{1,0:T(8,128)(2,1)S(1)} collective-permute-done((bf16[64,1792]{1,0:T(8,128)(2,1)S(1)}, bf16[64,1792]{1,0:T(8,128)(2,1)S(1)}, u32[]{:S(2)}, u32[]{:S(2)}) %collective-permute-start.2) | collective-permute-done | bytes 229408 | tf_op jit(solution)/shard_map/ppermute | solution.py:13
  18.1 2.1 %project.3 = bf16[4,64,2048]{2,1,0:T(8,128)(2,1)S(1)} custom-call(bf16[64,1792]{1,0:T(8,128)(2,1)S(1)} %collective-permute-done.refs_0_.refs_3_, bf16[64,1792]{1,0:T(8,128)(2,1)S(1)} %collective-permute-done.2.refs_1_.refs_2_, bf16[64,1792]{1,0:T(8,128)(2,1)S(1)} %collective-permute-done.4.refs_2_.refs_1_, ...), custom_call_target="tpu_custom_call" | custom-call | flops 1879048192 | bytes 9306112 | tf_op jit(solution)/shard_map/project/pallas_call | solution.py:181
  20.3 1.9 %collective-permute-start.8 = (bf16[64,2048]{1,0:T(8,128)(2,1)S(1)}, bf16[64,2048]{1,0:T(8,128)(2,1)S(1)}, u32[]{:S(2)}, u32[]{:S(2)}) collective-permute-start(bf16[64,2048]{1,0:T(8,128)(2,1)S(1)} %get-tuple-element.56), channel_id=1, source_target_pairs={{0,1},{1,2},{2,3},{3,0},{4,5},{5,6},{6,7},{7,4},{8,9},{9,10},{10,1... | collective-permute-start | bytes 786440 | tf_op jit(solution)/shard_map/ppermute | solution.py:273
  22.2 2.1 %collective-permute-start.11 = (bf16[64,2048]{1,0:T(8,128)(2,1)S(1)}, bf16[64,2048]{1,0:T(8,128)(2,1)S(1)}, u32[]{:S(2)}, u32[]{:S(2)}) collective-permute-start(bf16[64,2048]{1,0:T(8,128)(2,1)S(1)} %get-tuple-element.31), channel_id=1, source_target_pairs={{0,3},{1,0},{2,1},{3,2},{4,7},{5,4},{6,5},{7,6},{8,11},{9,8},{10,9... | collective-permute-start | bytes 786440 | tf_op jit(solution)/shard_map/ppermute | solution.py:273
  24.3 2.1 %project.2 = bf16[4,64,2048]{2,1,0:T(8,128)(2,1)S(1)} custom-call(bf16[64,1792]{1,0:T(8,128)(2,1)S(1)} %collective-permute-done.1.refs_0_.refs_7_, bf16[64,1792]{1,0:T(8,128)(2,1)S(1)} %collective-permute-done.3.refs_1_.refs_6_, bf16[64,1792]{1,0:T(8,128)(2,1)S(1)} %collective-permute-done.5.refs_2_.refs_5_, ...), custom_call_target="tpu_custom_call" | custom-call | flops 1879048192 | bytes 9306112 | tf_op jit(solution)/shard_map/project/pallas_call | solution.py:181
  26.5 3.8 %collective-permute-start.12 = (bf16[64,2048]{1,0:T(8,128)(2,1)S(1)}, bf16[64,2048]{1,0:T(8,128)(2,1)S(1)}, u32[]{:S(2)}, u32[]{:S(2)}) collective-permute-start(bf16[64,2048]{1,0:T(8,128)(2,1)S(1)} %get-tuple-element.33), channel_id=1, source_target_pairs={{0,3},{1,0},{2,1},{3,2},{4,7},{5,4},{6,5},{7,6},{8,11},{9,8},{10,9... | collective-permute-start | bytes 786440 | tf_op jit(solution)/shard_map/ppermute | solution.py:273
  30.3 1.0 collective-permute-done.8
  31.4 4.3 %collective-permute-start.10 = (bf16[64,2048]{1,0:T(8,128)(2,1)S(1)}, bf16[64,2048]{1,0:T(8,128)(2,1)S(1)}, u32[]{:S(2)}, u32[]{:S(2)}) collective-permute-start(bf16[64,2048]{1,0:T(8,128)(2,1)S(1)} %fusion.8), channel_id=1, source_target_pairs={{0,1},{1,2},{2,3},{3,0},{4,5},{5,6},{6,7},{7,4},{8,9},{9,10},{10,1... | collective-permute-start | bytes 786440 | tf_op jit(solution)/shard_map/ppermute | solution.py:273
  35.7 6.9 %collective-permute-done.7 = bf16[64,2048]{1,0:T(8,128)(2,1)S(1)} collective-permute-done((bf16[64,2048]{1,0:T(8,128)(2,1)S(1)}, bf16[64,2048]{1,0:T(8,128)(2,1)S(1)}, u32[]{:S(2)}, u32[]{:S(2)}) %collective-permute-start.7) | collective-permute-done | bytes 262176 | tf_op jit(solution)/shard_map/ppermute | solution.py:273
  42.7 4.2 %collective-permute-start.9 = (bf16[64,2048]{1,0:T(8,128)(2,1)S(1)}, bf16[64,2048]{1,0:T(8,128)(2,1)S(1)}, u32[]{:S(2)}, u32[]{:S(2)}) collective-permute-start(bf16[64,2048]{1,0:T(8,128)(2,1)S(1)} %fusion.9), channel_id=1, source_target_pairs={{0,1},{1,2},{2,3},{3,0},{4,5},{5,6},{6,7},{7,4},{8,9},{9,10},{10,1... | collective-permute-start | bytes 786440 | tf_op jit(solution)/shard_map/ppermute | solution.py:273
  46.9 6.9 %collective-permute-done.10 = bf16[64,2048]{1,0:T(8,128)(2,1)S(1)} collective-permute-done((bf16[64,2048]{1,0:T(8,128)(2,1)S(1)}, bf16[64,2048]{1,0:T(8,128)(2,1)S(1)}, u32[]{:S(2)}, u32[]{:S(2)}) %collective-permute-start.10) | collective-permute-done | bytes 262176 | tf_op jit(solution)/shard_map/ppermute | solution.py:273
  54.2 3.8 %collective-permute-start.14 = (bf16[64,2048]{1,0:T(8,128)(2,1)S(1)}, bf16[64,2048]{1,0:T(8,128)(2,1)S(1)}, u32[]{:S(2)}, u32[]{:S(2)}) collective-permute-start(bf16[64,2048]{1,0:T(8,128)(2,1)S(1)} %pad_maximum_fusion), channel_id=1, source_target_pairs={{0,3},{1,0},{2,1},{3,2},{4,7},{5,4},{6,5},{7,6},{8,11},{9,8},{10,9... | collective-permute-start | bytes 786440 | tf_op jit(solution)/shard_map/ppermute | solution.py:273
  58.2 1.4 %collective-permute-done.9 = bf16[64,2048]{1,0:T(8,128)(2,1)S(1)} collective-permute-done((bf16[64,2048]{1,0:T(8,128)(2,1)S(1)}, bf16[64,2048]{1,0:T(8,128)(2,1)S(1)}, u32[]{:S(2)}, u32[]{:S(2)}) %collective-permute-start.9) | collective-permute-done | bytes 262176 | tf_op jit(solution)/shard_map/ppermute | solution.py:273
  60.0 3.8 %collective-permute-start.16 = (bf16[64,2048]{1,0:T(8,128)(2,1)S(1)}, bf16[64,2048]{1,0:T(8,128)(2,1)S(1)}, u32[]{:S(2)}, u32[]{:S(2)}) collective-permute-start(bf16[64,2048]{1,0:T(8,128)(2,1)S(1)} %pad_maximum_fusion.1), channel_id=1, source_target_pairs={{0,3},{1,0},{2,1},{3,2},{4,7},{5,4},{6,5},{7,6},{8,11},{9,8},{10,9... | collective-permute-start | bytes 786440 | tf_op jit(solution)/shard_map/ppermute | solution.py:273
  65.2 4.0 %collective-permute-start.15 = (bf16[64,2048]{1,0:T(8,128)(2,1)S(1)}, bf16[64,2048]{1,0:T(8,128)(2,1)S(1)}, u32[]{:S(2)}, u32[]{:S(2)}) collective-permute-start(bf16[64,2048]{1,0:T(8,128)(2,1)S(1)} %collective-permute-done.13), channel_id=1, source_target_pairs={{0,1},{1,2},{2,3},{3,0},{4,5},{5,6},{6,7},{7,4},{8,9},{9,10},{10,1... | collective-permute-start | bytes 786440 | tf_op jit(solution)/shard_map/ppermute | solution.py:273
  69.2 1.8 %collective-permute-done.14 = bf16[64,2048]{1,0:T(8,128)(2,1)S(1)} collective-permute-done((bf16[64,2048]{1,0:T(8,128)(2,1)S(1)}, bf16[64,2048]{1,0:T(8,128)(2,1)S(1)}, u32[]{:S(2)}, u32[]{:S(2)}) %collective-permute-start.14) | collective-permute-done | bytes 262176 | tf_op jit(solution)/shard_map/ppermute | solution.py:273
  71.1 5.4 %collective-permute-done.17 = bf16[64,2048]{1,0:T(8,128)(2,1)S(1)} collective-permute-done((bf16[64,2048]{1,0:T(8,128)(2,1)S(1)}, bf16[64,2048]{1,0:T(8,128)(2,1)S(1)}, u32[]{:S(2)}, u32[]{:S(2)}) %collective-permute-start.17) | collective-permute-done | bytes 262176 | tf_op jit(solution)/shard_map/ppermute | solution.py:273
  76.5 3.9 %collective-permute-start.18 = (bf16[64,2048]{1,0:T(8,128)(2,1)S(1)}, bf16[64,2048]{1,0:T(8,128)(2,1)S(1)}, u32[]{:S(2)}, u32[]{:S(2)}) collective-permute-start(bf16[64,2048]{1,0:T(8,128)(2,1)S(1)} %collective-permute-done.17), channel_id=1, source_target_pairs={{0,1},{1,2},{2,3},{3,0},{4,5},{5,6},{6,7},{7,4},{8,9},{9,10},{10,1... | collective-permute-start | bytes 786440 | tf_op jit(solution)/shard_map/ppermute | solution.py:273
  80.4 1.5 %collective-permute-done.16 = bf16[64,2048]{1,0:T(8,128)(2,1)S(1)} collective-permute-done((bf16[64,2048]{1,0:T(8,128)(2,1)S(1)}, bf16[64,2048]{1,0:T(8,128)(2,1)S(1)}, u32[]{:S(2)}, u32[]{:S(2)}) %collective-permute-start.16) | collective-permute-done | bytes 262176 | tf_op jit(solution)/shard_map/ppermute | solution.py:273
  82.0 5.8 %collective-permute-done.15 = bf16[64,2048]{1,0:T(8,128)(2,1)S(1)} collective-permute-done((bf16[64,2048]{1,0:T(8,128)(2,1)S(1)}, bf16[64,2048]{1,0:T(8,128)(2,1)S(1)}, u32[]{:S(2)}, u32[]{:S(2)}) %collective-permute-start.15) | collective-permute-done | bytes 262176 | tf_op jit(solution)/shard_map/ppermute | solution.py:273
  87.8 2.1 %convolution_convert_fusion.1 = bf16[256,1792]{1,0:T(8,128)(2,1)S(1)} fusion(bf16[256,2048]{1,0:T(8,128)(2,1)S(1)} %bitcast.61, bf16[1792,2048]{1,0:T(8,128)(2,1)S(1)} %scale_weights.1.refs_4_), kind=kOutput, calls=%fused_computation.1 | convolution fusion | flops 1879506944 | bytes 9306112 | tf_op jit(solution)/shard_map/dot_general | solution.py:353
  90.0 2.8 %collective-permute-done.18 = bf16[64,2048]{1,0:T(8,128)(2,1)S(1)} collective-permute-done((bf16[64,2048]{1,0:T(8,128)(2,1)S(1)}, bf16[64,2048]{1,0:T(8,128)(2,1)S(1)}, u32[]{:S(2)}, u32[]{:S(2)}) %collective-permute-start.18) | collective-permute-done | bytes 262176 | tf_op jit(solution)/shard_map/ppermute | solution.py:273
  92.9 2.1 %convolution_convert_fusion = bf16[256,1792]{1,0:T(8,128)(2,1)S(1)} fusion(bf16[256,2048]{1,0:T(8,128)(2,1)S(1)} %bitcast.59, bf16[1792,2048]{1,0:T(8,128)(2,1)S(1)} %scale_weights.1.refs_4_), kind=kOutput, calls=%fused_computation | convolution fusion | flops 1879506944 | bytes 9306112 | tf_op jit(solution)/shard_map/dot_general | solution.py:353
  95.2 1.6 %collective-permute-start.20 = (bf16[64,1792]{1,0:T(8,128)(2,1)S(1)}, bf16[64,1792]{1,0:T(8,128)(2,1)S(1)}, u32[]{:S(2)}, u32[]{:S(2)}) collective-permute-start(bf16[64,1792]{1,0:T(8,128)(2,1)S(1)} %get-tuple-element.50), channel_id=1, source_target_pairs={{0,24},{4,28},{8,16},{12,20},{16,8},{20,12},{24,0},{28,4},{1,25},{... | collective-permute-start | bytes 688136 | tf_op jit(solution)/shard_map/ppermute | solution.py:13
  96.8 1.4 %collective-permute-start.21 = (bf16[64,1792]{1,0:T(8,128)(2,1)S(1)}, bf16[64,1792]{1,0:T(8,128)(2,1)S(1)}, u32[]{:S(2)}, u32[]{:S(2)}) collective-permute-start(bf16[64,1792]{1,0:T(8,128)(2,1)S(1)} %get-tuple-element.53), channel_id=1, source_target_pairs={{0,16},{4,20},{8,24},{12,28},{16,0},{20,4},{24,8},{28,12},{1,17},{... | collective-permute-start | bytes 688136 | tf_op jit(solution)/shard_map/ppermute | solution.py:13
  98.8 6.6 %weight_grads.1 = (bf16[1,1792,1024]{2,1,0:T(8,128)(2,1)}, bf16[1,1792,1024]{2,1,0:T(8,128)(2,1)}) custom-call(bf16[64,1792]{1,0:T(8,128)(2,1)S(1)} %collective-permute-done.6.refs_3_.refs_0_, bf16[64,1792]{1,0:T(8,128)(2,1)S(1)} %collective-permute-done.4.refs_2_.refs_1_, bf16[64,1792]{1,0:T(8,128)(2,1)S(1)} %collective-permute-done.2.refs_1_.refs_2_, ...), custom_call_target="tpu_custom_call" | custom-call | flops 3758096384 | bytes 11272192 | tf_op jit(solution)/shard_map/weight_grads/pallas_call | solution.py:229
  105.3 2.9 %collective-permute-done.21 = bf16[64,1792]{1,0:T(8,128)(2,1)S(1)} collective-permute-done((bf16[64,1792]{1,0:T(8,128)(2,1)S(1)}, bf16[64,1792]{1,0:T(8,128)(2,1)S(1)}, u32[]{:S(2)}, u32[]{:S(2)}) %collective-permute-start.21) | collective-permute-done | bytes 229408 | tf_op jit(solution)/shard_map/ppermute | solution.py:13
  108.6 1.1 convolution_convert_fusion.2
  (52 shorter events, 7.6 us)
Async XLA Ops:
  2.8 9.4 %collective-permute-start = (bf16[64,1792]{1,0:T(8,128)(2,1)S(1)}, bf16[64,1792]{1,0:T(8,128)(2,1)S(1)}, u32[]{:S(2)}, u32[]{:S(2)}) collective-permute-start(bf16[64,1792]{1,0:T(8,128)(2,1)S(1)} %get-tuple-element.27), channel_id=1, source_target_pairs={{0,28},{4,24},{8,20},{12,16},{16,12},{20,8},{24,4},{28,0},{1,29},{... | collective-permute-start | bytes 688136 | tf_op jit(solution)/shard_map/ppermute | solution.py:13
  6.1 11.0 %collective-permute-start.2 = (bf16[64,1792]{1,0:T(8,128)(2,1)S(1)}, bf16[64,1792]{1,0:T(8,128)(2,1)S(1)}, u32[]{:S(2)}, u32[]{:S(2)}) collective-permute-start(bf16[64,1792]{1,0:T(8,128)(2,1)S(1)} %get-tuple-element.28), channel_id=1, source_target_pairs={{0,20},{4,16},{8,28},{12,24},{16,4},{20,0},{24,12},{28,8},{1,21},{... | collective-permute-start | bytes 688136 | tf_op jit(solution)/shard_map/ppermute | solution.py:13
  6.9 11.1 %collective-permute-start.4 = (bf16[64,1792]{1,0:T(8,128)(2,1)S(1)}, bf16[64,1792]{1,0:T(8,128)(2,1)S(1)}, u32[]{:S(2)}, u32[]{:S(2)}) collective-permute-start(bf16[64,1792]{1,0:T(8,128)(2,1)S(1)} %get-tuple-element.29), channel_id=1, source_target_pairs={{0,12},{4,8},{8,4},{12,0},{16,28},{20,24},{24,20},{28,16},{1,13},{... | collective-permute-start | bytes 688136 | tf_op jit(solution)/shard_map/ppermute | solution.py:13
  6.9 11.2 %collective-permute-start.6 = (bf16[64,1792]{1,0:T(8,128)(2,1)S(1)}, bf16[64,1792]{1,0:T(8,128)(2,1)S(1)}, u32[]{:S(2)}, u32[]{:S(2)}) collective-permute-start(bf16[64,1792]{1,0:T(8,128)(2,1)S(1)} %get-tuple-element.30.refs_3_.refs_4_), channel_id=1, source_target_pairs={{0,4},{4,0},{8,12},{12,8},{16,20},{20,16},{24,28},{28,24},{1,5},{5... | collective-permute-start | bytes 688136 | tf_op jit(solution)/shard_map/ppermute | solution.py:13
  6.9 0.7 copy-start
  7.6 0.7 copy-start.1
  12.1 12.1 %collective-permute-start.1 = (bf16[64,1792]{1,0:T(8,128)(2,1)S(1)}, bf16[64,1792]{1,0:T(8,128)(2,1)S(1)}, u32[]{:S(2)}, u32[]{:S(2)}) collective-permute-start(bf16[64,1792]{1,0:T(8,128)(2,1)S(1)} %collective-permute-done.refs_0_.refs_3_), channel_id=1, source_target_pairs={{0,4},{4,0},{8,12},{12,8},{16,20},{20,16},{24,28},{28,24},{1,5},{5... | collective-permute-start | bytes 688136 | tf_op jit(solution)/shard_map/ppermute | solution.py:13
  17.1 7.2 %collective-permute-start.3 = (bf16[64,1792]{1,0:T(8,128)(2,1)S(1)}, bf16[64,1792]{1,0:T(8,128)(2,1)S(1)}, u32[]{:S(2)}, u32[]{:S(2)}) collective-permute-start(bf16[64,1792]{1,0:T(8,128)(2,1)S(1)} %collective-permute-done.2.refs_1_.refs_2_), channel_id=1, source_target_pairs={{0,4},{4,0},{8,12},{12,8},{16,20},{20,16},{24,28},{28,24},{1,5},{5... | collective-permute-start | bytes 688136 | tf_op jit(solution)/shard_map/ppermute | solution.py:13
  18.0 6.3 %collective-permute-start.5 = (bf16[64,1792]{1,0:T(8,128)(2,1)S(1)}, bf16[64,1792]{1,0:T(8,128)(2,1)S(1)}, u32[]{:S(2)}, u32[]{:S(2)}) collective-permute-start(bf16[64,1792]{1,0:T(8,128)(2,1)S(1)} %collective-permute-done.4.refs_2_.refs_1_), channel_id=1, source_target_pairs={{0,4},{4,0},{8,12},{12,8},{16,20},{20,16},{24,28},{28,24},{1,5},{5... | collective-permute-start | bytes 688136 | tf_op jit(solution)/shard_map/ppermute | solution.py:13
  20.3 11.0 %collective-permute-start.8 = (bf16[64,2048]{1,0:T(8,128)(2,1)S(1)}, bf16[64,2048]{1,0:T(8,128)(2,1)S(1)}, u32[]{:S(2)}, u32[]{:S(2)}) collective-permute-start(bf16[64,2048]{1,0:T(8,128)(2,1)S(1)} %get-tuple-element.56), channel_id=1, source_target_pairs={{0,1},{1,2},{2,3},{3,0},{4,5},{5,6},{6,7},{7,4},{8,9},{9,10},{10,1... | collective-permute-start | bytes 786440 | tf_op jit(solution)/shard_map/ppermute | solution.py:273
  22.2 24.8 %collective-permute-start.11 = (bf16[64,2048]{1,0:T(8,128)(2,1)S(1)}, bf16[64,2048]{1,0:T(8,128)(2,1)S(1)}, u32[]{:S(2)}, u32[]{:S(2)}) collective-permute-start(bf16[64,2048]{1,0:T(8,128)(2,1)S(1)} %get-tuple-element.31), channel_id=1, source_target_pairs={{0,3},{1,0},{2,1},{3,2},{4,7},{5,4},{6,5},{7,6},{8,11},{9,8},{10,9... | collective-permute-start | bytes 786440 | tf_op jit(solution)/shard_map/ppermute | solution.py:273
  26.3 27.6 %copy-start.2 = (bf16[1,128,1024]{2,1,0:T(8,128)(2,1)S(1)}, bf16[1,128,1024]{2,1,0:T(8,128)(2,1)}, u32[]{:S(2)}) copy-start(bf16[1,128,1024]{2,1,0:T(8,128)(2,1)} %param.13) | copy-start | bytes 786436
  26.4 16.2 %collective-permute-start.7 = (bf16[64,2048]{1,0:T(8,128)(2,1)S(1)}, bf16[64,2048]{1,0:T(8,128)(2,1)S(1)}, u32[]{:S(2)}, u32[]{:S(2)}) collective-permute-start(bf16[64,2048]{1,0:T(8,128)(2,1)S(1)} %get-tuple-element.32), channel_id=1, source_target_pairs={{0,1},{1,2},{2,3},{3,0},{4,5},{5,6},{6,7},{7,4},{8,9},{9,10},{10,1... | collective-permute-start | bytes 786440 | tf_op jit(solution)/shard_map/ppermute | solution.py:273
  26.5 31.5 %collective-permute-start.12 = (bf16[64,2048]{1,0:T(8,128)(2,1)S(1)}, bf16[64,2048]{1,0:T(8,128)(2,1)S(1)}, u32[]{:S(2)}, u32[]{:S(2)}) collective-permute-start(bf16[64,2048]{1,0:T(8,128)(2,1)S(1)} %get-tuple-element.33), channel_id=1, source_target_pairs={{0,3},{1,0},{2,1},{3,2},{4,7},{5,4},{6,5},{7,6},{8,11},{9,8},{10,9... | collective-permute-start | bytes 786440 | tf_op jit(solution)/shard_map/ppermute | solution.py:273
  31.4 22.4 %collective-permute-start.10 = (bf16[64,2048]{1,0:T(8,128)(2,1)S(1)}, bf16[64,2048]{1,0:T(8,128)(2,1)S(1)}, u32[]{:S(2)}, u32[]{:S(2)}) collective-permute-start(bf16[64,2048]{1,0:T(8,128)(2,1)S(1)} %fusion.8), channel_id=1, source_target_pairs={{0,1},{1,2},{2,3},{3,0},{4,5},{5,6},{6,7},{7,4},{8,9},{9,10},{10,1... | collective-permute-start | bytes 786440 | tf_op jit(solution)/shard_map/ppermute | solution.py:273
  42.7 16.9 %collective-permute-start.9 = (bf16[64,2048]{1,0:T(8,128)(2,1)S(1)}, bf16[64,2048]{1,0:T(8,128)(2,1)S(1)}, u32[]{:S(2)}, u32[]{:S(2)}) collective-permute-start(bf16[64,2048]{1,0:T(8,128)(2,1)S(1)} %fusion.9), channel_id=1, source_target_pairs={{0,1},{1,2},{2,3},{3,0},{4,5},{5,6},{6,7},{7,4},{8,9},{9,10},{10,1... | collective-permute-start | bytes 786440 | tf_op jit(solution)/shard_map/ppermute | solution.py:273
  54.1 11.1 %collective-permute-start.13 = (bf16[64,2048]{1,0:T(8,128)(2,1)S(1)}, bf16[64,2048]{1,0:T(8,128)(2,1)S(1)}, u32[]{:S(2)}, u32[]{:S(2)}) collective-permute-start(bf16[64,2048]{1,0:T(8,128)(2,1)S(1)} %pad_maximum_fusion), channel_id=1, source_target_pairs={{0,1},{1,2},{2,3},{3,0},{4,5},{5,6},{6,7},{7,4},{8,9},{9,10},{10,1... | collective-permute-start | bytes 786440 | tf_op jit(solution)/shard_map/ppermute | solution.py:273
  54.2 16.8 %collective-permute-start.14 = (bf16[64,2048]{1,0:T(8,128)(2,1)S(1)}, bf16[64,2048]{1,0:T(8,128)(2,1)S(1)}, u32[]{:S(2)}, u32[]{:S(2)}) collective-permute-start(bf16[64,2048]{1,0:T(8,128)(2,1)S(1)} %pad_maximum_fusion), channel_id=1, source_target_pairs={{0,3},{1,0},{2,1},{3,2},{4,7},{5,4},{6,5},{7,6},{8,11},{9,8},{10,9... | collective-permute-start | bytes 786440 | tf_op jit(solution)/shard_map/ppermute | solution.py:273
  59.9 16.6 %collective-permute-start.17 = (bf16[64,2048]{1,0:T(8,128)(2,1)S(1)}, bf16[64,2048]{1,0:T(8,128)(2,1)S(1)}, u32[]{:S(2)}, u32[]{:S(2)}) collective-permute-start(bf16[64,2048]{1,0:T(8,128)(2,1)S(1)} %pad_maximum_fusion.1), channel_id=1, source_target_pairs={{0,1},{1,2},{2,3},{3,0},{4,5},{5,6},{6,7},{7,4},{8,9},{9,10},{10,1... | collective-permute-start | bytes 786440 | tf_op jit(solution)/shard_map/ppermute | solution.py:273
  60.0 22.0 %collective-permute-start.16 = (bf16[64,2048]{1,0:T(8,128)(2,1)S(1)}, bf16[64,2048]{1,0:T(8,128)(2,1)S(1)}, u32[]{:S(2)}, u32[]{:S(2)}) collective-permute-start(bf16[64,2048]{1,0:T(8,128)(2,1)S(1)} %pad_maximum_fusion.1), channel_id=1, source_target_pairs={{0,3},{1,0},{2,1},{3,2},{4,7},{5,4},{6,5},{7,6},{8,11},{9,8},{10,9... | collective-permute-start | bytes 786440 | tf_op jit(solution)/shard_map/ppermute | solution.py:273
  65.2 22.5 %collective-permute-start.15 = (bf16[64,2048]{1,0:T(8,128)(2,1)S(1)}, bf16[64,2048]{1,0:T(8,128)(2,1)S(1)}, u32[]{:S(2)}, u32[]{:S(2)}) collective-permute-start(bf16[64,2048]{1,0:T(8,128)(2,1)S(1)} %collective-permute-done.13), channel_id=1, source_target_pairs={{0,1},{1,2},{2,3},{3,0},{4,5},{5,6},{6,7},{7,4},{8,9},{9,10},{10,1... | collective-permute-start | bytes 786440 | tf_op jit(solution)/shard_map/ppermute | solution.py:273
  76.5 16.3 %collective-permute-start.18 = (bf16[64,2048]{1,0:T(8,128)(2,1)S(1)}, bf16[64,2048]{1,0:T(8,128)(2,1)S(1)}, u32[]{:S(2)}, u32[]{:S(2)}) collective-permute-start(bf16[64,2048]{1,0:T(8,128)(2,1)S(1)} %collective-permute-done.17), channel_id=1, source_target_pairs={{0,1},{1,2},{2,3},{3,0},{4,5},{5,6},{6,7},{7,4},{8,9},{9,10},{10,1... | collective-permute-start | bytes 786440 | tf_op jit(solution)/shard_map/ppermute | solution.py:273
  89.9 3.0 %collective-permute-start.19 = (bf16[256,1792]{1,0:T(8,128)(2,1)S(1)}, bf16[256,1792]{1,0:T(8,128)(2,1)S(1)}, u32[]{:S(2)}, u32[]{:S(2)}) collective-permute-start(bf16[256,1792]{1,0:T(8,128)(2,1)S(1)} %convolution_convert_fusion.1), channel_id=1, source_target_pairs={{0,4},{4,0},{8,12},{12,8},{16,20},{20,16},{24,28},{28,24},{1,5},{5... | collective-permute-start | bytes 2752520 | tf_op jit(solution)/shard_map/ppermute | solution.py:13
  95.2 10.2 %collective-permute-start.20 = (bf16[64,1792]{1,0:T(8,128)(2,1)S(1)}, bf16[64,1792]{1,0:T(8,128)(2,1)S(1)}, u32[]{:S(2)}, u32[]{:S(2)}) collective-permute-start(bf16[64,1792]{1,0:T(8,128)(2,1)S(1)} %get-tuple-element.50), channel_id=1, source_target_pairs={{0,24},{4,28},{8,16},{12,20},{16,8},{20,12},{24,0},{28,4},{1,25},{... | collective-permute-start | bytes 688136 | tf_op jit(solution)/shard_map/ppermute | solution.py:13
  96.8 11.5 %collective-permute-start.21 = (bf16[64,1792]{1,0:T(8,128)(2,1)S(1)}, bf16[64,1792]{1,0:T(8,128)(2,1)S(1)}, u32[]{:S(2)}, u32[]{:S(2)}) collective-permute-start(bf16[64,1792]{1,0:T(8,128)(2,1)S(1)} %get-tuple-element.53), channel_id=1, source_target_pairs={{0,16},{4,20},{8,24},{12,28},{16,0},{20,4},{24,8},{28,12},{1,17},{... | collective-permute-start | bytes 688136 | tf_op jit(solution)/shard_map/ppermute | solution.py:13
  98.2 10.4 %copy-start.3 = (bf16[256,128]{1,0:T(8,128)(2,1)S(1)}, bf16[256,128]{1,0:T(8,128)(2,1)}, u32[]{:S(2)}) copy-start(bf16[256,128]{1,0:T(8,128)(2,1)} %get-tuple-element.48) | copy-start | bytes 196612
  98.2 10.4 %collective-permute-start.22 = (bf16[64,1792]{1,0:T(8,128)(2,1)S(1)}, bf16[64,1792]{1,0:T(8,128)(2,1)S(1)}, u32[]{:S(2)}, u32[]{:S(2)}) collective-permute-start(bf16[64,1792]{1,0:T(8,128)(2,1)S(1)} %get-tuple-element.52), channel_id=1, source_target_pairs={{0,8},{4,12},{8,0},{12,4},{16,24},{20,28},{24,16},{28,20},{1,9},{5... | collective-permute-start | bytes 688136 | tf_op jit(solution)/shard_map/ppermute | solution.py:13

commit v10 on v9

--- a/solution.py
+++ b/solution.py
@@ -155,7 +155,10 @@
             transcendentals=0,
         ),
         name="pack_rows",
-    )(counts, pltpu.with_memory_space_constraint(tokens, pltpu.HBM))
+    )(
+        pltpu.with_memory_space_constraint(counts, pltpu.HBM),
+        pltpu.with_memory_space_constraint(tokens, pltpu.HBM),
+    )
     return chooser, packed
 
 

time: 110 us -> 110 us (level)
  no operation moved by 1% of the time
where the time goes in v10:
time: 110 us
  waiting for transfers between devices  42.9 us (39%)
  starting transfers between devices  41 us (37%)
  Pallas kernels  16.2 us (15%)
  matrix products  5.3 us (5%)
  local copies, waits for them, and re-layouts  1.83 us (2%)
  other arithmetic  1.69 us (2%)
    ppermute x12, waiting for transfers between devices, send(): self.came[way] = lax.ppermute(value, 'fsdp', ring)  34.2 us
    ppermute x12, starting transfers between devices, send(): self.came[way] = lax.ppermute(value, 'fsdp', ring)  32 us
    ppermute x11, starting transfers between devices, swap(): return lax.ppermute(value, axis, pairs)  8.93 us
    ppermute x11, waiting for transfers between devices, swap(): return lax.ppermute(value, axis, pairs)  8.67 us
    pallas_call x1, Pallas kernels, weight_grads(): pl.pallas_call(lambda *refs: weight_kernel(count, *refs), out_shape=(out,...  6.59 us
    dot_general x2, matrix products, back(): lax.dot_general(whole, weights, (((1,), (1,)), ((), ())), preferred_eleme...  4.21 us
    pallas_call x2, Pallas kernels, projected(): pl.pallas_call(project_kernel, out_shape=jax.ShapeDtypeStruct((count, cap...  4.19 us
    pallas_call x1, Pallas kernels, scaled_weights(): pl.pallas_call(lambda *refs: scale_kernel(sub, *refs), out_shape=jax.Shap...  3.3 us
  transfers between devices with their start and end apart: 23, of which 15 were waited for; matrix products, arithmetic and copies ran while one was open for 4% of the time, Pallas kernels for 13%

profile of v10, /device:TPU:0, one launch (start us, length us, event | category | flops | bytes accessed | tf_op | source)
XLA Modules:
  0.0 109.7 jit_solution(2861431334951041890)
XLA Ops:
  0.6 2.1 %pack_rows.1 = (bf16[256,128]{1,0:T(8,128)(2,1)}, bf16[64,1792]{1,0:T(8,128)(2,1)S(1)}, bf16[64,1792]{1,0:T(8,128)(2,1)S(1)}, bf16[64,1792]{1,0:T(8,128)(2,1)S(1)}, bf16[64,1792]{1,0:T(8,128)(2,1)S(1)}) custom-call(s32[1,4]{1,0:T(1,128)} %counts_ref.1, bf16[128,1792]{1,0:T(8,128)(2,1)} %tokens_ref.1), custom_call_target="tpu_custom_call" | custom-call | flops 117440512 | bytes 1376256 | tf_op jit(solution)/shard_map/pack_rows/pallas_call | solution.py:141
  2.8 3.3 %collective-permute-start = (bf16[64,1792]{1,0:T(8,128)(2,1)S(1)}, bf16[64,1792]{1,0:T(8,128)(2,1)S(1)}, u32[]{:S(2)}, u32[]{:S(2)}) collective-permute-start(bf16[64,1792]{1,0:T(8,128)(2,1)S(1)} %get-tuple-element.27), channel_id=1, source_target_pairs={{0,28},{4,24},{8,20},{12,16},{16,12},{20,8},{24,4},{28,0},{1,29},{... | collective-permute-start | bytes 688136 | tf_op jit(solution)/shard_map/ppermute | solution.py:13
  8.3 3.3 %scale_weights.1.refs_4_ = bf16[1792,2048]{1,0:T(8,128)(2,1)S(1)} custom-call(s32[1]{0:T(128)} %bitcast.refs_0_, bf16[1,1792,1024]{2,1,0:T(8,128)(2,1)} %refs_1_.1, bf16[1,1792,1024]{2,1,0:T(8,128)(2,1)} %refs_2_.1, f32[1,8,56]{2,1,0:T(8,128)S(1)} %bitcast.63, f32[1,8,56]{2,1,0:T(8,128)S(1)} %bitcast.64), custom_call_target="tpu_custom_call" | custom-call | flops 3670016 | bytes 14680064 | tf_op jit(solution)/shard_map/scale_weights/pallas_call | solution.py:84
  12.1 0.8 collective-permute-start.1
  12.9 4.1 %collective-permute-done.2.refs_1_.refs_2_ = bf16[64,1792]{1,0:T(8,128)(2,1)S(1)} collective-permute-done((bf16[64,1792]{1,0:T(8,128)(2,1)S(1)}, bf16[64,1792]{1,0:T(8,128)(2,1)S(1)}, u32[]{:S(2)}, u32[]{:S(2)}) %collective-permute-start.2) | collective-permute-done | bytes 229408 | tf_op jit(solution)/shard_map/ppermute | solution.py:13
  18.1 2.1 %project.3 = bf16[4,64,2048]{2,1,0:T(8,128)(2,1)S(1)} custom-call(bf16[64,1792]{1,0:T(8,128)(2,1)S(1)} %collective-permute-done.refs_0_.refs_3_, bf16[64,1792]{1,0:T(8,128)(2,1)S(1)} %collective-permute-done.2.refs_1_.refs_2_, bf16[64,1792]{1,0:T(8,128)(2,1)S(1)} %collective-permute-done.4.refs_2_.refs_1_, ...), custom_call_target="tpu_custom_call" | custom-call | flops 1879048192 | bytes 9306112 | tf_op jit(solution)/shard_map/project/pallas_call | solution.py:184
  20.3 1.9 %collective-permute-start.8 = (bf16[64,2048]{1,0:T(8,128)(2,1)S(1)}, bf16[64,2048]{1,0:T(8,128)(2,1)S(1)}, u32[]{:S(2)}, u32[]{:S(2)}) collective-permute-start(bf16[64,2048]{1,0:T(8,128)(2,1)S(1)} %get-tuple-element.56), channel_id=1, source_target_pairs={{0,1},{1,2},{2,3},{3,0},{4,5},{5,6},{6,7},{7,4},{8,9},{9,10},{10,1... | collective-permute-start | bytes 786440 | tf_op jit(solution)/shard_map/ppermute | solution.py:276
  22.2 2.1 %collective-permute-start.11 = (bf16[64,2048]{1,0:T(8,128)(2,1)S(1)}, bf16[64,2048]{1,0:T(8,128)(2,1)S(1)}, u32[]{:S(2)}, u32[]{:S(2)}) collective-permute-start(bf16[64,2048]{1,0:T(8,128)(2,1)S(1)} %get-tuple-element.31), channel_id=1, source_target_pairs={{0,3},{1,0},{2,1},{3,2},{4,7},{5,4},{6,5},{7,6},{8,11},{9,8},{10,9... | collective-permute-start | bytes 786440 | tf_op jit(solution)/shard_map/ppermute | solution.py:276
  24.3 2.1 %project.2 = bf16[4,64,2048]{2,1,0:T(8,128)(2,1)S(1)} custom-call(bf16[64,1792]{1,0:T(8,128)(2,1)S(1)} %collective-permute-done.1.refs_0_.refs_7_, bf16[64,1792]{1,0:T(8,128)(2,1)S(1)} %collective-permute-done.3.refs_1_.refs_6_, bf16[64,1792]{1,0:T(8,128)(2,1)S(1)} %collective-permute-done.5.refs_2_.refs_5_, ...), custom_call_target="tpu_custom_call" | custom-call | flops 1879048192 | bytes 9306112 | tf_op jit(solution)/shard_map/project/pallas_call | solution.py:184
  26.5 3.8 %collective-permute-start.12 = (bf16[64,2048]{1,0:T(8,128)(2,1)S(1)}, bf16[64,2048]{1,0:T(8,128)(2,1)S(1)}, u32[]{:S(2)}, u32[]{:S(2)}) collective-permute-start(bf16[64,2048]{1,0:T(8,128)(2,1)S(1)} %get-tuple-element.33), channel_id=1, source_target_pairs={{0,3},{1,0},{2,1},{3,2},{4,7},{5,4},{6,5},{7,6},{8,11},{9,8},{10,9... | collective-permute-start | bytes 786440 | tf_op jit(solution)/shard_map/ppermute | solution.py:276
  30.3 1.0 collective-permute-done.8
  31.4 4.3 %collective-permute-start.10 = (bf16[64,2048]{1,0:T(8,128)(2,1)S(1)}, bf16[64,2048]{1,0:T(8,128)(2,1)S(1)}, u32[]{:S(2)}, u32[]{:S(2)}) collective-permute-start(bf16[64,2048]{1,0:T(8,128)(2,1)S(1)} %fusion.8), channel_id=1, source_target_pairs={{0,1},{1,2},{2,3},{3,0},{4,5},{5,6},{6,7},{7,4},{8,9},{9,10},{10,1... | collective-permute-start | bytes 786440 | tf_op jit(solution)/shard_map/ppermute | solution.py:276
  35.7 6.9 %collective-permute-done.7 = bf16[64,2048]{1,0:T(8,128)(2,1)S(1)} collective-permute-done((bf16[64,2048]{1,0:T(8,128)(2,1)S(1)}, bf16[64,2048]{1,0:T(8,128)(2,1)S(1)}, u32[]{:S(2)}, u32[]{:S(2)}) %collective-permute-start.7) | collective-permute-done | bytes 262176 | tf_op jit(solution)/shard_map/ppermute | solution.py:276
  42.7 4.2 %collective-permute-start.9 = (bf16[64,2048]{1,0:T(8,128)(2,1)S(1)}, bf16[64,2048]{1,0:T(8,128)(2,1)S(1)}, u32[]{:S(2)}, u32[]{:S(2)}) collective-permute-start(bf16[64,2048]{1,0:T(8,128)(2,1)S(1)} %fusion.9), channel_id=1, source_target_pairs={{0,1},{1,2},{2,3},{3,0},{4,5},{5,6},{6,7},{7,4},{8,9},{9,10},{10,1... | collective-permute-start | bytes 786440 | tf_op jit(solution)/shard_map/ppermute | solution.py:276
  46.9 6.9 %collective-permute-done.10 = bf16[64,2048]{1,0:T(8,128)(2,1)S(1)} collective-permute-done((bf16[64,2048]{1,0:T(8,128)(2,1)S(1)}, bf16[64,2048]{1,0:T(8,128)(2,1)S(1)}, u32[]{:S(2)}, u32[]{:S(2)}) %collective-permute-start.10) | collective-permute-done | bytes 262176 | tf_op jit(solution)/shard_map/ppermute | solution.py:276
  54.2 3.8 %collective-permute-start.14 = (bf16[64,2048]{1,0:T(8,128)(2,1)S(1)}, bf16[64,2048]{1,0:T(8,128)(2,1)S(1)}, u32[]{:S(2)}, u32[]{:S(2)}) collective-permute-start(bf16[64,2048]{1,0:T(8,128)(2,1)S(1)} %pad_maximum_fusion), channel_id=1, source_target_pairs={{0,3},{1,0},{2,1},{3,2},{4,7},{5,4},{6,5},{7,6},{8,11},{9,8},{10,9... | collective-permute-start | bytes 786440 | tf_op jit(solution)/shard_map/ppermute | solution.py:276
  58.2 1.4 %collective-permute-done.9 = bf16[64,2048]{1,0:T(8,128)(2,1)S(1)} collective-permute-done((bf16[64,2048]{1,0:T(8,128)(2,1)S(1)}, bf16[64,2048]{1,0:T(8,128)(2,1)S(1)}, u32[]{:S(2)}, u32[]{:S(2)}) %collective-permute-start.9) | collective-permute-done | bytes 262176 | tf_op jit(solution)/shard_map/ppermute | solution.py:276
  60.0 3.8 %collective-permute-start.16 = (bf16[64,2048]{1,0:T(8,128)(2,1)S(1)}, bf16[64,2048]{1,0:T(8,128)(2,1)S(1)}, u32[]{:S(2)}, u32[]{:S(2)}) collective-permute-start(bf16[64,2048]{1,0:T(8,128)(2,1)S(1)} %pad_maximum_fusion.1), channel_id=1, source_target_pairs={{0,3},{1,0},{2,1},{3,2},{4,7},{5,4},{6,5},{7,6},{8,11},{9,8},{10,9... | collective-permute-start | bytes 786440 | tf_op jit(solution)/shard_map/ppermute | solution.py:276
  65.2 4.0 %collective-permute-start.15 = (bf16[64,2048]{1,0:T(8,128)(2,1)S(1)}, bf16[64,2048]{1,0:T(8,128)(2,1)S(1)}, u32[]{:S(2)}, u32[]{:S(2)}) collective-permute-start(bf16[64,2048]{1,0:T(8,128)(2,1)S(1)} %collective-permute-done.13), channel_id=1, source_target_pairs={{0,1},{1,2},{2,3},{3,0},{4,5},{5,6},{6,7},{7,4},{8,9},{9,10},{10,1... | collective-permute-start | bytes 786440 | tf_op jit(solution)/shard_map/ppermute | solution.py:276
  69.2 1.8 %collective-permute-done.14 = bf16[64,2048]{1,0:T(8,128)(2,1)S(1)} collective-permute-done((bf16[64,2048]{1,0:T(8,128)(2,1)S(1)}, bf16[64,2048]{1,0:T(8,128)(2,1)S(1)}, u32[]{:S(2)}, u32[]{:S(2)}) %collective-permute-start.14) | collective-permute-done | bytes 262176 | tf_op jit(solution)/shard_map/ppermute | solution.py:276
  71.1 5.4 %collective-permute-done.17 = bf16[64,2048]{1,0:T(8,128)(2,1)S(1)} collective-permute-done((bf16[64,2048]{1,0:T(8,128)(2,1)S(1)}, bf16[64,2048]{1,0:T(8,128)(2,1)S(1)}, u32[]{:S(2)}, u32[]{:S(2)}) %collective-permute-start.17) | collective-permute-done | bytes 262176 | tf_op jit(solution)/shard_map/ppermute | solution.py:276
  76.5 3.9 %collective-permute-start.18 = (bf16[64,2048]{1,0:T(8,128)(2,1)S(1)}, bf16[64,2048]{1,0:T(8,128)(2,1)S(1)}, u32[]{:S(2)}, u32[]{:S(2)}) collective-permute-start(bf16[64,2048]{1,0:T(8,128)(2,1)S(1)} %collective-permute-done.17), channel_id=1, source_target_pairs={{0,1},{1,2},{2,3},{3,0},{4,5},{5,6},{6,7},{7,4},{8,9},{9,10},{10,1... | collective-permute-start | bytes 786440 | tf_op jit(solution)/shard_map/ppermute | solution.py:276
  80.4 1.5 %collective-permute-done.16 = bf16[64,2048]{1,0:T(8,128)(2,1)S(1)} collective-permute-done((bf16[64,2048]{1,0:T(8,128)(2,1)S(1)}, bf16[64,2048]{1,0:T(8,128)(2,1)S(1)}, u32[]{:S(2)}, u32[]{:S(2)}) %collective-permute-start.16) | collective-permute-done | bytes 262176 | tf_op jit(solution)/shard_map/ppermute | solution.py:276
  82.0 5.8 %collective-permute-done.15 = bf16[64,2048]{1,0:T(8,128)(2,1)S(1)} collective-permute-done((bf16[64,2048]{1,0:T(8,128)(2,1)S(1)}, bf16[64,2048]{1,0:T(8,128)(2,1)S(1)}, u32[]{:S(2)}, u32[]{:S(2)}) %collective-permute-start.15) | collective-permute-done | bytes 262176 | tf_op jit(solution)/shard_map/ppermute | solution.py:276
  87.8 2.1 %convolution_convert_fusion.1 = bf16[256,1792]{1,0:T(8,128)(2,1)S(1)} fusion(bf16[256,2048]{1,0:T(8,128)(2,1)S(1)} %bitcast.61, bf16[1792,2048]{1,0:T(8,128)(2,1)S(1)} %scale_weights.1.refs_4_), kind=kOutput, calls=%fused_computation.1 | convolution fusion | flops 1879506944 | bytes 9306112 | tf_op jit(solution)/shard_map/dot_general | solution.py:356
  90.0 2.8 %collective-permute-done.18 = bf16[64,2048]{1,0:T(8,128)(2,1)S(1)} collective-permute-done((bf16[64,2048]{1,0:T(8,128)(2,1)S(1)}, bf16[64,2048]{1,0:T(8,128)(2,1)S(1)}, u32[]{:S(2)}, u32[]{:S(2)}) %collective-permute-start.18) | collective-permute-done | bytes 262176 | tf_op jit(solution)/shard_map/ppermute | solution.py:276
  92.9 2.1 %convolution_convert_fusion = bf16[256,1792]{1,0:T(8,128)(2,1)S(1)} fusion(bf16[256,2048]{1,0:T(8,128)(2,1)S(1)} %bitcast.59, bf16[1792,2048]{1,0:T(8,128)(2,1)S(1)} %scale_weights.1.refs_4_), kind=kOutput, calls=%fused_computation | convolution fusion | flops 1879506944 | bytes 9306112 | tf_op jit(solution)/shard_map/dot_general | solution.py:356
  95.2 1.6 %collective-permute-start.20 = (bf16[64,1792]{1,0:T(8,128)(2,1)S(1)}, bf16[64,1792]{1,0:T(8,128)(2,1)S(1)}, u32[]{:S(2)}, u32[]{:S(2)}) collective-permute-start(bf16[64,1792]{1,0:T(8,128)(2,1)S(1)} %get-tuple-element.50), channel_id=1, source_target_pairs={{0,24},{4,28},{8,16},{12,20},{16,8},{20,12},{24,0},{28,4},{1,25},{... | collective-permute-start | bytes 688136 | tf_op jit(solution)/shard_map/ppermute | solution.py:13
  96.8 1.4 %collective-permute-start.21 = (bf16[64,1792]{1,0:T(8,128)(2,1)S(1)}, bf16[64,1792]{1,0:T(8,128)(2,1)S(1)}, u32[]{:S(2)}, u32[]{:S(2)}) collective-permute-start(bf16[64,1792]{1,0:T(8,128)(2,1)S(1)} %get-tuple-element.53), channel_id=1, source_target_pairs={{0,16},{4,20},{8,24},{12,28},{16,0},{20,4},{24,8},{28,12},{1,17},{... | collective-permute-start | bytes 688136 | tf_op jit(solution)/shard_map/ppermute | solution.py:13
  98.8 6.6 %weight_grads.1 = (bf16[1,1792,1024]{2,1,0:T(8,128)(2,1)}, bf16[1,1792,1024]{2,1,0:T(8,128)(2,1)}) custom-call(bf16[64,1792]{1,0:T(8,128)(2,1)S(1)} %collective-permute-done.6.refs_3_.refs_0_, bf16[64,1792]{1,0:T(8,128)(2,1)S(1)} %collective-permute-done.4.refs_2_.refs_1_, bf16[64,1792]{1,0:T(8,128)(2,1)S(1)} %collective-permute-done.2.refs_1_.refs_2_, ...), custom_call_target="tpu_custom_call" | custom-call | flops 3758096384 | bytes 11272192 | tf_op jit(solution)/shard_map/weight_grads/pallas_call | solution.py:232
  105.3 2.9 %collective-permute-done.21 = bf16[64,1792]{1,0:T(8,128)(2,1)S(1)} collective-permute-done((bf16[64,1792]{1,0:T(8,128)(2,1)S(1)}, bf16[64,1792]{1,0:T(8,128)(2,1)S(1)}, u32[]{:S(2)}, u32[]{:S(2)}) %collective-permute-start.21) | collective-permute-done | bytes 229408 | tf_op jit(solution)/shard_map/ppermute | solution.py:13
  108.6 1.1 convolution_convert_fusion.2
  (52 shorter events, 7.6 us)
Async XLA Ops:
  2.8 9.4 %collective-permute-start = (bf16[64,1792]{1,0:T(8,128)(2,1)S(1)}, bf16[64,1792]{1,0:T(8,128)(2,1)S(1)}, u32[]{:S(2)}, u32[]{:S(2)}) collective-permute-start(bf16[64,1792]{1,0:T(8,128)(2,1)S(1)} %get-tuple-element.27), channel_id=1, source_target_pairs={{0,28},{4,24},{8,20},{12,16},{16,12},{20,8},{24,4},{28,0},{1,29},{... | collective-permute-start | bytes 688136 | tf_op jit(solution)/shard_map/ppermute | solution.py:13
  6.1 11.0 %collective-permute-start.2 = (bf16[64,1792]{1,0:T(8,128)(2,1)S(1)}, bf16[64,1792]{1,0:T(8,128)(2,1)S(1)}, u32[]{:S(2)}, u32[]{:S(2)}) collective-permute-start(bf16[64,1792]{1,0:T(8,128)(2,1)S(1)} %get-tuple-element.28), channel_id=1, source_target_pairs={{0,20},{4,16},{8,28},{12,24},{16,4},{20,0},{24,12},{28,8},{1,21},{... | collective-permute-start | bytes 688136 | tf_op jit(solution)/shard_map/ppermute | solution.py:13
  6.9 11.1 %collective-permute-start.4 = (bf16[64,1792]{1,0:T(8,128)(2,1)S(1)}, bf16[64,1792]{1,0:T(8,128)(2,1)S(1)}, u32[]{:S(2)}, u32[]{:S(2)}) collective-permute-start(bf16[64,1792]{1,0:T(8,128)(2,1)S(1)} %get-tuple-element.29), channel_id=1, source_target_pairs={{0,12},{4,8},{8,4},{12,0},{16,28},{20,24},{24,20},{28,16},{1,13},{... | collective-permute-start | bytes 688136 | tf_op jit(solution)/shard_map/ppermute | solution.py:13
  6.9 11.2 %collective-permute-start.6 = (bf16[64,1792]{1,0:T(8,128)(2,1)S(1)}, bf16[64,1792]{1,0:T(8,128)(2,1)S(1)}, u32[]{:S(2)}, u32[]{:S(2)}) collective-permute-start(bf16[64,1792]{1,0:T(8,128)(2,1)S(1)} %get-tuple-element.30.refs_3_.refs_4_), channel_id=1, source_target_pairs={{0,4},{4,0},{8,12},{12,8},{16,20},{20,16},{24,28},{28,24},{1,5},{5... | collective-permute-start | bytes 688136 | tf_op jit(solution)/shard_map/ppermute | solution.py:13
  6.9 0.7 copy-start
  7.6 0.7 copy-start.1
  12.1 12.1 %collective-permute-start.1 = (bf16[64,1792]{1,0:T(8,128)(2,1)S(1)}, bf16[64,1792]{1,0:T(8,128)(2,1)S(1)}, u32[]{:S(2)}, u32[]{:S(2)}) collective-permute-start(bf16[64,1792]{1,0:T(8,128)(2,1)S(1)} %collective-permute-done.refs_0_.refs_3_), channel_id=1, source_target_pairs={{0,4},{4,0},{8,12},{12,8},{16,20},{20,16},{24,28},{28,24},{1,5},{5... | collective-permute-start | bytes 688136 | tf_op jit(solution)/shard_map/ppermute | solution.py:13
  17.1 7.2 %collective-permute-start.3 = (bf16[64,1792]{1,0:T(8,128)(2,1)S(1)}, bf16[64,1792]{1,0:T(8,128)(2,1)S(1)}, u32[]{:S(2)}, u32[]{:S(2)}) collective-permute-start(bf16[64,1792]{1,0:T(8,128)(2,1)S(1)} %collective-permute-done.2.refs_1_.refs_2_), channel_id=1, source_target_pairs={{0,4},{4,0},{8,12},{12,8},{16,20},{20,16},{24,28},{28,24},{1,5},{5... | collective-permute-start | bytes 688136 | tf_op jit(solution)/shard_map/ppermute | solution.py:13
  18.0 6.3 %collective-permute-start.5 = (bf16[64,1792]{1,0:T(8,128)(2,1)S(1)}, bf16[64,1792]{1,0:T(8,128)(2,1)S(1)}, u32[]{:S(2)}, u32[]{:S(2)}) collective-permute-start(bf16[64,1792]{1,0:T(8,128)(2,1)S(1)} %collective-permute-done.4.refs_2_.refs_1_), channel_id=1, source_target_pairs={{0,4},{4,0},{8,12},{12,8},{16,20},{20,16},{24,28},{28,24},{1,5},{5... | collective-permute-start | bytes 688136 | tf_op jit(solution)/shard_map/ppermute | solution.py:13
  20.3 11.0 %collective-permute-start.8 = (bf16[64,2048]{1,0:T(8,128)(2,1)S(1)}, bf16[64,2048]{1,0:T(8,128)(2,1)S(1)}, u32[]{:S(2)}, u32[]{:S(2)}) collective-permute-start(bf16[64,2048]{1,0:T(8,128)(2,1)S(1)} %get-tuple-element.56), channel_id=1, source_target_pairs={{0,1},{1,2},{2,3},{3,0},{4,5},{5,6},{6,7},{7,4},{8,9},{9,10},{10,1... | collective-permute-start | bytes 786440 | tf_op jit(solution)/shard_map/ppermute | solution.py:276
  22.2 24.8 %collective-permute-start.11 = (bf16[64,2048]{1,0:T(8,128)(2,1)S(1)}, bf16[64,2048]{1,0:T(8,128)(2,1)S(1)}, u32[]{:S(2)}, u32[]{:S(2)}) collective-permute-start(bf16[64,2048]{1,0:T(8,128)(2,1)S(1)} %get-tuple-element.31), channel_id=1, source_target_pairs={{0,3},{1,0},{2,1},{3,2},{4,7},{5,4},{6,5},{7,6},{8,11},{9,8},{10,9... | collective-permute-start | bytes 786440 | tf_op jit(solution)/shard_map/ppermute | solution.py:276
  26.3 27.6 %copy-start.2 = (bf16[1,128,1024]{2,1,0:T(8,128)(2,1)S(1)}, bf16[1,128,1024]{2,1,0:T(8,128)(2,1)}, u32[]{:S(2)}) copy-start(bf16[1,128,1024]{2,1,0:T(8,128)(2,1)} %param.13) | copy-start | bytes 786436
  26.4 16.2 %collective-permute-start.7 = (bf16[64,2048]{1,0:T(8,128)(2,1)S(1)}, bf16[64,2048]{1,0:T(8,128)(2,1)S(1)}, u32[]{:S(2)}, u32[]{:S(2)}) collective-permute-start(bf16[64,2048]{1,0:T(8,128)(2,1)S(1)} %get-tuple-element.32), channel_id=1, source_target_pairs={{0,1},{1,2},{2,3},{3,0},{4,5},{5,6},{6,7},{7,4},{8,9},{9,10},{10,1... | collective-permute-start | bytes 786440 | tf_op jit(solution)/shard_map/ppermute | solution.py:276
  26.5 31.5 %collective-permute-start.12 = (bf16[64,2048]{1,0:T(8,128)(2,1)S(1)}, bf16[64,2048]{1,0:T(8,128)(2,1)S(1)}, u32[]{:S(2)}, u32[]{:S(2)}) collective-permute-start(bf16[64,2048]{1,0:T(8,128)(2,1)S(1)} %get-tuple-element.33), channel_id=1, source_target_pairs={{0,3},{1,0},{2,1},{3,2},{4,7},{5,4},{6,5},{7,6},{8,11},{9,8},{10,9... | collective-permute-start | bytes 786440 | tf_op jit(solution)/shard_map/ppermute | solution.py:276
  31.4 22.4 %collective-permute-start.10 = (bf16[64,2048]{1,0:T(8,128)(2,1)S(1)}, bf16[64,2048]{1,0:T(8,128)(2,1)S(1)}, u32[]{:S(2)}, u32[]{:S(2)}) collective-permute-start(bf16[64,2048]{1,0:T(8,128)(2,1)S(1)} %fusion.8), channel_id=1, source_target_pairs={{0,1},{1,2},{2,3},{3,0},{4,5},{5,6},{6,7},{7,4},{8,9},{9,10},{10,1... | collective-permute-start | bytes 786440 | tf_op jit(solution)/shard_map/ppermute | solution.py:276
  42.7 16.9 %collective-permute-start.9 = (bf16[64,2048]{1,0:T(8,128)(2,1)S(1)}, bf16[64,2048]{1,0:T(8,128)(2,1)S(1)}, u32[]{:S(2)}, u32[]{:S(2)}) collective-permute-start(bf16[64,2048]{1,0:T(8,128)(2,1)S(1)} %fusion.9), channel_id=1, source_target_pairs={{0,1},{1,2},{2,3},{3,0},{4,5},{5,6},{6,7},{7,4},{8,9},{9,10},{10,1... | collective-permute-start | bytes 786440 | tf_op jit(solution)/shard_map/ppermute | solution.py:276
  54.1 11.1 %collective-permute-start.13 = (bf16[64,2048]{1,0:T(8,128)(2,1)S(1)}, bf16[64,2048]{1,0:T(8,128)(2,1)S(1)}, u32[]{:S(2)}, u32[]{:S(2)}) collective-permute-start(bf16[64,2048]{1,0:T(8,128)(2,1)S(1)} %pad_maximum_fusion), channel_id=1, source_target_pairs={{0,1},{1,2},{2,3},{3,0},{4,5},{5,6},{6,7},{7,4},{8,9},{9,10},{10,1... | collective-permute-start | bytes 786440 | tf_op jit(solution)/shard_map/ppermute | solution.py:276
  54.2 16.8 %collective-permute-start.14 = (bf16[64,2048]{1,0:T(8,128)(2,1)S(1)}, bf16[64,2048]{1,0:T(8,128)(2,1)S(1)}, u32[]{:S(2)}, u32[]{:S(2)}) collective-permute-start(bf16[64,2048]{1,0:T(8,128)(2,1)S(1)} %pad_maximum_fusion), channel_id=1, source_target_pairs={{0,3},{1,0},{2,1},{3,2},{4,7},{5,4},{6,5},{7,6},{8,11},{9,8},{10,9... | collective-permute-start | bytes 786440 | tf_op jit(solution)/shard_map/ppermute | solution.py:276
  59.9 16.6 %collective-permute-start.17 = (bf16[64,2048]{1,0:T(8,128)(2,1)S(1)}, bf16[64,2048]{1,0:T(8,128)(2,1)S(1)}, u32[]{:S(2)}, u32[]{:S(2)}) collective-permute-start(bf16[64,2048]{1,0:T(8,128)(2,1)S(1)} %pad_maximum_fusion.1), channel_id=1, source_target_pairs={{0,1},{1,2},{2,3},{3,0},{4,5},{5,6},{6,7},{7,4},{8,9},{9,10},{10,1... | collective-permute-start | bytes 786440 | tf_op jit(solution)/shard_map/ppermute | solution.py:276
  60.0 22.0 %collective-permute-start.16 = (bf16[64,2048]{1,0:T(8,128)(2,1)S(1)}, bf16[64,2048]{1,0:T(8,128)(2,1)S(1)}, u32[]{:S(2)}, u32[]{:S(2)}) collective-permute-start(bf16[64,2048]{1,0:T(8,128)(2,1)S(1)} %pad_maximum_fusion.1), channel_id=1, source_target_pairs={{0,3},{1,0},{2,1},{3,2},{4,7},{5,4},{6,5},{7,6},{8,11},{9,8},{10,9... | collective-permute-start | bytes 786440 | tf_op jit(solution)/shard_map/ppermute | solution.py:276
  65.2 22.5 %collective-permute-start.15 = (bf16[64,2048]{1,0:T(8,128)(2,1)S(1)}, bf16[64,2048]{1,0:T(8,128)(2,1)S(1)}, u32[]{:S(2)}, u32[]{:S(2)}) collective-permute-start(bf16[64,2048]{1,0:T(8,128)(2,1)S(1)} %collective-permute-done.13), channel_id=1, source_target_pairs={{0,1},{1,2},{2,3},{3,0},{4,5},{5,6},{6,7},{7,4},{8,9},{9,10},{10,1... | collective-permute-start | bytes 786440 | tf_op jit(solution)/shard_map/ppermute | solution.py:276
  76.5 16.3 %collective-permute-start.18 = (bf16[64,2048]{1,0:T(8,128)(2,1)S(1)}, bf16[64,2048]{1,0:T(8,128)(2,1)S(1)}, u32[]{:S(2)}, u32[]{:S(2)}) collective-permute-start(bf16[64,2048]{1,0:T(8,128)(2,1)S(1)} %collective-permute-done.17), channel_id=1, source_target_pairs={{0,1},{1,2},{2,3},{3,0},{4,5},{5,6},{6,7},{7,4},{8,9},{9,10},{10,1... | collective-permute-start | bytes 786440 | tf_op jit(solution)/shard_map/ppermute | solution.py:276
  89.9 3.0 %collective-permute-start.19 = (bf16[256,1792]{1,0:T(8,128)(2,1)S(1)}, bf16[256,1792]{1,0:T(8,128)(2,1)S(1)}, u32[]{:S(2)}, u32[]{:S(2)}) collective-permute-start(bf16[256,1792]{1,0:T(8,128)(2,1)S(1)} %convolution_convert_fusion.1), channel_id=1, source_target_pairs={{0,4},{4,0},{8,12},{12,8},{16,20},{20,16},{24,28},{28,24},{1,5},{5... | collective-permute-start | bytes 2752520 | tf_op jit(solution)/shard_map/ppermute | solution.py:13
  95.2 10.2 %collective-permute-start.20 = (bf16[64,1792]{1,0:T(8,128)(2,1)S(1)}, bf16[64,1792]{1,0:T(8,128)(2,1)S(1)}, u32[]{:S(2)}, u32[]{:S(2)}) collective-permute-start(bf16[64,1792]{1,0:T(8,128)(2,1)S(1)} %get-tuple-element.50), channel_id=1, source_target_pairs={{0,24},{4,28},{8,16},{12,20},{16,8},{20,12},{24,0},{28,4},{1,25},{... | collective-permute-start | bytes 688136 | tf_op jit(solution)/shard_map/ppermute | solution.py:13
  96.8 11.5 %collective-permute-start.21 = (bf16[64,1792]{1,0:T(8,128)(2,1)S(1)}, bf16[64,1792]{1,0:T(8,128)(2,1)S(1)}, u32[]{:S(2)}, u32[]{:S(2)}) collective-permute-start(bf16[64,1792]{1,0:T(8,128)(2,1)S(1)} %get-tuple-element.53), channel_id=1, source_target_pairs={{0,16},{4,20},{8,24},{12,28},{16,0},{20,4},{24,8},{28,12},{1,17},{... | collective-permute-start | bytes 688136 | tf_op jit(solution)/shard_map/ppermute | solution.py:13
  98.2 10.4 %copy-start.3 = (bf16[256,128]{1,0:T(8,128)(2,1)S(1)}, bf16[256,128]{1,0:T(8,128)(2,1)}, u32[]{:S(2)}) copy-start(bf16[256,128]{1,0:T(8,128)(2,1)} %get-tuple-element.48) | copy-start | bytes 196612
  98.2 10.4 %collective-permute-start.22 = (bf16[64,1792]{1,0:T(8,128)(2,1)S(1)}, bf16[64,1792]{1,0:T(8,128)(2,1)S(1)}, u32[]{:S(2)}, u32[]{:S(2)}) collective-permute-start(bf16[64,1792]{1,0:T(8,128)(2,1)S(1)} %get-tuple-element.52), channel_id=1, source_target_pairs={{0,8},{4,12},{8,0},{12,4},{16,24},{20,28},{24,16},{28,20},{1,9},{5... | collective-permute-start | bytes 688136 | tf_op jit(solution)/shard_map/ppermute | solution.py:13

commit v11 on v9

--- a/solution.py
+++ b/solution.py
@@ -371,8 +371,8 @@
     for group in range(2):
         activate(group)
     for step in steps:
-        for group in range(2):
-            for way, reach in chains[group].reach.items():
+        for way, reach in chains[0].reach.items():
+            for group in range(2):
                 if step <= reach:
                     gather(group, way, step)
     wholes = [chain.whole.reshape(chips * capacity, 2 * half_units) for chain in chains]

time: 110 us -> 110 us (level)
  transfers between devices with their start and end apart: 23 -> 23, of which waited for: 15 -> 14; matrix products, arithmetic and copies ran while one was open for 4% -> 4% of each run, Pallas kernels for 13% -> 13%
where the time goes in v11:
time: 110 us
  waiting for transfers between devices  42.9 us (39%)
  starting transfers between devices  41 us (37%)
  Pallas kernels  16.2 us (15%)
  matrix products  5.3 us (5%)
  local copies, waits for them, and re-layouts  1.83 us (2%)
  other arithmetic  1.69 us (2%)
    ppermute x12, waiting for transfers between devices, send(): self.came[way] = lax.ppermute(value, 'fsdp', ring)  34.2 us
    ppermute x12, starting transfers between devices, send(): self.came[way] = lax.ppermute(value, 'fsdp', ring)  32 us
    ppermute x11, starting transfers between devices, swap(): return lax.ppermute(value, axis, pairs)  8.93 us
    ppermute x11, waiting for transfers between devices, swap(): return lax.ppermute(value, axis, pairs)  8.67 us
    pallas_call x1, Pallas kernels, weight_grads(): pl.pallas_call(lambda *refs: weight_kernel(count, *refs), out_shape=(out,...  6.59 us
    dot_general x2, matrix products, back(): lax.dot_general(whole, weights, (((1,), (1,)), ((), ())), preferred_eleme...  4.21 us
    pallas_call x2, Pallas kernels, projected(): pl.pallas_call(project_kernel, out_shape=jax.ShapeDtypeStruct((count, cap...  4.19 us
    pallas_call x1, Pallas kernels, scaled_weights(): pl.pallas_call(lambda *refs: scale_kernel(sub, *refs), out_shape=jax.Shap...  3.3 us
  transfers between devices with their start and end apart: 23, of which 14 were waited for; matrix products, arithmetic and copies ran while one was open for 4% of the time, Pallas kernels for 13%

profile of v11, /device:TPU:0, one launch (start us, length us, event | category | flops | bytes accessed | tf_op | source)
XLA Modules:
  0.0 109.7 jit_solution(1090781090547512433)
XLA Ops:
  0.6 2.1 %pack_rows.1 = (bf16[256,128]{1,0:T(8,128)(2,1)}, bf16[64,1792]{1,0:T(8,128)(2,1)S(1)}, bf16[64,1792]{1,0:T(8,128)(2,1)S(1)}, bf16[64,1792]{1,0:T(8,128)(2,1)S(1)}, bf16[64,1792]{1,0:T(8,128)(2,1)S(1)}) custom-call(s32[1,4]{1,0:T(1,128)} %counts_ref.1, bf16[128,1792]{1,0:T(8,128)(2,1)} %tokens_ref.1), custom_call_target="tpu_custom_call" | custom-call | flops 117440512 | bytes 1376256 | tf_op jit(solution)/shard_map/pack_rows/pallas_call | solution.py:141
  2.8 3.3 %collective-permute-start = (bf16[64,1792]{1,0:T(8,128)(2,1)S(1)}, bf16[64,1792]{1,0:T(8,128)(2,1)S(1)}, u32[]{:S(2)}, u32[]{:S(2)}) collective-permute-start(bf16[64,1792]{1,0:T(8,128)(2,1)S(1)} %get-tuple-element.27), channel_id=1, source_target_pairs={{0,28},{4,24},{8,20},{12,16},{16,12},{20,8},{24,4},{28,0},{1,29},{... | collective-permute-start | bytes 688136 | tf_op jit(solution)/shard_map/ppermute | solution.py:13
  6.1 0.8 collective-permute-start.2
  8.3 3.3 %scale_weights.1.refs_4_ = bf16[1792,2048]{1,0:T(8,128)(2,1)S(1)} custom-call(s32[1]{0:T(128)} %bitcast.refs_0_, bf16[1,1792,1024]{2,1,0:T(8,128)(2,1)} %refs_1_.1, bf16[1,1792,1024]{2,1,0:T(8,128)(2,1)} %refs_2_.1, f32[1,8,56]{2,1,0:T(8,128)S(1)} %bitcast.63, f32[1,8,56]{2,1,0:T(8,128)S(1)} %bitcast.64), custom_call_target="tpu_custom_call" | custom-call | flops 3670016 | bytes 14680064 | tf_op jit(solution)/shard_map/scale_weights/pallas_call | solution.py:84
  12.1 0.8 collective-permute-start.1
  12.9 4.1 %collective-permute-done.2.refs_1_.refs_2_ = bf16[64,1792]{1,0:T(8,128)(2,1)S(1)} collective-permute-done((bf16[64,1792]{1,0:T(8,128)(2,1)S(1)}, bf16[64,1792]{1,0:T(8,128)(2,1)S(1)}, u32[]{:S(2)}, u32[]{:S(2)}) %collective-permute-start.2) | collective-permute-done | bytes 229408 | tf_op jit(solution)/shard_map/ppermute | solution.py:13
  18.1 2.1 %project.3 = bf16[4,64,2048]{2,1,0:T(8,128)(2,1)S(1)} custom-call(bf16[64,1792]{1,0:T(8,128)(2,1)S(1)} %collective-permute-done.refs_0_.refs_3_, bf16[64,1792]{1,0:T(8,128)(2,1)S(1)} %collective-permute-done.2.refs_1_.refs_2_, bf16[64,1792]{1,0:T(8,128)(2,1)S(1)} %collective-permute-done.4.refs_2_.refs_1_, ...), custom_call_target="tpu_custom_call" | custom-call | flops 1879048192 | bytes 9306112 | tf_op jit(solution)/shard_map/project/pallas_call | solution.py:181
  20.3 1.9 %collective-permute-start.8 = (bf16[64,2048]{1,0:T(8,128)(2,1)S(1)}, bf16[64,2048]{1,0:T(8,128)(2,1)S(1)}, u32[]{:S(2)}, u32[]{:S(2)}) collective-permute-start(bf16[64,2048]{1,0:T(8,128)(2,1)S(1)} %get-tuple-element.56), channel_id=1, source_target_pairs={{0,1},{1,2},{2,3},{3,0},{4,5},{5,6},{6,7},{7,4},{8,9},{9,10},{10,1... | collective-permute-start | bytes 786440 | tf_op jit(solution)/shard_map/ppermute | solution.py:273
  22.2 2.1 %collective-permute-start.11 = (bf16[64,2048]{1,0:T(8,128)(2,1)S(1)}, bf16[64,2048]{1,0:T(8,128)(2,1)S(1)}, u32[]{:S(2)}, u32[]{:S(2)}) collective-permute-start(bf16[64,2048]{1,0:T(8,128)(2,1)S(1)} %get-tuple-element.31), channel_id=1, source_target_pairs={{0,3},{1,0},{2,1},{3,2},{4,7},{5,4},{6,5},{7,6},{8,11},{9,8},{10,9... | collective-permute-start | bytes 786440 | tf_op jit(solution)/shard_map/ppermute | solution.py:273
  24.3 2.1 %project.2 = bf16[4,64,2048]{2,1,0:T(8,128)(2,1)S(1)} custom-call(bf16[64,1792]{1,0:T(8,128)(2,1)S(1)} %collective-permute-done.1.refs_0_.refs_7_, bf16[64,1792]{1,0:T(8,128)(2,1)S(1)} %collective-permute-done.3.refs_1_.refs_6_, bf16[64,1792]{1,0:T(8,128)(2,1)S(1)} %collective-permute-done.5.refs_2_.refs_5_, ...), custom_call_target="tpu_custom_call" | custom-call | flops 1879048192 | bytes 9306112 | tf_op jit(solution)/shard_map/project/pallas_call | solution.py:181
  26.5 3.8 %collective-permute-start.12 = (bf16[64,2048]{1,0:T(8,128)(2,1)S(1)}, bf16[64,2048]{1,0:T(8,128)(2,1)S(1)}, u32[]{:S(2)}, u32[]{:S(2)}) collective-permute-start(bf16[64,2048]{1,0:T(8,128)(2,1)S(1)} %get-tuple-element.33), channel_id=1, source_target_pairs={{0,3},{1,0},{2,1},{3,2},{4,7},{5,4},{6,5},{7,6},{8,11},{9,8},{10,9... | collective-permute-start | bytes 786440 | tf_op jit(solution)/shard_map/ppermute | solution.py:273
  30.3 1.0 collective-permute-done.8
  31.4 4.3 %collective-permute-start.10 = (bf16[64,2048]{1,0:T(8,128)(2,1)S(1)}, bf16[64,2048]{1,0:T(8,128)(2,1)S(1)}, u32[]{:S(2)}, u32[]{:S(2)}) collective-permute-start(bf16[64,2048]{1,0:T(8,128)(2,1)S(1)} %fusion.8), channel_id=1, source_target_pairs={{0,1},{1,2},{2,3},{3,0},{4,5},{5,6},{6,7},{7,4},{8,9},{9,10},{10,1... | collective-permute-start | bytes 786440 | tf_op jit(solution)/shard_map/ppermute | solution.py:273
  35.7 6.9 %collective-permute-done.7 = bf16[64,2048]{1,0:T(8,128)(2,1)S(1)} collective-permute-done((bf16[64,2048]{1,0:T(8,128)(2,1)S(1)}, bf16[64,2048]{1,0:T(8,128)(2,1)S(1)}, u32[]{:S(2)}, u32[]{:S(2)}) %collective-permute-start.7) | collective-permute-done | bytes 262176 | tf_op jit(solution)/shard_map/ppermute | solution.py:273
  42.7 4.2 %collective-permute-start.9 = (bf16[64,2048]{1,0:T(8,128)(2,1)S(1)}, bf16[64,2048]{1,0:T(8,128)(2,1)S(1)}, u32[]{:S(2)}, u32[]{:S(2)}) collective-permute-start(bf16[64,2048]{1,0:T(8,128)(2,1)S(1)} %fusion.9), channel_id=1, source_target_pairs={{0,1},{1,2},{2,3},{3,0},{4,5},{5,6},{6,7},{7,4},{8,9},{9,10},{10,1... | collective-permute-start | bytes 786440 | tf_op jit(solution)/shard_map/ppermute | solution.py:273
  46.9 6.9 %collective-permute-done.10 = bf16[64,2048]{1,0:T(8,128)(2,1)S(1)} collective-permute-done((bf16[64,2048]{1,0:T(8,128)(2,1)S(1)}, bf16[64,2048]{1,0:T(8,128)(2,1)S(1)}, u32[]{:S(2)}, u32[]{:S(2)}) %collective-permute-start.10) | collective-permute-done | bytes 262176 | tf_op jit(solution)/shard_map/ppermute | solution.py:273
  54.2 3.8 %collective-permute-start.14 = (bf16[64,2048]{1,0:T(8,128)(2,1)S(1)}, bf16[64,2048]{1,0:T(8,128)(2,1)S(1)}, u32[]{:S(2)}, u32[]{:S(2)}) collective-permute-start(bf16[64,2048]{1,0:T(8,128)(2,1)S(1)} %pad_maximum_fusion), channel_id=1, source_target_pairs={{0,3},{1,0},{2,1},{3,2},{4,7},{5,4},{6,5},{7,6},{8,11},{9,8},{10,9... | collective-permute-start | bytes 786440 | tf_op jit(solution)/shard_map/ppermute | solution.py:273
  58.2 1.4 %collective-permute-done.9 = bf16[64,2048]{1,0:T(8,128)(2,1)S(1)} collective-permute-done((bf16[64,2048]{1,0:T(8,128)(2,1)S(1)}, bf16[64,2048]{1,0:T(8,128)(2,1)S(1)}, u32[]{:S(2)}, u32[]{:S(2)}) %collective-permute-start.9) | collective-permute-done | bytes 262176 | tf_op jit(solution)/shard_map/ppermute | solution.py:273
  60.0 3.8 %collective-permute-start.17 = (bf16[64,2048]{1,0:T(8,128)(2,1)S(1)}, bf16[64,2048]{1,0:T(8,128)(2,1)S(1)}, u32[]{:S(2)}, u32[]{:S(2)}) collective-permute-start(bf16[64,2048]{1,0:T(8,128)(2,1)S(1)} %pad_maximum_fusion.1), channel_id=1, source_target_pairs={{0,3},{1,0},{2,1},{3,2},{4,7},{5,4},{6,5},{7,6},{8,11},{9,8},{10,9... | collective-permute-start | bytes 786440 | tf_op jit(solution)/shard_map/ppermute | solution.py:273
  65.2 4.0 %collective-permute-start.16 = (bf16[64,2048]{1,0:T(8,128)(2,1)S(1)}, bf16[64,2048]{1,0:T(8,128)(2,1)S(1)}, u32[]{:S(2)}, u32[]{:S(2)}) collective-permute-start(bf16[64,2048]{1,0:T(8,128)(2,1)S(1)} %collective-permute-done.13), channel_id=1, source_target_pairs={{0,1},{1,2},{2,3},{3,0},{4,5},{5,6},{6,7},{7,4},{8,9},{9,10},{10,1... | collective-permute-start | bytes 786440 | tf_op jit(solution)/shard_map/ppermute | solution.py:273
  69.3 7.3 %collective-permute-done.15 = bf16[64,2048]{1,0:T(8,128)(2,1)S(1)} collective-permute-done((bf16[64,2048]{1,0:T(8,128)(2,1)S(1)}, bf16[64,2048]{1,0:T(8,128)(2,1)S(1)}, u32[]{:S(2)}, u32[]{:S(2)}) %collective-permute-start.15) | collective-permute-done | bytes 262176 | tf_op jit(solution)/shard_map/ppermute | solution.py:273
  76.5 3.9 %collective-permute-start.18 = (bf16[64,2048]{1,0:T(8,128)(2,1)S(1)}, bf16[64,2048]{1,0:T(8,128)(2,1)S(1)}, u32[]{:S(2)}, u32[]{:S(2)}) collective-permute-start(bf16[64,2048]{1,0:T(8,128)(2,1)S(1)} %collective-permute-done.15), channel_id=1, source_target_pairs={{0,1},{1,2},{2,3},{3,0},{4,5},{5,6},{6,7},{7,4},{8,9},{9,10},{10,1... | collective-permute-start | bytes 786440 | tf_op jit(solution)/shard_map/ppermute | solution.py:273
  80.4 1.5 %collective-permute-done.17 = bf16[64,2048]{1,0:T(8,128)(2,1)S(1)} collective-permute-done((bf16[64,2048]{1,0:T(8,128)(2,1)S(1)}, bf16[64,2048]{1,0:T(8,128)(2,1)S(1)}, u32[]{:S(2)}, u32[]{:S(2)}) %collective-permute-start.17) | collective-permute-done | bytes 262176 | tf_op jit(solution)/shard_map/ppermute | solution.py:273
  82.0 5.7 %collective-permute-done.16 = bf16[64,2048]{1,0:T(8,128)(2,1)S(1)} collective-permute-done((bf16[64,2048]{1,0:T(8,128)(2,1)S(1)}, bf16[64,2048]{1,0:T(8,128)(2,1)S(1)}, u32[]{:S(2)}, u32[]{:S(2)}) %collective-permute-start.16) | collective-permute-done | bytes 262176 | tf_op jit(solution)/shard_map/ppermute | solution.py:273
  87.8 2.1 %convolution_convert_fusion.1 = bf16[256,1792]{1,0:T(8,128)(2,1)S(1)} fusion(bf16[256,2048]{1,0:T(8,128)(2,1)S(1)} %bitcast.61, bf16[1792,2048]{1,0:T(8,128)(2,1)S(1)} %scale_weights.1.refs_4_), kind=kOutput, calls=%fused_computation.1 | convolution fusion | flops 1879506944 | bytes 9306112 | tf_op jit(solution)/shard_map/dot_general | solution.py:353
  90.0 2.8 %collective-permute-done.18 = bf16[64,2048]{1,0:T(8,128)(2,1)S(1)} collective-permute-done((bf16[64,2048]{1,0:T(8,128)(2,1)S(1)}, bf16[64,2048]{1,0:T(8,128)(2,1)S(1)}, u32[]{:S(2)}, u32[]{:S(2)}) %collective-permute-start.18) | collective-permute-done | bytes 262176 | tf_op jit(solution)/shard_map/ppermute | solution.py:273
  92.9 2.1 %convolution_convert_fusion = bf16[256,1792]{1,0:T(8,128)(2,1)S(1)} fusion(bf16[256,2048]{1,0:T(8,128)(2,1)S(1)} %bitcast.59, bf16[1792,2048]{1,0:T(8,128)(2,1)S(1)} %scale_weights.1.refs_4_), kind=kOutput, calls=%fused_computation | convolution fusion | flops 1879506944 | bytes 9306112 | tf_op jit(solution)/shard_map/dot_general | solution.py:353
  95.2 1.6 %collective-permute-start.20 = (bf16[64,1792]{1,0:T(8,128)(2,1)S(1)}, bf16[64,1792]{1,0:T(8,128)(2,1)S(1)}, u32[]{:S(2)}, u32[]{:S(2)}) collective-permute-start(bf16[64,1792]{1,0:T(8,128)(2,1)S(1)} %get-tuple-element.50), channel_id=1, source_target_pairs={{0,24},{4,28},{8,16},{12,20},{16,8},{20,12},{24,0},{28,4},{1,25},{... | collective-permute-start | bytes 688136 | tf_op jit(solution)/shard_map/ppermute | solution.py:13
  96.8 1.4 %collective-permute-start.21 = (bf16[64,1792]{1,0:T(8,128)(2,1)S(1)}, bf16[64,1792]{1,0:T(8,128)(2,1)S(1)}, u32[]{:S(2)}, u32[]{:S(2)}) collective-permute-start(bf16[64,1792]{1,0:T(8,128)(2,1)S(1)} %get-tuple-element.53), channel_id=1, source_target_pairs={{0,16},{4,20},{8,24},{12,28},{16,0},{20,4},{24,8},{28,12},{1,17},{... | collective-permute-start | bytes 688136 | tf_op jit(solution)/shard_map/ppermute | solution.py:13
  98.8 6.6 %weight_grads.1 = (bf16[1,1792,1024]{2,1,0:T(8,128)(2,1)}, bf16[1,1792,1024]{2,1,0:T(8,128)(2,1)}) custom-call(bf16[64,1792]{1,0:T(8,128)(2,1)S(1)} %collective-permute-done.6.refs_3_.refs_0_, bf16[64,1792]{1,0:T(8,128)(2,1)S(1)} %collective-permute-done.4.refs_2_.refs_1_, bf16[64,1792]{1,0:T(8,128)(2,1)S(1)} %collective-permute-done.2.refs_1_.refs_2_, ...), custom_call_target="tpu_custom_call" | custom-call | flops 3758096384 | bytes 11272192 | tf_op jit(solution)/shard_map/weight_grads/pallas_call | solution.py:229
  105.3 2.9 %collective-permute-done.21 = bf16[64,1792]{1,0:T(8,128)(2,1)S(1)} collective-permute-done((bf16[64,1792]{1,0:T(8,128)(2,1)S(1)}, bf16[64,1792]{1,0:T(8,128)(2,1)S(1)}, u32[]{:S(2)}, u32[]{:S(2)}) %collective-permute-start.21) | collective-permute-done | bytes 229408 | tf_op jit(solution)/shard_map/ppermute | solution.py:13
  108.6 1.1 convolution_convert_fusion.2
  (52 shorter events, 6.9 us)
Async XLA Ops:
  2.8 9.4 %collective-permute-start = (bf16[64,1792]{1,0:T(8,128)(2,1)S(1)}, bf16[64,1792]{1,0:T(8,128)(2,1)S(1)}, u32[]{:S(2)}, u32[]{:S(2)}) collective-permute-start(bf16[64,1792]{1,0:T(8,128)(2,1)S(1)} %get-tuple-element.27), channel_id=1, source_target_pairs={{0,28},{4,24},{8,20},{12,16},{16,12},{20,8},{24,4},{28,0},{1,29},{... | collective-permute-start | bytes 688136 | tf_op jit(solution)/shard_map/ppermute | solution.py:13
  6.1 11.0 %collective-permute-start.2 = (bf16[64,1792]{1,0:T(8,128)(2,1)S(1)}, bf16[64,1792]{1,0:T(8,128)(2,1)S(1)}, u32[]{:S(2)}, u32[]{:S(2)}) collective-permute-start(bf16[64,1792]{1,0:T(8,128)(2,1)S(1)} %get-tuple-element.28), channel_id=1, source_target_pairs={{0,20},{4,16},{8,28},{12,24},{16,4},{20,0},{24,12},{28,8},{1,21},{... | collective-permute-start | bytes 688136 | tf_op jit(solution)/shard_map/ppermute | solution.py:13
  6.9 11.1 %collective-permute-start.4 = (bf16[64,1792]{1,0:T(8,128)(2,1)S(1)}, bf16[64,1792]{1,0:T(8,128)(2,1)S(1)}, u32[]{:S(2)}, u32[]{:S(2)}) collective-permute-start(bf16[64,1792]{1,0:T(8,128)(2,1)S(1)} %get-tuple-element.29), channel_id=1, source_target_pairs={{0,12},{4,8},{8,4},{12,0},{16,28},{20,24},{24,20},{28,16},{1,13},{... | collective-permute-start | bytes 688136 | tf_op jit(solution)/shard_map/ppermute | solution.py:13
  6.9 11.2 %collective-permute-start.6 = (bf16[64,1792]{1,0:T(8,128)(2,1)S(1)}, bf16[64,1792]{1,0:T(8,128)(2,1)S(1)}, u32[]{:S(2)}, u32[]{:S(2)}) collective-permute-start(bf16[64,1792]{1,0:T(8,128)(2,1)S(1)} %get-tuple-element.30.refs_3_.refs_4_), channel_id=1, source_target_pairs={{0,4},{4,0},{8,12},{12,8},{16,20},{20,16},{24,28},{28,24},{1,5},{5... | collective-permute-start | bytes 688136 | tf_op jit(solution)/shard_map/ppermute | solution.py:13
  6.9 0.7 copy-start
  7.6 0.7 copy-start.1
  12.1 12.1 %collective-permute-start.1 = (bf16[64,1792]{1,0:T(8,128)(2,1)S(1)}, bf16[64,1792]{1,0:T(8,128)(2,1)S(1)}, u32[]{:S(2)}, u32[]{:S(2)}) collective-permute-start(bf16[64,1792]{1,0:T(8,128)(2,1)S(1)} %collective-permute-done.refs_0_.refs_3_), channel_id=1, source_target_pairs={{0,4},{4,0},{8,12},{12,8},{16,20},{20,16},{24,28},{28,24},{1,5},{5... | collective-permute-start | bytes 688136 | tf_op jit(solution)/shard_map/ppermute | solution.py:13
  17.1 7.2 %collective-permute-start.3 = (bf16[64,1792]{1,0:T(8,128)(2,1)S(1)}, bf16[64,1792]{1,0:T(8,128)(2,1)S(1)}, u32[]{:S(2)}, u32[]{:S(2)}) collective-permute-start(bf16[64,1792]{1,0:T(8,128)(2,1)S(1)} %collective-permute-done.2.refs_1_.refs_2_), channel_id=1, source_target_pairs={{0,4},{4,0},{8,12},{12,8},{16,20},{20,16},{24,28},{28,24},{1,5},{5... | collective-permute-start | bytes 688136 | tf_op jit(solution)/shard_map/ppermute | solution.py:13
  18.0 6.3 %collective-permute-start.5 = (bf16[64,1792]{1,0:T(8,128)(2,1)S(1)}, bf16[64,1792]{1,0:T(8,128)(2,1)S(1)}, u32[]{:S(2)}, u32[]{:S(2)}) collective-permute-start(bf16[64,1792]{1,0:T(8,128)(2,1)S(1)} %collective-permute-done.4.refs_2_.refs_1_), channel_id=1, source_target_pairs={{0,4},{4,0},{8,12},{12,8},{16,20},{20,16},{24,28},{28,24},{1,5},{5... | collective-permute-start | bytes 688136 | tf_op jit(solution)/shard_map/ppermute | solution.py:13
  20.3 11.0 %collective-permute-start.8 = (bf16[64,2048]{1,0:T(8,128)(2,1)S(1)}, bf16[64,2048]{1,0:T(8,128)(2,1)S(1)}, u32[]{:S(2)}, u32[]{:S(2)}) collective-permute-start(bf16[64,2048]{1,0:T(8,128)(2,1)S(1)} %get-tuple-element.56), channel_id=1, source_target_pairs={{0,1},{1,2},{2,3},{3,0},{4,5},{5,6},{6,7},{7,4},{8,9},{9,10},{10,1... | collective-permute-start | bytes 786440 | tf_op jit(solution)/shard_map/ppermute | solution.py:273
  22.2 24.8 %collective-permute-start.11 = (bf16[64,2048]{1,0:T(8,128)(2,1)S(1)}, bf16[64,2048]{1,0:T(8,128)(2,1)S(1)}, u32[]{:S(2)}, u32[]{:S(2)}) collective-permute-start(bf16[64,2048]{1,0:T(8,128)(2,1)S(1)} %get-tuple-element.31), channel_id=1, source_target_pairs={{0,3},{1,0},{2,1},{3,2},{4,7},{5,4},{6,5},{7,6},{8,11},{9,8},{10,9... | collective-permute-start | bytes 786440 | tf_op jit(solution)/shard_map/ppermute | solution.py:273
  26.3 27.6 %copy-start.2 = (bf16[1,128,1024]{2,1,0:T(8,128)(2,1)S(1)}, bf16[1,128,1024]{2,1,0:T(8,128)(2,1)}, u32[]{:S(2)}) copy-start(bf16[1,128,1024]{2,1,0:T(8,128)(2,1)} %param.13) | copy-start | bytes 786436
  26.4 16.2 %collective-permute-start.7 = (bf16[64,2048]{1,0:T(8,128)(2,1)S(1)}, bf16[64,2048]{1,0:T(8,128)(2,1)S(1)}, u32[]{:S(2)}, u32[]{:S(2)}) collective-permute-start(bf16[64,2048]{1,0:T(8,128)(2,1)S(1)} %get-tuple-element.32), channel_id=1, source_target_pairs={{0,1},{1,2},{2,3},{3,0},{4,5},{5,6},{6,7},{7,4},{8,9},{9,10},{10,1... | collective-permute-start | bytes 786440 | tf_op jit(solution)/shard_map/ppermute | solution.py:273
  26.5 31.5 %collective-permute-start.12 = (bf16[64,2048]{1,0:T(8,128)(2,1)S(1)}, bf16[64,2048]{1,0:T(8,128)(2,1)S(1)}, u32[]{:S(2)}, u32[]{:S(2)}) collective-permute-start(bf16[64,2048]{1,0:T(8,128)(2,1)S(1)} %get-tuple-element.33), channel_id=1, source_target_pairs={{0,3},{1,0},{2,1},{3,2},{4,7},{5,4},{6,5},{7,6},{8,11},{9,8},{10,9... | collective-permute-start | bytes 786440 | tf_op jit(solution)/shard_map/ppermute | solution.py:273
  31.4 22.4 %collective-permute-start.10 = (bf16[64,2048]{1,0:T(8,128)(2,1)S(1)}, bf16[64,2048]{1,0:T(8,128)(2,1)S(1)}, u32[]{:S(2)}, u32[]{:S(2)}) collective-permute-start(bf16[64,2048]{1,0:T(8,128)(2,1)S(1)} %fusion.8), channel_id=1, source_target_pairs={{0,1},{1,2},{2,3},{3,0},{4,5},{5,6},{6,7},{7,4},{8,9},{9,10},{10,1... | collective-permute-start | bytes 786440 | tf_op jit(solution)/shard_map/ppermute | solution.py:273
  42.7 16.9 %collective-permute-start.9 = (bf16[64,2048]{1,0:T(8,128)(2,1)S(1)}, bf16[64,2048]{1,0:T(8,128)(2,1)S(1)}, u32[]{:S(2)}, u32[]{:S(2)}) collective-permute-start(bf16[64,2048]{1,0:T(8,128)(2,1)S(1)} %fusion.9), channel_id=1, source_target_pairs={{0,1},{1,2},{2,3},{3,0},{4,5},{5,6},{6,7},{7,4},{8,9},{9,10},{10,1... | collective-permute-start | bytes 786440 | tf_op jit(solution)/shard_map/ppermute | solution.py:273
  54.1 11.1 %collective-permute-start.13 = (bf16[64,2048]{1,0:T(8,128)(2,1)S(1)}, bf16[64,2048]{1,0:T(8,128)(2,1)S(1)}, u32[]{:S(2)}, u32[]{:S(2)}) collective-permute-start(bf16[64,2048]{1,0:T(8,128)(2,1)S(1)} %pad_maximum_fusion), channel_id=1, source_target_pairs={{0,1},{1,2},{2,3},{3,0},{4,5},{5,6},{6,7},{7,4},{8,9},{9,10},{10,1... | collective-permute-start | bytes 786440 | tf_op jit(solution)/shard_map/ppermute | solution.py:273
  54.2 26.2 %collective-permute-start.14 = (bf16[64,2048]{1,0:T(8,128)(2,1)S(1)}, bf16[64,2048]{1,0:T(8,128)(2,1)S(1)}, u32[]{:S(2)}, u32[]{:S(2)}) collective-permute-start(bf16[64,2048]{1,0:T(8,128)(2,1)S(1)} %pad_maximum_fusion), channel_id=1, source_target_pairs={{0,3},{1,0},{2,1},{3,2},{4,7},{5,4},{6,5},{7,6},{8,11},{9,8},{10,9... | collective-permute-start | bytes 786440 | tf_op jit(solution)/shard_map/ppermute | solution.py:273
  59.9 16.6 %collective-permute-start.15 = (bf16[64,2048]{1,0:T(8,128)(2,1)S(1)}, bf16[64,2048]{1,0:T(8,128)(2,1)S(1)}, u32[]{:S(2)}, u32[]{:S(2)}) collective-permute-start(bf16[64,2048]{1,0:T(8,128)(2,1)S(1)} %pad_maximum_fusion.1), channel_id=1, source_target_pairs={{0,1},{1,2},{2,3},{3,0},{4,5},{5,6},{6,7},{7,4},{8,9},{9,10},{10,1... | collective-permute-start | bytes 786440 | tf_op jit(solution)/shard_map/ppermute | solution.py:273
  60.0 22.0 %collective-permute-start.17 = (bf16[64,2048]{1,0:T(8,128)(2,1)S(1)}, bf16[64,2048]{1,0:T(8,128)(2,1)S(1)}, u32[]{:S(2)}, u32[]{:S(2)}) collective-permute-start(bf16[64,2048]{1,0:T(8,128)(2,1)S(1)} %pad_maximum_fusion.1), channel_id=1, source_target_pairs={{0,3},{1,0},{2,1},{3,2},{4,7},{5,4},{6,5},{7,6},{8,11},{9,8},{10,9... | collective-permute-start | bytes 786440 | tf_op jit(solution)/shard_map/ppermute | solution.py:273
  65.2 22.5 %collective-permute-start.16 = (bf16[64,2048]{1,0:T(8,128)(2,1)S(1)}, bf16[64,2048]{1,0:T(8,128)(2,1)S(1)}, u32[]{:S(2)}, u32[]{:S(2)}) collective-permute-start(bf16[64,2048]{1,0:T(8,128)(2,1)S(1)} %collective-permute-done.13), channel_id=1, source_target_pairs={{0,1},{1,2},{2,3},{3,0},{4,5},{5,6},{6,7},{7,4},{8,9},{9,10},{10,1... | collective-permute-start | bytes 786440 | tf_op jit(solution)/shard_map/ppermute | solution.py:273
  76.5 16.3 %collective-permute-start.18 = (bf16[64,2048]{1,0:T(8,128)(2,1)S(1)}, bf16[64,2048]{1,0:T(8,128)(2,1)S(1)}, u32[]{:S(2)}, u32[]{:S(2)}) collective-permute-start(bf16[64,2048]{1,0:T(8,128)(2,1)S(1)} %collective-permute-done.15), channel_id=1, source_target_pairs={{0,1},{1,2},{2,3},{3,0},{4,5},{5,6},{6,7},{7,4},{8,9},{9,10},{10,1... | collective-permute-start | bytes 786440 | tf_op jit(solution)/shard_map/ppermute | solution.py:273
  89.9 3.0 %collective-permute-start.19 = (bf16[256,1792]{1,0:T(8,128)(2,1)S(1)}, bf16[256,1792]{1,0:T(8,128)(2,1)S(1)}, u32[]{:S(2)}, u32[]{:S(2)}) collective-permute-start(bf16[256,1792]{1,0:T(8,128)(2,1)S(1)} %convolution_convert_fusion.1), channel_id=1, source_target_pairs={{0,4},{4,0},{8,12},{12,8},{16,20},{20,16},{24,28},{28,24},{1,5},{5... | collective-permute-start | bytes 2752520 | tf_op jit(solution)/shard_map/ppermute | solution.py:13
  95.2 10.2 %collective-permute-start.20 = (bf16[64,1792]{1,0:T(8,128)(2,1)S(1)}, bf16[64,1792]{1,0:T(8,128)(2,1)S(1)}, u32[]{:S(2)}, u32[]{:S(2)}) collective-permute-start(bf16[64,1792]{1,0:T(8,128)(2,1)S(1)} %get-tuple-element.50), channel_id=1, source_target_pairs={{0,24},{4,28},{8,16},{12,20},{16,8},{20,12},{24,0},{28,4},{1,25},{... | collective-permute-start | bytes 688136 | tf_op jit(solution)/shard_map/ppermute | solution.py:13
  96.8 11.5 %collective-permute-start.21 = (bf16[64,1792]{1,0:T(8,128)(2,1)S(1)}, bf16[64,1792]{1,0:T(8,128)(2,1)S(1)}, u32[]{:S(2)}, u32[]{:S(2)}) collective-permute-start(bf16[64,1792]{1,0:T(8,128)(2,1)S(1)} %get-tuple-element.53), channel_id=1, source_target_pairs={{0,16},{4,20},{8,24},{12,28},{16,0},{20,4},{24,8},{28,12},{1,17},{... | collective-permute-start | bytes 688136 | tf_op jit(solution)/shard_map/ppermute | solution.py:13
  98.2 10.4 %copy-start.3 = (bf16[256,128]{1,0:T(8,128)(2,1)S(1)}, bf16[256,128]{1,0:T(8,128)(2,1)}, u32[]{:S(2)}) copy-start(bf16[256,128]{1,0:T(8,128)(2,1)} %get-tuple-element.48) | copy-start | bytes 196612
  98.2 10.4 %collective-permute-start.22 = (bf16[64,1792]{1,0:T(8,128)(2,1)S(1)}, bf16[64,1792]{1,0:T(8,128)(2,1)S(1)}, u32[]{:S(2)}, u32[]{:S(2)}) collective-permute-start(bf16[64,1792]{1,0:T(8,128)(2,1)S(1)} %get-tuple-element.52), channel_id=1, source_target_pairs={{0,8},{4,12},{8,0},{12,4},{16,24},{20,28},{24,16},{28,20},{1,9},{5... | collective-permute-start | bytes 688136 | tf_op jit(solution)/shard_map/ppermute | solution.py:13

commit v12 on v9

--- a/solution.py
+++ b/solution.py
@@ -136,7 +136,7 @@
 def packed_rows(tokens, counts, capacity):
     row_total, feat_cols = tokens.shape
     experts = counts.shape[1]
-    tile = feat_cols // 2 if feat_cols % 256 == 0 else feat_cols
+    tile = feat_cols
     block = pltpu.VMEM((capacity, feat_cols), jnp.bfloat16)
     chooser, *packed = pl.pallas_call(
         pack_kernel,

time: 110 us -> 110 us (level)
  no operation moved by 1% of the time
where the time goes in v12:
time: 110 us; the launch traced here: 109 us
  waiting for transfers between devices  43.1 us (39%)
  starting transfers between devices  40.8 us (37%)
  Pallas kernels  15.9 us (14%)
  matrix products  5.3 us (5%)
  local copies, waits for them, and re-layouts  1.83 us (2%)
  other arithmetic  1.69 us (2%)
    ppermute x12, waiting for transfers between devices, send(): self.came[way] = lax.ppermute(value, 'fsdp', ring)  34.4 us
    ppermute x12, starting transfers between devices, send(): self.came[way] = lax.ppermute(value, 'fsdp', ring)  31.8 us
    ppermute x11, starting transfers between devices, swap(): return lax.ppermute(value, axis, pairs)  8.93 us
    ppermute x11, waiting for transfers between devices, swap(): return lax.ppermute(value, axis, pairs)  8.68 us
    pallas_call x1, Pallas kernels, weight_grads(): pl.pallas_call(lambda *refs: weight_kernel(count, *refs), out_shape=(out,...  6.59 us
    dot_general x2, matrix products, back(): lax.dot_general(whole, weights, (((1,), (1,)), ((), ())), preferred_eleme...  4.21 us
    pallas_call x2, Pallas kernels, projected(): pl.pallas_call(project_kernel, out_shape=jax.ShapeDtypeStruct((count, cap...  4.18 us
    pallas_call x1, Pallas kernels, scaled_weights(): pl.pallas_call(lambda *refs: scale_kernel(sub, *refs), out_shape=jax.Shap...  3.3 us
  transfers between devices with their start and end apart: 23, of which 15 were waited for; matrix products, arithmetic and copies ran while one was open for 4% of the time, Pallas kernels for 13%

profile of v12, /device:TPU:0, one launch (start us, length us, event | category | flops | bytes accessed | tf_op | source)
XLA Modules:
  0.0 109.4 jit_solution(7319928278384843445)
XLA Ops:
  0.6 1.8 %pack_rows.1 = (bf16[256,128]{1,0:T(8,128)(2,1)}, bf16[64,1792]{1,0:T(8,128)(2,1)S(1)}, bf16[64,1792]{1,0:T(8,128)(2,1)S(1)}, bf16[64,1792]{1,0:T(8,128)(2,1)S(1)}, bf16[64,1792]{1,0:T(8,128)(2,1)S(1)}) custom-call(s32[1,4]{1,0:T(1,128)} %counts_ref.1, bf16[128,1792]{1,0:T(8,128)(2,1)} %tokens_ref.1), custom_call_target="tpu_custom_call" | custom-call | flops 117440512 | bytes 1376256 | tf_op jit(solution)/shard_map/pack_rows/pallas_call | solution.py:141
  2.4 3.3 %collective-permute-start = (bf16[64,1792]{1,0:T(8,128)(2,1)S(1)}, bf16[64,1792]{1,0:T(8,128)(2,1)S(1)}, u32[]{:S(2)}, u32[]{:S(2)}) collective-permute-start(bf16[64,1792]{1,0:T(8,128)(2,1)S(1)} %get-tuple-element.27), channel_id=1, source_target_pairs={{0,28},{4,24},{8,20},{12,16},{16,12},{20,8},{24,4},{28,0},{1,29},{... | collective-permute-start | bytes 688136 | tf_op jit(solution)/shard_map/ppermute | solution.py:13
  8.0 3.3 %scale_weights.1.refs_4_ = bf16[1792,2048]{1,0:T(8,128)(2,1)S(1)} custom-call(s32[1]{0:T(128)} %bitcast.refs_0_, bf16[1,1792,1024]{2,1,0:T(8,128)(2,1)} %refs_1_.1, bf16[1,1792,1024]{2,1,0:T(8,128)(2,1)} %refs_2_.1, f32[1,8,56]{2,1,0:T(8,128)S(1)} %bitcast.63, f32[1,8,56]{2,1,0:T(8,128)S(1)} %bitcast.64), custom_call_target="tpu_custom_call" | custom-call | flops 3670016 | bytes 14680064 | tf_op jit(solution)/shard_map/scale_weights/pallas_call | solution.py:84
  11.8 0.8 collective-permute-start.1
  12.6 4.1 %collective-permute-done.2.refs_1_.refs_2_ = bf16[64,1792]{1,0:T(8,128)(2,1)S(1)} collective-permute-done((bf16[64,1792]{1,0:T(8,128)(2,1)S(1)}, bf16[64,1792]{1,0:T(8,128)(2,1)S(1)}, u32[]{:S(2)}, u32[]{:S(2)}) %collective-permute-start.2) | collective-permute-done | bytes 229408 | tf_op jit(solution)/shard_map/ppermute | solution.py:13
  17.8 2.1 %project.3 = bf16[4,64,2048]{2,1,0:T(8,128)(2,1)S(1)} custom-call(bf16[64,1792]{1,0:T(8,128)(2,1)S(1)} %collective-permute-done.refs_0_.refs_3_, bf16[64,1792]{1,0:T(8,128)(2,1)S(1)} %collective-permute-done.2.refs_1_.refs_2_, bf16[64,1792]{1,0:T(8,128)(2,1)S(1)} %collective-permute-done.4.refs_2_.refs_1_, ...), custom_call_target="tpu_custom_call" | custom-call | flops 1879048192 | bytes 9306112 | tf_op jit(solution)/shard_map/project/pallas_call | solution.py:181
  20.0 1.9 %collective-permute-start.8 = (bf16[64,2048]{1,0:T(8,128)(2,1)S(1)}, bf16[64,2048]{1,0:T(8,128)(2,1)S(1)}, u32[]{:S(2)}, u32[]{:S(2)}) collective-permute-start(bf16[64,2048]{1,0:T(8,128)(2,1)S(1)} %get-tuple-element.56), channel_id=1, source_target_pairs={{0,1},{1,2},{2,3},{3,0},{4,5},{5,6},{6,7},{7,4},{8,9},{9,10},{10,1... | collective-permute-start | bytes 786440 | tf_op jit(solution)/shard_map/ppermute | solution.py:273
  21.8 2.1 %collective-permute-start.11 = (bf16[64,2048]{1,0:T(8,128)(2,1)S(1)}, bf16[64,2048]{1,0:T(8,128)(2,1)S(1)}, u32[]{:S(2)}, u32[]{:S(2)}) collective-permute-start(bf16[64,2048]{1,0:T(8,128)(2,1)S(1)} %get-tuple-element.31), channel_id=1, source_target_pairs={{0,3},{1,0},{2,1},{3,2},{4,7},{5,4},{6,5},{7,6},{8,11},{9,8},{10,9... | collective-permute-start | bytes 786440 | tf_op jit(solution)/shard_map/ppermute | solution.py:273
  23.9 2.1 %project.2 = bf16[4,64,2048]{2,1,0:T(8,128)(2,1)S(1)} custom-call(bf16[64,1792]{1,0:T(8,128)(2,1)S(1)} %collective-permute-done.1.refs_0_.refs_7_, bf16[64,1792]{1,0:T(8,128)(2,1)S(1)} %collective-permute-done.3.refs_1_.refs_6_, bf16[64,1792]{1,0:T(8,128)(2,1)S(1)} %collective-permute-done.5.refs_2_.refs_5_, ...), custom_call_target="tpu_custom_call" | custom-call | flops 1879048192 | bytes 9306112 | tf_op jit(solution)/shard_map/project/pallas_call | solution.py:181
  26.2 3.8 %collective-permute-start.12 = (bf16[64,2048]{1,0:T(8,128)(2,1)S(1)}, bf16[64,2048]{1,0:T(8,128)(2,1)S(1)}, u32[]{:S(2)}, u32[]{:S(2)}) collective-permute-start(bf16[64,2048]{1,0:T(8,128)(2,1)S(1)} %get-tuple-element.33), channel_id=1, source_target_pairs={{0,3},{1,0},{2,1},{3,2},{4,7},{5,4},{6,5},{7,6},{8,11},{9,8},{10,9... | collective-permute-start | bytes 786440 | tf_op jit(solution)/shard_map/ppermute | solution.py:273
  30.0 1.0 collective-permute-done.8
  31.1 4.3 %collective-permute-start.10 = (bf16[64,2048]{1,0:T(8,128)(2,1)S(1)}, bf16[64,2048]{1,0:T(8,128)(2,1)S(1)}, u32[]{:S(2)}, u32[]{:S(2)}) collective-permute-start(bf16[64,2048]{1,0:T(8,128)(2,1)S(1)} %fusion.8), channel_id=1, source_target_pairs={{0,1},{1,2},{2,3},{3,0},{4,5},{5,6},{6,7},{7,4},{8,9},{9,10},{10,1... | collective-permute-start | bytes 786440 | tf_op jit(solution)/shard_map/ppermute | solution.py:273
  35.4 6.9 %collective-permute-done.7 = bf16[64,2048]{1,0:T(8,128)(2,1)S(1)} collective-permute-done((bf16[64,2048]{1,0:T(8,128)(2,1)S(1)}, bf16[64,2048]{1,0:T(8,128)(2,1)S(1)}, u32[]{:S(2)}, u32[]{:S(2)}) %collective-permute-start.7) | collective-permute-done | bytes 262176 | tf_op jit(solution)/shard_map/ppermute | solution.py:273
  42.4 4.2 %collective-permute-start.9 = (bf16[64,2048]{1,0:T(8,128)(2,1)S(1)}, bf16[64,2048]{1,0:T(8,128)(2,1)S(1)}, u32[]{:S(2)}, u32[]{:S(2)}) collective-permute-start(bf16[64,2048]{1,0:T(8,128)(2,1)S(1)} %fusion.9), channel_id=1, source_target_pairs={{0,1},{1,2},{2,3},{3,0},{4,5},{5,6},{6,7},{7,4},{8,9},{9,10},{10,1... | collective-permute-start | bytes 786440 | tf_op jit(solution)/shard_map/ppermute | solution.py:273
  46.6 7.0 %collective-permute-done.10 = bf16[64,2048]{1,0:T(8,128)(2,1)S(1)} collective-permute-done((bf16[64,2048]{1,0:T(8,128)(2,1)S(1)}, bf16[64,2048]{1,0:T(8,128)(2,1)S(1)}, u32[]{:S(2)}, u32[]{:S(2)}) %collective-permute-start.10) | collective-permute-done | bytes 262176 | tf_op jit(solution)/shard_map/ppermute | solution.py:273
  53.9 3.8 %collective-permute-start.14 = (bf16[64,2048]{1,0:T(8,128)(2,1)S(1)}, bf16[64,2048]{1,0:T(8,128)(2,1)S(1)}, u32[]{:S(2)}, u32[]{:S(2)}) collective-permute-start(bf16[64,2048]{1,0:T(8,128)(2,1)S(1)} %pad_maximum_fusion), channel_id=1, source_target_pairs={{0,3},{1,0},{2,1},{3,2},{4,7},{5,4},{6,5},{7,6},{8,11},{9,8},{10,9... | collective-permute-start | bytes 786440 | tf_op jit(solution)/shard_map/ppermute | solution.py:273
  57.9 1.4 %collective-permute-done.9 = bf16[64,2048]{1,0:T(8,128)(2,1)S(1)} collective-permute-done((bf16[64,2048]{1,0:T(8,128)(2,1)S(1)}, bf16[64,2048]{1,0:T(8,128)(2,1)S(1)}, u32[]{:S(2)}, u32[]{:S(2)}) %collective-permute-start.9) | collective-permute-done | bytes 262176 | tf_op jit(solution)/shard_map/ppermute | solution.py:273
  59.6 3.8 %collective-permute-start.16 = (bf16[64,2048]{1,0:T(8,128)(2,1)S(1)}, bf16[64,2048]{1,0:T(8,128)(2,1)S(1)}, u32[]{:S(2)}, u32[]{:S(2)}) collective-permute-start(bf16[64,2048]{1,0:T(8,128)(2,1)S(1)} %pad_maximum_fusion.1), channel_id=1, source_target_pairs={{0,3},{1,0},{2,1},{3,2},{4,7},{5,4},{6,5},{7,6},{8,11},{9,8},{10,9... | collective-permute-start | bytes 786440 | tf_op jit(solution)/shard_map/ppermute | solution.py:273
  64.9 3.9 %collective-permute-start.15 = (bf16[64,2048]{1,0:T(8,128)(2,1)S(1)}, bf16[64,2048]{1,0:T(8,128)(2,1)S(1)}, u32[]{:S(2)}, u32[]{:S(2)}) collective-permute-start(bf16[64,2048]{1,0:T(8,128)(2,1)S(1)} %collective-permute-done.13), channel_id=1, source_target_pairs={{0,1},{1,2},{2,3},{3,0},{4,5},{5,6},{6,7},{7,4},{8,9},{9,10},{10,1... | collective-permute-start | bytes 786440 | tf_op jit(solution)/shard_map/ppermute | solution.py:273
  68.9 1.8 %collective-permute-done.14 = bf16[64,2048]{1,0:T(8,128)(2,1)S(1)} collective-permute-done((bf16[64,2048]{1,0:T(8,128)(2,1)S(1)}, bf16[64,2048]{1,0:T(8,128)(2,1)S(1)}, u32[]{:S(2)}, u32[]{:S(2)}) %collective-permute-start.14) | collective-permute-done | bytes 262176 | tf_op jit(solution)/shard_map/ppermute | solution.py:273
  70.7 5.4 %collective-permute-done.17 = bf16[64,2048]{1,0:T(8,128)(2,1)S(1)} collective-permute-done((bf16[64,2048]{1,0:T(8,128)(2,1)S(1)}, bf16[64,2048]{1,0:T(8,128)(2,1)S(1)}, u32[]{:S(2)}, u32[]{:S(2)}) %collective-permute-start.17) | collective-permute-done | bytes 262176 | tf_op jit(solution)/shard_map/ppermute | solution.py:273
  76.2 3.9 %collective-permute-start.18 = (bf16[64,2048]{1,0:T(8,128)(2,1)S(1)}, bf16[64,2048]{1,0:T(8,128)(2,1)S(1)}, u32[]{:S(2)}, u32[]{:S(2)}) collective-permute-start(bf16[64,2048]{1,0:T(8,128)(2,1)S(1)} %collective-permute-done.17), channel_id=1, source_target_pairs={{0,1},{1,2},{2,3},{3,0},{4,5},{5,6},{6,7},{7,4},{8,9},{9,10},{10,1... | collective-permute-start | bytes 786440 | tf_op jit(solution)/shard_map/ppermute | solution.py:273
  80.1 1.6 %collective-permute-done.16 = bf16[64,2048]{1,0:T(8,128)(2,1)S(1)} collective-permute-done((bf16[64,2048]{1,0:T(8,128)(2,1)S(1)}, bf16[64,2048]{1,0:T(8,128)(2,1)S(1)}, u32[]{:S(2)}, u32[]{:S(2)}) %collective-permute-start.16) | collective-permute-done | bytes 262176 | tf_op jit(solution)/shard_map/ppermute | solution.py:273
  81.7 5.8 %collective-permute-done.15 = bf16[64,2048]{1,0:T(8,128)(2,1)S(1)} collective-permute-done((bf16[64,2048]{1,0:T(8,128)(2,1)S(1)}, bf16[64,2048]{1,0:T(8,128)(2,1)S(1)}, u32[]{:S(2)}, u32[]{:S(2)}) %collective-permute-start.15) | collective-permute-done | bytes 262176 | tf_op jit(solution)/shard_map/ppermute | solution.py:273
  87.5 2.1 %convolution_convert_fusion.1 = bf16[256,1792]{1,0:T(8,128)(2,1)S(1)} fusion(bf16[256,2048]{1,0:T(8,128)(2,1)S(1)} %bitcast.61, bf16[1792,2048]{1,0:T(8,128)(2,1)S(1)} %scale_weights.1.refs_4_), kind=kOutput, calls=%fused_computation.1 | convolution fusion | flops 1879506944 | bytes 9306112 | tf_op jit(solution)/shard_map/dot_general | solution.py:353
  89.7 2.8 %collective-permute-done.18 = bf16[64,2048]{1,0:T(8,128)(2,1)S(1)} collective-permute-done((bf16[64,2048]{1,0:T(8,128)(2,1)S(1)}, bf16[64,2048]{1,0:T(8,128)(2,1)S(1)}, u32[]{:S(2)}, u32[]{:S(2)}) %collective-permute-start.18) | collective-permute-done | bytes 262176 | tf_op jit(solution)/shard_map/ppermute | solution.py:273
  92.5 2.1 %convolution_convert_fusion = bf16[256,1792]{1,0:T(8,128)(2,1)S(1)} fusion(bf16[256,2048]{1,0:T(8,128)(2,1)S(1)} %bitcast.59, bf16[1792,2048]{1,0:T(8,128)(2,1)S(1)} %scale_weights.1.refs_4_), kind=kOutput, calls=%fused_computation | convolution fusion | flops 1879506944 | bytes 9306112 | tf_op jit(solution)/shard_map/dot_general | solution.py:353
  94.9 1.6 %collective-permute-start.20 = (bf16[64,1792]{1,0:T(8,128)(2,1)S(1)}, bf16[64,1792]{1,0:T(8,128)(2,1)S(1)}, u32[]{:S(2)}, u32[]{:S(2)}) collective-permute-start(bf16[64,1792]{1,0:T(8,128)(2,1)S(1)} %get-tuple-element.50), channel_id=1, source_target_pairs={{0,24},{4,28},{8,16},{12,20},{16,8},{20,12},{24,0},{28,4},{1,25},{... | collective-permute-start | bytes 688136 | tf_op jit(solution)/shard_map/ppermute | solution.py:13
  96.4 1.4 %collective-permute-start.21 = (bf16[64,1792]{1,0:T(8,128)(2,1)S(1)}, bf16[64,1792]{1,0:T(8,128)(2,1)S(1)}, u32[]{:S(2)}, u32[]{:S(2)}) collective-permute-start(bf16[64,1792]{1,0:T(8,128)(2,1)S(1)} %get-tuple-element.53), channel_id=1, source_target_pairs={{0,16},{4,20},{8,24},{12,28},{16,0},{20,4},{24,8},{28,12},{1,17},{... | collective-permute-start | bytes 688136 | tf_op jit(solution)/shard_map/ppermute | solution.py:13
  98.4 6.6 %weight_grads.1 = (bf16[1,1792,1024]{2,1,0:T(8,128)(2,1)}, bf16[1,1792,1024]{2,1,0:T(8,128)(2,1)}) custom-call(bf16[64,1792]{1,0:T(8,128)(2,1)S(1)} %collective-permute-done.6.refs_3_.refs_0_, bf16[64,1792]{1,0:T(8,128)(2,1)S(1)} %collective-permute-done.4.refs_2_.refs_1_, bf16[64,1792]{1,0:T(8,128)(2,1)S(1)} %collective-permute-done.2.refs_1_.refs_2_, ...), custom_call_target="tpu_custom_call" | custom-call | flops 3758096384 | bytes 11272192 | tf_op jit(solution)/shard_map/weight_grads/pallas_call | solution.py:229
  105.0 2.9 %collective-permute-done.21 = bf16[64,1792]{1,0:T(8,128)(2,1)S(1)} collective-permute-done((bf16[64,1792]{1,0:T(8,128)(2,1)S(1)}, bf16[64,1792]{1,0:T(8,128)(2,1)S(1)}, u32[]{:S(2)}, u32[]{:S(2)}) %collective-permute-start.21) | collective-permute-done | bytes 229408 | tf_op jit(solution)/shard_map/ppermute | solution.py:13
  108.3 1.1 convolution_convert_fusion.2
  (52 shorter events, 7.7 us)
Async XLA Ops:
  2.4 9.4 %collective-permute-start = (bf16[64,1792]{1,0:T(8,128)(2,1)S(1)}, bf16[64,1792]{1,0:T(8,128)(2,1)S(1)}, u32[]{:S(2)}, u32[]{:S(2)}) collective-permute-start(bf16[64,1792]{1,0:T(8,128)(2,1)S(1)} %get-tuple-element.27), channel_id=1, source_target_pairs={{0,28},{4,24},{8,20},{12,16},{16,12},{20,8},{24,4},{28,0},{1,29},{... | collective-permute-start | bytes 688136 | tf_op jit(solution)/shard_map/ppermute | solution.py:13
  5.8 11.0 %collective-permute-start.2 = (bf16[64,1792]{1,0:T(8,128)(2,1)S(1)}, bf16[64,1792]{1,0:T(8,128)(2,1)S(1)}, u32[]{:S(2)}, u32[]{:S(2)}) collective-permute-start(bf16[64,1792]{1,0:T(8,128)(2,1)S(1)} %get-tuple-element.28), channel_id=1, source_target_pairs={{0,20},{4,16},{8,28},{12,24},{16,4},{20,0},{24,12},{28,8},{1,21},{... | collective-permute-start | bytes 688136 | tf_op jit(solution)/shard_map/ppermute | solution.py:13
  6.6 11.1 %collective-permute-start.4 = (bf16[64,1792]{1,0:T(8,128)(2,1)S(1)}, bf16[64,1792]{1,0:T(8,128)(2,1)S(1)}, u32[]{:S(2)}, u32[]{:S(2)}) collective-permute-start(bf16[64,1792]{1,0:T(8,128)(2,1)S(1)} %get-tuple-element.29), channel_id=1, source_target_pairs={{0,12},{4,8},{8,4},{12,0},{16,28},{20,24},{24,20},{28,16},{1,13},{... | collective-permute-start | bytes 688136 | tf_op jit(solution)/shard_map/ppermute | solution.py:13
  6.6 11.2 %collective-permute-start.6 = (bf16[64,1792]{1,0:T(8,128)(2,1)S(1)}, bf16[64,1792]{1,0:T(8,128)(2,1)S(1)}, u32[]{:S(2)}, u32[]{:S(2)}) collective-permute-start(bf16[64,1792]{1,0:T(8,128)(2,1)S(1)} %get-tuple-element.30.refs_3_.refs_4_), channel_id=1, source_target_pairs={{0,4},{4,0},{8,12},{12,8},{16,20},{20,16},{24,28},{28,24},{1,5},{5... | collective-permute-start | bytes 688136 | tf_op jit(solution)/shard_map/ppermute | solution.py:13
  6.6 0.7 copy-start
  7.3 0.7 copy-start.1
  11.8 12.1 %collective-permute-start.1 = (bf16[64,1792]{1,0:T(8,128)(2,1)S(1)}, bf16[64,1792]{1,0:T(8,128)(2,1)S(1)}, u32[]{:S(2)}, u32[]{:S(2)}) collective-permute-start(bf16[64,1792]{1,0:T(8,128)(2,1)S(1)} %collective-permute-done.refs_0_.refs_3_), channel_id=1, source_target_pairs={{0,4},{4,0},{8,12},{12,8},{16,20},{20,16},{24,28},{28,24},{1,5},{5... | collective-permute-start | bytes 688136 | tf_op jit(solution)/shard_map/ppermute | solution.py:13
  16.8 7.2 %collective-permute-start.3 = (bf16[64,1792]{1,0:T(8,128)(2,1)S(1)}, bf16[64,1792]{1,0:T(8,128)(2,1)S(1)}, u32[]{:S(2)}, u32[]{:S(2)}) collective-permute-start(bf16[64,1792]{1,0:T(8,128)(2,1)S(1)} %collective-permute-done.2.refs_1_.refs_2_), channel_id=1, source_target_pairs={{0,4},{4,0},{8,12},{12,8},{16,20},{20,16},{24,28},{28,24},{1,5},{5... | collective-permute-start | bytes 688136 | tf_op jit(solution)/shard_map/ppermute | solution.py:13
  17.7 6.3 %collective-permute-start.5 = (bf16[64,1792]{1,0:T(8,128)(2,1)S(1)}, bf16[64,1792]{1,0:T(8,128)(2,1)S(1)}, u32[]{:S(2)}, u32[]{:S(2)}) collective-permute-start(bf16[64,1792]{1,0:T(8,128)(2,1)S(1)} %collective-permute-done.4.refs_2_.refs_1_), channel_id=1, source_target_pairs={{0,4},{4,0},{8,12},{12,8},{16,20},{20,16},{24,28},{28,24},{1,5},{5... | collective-permute-start | bytes 688136 | tf_op jit(solution)/shard_map/ppermute | solution.py:13
  20.0 11.0 %collective-permute-start.8 = (bf16[64,2048]{1,0:T(8,128)(2,1)S(1)}, bf16[64,2048]{1,0:T(8,128)(2,1)S(1)}, u32[]{:S(2)}, u32[]{:S(2)}) collective-permute-start(bf16[64,2048]{1,0:T(8,128)(2,1)S(1)} %get-tuple-element.56), channel_id=1, source_target_pairs={{0,1},{1,2},{2,3},{3,0},{4,5},{5,6},{6,7},{7,4},{8,9},{9,10},{10,1... | collective-permute-start | bytes 786440 | tf_op jit(solution)/shard_map/ppermute | solution.py:273
  21.8 24.7 %collective-permute-start.11 = (bf16[64,2048]{1,0:T(8,128)(2,1)S(1)}, bf16[64,2048]{1,0:T(8,128)(2,1)S(1)}, u32[]{:S(2)}, u32[]{:S(2)}) collective-permute-start(bf16[64,2048]{1,0:T(8,128)(2,1)S(1)} %get-tuple-element.31), channel_id=1, source_target_pairs={{0,3},{1,0},{2,1},{3,2},{4,7},{5,4},{6,5},{7,6},{8,11},{9,8},{10,9... | collective-permute-start | bytes 786440 | tf_op jit(solution)/shard_map/ppermute | solution.py:273
  26.0 27.6 %copy-start.2 = (bf16[1,128,1024]{2,1,0:T(8,128)(2,1)S(1)}, bf16[1,128,1024]{2,1,0:T(8,128)(2,1)}, u32[]{:S(2)}) copy-start(bf16[1,128,1024]{2,1,0:T(8,128)(2,1)} %param.13) | copy-start | bytes 786436
  26.1 16.2 %collective-permute-start.7 = (bf16[64,2048]{1,0:T(8,128)(2,1)S(1)}, bf16[64,2048]{1,0:T(8,128)(2,1)S(1)}, u32[]{:S(2)}, u32[]{:S(2)}) collective-permute-start(bf16[64,2048]{1,0:T(8,128)(2,1)S(1)} %get-tuple-element.32), channel_id=1, source_target_pairs={{0,1},{1,2},{2,3},{3,0},{4,5},{5,6},{6,7},{7,4},{8,9},{9,10},{10,1... | collective-permute-start | bytes 786440 | tf_op jit(solution)/shard_map/ppermute | solution.py:273
  26.2 31.5 %collective-permute-start.12 = (bf16[64,2048]{1,0:T(8,128)(2,1)S(1)}, bf16[64,2048]{1,0:T(8,128)(2,1)S(1)}, u32[]{:S(2)}, u32[]{:S(2)}) collective-permute-start(bf16[64,2048]{1,0:T(8,128)(2,1)S(1)} %get-tuple-element.33), channel_id=1, source_target_pairs={{0,3},{1,0},{2,1},{3,2},{4,7},{5,4},{6,5},{7,6},{8,11},{9,8},{10,9... | collective-permute-start | bytes 786440 | tf_op jit(solution)/shard_map/ppermute | solution.py:273
  31.1 22.4 %collective-permute-start.10 = (bf16[64,2048]{1,0:T(8,128)(2,1)S(1)}, bf16[64,2048]{1,0:T(8,128)(2,1)S(1)}, u32[]{:S(2)}, u32[]{:S(2)}) collective-permute-start(bf16[64,2048]{1,0:T(8,128)(2,1)S(1)} %fusion.8), channel_id=1, source_target_pairs={{0,1},{1,2},{2,3},{3,0},{4,5},{5,6},{6,7},{7,4},{8,9},{9,10},{10,1... | collective-permute-start | bytes 786440 | tf_op jit(solution)/shard_map/ppermute | solution.py:273
  42.4 16.9 %collective-permute-start.9 = (bf16[64,2048]{1,0:T(8,128)(2,1)S(1)}, bf16[64,2048]{1,0:T(8,128)(2,1)S(1)}, u32[]{:S(2)}, u32[]{:S(2)}) collective-permute-start(bf16[64,2048]{1,0:T(8,128)(2,1)S(1)} %fusion.9), channel_id=1, source_target_pairs={{0,1},{1,2},{2,3},{3,0},{4,5},{5,6},{6,7},{7,4},{8,9},{9,10},{10,1... | collective-permute-start | bytes 786440 | tf_op jit(solution)/shard_map/ppermute | solution.py:273
  53.8 11.1 %collective-permute-start.13 = (bf16[64,2048]{1,0:T(8,128)(2,1)S(1)}, bf16[64,2048]{1,0:T(8,128)(2,1)S(1)}, u32[]{:S(2)}, u32[]{:S(2)}) collective-permute-start(bf16[64,2048]{1,0:T(8,128)(2,1)S(1)} %pad_maximum_fusion), channel_id=1, source_target_pairs={{0,1},{1,2},{2,3},{3,0},{4,5},{5,6},{6,7},{7,4},{8,9},{9,10},{10,1... | collective-permute-start | bytes 786440 | tf_op jit(solution)/shard_map/ppermute | solution.py:273
  53.9 16.8 %collective-permute-start.14 = (bf16[64,2048]{1,0:T(8,128)(2,1)S(1)}, bf16[64,2048]{1,0:T(8,128)(2,1)S(1)}, u32[]{:S(2)}, u32[]{:S(2)}) collective-permute-start(bf16[64,2048]{1,0:T(8,128)(2,1)S(1)} %pad_maximum_fusion), channel_id=1, source_target_pairs={{0,3},{1,0},{2,1},{3,2},{4,7},{5,4},{6,5},{7,6},{8,11},{9,8},{10,9... | collective-permute-start | bytes 786440 | tf_op jit(solution)/shard_map/ppermute | solution.py:273
  59.6 16.6 %collective-permute-start.17 = (bf16[64,2048]{1,0:T(8,128)(2,1)S(1)}, bf16[64,2048]{1,0:T(8,128)(2,1)S(1)}, u32[]{:S(2)}, u32[]{:S(2)}) collective-permute-start(bf16[64,2048]{1,0:T(8,128)(2,1)S(1)} %pad_maximum_fusion.1), channel_id=1, source_target_pairs={{0,1},{1,2},{2,3},{3,0},{4,5},{5,6},{6,7},{7,4},{8,9},{9,10},{10,1... | collective-permute-start | bytes 786440 | tf_op jit(solution)/shard_map/ppermute | solution.py:273
  59.6 22.0 %collective-permute-start.16 = (bf16[64,2048]{1,0:T(8,128)(2,1)S(1)}, bf16[64,2048]{1,0:T(8,128)(2,1)S(1)}, u32[]{:S(2)}, u32[]{:S(2)}) collective-permute-start(bf16[64,2048]{1,0:T(8,128)(2,1)S(1)} %pad_maximum_fusion.1), channel_id=1, source_target_pairs={{0,3},{1,0},{2,1},{3,2},{4,7},{5,4},{6,5},{7,6},{8,11},{9,8},{10,9... | collective-permute-start | bytes 786440 | tf_op jit(solution)/shard_map/ppermute | solution.py:273
  64.9 22.5 %collective-permute-start.15 = (bf16[64,2048]{1,0:T(8,128)(2,1)S(1)}, bf16[64,2048]{1,0:T(8,128)(2,1)S(1)}, u32[]{:S(2)}, u32[]{:S(2)}) collective-permute-start(bf16[64,2048]{1,0:T(8,128)(2,1)S(1)} %collective-permute-done.13), channel_id=1, source_target_pairs={{0,1},{1,2},{2,3},{3,0},{4,5},{5,6},{6,7},{7,4},{8,9},{9,10},{10,1... | collective-permute-start | bytes 786440 | tf_op jit(solution)/shard_map/ppermute | solution.py:273
  76.2 16.3 %collective-permute-start.18 = (bf16[64,2048]{1,0:T(8,128)(2,1)S(1)}, bf16[64,2048]{1,0:T(8,128)(2,1)S(1)}, u32[]{:S(2)}, u32[]{:S(2)}) collective-permute-start(bf16[64,2048]{1,0:T(8,128)(2,1)S(1)} %collective-permute-done.17), channel_id=1, source_target_pairs={{0,1},{1,2},{2,3},{3,0},{4,5},{5,6},{6,7},{7,4},{8,9},{9,10},{10,1... | collective-permute-start | bytes 786440 | tf_op jit(solution)/shard_map/ppermute | solution.py:273
  89.6 3.0 %collective-permute-start.19 = (bf16[256,1792]{1,0:T(8,128)(2,1)S(1)}, bf16[256,1792]{1,0:T(8,128)(2,1)S(1)}, u32[]{:S(2)}, u32[]{:S(2)}) collective-permute-start(bf16[256,1792]{1,0:T(8,128)(2,1)S(1)} %convolution_convert_fusion.1), channel_id=1, source_target_pairs={{0,4},{4,0},{8,12},{12,8},{16,20},{20,16},{24,28},{28,24},{1,5},{5... | collective-permute-start | bytes 2752520 | tf_op jit(solution)/shard_map/ppermute | solution.py:13
  94.9 10.1 %collective-permute-start.20 = (bf16[64,1792]{1,0:T(8,128)(2,1)S(1)}, bf16[64,1792]{1,0:T(8,128)(2,1)S(1)}, u32[]{:S(2)}, u32[]{:S(2)}) collective-permute-start(bf16[64,1792]{1,0:T(8,128)(2,1)S(1)} %get-tuple-element.50), channel_id=1, source_target_pairs={{0,24},{4,28},{8,16},{12,20},{16,8},{20,12},{24,0},{28,4},{1,25},{... | collective-permute-start | bytes 688136 | tf_op jit(solution)/shard_map/ppermute | solution.py:13
  96.4 11.5 %collective-permute-start.21 = (bf16[64,1792]{1,0:T(8,128)(2,1)S(1)}, bf16[64,1792]{1,0:T(8,128)(2,1)S(1)}, u32[]{:S(2)}, u32[]{:S(2)}) collective-permute-start(bf16[64,1792]{1,0:T(8,128)(2,1)S(1)} %get-tuple-element.53), channel_id=1, source_target_pairs={{0,16},{4,20},{8,24},{12,28},{16,0},{20,4},{24,8},{28,12},{1,17},{... | collective-permute-start | bytes 688136 | tf_op jit(solution)/shard_map/ppermute | solution.py:13
  97.9 10.4 %copy-start.3 = (bf16[256,128]{1,0:T(8,128)(2,1)S(1)}, bf16[256,128]{1,0:T(8,128)(2,1)}, u32[]{:S(2)}) copy-start(bf16[256,128]{1,0:T(8,128)(2,1)} %get-tuple-element.48) | copy-start | bytes 196612
  97.9 10.4 %collective-permute-start.22 = (bf16[64,1792]{1,0:T(8,128)(2,1)S(1)}, bf16[64,1792]{1,0:T(8,128)(2,1)S(1)}, u32[]{:S(2)}, u32[]{:S(2)}) collective-permute-start(bf16[64,1792]{1,0:T(8,128)(2,1)S(1)} %get-tuple-element.52), channel_id=1, source_target_pairs={{0,8},{4,12},{8,0},{12,4},{16,24},{20,28},{24,16},{28,20},{1,9},{5... | collective-permute-start | bytes 688136 | tf_op jit(solution)/shard_map/ppermute | solution.py:13

commit v13 on v12

--- a/solution.py
+++ b/solution.py
@@ -155,7 +155,7 @@
             transcendentals=0,
         ),
         name="pack_rows",
-    )(counts, pltpu.with_memory_space_constraint(tokens, pltpu.HBM))
+    )(counts, tokens)
     return chooser, packed
 
 

time: 110 us -> 110 us (level)
  no operation moved by 1% of the time
where the time goes in v13:
time: 110 us; the launch traced here: 109 us
  waiting for transfers between devices  43.1 us (39%)
  starting transfers between devices  40.8 us (37%)
  Pallas kernels  15.9 us (14%)
  matrix products  5.3 us (5%)
  local copies, waits for them, and re-layouts  1.83 us (2%)
  other arithmetic  1.69 us (2%)
    ppermute x12, waiting for transfers between devices, send(): self.came[way] = lax.ppermute(value, 'fsdp', ring)  34.4 us
    ppermute x12, starting transfers between devices, send(): self.came[way] = lax.ppermute(value, 'fsdp', ring)  31.8 us
    ppermute x11, starting transfers between devices, swap(): return lax.ppermute(value, axis, pairs)  8.93 us
    ppermute x11, waiting for transfers between devices, swap(): return lax.ppermute(value, axis, pairs)  8.68 us
    pallas_call x1, Pallas kernels, weight_grads(): pl.pallas_call(lambda *refs: weight_kernel(count, *refs), out_shape=(out,...  6.59 us
    dot_general x2, matrix products, back(): lax.dot_general(whole, weights, (((1,), (1,)), ((), ())), preferred_eleme...  4.21 us
    pallas_call x2, Pallas kernels, projected(): pl.pallas_call(project_kernel, out_shape=jax.ShapeDtypeStruct((count, cap...  4.18 us
    pallas_call x1, Pallas kernels, scaled_weights(): pl.pallas_call(lambda *refs: scale_kernel(sub, *refs), out_shape=jax.Shap...  3.3 us
  transfers between devices with their start and end apart: 23, of which 15 were waited for; matrix products, arithmetic and copies ran while one was open for 4% of the time, Pallas kernels for 13%

profile of v13, /device:TPU:0, one launch (start us, length us, event | category | flops | bytes accessed | tf_op | source)
XLA Modules:
  0.0 109.4 jit_solution(7319928278384843445)
XLA Ops:
  0.6 1.8 %pack_rows.1 = (bf16[256,128]{1,0:T(8,128)(2,1)}, bf16[64,1792]{1,0:T(8,128)(2,1)S(1)}, bf16[64,1792]{1,0:T(8,128)(2,1)S(1)}, bf16[64,1792]{1,0:T(8,128)(2,1)S(1)}, bf16[64,1792]{1,0:T(8,128)(2,1)S(1)}) custom-call(s32[1,4]{1,0:T(1,128)} %counts_ref.1, bf16[128,1792]{1,0:T(8,128)(2,1)} %tokens_ref.1), custom_call_target="tpu_custom_call" | custom-call | flops 117440512 | bytes 1376256 | tf_op jit(solution)/shard_map/pack_rows/pallas_call | solution.py:141
  2.4 3.3 %collective-permute-start = (bf16[64,1792]{1,0:T(8,128)(2,1)S(1)}, bf16[64,1792]{1,0:T(8,128)(2,1)S(1)}, u32[]{:S(2)}, u32[]{:S(2)}) collective-permute-start(bf16[64,1792]{1,0:T(8,128)(2,1)S(1)} %get-tuple-element.27), channel_id=1, source_target_pairs={{0,28},{4,24},{8,20},{12,16},{16,12},{20,8},{24,4},{28,0},{1,29},{... | collective-permute-start | bytes 688136 | tf_op jit(solution)/shard_map/ppermute | solution.py:13
  8.0 3.3 %scale_weights.1.refs_4_ = bf16[1792,2048]{1,0:T(8,128)(2,1)S(1)} custom-call(s32[1]{0:T(128)} %bitcast.refs_0_, bf16[1,1792,1024]{2,1,0:T(8,128)(2,1)} %refs_1_.1, bf16[1,1792,1024]{2,1,0:T(8,128)(2,1)} %refs_2_.1, f32[1,8,56]{2,1,0:T(8,128)S(1)} %bitcast.63, f32[1,8,56]{2,1,0:T(8,128)S(1)} %bitcast.64), custom_call_target="tpu_custom_call" | custom-call | flops 3670016 | bytes 14680064 | tf_op jit(solution)/shard_map/scale_weights/pallas_call | solution.py:84
  11.8 0.8 collective-permute-start.1
  12.6 4.1 %collective-permute-done.2.refs_1_.refs_2_ = bf16[64,1792]{1,0:T(8,128)(2,1)S(1)} collective-permute-done((bf16[64,1792]{1,0:T(8,128)(2,1)S(1)}, bf16[64,1792]{1,0:T(8,128)(2,1)S(1)}, u32[]{:S(2)}, u32[]{:S(2)}) %collective-permute-start.2) | collective-permute-done | bytes 229408 | tf_op jit(solution)/shard_map/ppermute | solution.py:13
  17.8 2.1 %project.3 = bf16[4,64,2048]{2,1,0:T(8,128)(2,1)S(1)} custom-call(bf16[64,1792]{1,0:T(8,128)(2,1)S(1)} %collective-permute-done.refs_0_.refs_3_, bf16[64,1792]{1,0:T(8,128)(2,1)S(1)} %collective-permute-done.2.refs_1_.refs_2_, bf16[64,1792]{1,0:T(8,128)(2,1)S(1)} %collective-permute-done.4.refs_2_.refs_1_, ...), custom_call_target="tpu_custom_call" | custom-call | flops 1879048192 | bytes 9306112 | tf_op jit(solution)/shard_map/project/pallas_call | solution.py:181
  20.0 1.9 %collective-permute-start.8 = (bf16[64,2048]{1,0:T(8,128)(2,1)S(1)}, bf16[64,2048]{1,0:T(8,128)(2,1)S(1)}, u32[]{:S(2)}, u32[]{:S(2)}) collective-permute-start(bf16[64,2048]{1,0:T(8,128)(2,1)S(1)} %get-tuple-element.56), channel_id=1, source_target_pairs={{0,1},{1,2},{2,3},{3,0},{4,5},{5,6},{6,7},{7,4},{8,9},{9,10},{10,1... | collective-permute-start | bytes 786440 | tf_op jit(solution)/shard_map/ppermute | solution.py:273
  21.8 2.1 %collective-permute-start.11 = (bf16[64,2048]{1,0:T(8,128)(2,1)S(1)}, bf16[64,2048]{1,0:T(8,128)(2,1)S(1)}, u32[]{:S(2)}, u32[]{:S(2)}) collective-permute-start(bf16[64,2048]{1,0:T(8,128)(2,1)S(1)} %get-tuple-element.31), channel_id=1, source_target_pairs={{0,3},{1,0},{2,1},{3,2},{4,7},{5,4},{6,5},{7,6},{8,11},{9,8},{10,9... | collective-permute-start | bytes 786440 | tf_op jit(solution)/shard_map/ppermute | solution.py:273
  23.9 2.1 %project.2 = bf16[4,64,2048]{2,1,0:T(8,128)(2,1)S(1)} custom-call(bf16[64,1792]{1,0:T(8,128)(2,1)S(1)} %collective-permute-done.1.refs_0_.refs_7_, bf16[64,1792]{1,0:T(8,128)(2,1)S(1)} %collective-permute-done.3.refs_1_.refs_6_, bf16[64,1792]{1,0:T(8,128)(2,1)S(1)} %collective-permute-done.5.refs_2_.refs_5_, ...), custom_call_target="tpu_custom_call" | custom-call | flops 1879048192 | bytes 9306112 | tf_op jit(solution)/shard_map/project/pallas_call | solution.py:181
  26.2 3.8 %collective-permute-start.12 = (bf16[64,2048]{1,0:T(8,128)(2,1)S(1)}, bf16[64,2048]{1,0:T(8,128)(2,1)S(1)}, u32[]{:S(2)}, u32[]{:S(2)}) collective-permute-start(bf16[64,2048]{1,0:T(8,128)(2,1)S(1)} %get-tuple-element.33), channel_id=1, source_target_pairs={{0,3},{1,0},{2,1},{3,2},{4,7},{5,4},{6,5},{7,6},{8,11},{9,8},{10,9... | collective-permute-start | bytes 786440 | tf_op jit(solution)/shard_map/ppermute | solution.py:273
  30.0 1.0 collective-permute-done.8
  31.1 4.3 %collective-permute-start.10 = (bf16[64,2048]{1,0:T(8,128)(2,1)S(1)}, bf16[64,2048]{1,0:T(8,128)(2,1)S(1)}, u32[]{:S(2)}, u32[]{:S(2)}) collective-permute-start(bf16[64,2048]{1,0:T(8,128)(2,1)S(1)} %fusion.8), channel_id=1, source_target_pairs={{0,1},{1,2},{2,3},{3,0},{4,5},{5,6},{6,7},{7,4},{8,9},{9,10},{10,1... | collective-permute-start | bytes 786440 | tf_op jit(solution)/shard_map/ppermute | solution.py:273
  35.4 6.9 %collective-permute-done.7 = bf16[64,2048]{1,0:T(8,128)(2,1)S(1)} collective-permute-done((bf16[64,2048]{1,0:T(8,128)(2,1)S(1)}, bf16[64,2048]{1,0:T(8,128)(2,1)S(1)}, u32[]{:S(2)}, u32[]{:S(2)}) %collective-permute-start.7) | collective-permute-done | bytes 262176 | tf_op jit(solution)/shard_map/ppermute | solution.py:273
  42.4 4.2 %collective-permute-start.9 = (bf16[64,2048]{1,0:T(8,128)(2,1)S(1)}, bf16[64,2048]{1,0:T(8,128)(2,1)S(1)}, u32[]{:S(2)}, u32[]{:S(2)}) collective-permute-start(bf16[64,2048]{1,0:T(8,128)(2,1)S(1)} %fusion.9), channel_id=1, source_target_pairs={{0,1},{1,2},{2,3},{3,0},{4,5},{5,6},{6,7},{7,4},{8,9},{9,10},{10,1... | collective-permute-start | bytes 786440 | tf_op jit(solution)/shard_map/ppermute | solution.py:273
  46.6 7.0 %collective-permute-done.10 = bf16[64,2048]{1,0:T(8,128)(2,1)S(1)} collective-permute-done((bf16[64,2048]{1,0:T(8,128)(2,1)S(1)}, bf16[64,2048]{1,0:T(8,128)(2,1)S(1)}, u32[]{:S(2)}, u32[]{:S(2)}) %collective-permute-start.10) | collective-permute-done | bytes 262176 | tf_op jit(solution)/shard_map/ppermute | solution.py:273
  53.9 3.8 %collective-permute-start.14 = (bf16[64,2048]{1,0:T(8,128)(2,1)S(1)}, bf16[64,2048]{1,0:T(8,128)(2,1)S(1)}, u32[]{:S(2)}, u32[]{:S(2)}) collective-permute-start(bf16[64,2048]{1,0:T(8,128)(2,1)S(1)} %pad_maximum_fusion), channel_id=1, source_target_pairs={{0,3},{1,0},{2,1},{3,2},{4,7},{5,4},{6,5},{7,6},{8,11},{9,8},{10,9... | collective-permute-start | bytes 786440 | tf_op jit(solution)/shard_map/ppermute | solution.py:273
  57.9 1.4 %collective-permute-done.9 = bf16[64,2048]{1,0:T(8,128)(2,1)S(1)} collective-permute-done((bf16[64,2048]{1,0:T(8,128)(2,1)S(1)}, bf16[64,2048]{1,0:T(8,128)(2,1)S(1)}, u32[]{:S(2)}, u32[]{:S(2)}) %collective-permute-start.9) | collective-permute-done | bytes 262176 | tf_op jit(solution)/shard_map/ppermute | solution.py:273
  59.6 3.8 %collective-permute-start.16 = (bf16[64,2048]{1,0:T(8,128)(2,1)S(1)}, bf16[64,2048]{1,0:T(8,128)(2,1)S(1)}, u32[]{:S(2)}, u32[]{:S(2)}) collective-permute-start(bf16[64,2048]{1,0:T(8,128)(2,1)S(1)} %pad_maximum_fusion.1), channel_id=1, source_target_pairs={{0,3},{1,0},{2,1},{3,2},{4,7},{5,4},{6,5},{7,6},{8,11},{9,8},{10,9... | collective-permute-start | bytes 786440 | tf_op jit(solution)/shard_map/ppermute | solution.py:273
  64.9 3.9 %collective-permute-start.15 = (bf16[64,2048]{1,0:T(8,128)(2,1)S(1)}, bf16[64,2048]{1,0:T(8,128)(2,1)S(1)}, u32[]{:S(2)}, u32[]{:S(2)}) collective-permute-start(bf16[64,2048]{1,0:T(8,128)(2,1)S(1)} %collective-permute-done.13), channel_id=1, source_target_pairs={{0,1},{1,2},{2,3},{3,0},{4,5},{5,6},{6,7},{7,4},{8,9},{9,10},{10,1... | collective-permute-start | bytes 786440 | tf_op jit(solution)/shard_map/ppermute | solution.py:273
  68.9 1.8 %collective-permute-done.14 = bf16[64,2048]{1,0:T(8,128)(2,1)S(1)} collective-permute-done((bf16[64,2048]{1,0:T(8,128)(2,1)S(1)}, bf16[64,2048]{1,0:T(8,128)(2,1)S(1)}, u32[]{:S(2)}, u32[]{:S(2)}) %collective-permute-start.14) | collective-permute-done | bytes 262176 | tf_op jit(solution)/shard_map/ppermute | solution.py:273
  70.7 5.4 %collective-permute-done.17 = bf16[64,2048]{1,0:T(8,128)(2,1)S(1)} collective-permute-done((bf16[64,2048]{1,0:T(8,128)(2,1)S(1)}, bf16[64,2048]{1,0:T(8,128)(2,1)S(1)}, u32[]{:S(2)}, u32[]{:S(2)}) %collective-permute-start.17) | collective-permute-done | bytes 262176 | tf_op jit(solution)/shard_map/ppermute | solution.py:273
  76.2 3.9 %collective-permute-start.18 = (bf16[64,2048]{1,0:T(8,128)(2,1)S(1)}, bf16[64,2048]{1,0:T(8,128)(2,1)S(1)}, u32[]{:S(2)}, u32[]{:S(2)}) collective-permute-start(bf16[64,2048]{1,0:T(8,128)(2,1)S(1)} %collective-permute-done.17), channel_id=1, source_target_pairs={{0,1},{1,2},{2,3},{3,0},{4,5},{5,6},{6,7},{7,4},{8,9},{9,10},{10,1... | collective-permute-start | bytes 786440 | tf_op jit(solution)/shard_map/ppermute | solution.py:273
  80.1 1.6 %collective-permute-done.16 = bf16[64,2048]{1,0:T(8,128)(2,1)S(1)} collective-permute-done((bf16[64,2048]{1,0:T(8,128)(2,1)S(1)}, bf16[64,2048]{1,0:T(8,128)(2,1)S(1)}, u32[]{:S(2)}, u32[]{:S(2)}) %collective-permute-start.16) | collective-permute-done | bytes 262176 | tf_op jit(solution)/shard_map/ppermute | solution.py:273
  81.7 5.8 %collective-permute-done.15 = bf16[64,2048]{1,0:T(8,128)(2,1)S(1)} collective-permute-done((bf16[64,2048]{1,0:T(8,128)(2,1)S(1)}, bf16[64,2048]{1,0:T(8,128)(2,1)S(1)}, u32[]{:S(2)}, u32[]{:S(2)}) %collective-permute-start.15) | collective-permute-done | bytes 262176 | tf_op jit(solution)/shard_map/ppermute | solution.py:273
  87.5 2.1 %convolution_convert_fusion.1 = bf16[256,1792]{1,0:T(8,128)(2,1)S(1)} fusion(bf16[256,2048]{1,0:T(8,128)(2,1)S(1)} %bitcast.61, bf16[1792,2048]{1,0:T(8,128)(2,1)S(1)} %scale_weights.1.refs_4_), kind=kOutput, calls=%fused_computation.1 | convolution fusion | flops 1879506944 | bytes 9306112 | tf_op jit(solution)/shard_map/dot_general | solution.py:353
  89.7 2.8 %collective-permute-done.18 = bf16[64,2048]{1,0:T(8,128)(2,1)S(1)} collective-permute-done((bf16[64,2048]{1,0:T(8,128)(2,1)S(1)}, bf16[64,2048]{1,0:T(8,128)(2,1)S(1)}, u32[]{:S(2)}, u32[]{:S(2)}) %collective-permute-start.18) | collective-permute-done | bytes 262176 | tf_op jit(solution)/shard_map/ppermute | solution.py:273
  92.5 2.1 %convolution_convert_fusion = bf16[256,1792]{1,0:T(8,128)(2,1)S(1)} fusion(bf16[256,2048]{1,0:T(8,128)(2,1)S(1)} %bitcast.59, bf16[1792,2048]{1,0:T(8,128)(2,1)S(1)} %scale_weights.1.refs_4_), kind=kOutput, calls=%fused_computation | convolution fusion | flops 1879506944 | bytes 9306112 | tf_op jit(solution)/shard_map/dot_general | solution.py:353
  94.9 1.6 %collective-permute-start.20 = (bf16[64,1792]{1,0:T(8,128)(2,1)S(1)}, bf16[64,1792]{1,0:T(8,128)(2,1)S(1)}, u32[]{:S(2)}, u32[]{:S(2)}) collective-permute-start(bf16[64,1792]{1,0:T(8,128)(2,1)S(1)} %get-tuple-element.50), channel_id=1, source_target_pairs={{0,24},{4,28},{8,16},{12,20},{16,8},{20,12},{24,0},{28,4},{1,25},{... | collective-permute-start | bytes 688136 | tf_op jit(solution)/shard_map/ppermute | solution.py:13
  96.4 1.4 %collective-permute-start.21 = (bf16[64,1792]{1,0:T(8,128)(2,1)S(1)}, bf16[64,1792]{1,0:T(8,128)(2,1)S(1)}, u32[]{:S(2)}, u32[]{:S(2)}) collective-permute-start(bf16[64,1792]{1,0:T(8,128)(2,1)S(1)} %get-tuple-element.53), channel_id=1, source_target_pairs={{0,16},{4,20},{8,24},{12,28},{16,0},{20,4},{24,8},{28,12},{1,17},{... | collective-permute-start | bytes 688136 | tf_op jit(solution)/shard_map/ppermute | solution.py:13
  98.4 6.6 %weight_grads.1 = (bf16[1,1792,1024]{2,1,0:T(8,128)(2,1)}, bf16[1,1792,1024]{2,1,0:T(8,128)(2,1)}) custom-call(bf16[64,1792]{1,0:T(8,128)(2,1)S(1)} %collective-permute-done.6.refs_3_.refs_0_, bf16[64,1792]{1,0:T(8,128)(2,1)S(1)} %collective-permute-done.4.refs_2_.refs_1_, bf16[64,1792]{1,0:T(8,128)(2,1)S(1)} %collective-permute-done.2.refs_1_.refs_2_, ...), custom_call_target="tpu_custom_call" | custom-call | flops 3758096384 | bytes 11272192 | tf_op jit(solution)/shard_map/weight_grads/pallas_call | solution.py:229
  105.0 2.9 %collective-permute-done.21 = bf16[64,1792]{1,0:T(8,128)(2,1)S(1)} collective-permute-done((bf16[64,1792]{1,0:T(8,128)(2,1)S(1)}, bf16[64,1792]{1,0:T(8,128)(2,1)S(1)}, u32[]{:S(2)}, u32[]{:S(2)}) %collective-permute-start.21) | collective-permute-done | bytes 229408 | tf_op jit(solution)/shard_map/ppermute | solution.py:13
  108.3 1.1 convolution_convert_fusion.2
  (52 shorter events, 7.7 us)
Async XLA Ops:
  2.4 9.4 %collective-permute-start = (bf16[64,1792]{1,0:T(8,128)(2,1)S(1)}, bf16[64,1792]{1,0:T(8,128)(2,1)S(1)}, u32[]{:S(2)}, u32[]{:S(2)}) collective-permute-start(bf16[64,1792]{1,0:T(8,128)(2,1)S(1)} %get-tuple-element.27), channel_id=1, source_target_pairs={{0,28},{4,24},{8,20},{12,16},{16,12},{20,8},{24,4},{28,0},{1,29},{... | collective-permute-start | bytes 688136 | tf_op jit(solution)/shard_map/ppermute | solution.py:13
  5.8 11.0 %collective-permute-start.2 = (bf16[64,1792]{1,0:T(8,128)(2,1)S(1)}, bf16[64,1792]{1,0:T(8,128)(2,1)S(1)}, u32[]{:S(2)}, u32[]{:S(2)}) collective-permute-start(bf16[64,1792]{1,0:T(8,128)(2,1)S(1)} %get-tuple-element.28), channel_id=1, source_target_pairs={{0,20},{4,16},{8,28},{12,24},{16,4},{20,0},{24,12},{28,8},{1,21},{... | collective-permute-start | bytes 688136 | tf_op jit(solution)/shard_map/ppermute | solution.py:13
  6.6 11.1 %collective-permute-start.4 = (bf16[64,1792]{1,0:T(8,128)(2,1)S(1)}, bf16[64,1792]{1,0:T(8,128)(2,1)S(1)}, u32[]{:S(2)}, u32[]{:S(2)}) collective-permute-start(bf16[64,1792]{1,0:T(8,128)(2,1)S(1)} %get-tuple-element.29), channel_id=1, source_target_pairs={{0,12},{4,8},{8,4},{12,0},{16,28},{20,24},{24,20},{28,16},{1,13},{... | collective-permute-start | bytes 688136 | tf_op jit(solution)/shard_map/ppermute | solution.py:13
  6.6 11.2 %collective-permute-start.6 = (bf16[64,1792]{1,0:T(8,128)(2,1)S(1)}, bf16[64,1792]{1,0:T(8,128)(2,1)S(1)}, u32[]{:S(2)}, u32[]{:S(2)}) collective-permute-start(bf16[64,1792]{1,0:T(8,128)(2,1)S(1)} %get-tuple-element.30.refs_3_.refs_4_), channel_id=1, source_target_pairs={{0,4},{4,0},{8,12},{12,8},{16,20},{20,16},{24,28},{28,24},{1,5},{5... | collective-permute-start | bytes 688136 | tf_op jit(solution)/shard_map/ppermute | solution.py:13
  6.6 0.7 copy-start
  7.3 0.7 copy-start.1
  11.8 12.1 %collective-permute-start.1 = (bf16[64,1792]{1,0:T(8,128)(2,1)S(1)}, bf16[64,1792]{1,0:T(8,128)(2,1)S(1)}, u32[]{:S(2)}, u32[]{:S(2)}) collective-permute-start(bf16[64,1792]{1,0:T(8,128)(2,1)S(1)} %collective-permute-done.refs_0_.refs_3_), channel_id=1, source_target_pairs={{0,4},{4,0},{8,12},{12,8},{16,20},{20,16},{24,28},{28,24},{1,5},{5... | collective-permute-start | bytes 688136 | tf_op jit(solution)/shard_map/ppermute | solution.py:13
  16.8 7.2 %collective-permute-start.3 = (bf16[64,1792]{1,0:T(8,128)(2,1)S(1)}, bf16[64,1792]{1,0:T(8,128)(2,1)S(1)}, u32[]{:S(2)}, u32[]{:S(2)}) collective-permute-start(bf16[64,1792]{1,0:T(8,128)(2,1)S(1)} %collective-permute-done.2.refs_1_.refs_2_), channel_id=1, source_target_pairs={{0,4},{4,0},{8,12},{12,8},{16,20},{20,16},{24,28},{28,24},{1,5},{5... | collective-permute-start | bytes 688136 | tf_op jit(solution)/shard_map/ppermute | solution.py:13
  17.7 6.3 %collective-permute-start.5 = (bf16[64,1792]{1,0:T(8,128)(2,1)S(1)}, bf16[64,1792]{1,0:T(8,128)(2,1)S(1)}, u32[]{:S(2)}, u32[]{:S(2)}) collective-permute-start(bf16[64,1792]{1,0:T(8,128)(2,1)S(1)} %collective-permute-done.4.refs_2_.refs_1_), channel_id=1, source_target_pairs={{0,4},{4,0},{8,12},{12,8},{16,20},{20,16},{24,28},{28,24},{1,5},{5... | collective-permute-start | bytes 688136 | tf_op jit(solution)/shard_map/ppermute | solution.py:13
  20.0 11.0 %collective-permute-start.8 = (bf16[64,2048]{1,0:T(8,128)(2,1)S(1)}, bf16[64,2048]{1,0:T(8,128)(2,1)S(1)}, u32[]{:S(2)}, u32[]{:S(2)}) collective-permute-start(bf16[64,2048]{1,0:T(8,128)(2,1)S(1)} %get-tuple-element.56), channel_id=1, source_target_pairs={{0,1},{1,2},{2,3},{3,0},{4,5},{5,6},{6,7},{7,4},{8,9},{9,10},{10,1... | collective-permute-start | bytes 786440 | tf_op jit(solution)/shard_map/ppermute | solution.py:273
  21.8 24.7 %collective-permute-start.11 = (bf16[64,2048]{1,0:T(8,128)(2,1)S(1)}, bf16[64,2048]{1,0:T(8,128)(2,1)S(1)}, u32[]{:S(2)}, u32[]{:S(2)}) collective-permute-start(bf16[64,2048]{1,0:T(8,128)(2,1)S(1)} %get-tuple-element.31), channel_id=1, source_target_pairs={{0,3},{1,0},{2,1},{3,2},{4,7},{5,4},{6,5},{7,6},{8,11},{9,8},{10,9... | collective-permute-start | bytes 786440 | tf_op jit(solution)/shard_map/ppermute | solution.py:273
  26.0 27.6 %copy-start.2 = (bf16[1,128,1024]{2,1,0:T(8,128)(2,1)S(1)}, bf16[1,128,1024]{2,1,0:T(8,128)(2,1)}, u32[]{:S(2)}) copy-start(bf16[1,128,1024]{2,1,0:T(8,128)(2,1)} %param.13) | copy-start | bytes 786436
  26.1 16.2 %collective-permute-start.7 = (bf16[64,2048]{1,0:T(8,128)(2,1)S(1)}, bf16[64,2048]{1,0:T(8,128)(2,1)S(1)}, u32[]{:S(2)}, u32[]{:S(2)}) collective-permute-start(bf16[64,2048]{1,0:T(8,128)(2,1)S(1)} %get-tuple-element.32), channel_id=1, source_target_pairs={{0,1},{1,2},{2,3},{3,0},{4,5},{5,6},{6,7},{7,4},{8,9},{9,10},{10,1... | collective-permute-start | bytes 786440 | tf_op jit(solution)/shard_map/ppermute | solution.py:273
  26.2 31.5 %collective-permute-start.12 = (bf16[64,2048]{1,0:T(8,128)(2,1)S(1)}, bf16[64,2048]{1,0:T(8,128)(2,1)S(1)}, u32[]{:S(2)}, u32[]{:S(2)}) collective-permute-start(bf16[64,2048]{1,0:T(8,128)(2,1)S(1)} %get-tuple-element.33), channel_id=1, source_target_pairs={{0,3},{1,0},{2,1},{3,2},{4,7},{5,4},{6,5},{7,6},{8,11},{9,8},{10,9... | collective-permute-start | bytes 786440 | tf_op jit(solution)/shard_map/ppermute | solution.py:273
  31.1 22.4 %collective-permute-start.10 = (bf16[64,2048]{1,0:T(8,128)(2,1)S(1)}, bf16[64,2048]{1,0:T(8,128)(2,1)S(1)}, u32[]{:S(2)}, u32[]{:S(2)}) collective-permute-start(bf16[64,2048]{1,0:T(8,128)(2,1)S(1)} %fusion.8), channel_id=1, source_target_pairs={{0,1},{1,2},{2,3},{3,0},{4,5},{5,6},{6,7},{7,4},{8,9},{9,10},{10,1... | collective-permute-start | bytes 786440 | tf_op jit(solution)/shard_map/ppermute | solution.py:273
  42.4 16.9 %collective-permute-start.9 = (bf16[64,2048]{1,0:T(8,128)(2,1)S(1)}, bf16[64,2048]{1,0:T(8,128)(2,1)S(1)}, u32[]{:S(2)}, u32[]{:S(2)}) collective-permute-start(bf16[64,2048]{1,0:T(8,128)(2,1)S(1)} %fusion.9), channel_id=1, source_target_pairs={{0,1},{1,2},{2,3},{3,0},{4,5},{5,6},{6,7},{7,4},{8,9},{9,10},{10,1... | collective-permute-start | bytes 786440 | tf_op jit(solution)/shard_map/ppermute | solution.py:273
  53.8 11.1 %collective-permute-start.13 = (bf16[64,2048]{1,0:T(8,128)(2,1)S(1)}, bf16[64,2048]{1,0:T(8,128)(2,1)S(1)}, u32[]{:S(2)}, u32[]{:S(2)}) collective-permute-start(bf16[64,2048]{1,0:T(8,128)(2,1)S(1)} %pad_maximum_fusion), channel_id=1, source_target_pairs={{0,1},{1,2},{2,3},{3,0},{4,5},{5,6},{6,7},{7,4},{8,9},{9,10},{10,1... | collective-permute-start | bytes 786440 | tf_op jit(solution)/shard_map/ppermute | solution.py:273
  53.9 16.8 %collective-permute-start.14 = (bf16[64,2048]{1,0:T(8,128)(2,1)S(1)}, bf16[64,2048]{1,0:T(8,128)(2,1)S(1)}, u32[]{:S(2)}, u32[]{:S(2)}) collective-permute-start(bf16[64,2048]{1,0:T(8,128)(2,1)S(1)} %pad_maximum_fusion), channel_id=1, source_target_pairs={{0,3},{1,0},{2,1},{3,2},{4,7},{5,4},{6,5},{7,6},{8,11},{9,8},{10,9... | collective-permute-start | bytes 786440 | tf_op jit(solution)/shard_map/ppermute | solution.py:273
  59.6 16.6 %collective-permute-start.17 = (bf16[64,2048]{1,0:T(8,128)(2,1)S(1)}, bf16[64,2048]{1,0:T(8,128)(2,1)S(1)}, u32[]{:S(2)}, u32[]{:S(2)}) collective-permute-start(bf16[64,2048]{1,0:T(8,128)(2,1)S(1)} %pad_maximum_fusion.1), channel_id=1, source_target_pairs={{0,1},{1,2},{2,3},{3,0},{4,5},{5,6},{6,7},{7,4},{8,9},{9,10},{10,1... | collective-permute-start | bytes 786440 | tf_op jit(solution)/shard_map/ppermute | solution.py:273
  59.6 22.0 %collective-permute-start.16 = (bf16[64,2048]{1,0:T(8,128)(2,1)S(1)}, bf16[64,2048]{1,0:T(8,128)(2,1)S(1)}, u32[]{:S(2)}, u32[]{:S(2)}) collective-permute-start(bf16[64,2048]{1,0:T(8,128)(2,1)S(1)} %pad_maximum_fusion.1), channel_id=1, source_target_pairs={{0,3},{1,0},{2,1},{3,2},{4,7},{5,4},{6,5},{7,6},{8,11},{9,8},{10,9... | collective-permute-start | bytes 786440 | tf_op jit(solution)/shard_map/ppermute | solution.py:273
  64.9 22.5 %collective-permute-start.15 = (bf16[64,2048]{1,0:T(8,128)(2,1)S(1)}, bf16[64,2048]{1,0:T(8,128)(2,1)S(1)}, u32[]{:S(2)}, u32[]{:S(2)}) collective-permute-start(bf16[64,2048]{1,0:T(8,128)(2,1)S(1)} %collective-permute-done.13), channel_id=1, source_target_pairs={{0,1},{1,2},{2,3},{3,0},{4,5},{5,6},{6,7},{7,4},{8,9},{9,10},{10,1... | collective-permute-start | bytes 786440 | tf_op jit(solution)/shard_map/ppermute | solution.py:273
  76.2 16.3 %collective-permute-start.18 = (bf16[64,2048]{1,0:T(8,128)(2,1)S(1)}, bf16[64,2048]{1,0:T(8,128)(2,1)S(1)}, u32[]{:S(2)}, u32[]{:S(2)}) collective-permute-start(bf16[64,2048]{1,0:T(8,128)(2,1)S(1)} %collective-permute-done.17), channel_id=1, source_target_pairs={{0,1},{1,2},{2,3},{3,0},{4,5},{5,6},{6,7},{7,4},{8,9},{9,10},{10,1... | collective-permute-start | bytes 786440 | tf_op jit(solution)/shard_map/ppermute | solution.py:273
  89.6 3.0 %collective-permute-start.19 = (bf16[256,1792]{1,0:T(8,128)(2,1)S(1)}, bf16[256,1792]{1,0:T(8,128)(2,1)S(1)}, u32[]{:S(2)}, u32[]{:S(2)}) collective-permute-start(bf16[256,1792]{1,0:T(8,128)(2,1)S(1)} %convolution_convert_fusion.1), channel_id=1, source_target_pairs={{0,4},{4,0},{8,12},{12,8},{16,20},{20,16},{24,28},{28,24},{1,5},{5... | collective-permute-start | bytes 2752520 | tf_op jit(solution)/shard_map/ppermute | solution.py:13
  94.9 10.1 %collective-permute-start.20 = (bf16[64,1792]{1,0:T(8,128)(2,1)S(1)}, bf16[64,1792]{1,0:T(8,128)(2,1)S(1)}, u32[]{:S(2)}, u32[]{:S(2)}) collective-permute-start(bf16[64,1792]{1,0:T(8,128)(2,1)S(1)} %get-tuple-element.50), channel_id=1, source_target_pairs={{0,24},{4,28},{8,16},{12,20},{16,8},{20,12},{24,0},{28,4},{1,25},{... | collective-permute-start | bytes 688136 | tf_op jit(solution)/shard_map/ppermute | solution.py:13
  96.4 11.5 %collective-permute-start.21 = (bf16[64,1792]{1,0:T(8,128)(2,1)S(1)}, bf16[64,1792]{1,0:T(8,128)(2,1)S(1)}, u32[]{:S(2)}, u32[]{:S(2)}) collective-permute-start(bf16[64,1792]{1,0:T(8,128)(2,1)S(1)} %get-tuple-element.53), channel_id=1, source_target_pairs={{0,16},{4,20},{8,24},{12,28},{16,0},{20,4},{24,8},{28,12},{1,17},{... | collective-permute-start | bytes 688136 | tf_op jit(solution)/shard_map/ppermute | solution.py:13
  97.9 10.4 %copy-start.3 = (bf16[256,128]{1,0:T(8,128)(2,1)S(1)}, bf16[256,128]{1,0:T(8,128)(2,1)}, u32[]{:S(2)}) copy-start(bf16[256,128]{1,0:T(8,128)(2,1)} %get-tuple-element.48) | copy-start | bytes 196612
  97.9 10.4 %collective-permute-start.22 = (bf16[64,1792]{1,0:T(8,128)(2,1)S(1)}, bf16[64,1792]{1,0:T(8,128)(2,1)S(1)}, u32[]{:S(2)}, u32[]{:S(2)}) collective-permute-start(bf16[64,1792]{1,0:T(8,128)(2,1)S(1)} %get-tuple-element.52), channel_id=1, source_target_pairs={{0,8},{4,12},{8,0},{12,4},{16,24},{20,28},{24,16},{28,20},{1,9},{5... | collective-permute-start | bytes 688136 | tf_op jit(solution)/shard_map/ppermute | solution.py:13

commit v14 on v13

--- a/solution.py
+++ b/solution.py
@@ -117,14 +117,16 @@
     chip = lax.axis_index("expert") // 2
     row_total = tokens_ref.shape[0]
     capacity = out_refs[0].shape[0]
-    counts = counts_ref[...].astype(jnp.float32)
-    expert = lax.broadcasted_iota(jnp.int32, counts.shape, 1)
-    row = lax.broadcasted_iota(jnp.int32, (capacity, row_total), 1).astype(jnp.float32)
-    slot = lax.broadcasted_iota(jnp.int32, (capacity, row_total), 0).astype(jnp.float32)
+    experts = counts_ref.shape[1]
+    row = lax.broadcasted_iota(jnp.int32, (capacity, row_total), 1)
+    slot = lax.broadcasted_iota(jnp.int32, (capacity, row_total), 0)
     hits = []
     for mask in reversed(range(len(out_refs))):
-        first = jnp.sum(jnp.where(expert < (chip ^ mask), counts, 0.0), 1, keepdims=True)
-        live = jnp.sum(jnp.where(expert == (chip ^ mask), counts, 0.0), 1, keepdims=True)
+        first = live = jnp.int32(0)
+        for expert in range(experts):
+            count = counts_ref[0, expert]
+            first = first + jnp.where(expert < (chip ^ mask), count, 0)
+            live = jnp.where(expert == (chip ^ mask), count, live)
         hits.append(((row == first + slot) & (slot < live)).astype(jnp.float32))
     chooser = jnp.concatenate(hits, 0).astype(jnp.bfloat16)
     chooser_ref[...] = chooser
@@ -144,7 +146,7 @@
         + (block,) * experts,
         grid=(feat_cols // tile,),
         in_specs=[
-            pl.BlockSpec(counts.shape, lambda i: (0, 0)),
+            pl.BlockSpec(memory_space=pltpu.SMEM),
             pl.BlockSpec((row_total, tile), lambda i: (0, i)),
         ],
         out_specs=(pl.BlockSpec((experts * capacity, row_total), lambda i: (0, 0)),)

time: 110 us -> 110 us (level)
  no operation moved by 1% of the time
where the time goes in v14:
time: 110 us; the launch traced here: 109 us
  waiting for transfers between devices  42.9 us (39%)
  starting transfers between devices  40.9 us (37%)
  Pallas kernels  15.8 us (14%)
  matrix products  5.3 us (5%)
  local copies, waits for them, and re-layouts  1.83 us (2%)
  other arithmetic  1.69 us (2%)
    ppermute x12, waiting for transfers between devices, send(): self.came[way] = lax.ppermute(value, 'fsdp', ring)  34.2 us
    ppermute x12, starting transfers between devices, send(): self.came[way] = lax.ppermute(value, 'fsdp', ring)  32 us
    ppermute x11, starting transfers between devices, swap(): return lax.ppermute(value, axis, pairs)  8.93 us
    ppermute x11, waiting for transfers between devices, swap(): return lax.ppermute(value, axis, pairs)  8.69 us
    pallas_call x1, Pallas kernels, weight_grads(): pl.pallas_call(lambda *refs: weight_kernel(count, *refs), out_shape=(out,...  6.59 us
    dot_general x2, matrix products, back(): lax.dot_general(whole, weights, (((1,), (1,)), ((), ())), preferred_eleme...  4.22 us
    pallas_call x2, Pallas kernels, projected(): pl.pallas_call(project_kernel, out_shape=jax.ShapeDtypeStruct((count, cap...  4.18 us
    pallas_call x1, Pallas kernels, scaled_weights(): pl.pallas_call(lambda *refs: scale_kernel(sub, *refs), out_shape=jax.Shap...  3.3 us
  transfers between devices with their start and end apart: 23, of which 15 were waited for; matrix products, arithmetic and copies ran while one was open for 4% of the time, Pallas kernels for 13%

profile of v14, /device:TPU:0, one launch (start us, length us, event | category | flops | bytes accessed | tf_op | source)
XLA Modules:
  0.0 109.3 jit_solution(14080614920116704718)
XLA Ops:
  0.6 1.7 %pack_rows.1 = (bf16[256,128]{1,0:T(8,128)(2,1)}, bf16[64,1792]{1,0:T(8,128)(2,1)S(1)}, bf16[64,1792]{1,0:T(8,128)(2,1)S(1)}, bf16[64,1792]{1,0:T(8,128)(2,1)S(1)}, bf16[64,1792]{1,0:T(8,128)(2,1)S(1)}) custom-call(s32[1,4]{1,0:T(1,128)} %counts_ref.1, bf16[128,1792]{1,0:T(8,128)(2,1)} %tokens_ref.1), custom_call_target="tpu_custom_call" | custom-call | flops 117440512 | bytes 1376256 | tf_op jit(solution)/shard_map/pack_rows/pallas_call | solution.py:143
  2.4 3.3 %collective-permute-start = (bf16[64,1792]{1,0:T(8,128)(2,1)S(1)}, bf16[64,1792]{1,0:T(8,128)(2,1)S(1)}, u32[]{:S(2)}, u32[]{:S(2)}) collective-permute-start(bf16[64,1792]{1,0:T(8,128)(2,1)S(1)} %get-tuple-element.27), channel_id=1, source_target_pairs={{0,28},{4,24},{8,20},{12,16},{16,12},{20,8},{24,4},{28,0},{1,29},{... | collective-permute-start | bytes 688136 | tf_op jit(solution)/shard_map/ppermute | solution.py:13
  7.9 3.3 %scale_weights.1.refs_4_ = bf16[1792,2048]{1,0:T(8,128)(2,1)S(1)} custom-call(s32[1]{0:T(128)} %bitcast.refs_0_, bf16[1,1792,1024]{2,1,0:T(8,128)(2,1)} %refs_1_.1, bf16[1,1792,1024]{2,1,0:T(8,128)(2,1)} %refs_2_.1, f32[1,8,56]{2,1,0:T(8,128)S(1)} %bitcast.63, f32[1,8,56]{2,1,0:T(8,128)S(1)} %bitcast.64), custom_call_target="tpu_custom_call" | custom-call | flops 3670016 | bytes 14680064 | tf_op jit(solution)/shard_map/scale_weights/pallas_call | solution.py:84
  11.7 0.8 collective-permute-start.1
  12.5 4.1 %collective-permute-done.2.refs_1_.refs_2_ = bf16[64,1792]{1,0:T(8,128)(2,1)S(1)} collective-permute-done((bf16[64,1792]{1,0:T(8,128)(2,1)S(1)}, bf16[64,1792]{1,0:T(8,128)(2,1)S(1)}, u32[]{:S(2)}, u32[]{:S(2)}) %collective-permute-start.2) | collective-permute-done | bytes 229408 | tf_op jit(solution)/shard_map/ppermute | solution.py:13
  17.7 2.1 %project.3 = bf16[4,64,2048]{2,1,0:T(8,128)(2,1)S(1)} custom-call(bf16[64,1792]{1,0:T(8,128)(2,1)S(1)} %collective-permute-done.refs_0_.refs_3_, bf16[64,1792]{1,0:T(8,128)(2,1)S(1)} %collective-permute-done.2.refs_1_.refs_2_, bf16[64,1792]{1,0:T(8,128)(2,1)S(1)} %collective-permute-done.4.refs_2_.refs_1_, ...), custom_call_target="tpu_custom_call" | custom-call | flops 1879048192 | bytes 9306112 | tf_op jit(solution)/shard_map/project/pallas_call | solution.py:183
  19.9 1.9 %collective-permute-start.8 = (bf16[64,2048]{1,0:T(8,128)(2,1)S(1)}, bf16[64,2048]{1,0:T(8,128)(2,1)S(1)}, u32[]{:S(2)}, u32[]{:S(2)}) collective-permute-start(bf16[64,2048]{1,0:T(8,128)(2,1)S(1)} %get-tuple-element.56), channel_id=1, source_target_pairs={{0,1},{1,2},{2,3},{3,0},{4,5},{5,6},{6,7},{7,4},{8,9},{9,10},{10,1... | collective-permute-start | bytes 786440 | tf_op jit(solution)/shard_map/ppermute | solution.py:275
  21.8 2.1 %collective-permute-start.11 = (bf16[64,2048]{1,0:T(8,128)(2,1)S(1)}, bf16[64,2048]{1,0:T(8,128)(2,1)S(1)}, u32[]{:S(2)}, u32[]{:S(2)}) collective-permute-start(bf16[64,2048]{1,0:T(8,128)(2,1)S(1)} %get-tuple-element.31), channel_id=1, source_target_pairs={{0,3},{1,0},{2,1},{3,2},{4,7},{5,4},{6,5},{7,6},{8,11},{9,8},{10,9... | collective-permute-start | bytes 786440 | tf_op jit(solution)/shard_map/ppermute | solution.py:275
  23.9 2.1 %project.2 = bf16[4,64,2048]{2,1,0:T(8,128)(2,1)S(1)} custom-call(bf16[64,1792]{1,0:T(8,128)(2,1)S(1)} %collective-permute-done.1.refs_0_.refs_7_, bf16[64,1792]{1,0:T(8,128)(2,1)S(1)} %collective-permute-done.3.refs_1_.refs_6_, bf16[64,1792]{1,0:T(8,128)(2,1)S(1)} %collective-permute-done.5.refs_2_.refs_5_, ...), custom_call_target="tpu_custom_call" | custom-call | flops 1879048192 | bytes 9306112 | tf_op jit(solution)/shard_map/project/pallas_call | solution.py:183
  26.1 3.8 %collective-permute-start.12 = (bf16[64,2048]{1,0:T(8,128)(2,1)S(1)}, bf16[64,2048]{1,0:T(8,128)(2,1)S(1)}, u32[]{:S(2)}, u32[]{:S(2)}) collective-permute-start(bf16[64,2048]{1,0:T(8,128)(2,1)S(1)} %get-tuple-element.33), channel_id=1, source_target_pairs={{0,3},{1,0},{2,1},{3,2},{4,7},{5,4},{6,5},{7,6},{8,11},{9,8},{10,9... | collective-permute-start | bytes 786440 | tf_op jit(solution)/shard_map/ppermute | solution.py:275
  29.9 1.0 collective-permute-done.8
  31.0 4.3 %collective-permute-start.10 = (bf16[64,2048]{1,0:T(8,128)(2,1)S(1)}, bf16[64,2048]{1,0:T(8,128)(2,1)S(1)}, u32[]{:S(2)}, u32[]{:S(2)}) collective-permute-start(bf16[64,2048]{1,0:T(8,128)(2,1)S(1)} %fusion.8), channel_id=1, source_target_pairs={{0,1},{1,2},{2,3},{3,0},{4,5},{5,6},{6,7},{7,4},{8,9},{9,10},{10,1... | collective-permute-start | bytes 786440 | tf_op jit(solution)/shard_map/ppermute | solution.py:275
  35.3 6.9 %collective-permute-done.7 = bf16[64,2048]{1,0:T(8,128)(2,1)S(1)} collective-permute-done((bf16[64,2048]{1,0:T(8,128)(2,1)S(1)}, bf16[64,2048]{1,0:T(8,128)(2,1)S(1)}, u32[]{:S(2)}, u32[]{:S(2)}) %collective-permute-start.7) | collective-permute-done | bytes 262176 | tf_op jit(solution)/shard_map/ppermute | solution.py:275
  42.3 4.2 %collective-permute-start.9 = (bf16[64,2048]{1,0:T(8,128)(2,1)S(1)}, bf16[64,2048]{1,0:T(8,128)(2,1)S(1)}, u32[]{:S(2)}, u32[]{:S(2)}) collective-permute-start(bf16[64,2048]{1,0:T(8,128)(2,1)S(1)} %fusion.9), channel_id=1, source_target_pairs={{0,1},{1,2},{2,3},{3,0},{4,5},{5,6},{6,7},{7,4},{8,9},{9,10},{10,1... | collective-permute-start | bytes 786440 | tf_op jit(solution)/shard_map/ppermute | solution.py:275
  46.5 6.9 %collective-permute-done.10 = bf16[64,2048]{1,0:T(8,128)(2,1)S(1)} collective-permute-done((bf16[64,2048]{1,0:T(8,128)(2,1)S(1)}, bf16[64,2048]{1,0:T(8,128)(2,1)S(1)}, u32[]{:S(2)}, u32[]{:S(2)}) %collective-permute-start.10) | collective-permute-done | bytes 262176 | tf_op jit(solution)/shard_map/ppermute | solution.py:275
  53.8 3.8 %collective-permute-start.14 = (bf16[64,2048]{1,0:T(8,128)(2,1)S(1)}, bf16[64,2048]{1,0:T(8,128)(2,1)S(1)}, u32[]{:S(2)}, u32[]{:S(2)}) collective-permute-start(bf16[64,2048]{1,0:T(8,128)(2,1)S(1)} %pad_maximum_fusion), channel_id=1, source_target_pairs={{0,3},{1,0},{2,1},{3,2},{4,7},{5,4},{6,5},{7,6},{8,11},{9,8},{10,9... | collective-permute-start | bytes 786440 | tf_op jit(solution)/shard_map/ppermute | solution.py:275
  57.8 1.4 %collective-permute-done.9 = bf16[64,2048]{1,0:T(8,128)(2,1)S(1)} collective-permute-done((bf16[64,2048]{1,0:T(8,128)(2,1)S(1)}, bf16[64,2048]{1,0:T(8,128)(2,1)S(1)}, u32[]{:S(2)}, u32[]{:S(2)}) %collective-permute-start.9) | collective-permute-done | bytes 262176 | tf_op jit(solution)/shard_map/ppermute | solution.py:275
  59.6 3.8 %collective-permute-start.16 = (bf16[64,2048]{1,0:T(8,128)(2,1)S(1)}, bf16[64,2048]{1,0:T(8,128)(2,1)S(1)}, u32[]{:S(2)}, u32[]{:S(2)}) collective-permute-start(bf16[64,2048]{1,0:T(8,128)(2,1)S(1)} %pad_maximum_fusion.1), channel_id=1, source_target_pairs={{0,3},{1,0},{2,1},{3,2},{4,7},{5,4},{6,5},{7,6},{8,11},{9,8},{10,9... | collective-permute-start | bytes 786440 | tf_op jit(solution)/shard_map/ppermute | solution.py:275
  64.8 4.0 %collective-permute-start.15 = (bf16[64,2048]{1,0:T(8,128)(2,1)S(1)}, bf16[64,2048]{1,0:T(8,128)(2,1)S(1)}, u32[]{:S(2)}, u32[]{:S(2)}) collective-permute-start(bf16[64,2048]{1,0:T(8,128)(2,1)S(1)} %collective-permute-done.13), channel_id=1, source_target_pairs={{0,1},{1,2},{2,3},{3,0},{4,5},{5,6},{6,7},{7,4},{8,9},{9,10},{10,1... | collective-permute-start | bytes 786440 | tf_op jit(solution)/shard_map/ppermute | solution.py:275
  68.8 1.8 %collective-permute-done.14 = bf16[64,2048]{1,0:T(8,128)(2,1)S(1)} collective-permute-done((bf16[64,2048]{1,0:T(8,128)(2,1)S(1)}, bf16[64,2048]{1,0:T(8,128)(2,1)S(1)}, u32[]{:S(2)}, u32[]{:S(2)}) %collective-permute-start.14) | collective-permute-done | bytes 262176 | tf_op jit(solution)/shard_map/ppermute | solution.py:275
  70.7 5.4 %collective-permute-done.17 = bf16[64,2048]{1,0:T(8,128)(2,1)S(1)} collective-permute-done((bf16[64,2048]{1,0:T(8,128)(2,1)S(1)}, bf16[64,2048]{1,0:T(8,128)(2,1)S(1)}, u32[]{:S(2)}, u32[]{:S(2)}) %collective-permute-start.17) | collective-permute-done | bytes 262176 | tf_op jit(solution)/shard_map/ppermute | solution.py:275
  76.1 3.9 %collective-permute-start.18 = (bf16[64,2048]{1,0:T(8,128)(2,1)S(1)}, bf16[64,2048]{1,0:T(8,128)(2,1)S(1)}, u32[]{:S(2)}, u32[]{:S(2)}) collective-permute-start(bf16[64,2048]{1,0:T(8,128)(2,1)S(1)} %collective-permute-done.17), channel_id=1, source_target_pairs={{0,1},{1,2},{2,3},{3,0},{4,5},{5,6},{6,7},{7,4},{8,9},{9,10},{10,1... | collective-permute-start | bytes 786440 | tf_op jit(solution)/shard_map/ppermute | solution.py:275
  80.0 1.5 %collective-permute-done.16 = bf16[64,2048]{1,0:T(8,128)(2,1)S(1)} collective-permute-done((bf16[64,2048]{1,0:T(8,128)(2,1)S(1)}, bf16[64,2048]{1,0:T(8,128)(2,1)S(1)}, u32[]{:S(2)}, u32[]{:S(2)}) %collective-permute-start.16) | collective-permute-done | bytes 262176 | tf_op jit(solution)/shard_map/ppermute | solution.py:275
  81.6 5.8 %collective-permute-done.15 = bf16[64,2048]{1,0:T(8,128)(2,1)S(1)} collective-permute-done((bf16[64,2048]{1,0:T(8,128)(2,1)S(1)}, bf16[64,2048]{1,0:T(8,128)(2,1)S(1)}, u32[]{:S(2)}, u32[]{:S(2)}) %collective-permute-start.15) | collective-permute-done | bytes 262176 | tf_op jit(solution)/shard_map/ppermute | solution.py:275
  87.4 2.1 %convolution_convert_fusion.1 = bf16[256,1792]{1,0:T(8,128)(2,1)S(1)} fusion(bf16[256,2048]{1,0:T(8,128)(2,1)S(1)} %bitcast.61, bf16[1792,2048]{1,0:T(8,128)(2,1)S(1)} %scale_weights.1.refs_4_), kind=kOutput, calls=%fused_computation.1 | convolution fusion | flops 1879506944 | bytes 9306112 | tf_op jit(solution)/shard_map/dot_general | solution.py:355
  89.6 2.8 %collective-permute-done.18 = bf16[64,2048]{1,0:T(8,128)(2,1)S(1)} collective-permute-done((bf16[64,2048]{1,0:T(8,128)(2,1)S(1)}, bf16[64,2048]{1,0:T(8,128)(2,1)S(1)}, u32[]{:S(2)}, u32[]{:S(2)}) %collective-permute-start.18) | collective-permute-done | bytes 262176 | tf_op jit(solution)/shard_map/ppermute | solution.py:275
  92.5 2.1 %convolution_convert_fusion = bf16[256,1792]{1,0:T(8,128)(2,1)S(1)} fusion(bf16[256,2048]{1,0:T(8,128)(2,1)S(1)} %bitcast.59, bf16[1792,2048]{1,0:T(8,128)(2,1)S(1)} %scale_weights.1.refs_4_), kind=kOutput, calls=%fused_computation | convolution fusion | flops 1879506944 | bytes 9306112 | tf_op jit(solution)/shard_map/dot_general | solution.py:355
  94.8 1.6 %collective-permute-start.20 = (bf16[64,1792]{1,0:T(8,128)(2,1)S(1)}, bf16[64,1792]{1,0:T(8,128)(2,1)S(1)}, u32[]{:S(2)}, u32[]{:S(2)}) collective-permute-start(bf16[64,1792]{1,0:T(8,128)(2,1)S(1)} %get-tuple-element.50), channel_id=1, source_target_pairs={{0,24},{4,28},{8,16},{12,20},{16,8},{20,12},{24,0},{28,4},{1,25},{... | collective-permute-start | bytes 688136 | tf_op jit(solution)/shard_map/ppermute | solution.py:13
  96.4 1.4 %collective-permute-start.21 = (bf16[64,1792]{1,0:T(8,128)(2,1)S(1)}, bf16[64,1792]{1,0:T(8,128)(2,1)S(1)}, u32[]{:S(2)}, u32[]{:S(2)}) collective-permute-start(bf16[64,1792]{1,0:T(8,128)(2,1)S(1)} %get-tuple-element.53), channel_id=1, source_target_pairs={{0,16},{4,20},{8,24},{12,28},{16,0},{20,4},{24,8},{28,12},{1,17},{... | collective-permute-start | bytes 688136 | tf_op jit(solution)/shard_map/ppermute | solution.py:13
  98.4 6.6 %weight_grads.1 = (bf16[1,1792,1024]{2,1,0:T(8,128)(2,1)}, bf16[1,1792,1024]{2,1,0:T(8,128)(2,1)}) custom-call(bf16[64,1792]{1,0:T(8,128)(2,1)S(1)} %collective-permute-done.6.refs_3_.refs_0_, bf16[64,1792]{1,0:T(8,128)(2,1)S(1)} %collective-permute-done.4.refs_2_.refs_1_, bf16[64,1792]{1,0:T(8,128)(2,1)S(1)} %collective-permute-done.2.refs_1_.refs_2_, ...), custom_call_target="tpu_custom_call" | custom-call | flops 3758096384 | bytes 11272192 | tf_op jit(solution)/shard_map/weight_grads/pallas_call | solution.py:231
  104.9 3.0 %collective-permute-done.21 = bf16[64,1792]{1,0:T(8,128)(2,1)S(1)} collective-permute-done((bf16[64,1792]{1,0:T(8,128)(2,1)S(1)}, bf16[64,1792]{1,0:T(8,128)(2,1)S(1)}, u32[]{:S(2)}, u32[]{:S(2)}) %collective-permute-start.21) | collective-permute-done | bytes 229408 | tf_op jit(solution)/shard_map/ppermute | solution.py:13
  108.3 1.1 convolution_convert_fusion.2
  (52 shorter events, 7.6 us)
Async XLA Ops:
  2.4 9.4 %collective-permute-start = (bf16[64,1792]{1,0:T(8,128)(2,1)S(1)}, bf16[64,1792]{1,0:T(8,128)(2,1)S(1)}, u32[]{:S(2)}, u32[]{:S(2)}) collective-permute-start(bf16[64,1792]{1,0:T(8,128)(2,1)S(1)} %get-tuple-element.27), channel_id=1, source_target_pairs={{0,28},{4,24},{8,20},{12,16},{16,12},{20,8},{24,4},{28,0},{1,29},{... | collective-permute-start | bytes 688136 | tf_op jit(solution)/shard_map/ppermute | solution.py:13
  5.7 11.0 %collective-permute-start.2 = (bf16[64,1792]{1,0:T(8,128)(2,1)S(1)}, bf16[64,1792]{1,0:T(8,128)(2,1)S(1)}, u32[]{:S(2)}, u32[]{:S(2)}) collective-permute-start(bf16[64,1792]{1,0:T(8,128)(2,1)S(1)} %get-tuple-element.28), channel_id=1, source_target_pairs={{0,20},{4,16},{8,28},{12,24},{16,4},{20,0},{24,12},{28,8},{1,21},{... | collective-permute-start | bytes 688136 | tf_op jit(solution)/shard_map/ppermute | solution.py:13
  6.5 11.1 %collective-permute-start.4 = (bf16[64,1792]{1,0:T(8,128)(2,1)S(1)}, bf16[64,1792]{1,0:T(8,128)(2,1)S(1)}, u32[]{:S(2)}, u32[]{:S(2)}) collective-permute-start(bf16[64,1792]{1,0:T(8,128)(2,1)S(1)} %get-tuple-element.29), channel_id=1, source_target_pairs={{0,12},{4,8},{8,4},{12,0},{16,28},{20,24},{24,20},{28,16},{1,13},{... | collective-permute-start | bytes 688136 | tf_op jit(solution)/shard_map/ppermute | solution.py:13
  6.5 11.2 %collective-permute-start.6 = (bf16[64,1792]{1,0:T(8,128)(2,1)S(1)}, bf16[64,1792]{1,0:T(8,128)(2,1)S(1)}, u32[]{:S(2)}, u32[]{:S(2)}) collective-permute-start(bf16[64,1792]{1,0:T(8,128)(2,1)S(1)} %get-tuple-element.30.refs_3_.refs_4_), channel_id=1, source_target_pairs={{0,4},{4,0},{8,12},{12,8},{16,20},{20,16},{24,28},{28,24},{1,5},{5... | collective-permute-start | bytes 688136 | tf_op jit(solution)/shard_map/ppermute | solution.py:13
  6.5 0.7 copy-start
  7.2 0.7 copy-start.1
  11.7 12.1 %collective-permute-start.1 = (bf16[64,1792]{1,0:T(8,128)(2,1)S(1)}, bf16[64,1792]{1,0:T(8,128)(2,1)S(1)}, u32[]{:S(2)}, u32[]{:S(2)}) collective-permute-start(bf16[64,1792]{1,0:T(8,128)(2,1)S(1)} %collective-permute-done.refs_0_.refs_3_), channel_id=1, source_target_pairs={{0,4},{4,0},{8,12},{12,8},{16,20},{20,16},{24,28},{28,24},{1,5},{5... | collective-permute-start | bytes 688136 | tf_op jit(solution)/shard_map/ppermute | solution.py:13
  16.7 7.2 %collective-permute-start.3 = (bf16[64,1792]{1,0:T(8,128)(2,1)S(1)}, bf16[64,1792]{1,0:T(8,128)(2,1)S(1)}, u32[]{:S(2)}, u32[]{:S(2)}) collective-permute-start(bf16[64,1792]{1,0:T(8,128)(2,1)S(1)} %collective-permute-done.2.refs_1_.refs_2_), channel_id=1, source_target_pairs={{0,4},{4,0},{8,12},{12,8},{16,20},{20,16},{24,28},{28,24},{1,5},{5... | collective-permute-start | bytes 688136 | tf_op jit(solution)/shard_map/ppermute | solution.py:13
  17.6 6.3 %collective-permute-start.5 = (bf16[64,1792]{1,0:T(8,128)(2,1)S(1)}, bf16[64,1792]{1,0:T(8,128)(2,1)S(1)}, u32[]{:S(2)}, u32[]{:S(2)}) collective-permute-start(bf16[64,1792]{1,0:T(8,128)(2,1)S(1)} %collective-permute-done.4.refs_2_.refs_1_), channel_id=1, source_target_pairs={{0,4},{4,0},{8,12},{12,8},{16,20},{20,16},{24,28},{28,24},{1,5},{5... | collective-permute-start | bytes 688136 | tf_op jit(solution)/shard_map/ppermute | solution.py:13
  19.9 11.0 %collective-permute-start.8 = (bf16[64,2048]{1,0:T(8,128)(2,1)S(1)}, bf16[64,2048]{1,0:T(8,128)(2,1)S(1)}, u32[]{:S(2)}, u32[]{:S(2)}) collective-permute-start(bf16[64,2048]{1,0:T(8,128)(2,1)S(1)} %get-tuple-element.56), channel_id=1, source_target_pairs={{0,1},{1,2},{2,3},{3,0},{4,5},{5,6},{6,7},{7,4},{8,9},{9,10},{10,1... | collective-permute-start | bytes 786440 | tf_op jit(solution)/shard_map/ppermute | solution.py:275
  21.8 24.8 %collective-permute-start.11 = (bf16[64,2048]{1,0:T(8,128)(2,1)S(1)}, bf16[64,2048]{1,0:T(8,128)(2,1)S(1)}, u32[]{:S(2)}, u32[]{:S(2)}) collective-permute-start(bf16[64,2048]{1,0:T(8,128)(2,1)S(1)} %get-tuple-element.31), channel_id=1, source_target_pairs={{0,3},{1,0},{2,1},{3,2},{4,7},{5,4},{6,5},{7,6},{8,11},{9,8},{10,9... | collective-permute-start | bytes 786440 | tf_op jit(solution)/shard_map/ppermute | solution.py:275
  25.9 27.6 %copy-start.2 = (bf16[1,128,1024]{2,1,0:T(8,128)(2,1)S(1)}, bf16[1,128,1024]{2,1,0:T(8,128)(2,1)}, u32[]{:S(2)}) copy-start(bf16[1,128,1024]{2,1,0:T(8,128)(2,1)} %param.13) | copy-start | bytes 786436
  26.0 16.2 %collective-permute-start.7 = (bf16[64,2048]{1,0:T(8,128)(2,1)S(1)}, bf16[64,2048]{1,0:T(8,128)(2,1)S(1)}, u32[]{:S(2)}, u32[]{:S(2)}) collective-permute-start(bf16[64,2048]{1,0:T(8,128)(2,1)S(1)} %get-tuple-element.32), channel_id=1, source_target_pairs={{0,1},{1,2},{2,3},{3,0},{4,5},{5,6},{6,7},{7,4},{8,9},{9,10},{10,1... | collective-permute-start | bytes 786440 | tf_op jit(solution)/shard_map/ppermute | solution.py:275
  26.1 31.5 %collective-permute-start.12 = (bf16[64,2048]{1,0:T(8,128)(2,1)S(1)}, bf16[64,2048]{1,0:T(8,128)(2,1)S(1)}, u32[]{:S(2)}, u32[]{:S(2)}) collective-permute-start(bf16[64,2048]{1,0:T(8,128)(2,1)S(1)} %get-tuple-element.33), channel_id=1, source_target_pairs={{0,3},{1,0},{2,1},{3,2},{4,7},{5,4},{6,5},{7,6},{8,11},{9,8},{10,9... | collective-permute-start | bytes 786440 | tf_op jit(solution)/shard_map/ppermute | solution.py:275
  31.0 22.4 %collective-permute-start.10 = (bf16[64,2048]{1,0:T(8,128)(2,1)S(1)}, bf16[64,2048]{1,0:T(8,128)(2,1)S(1)}, u32[]{:S(2)}, u32[]{:S(2)}) collective-permute-start(bf16[64,2048]{1,0:T(8,128)(2,1)S(1)} %fusion.8), channel_id=1, source_target_pairs={{0,1},{1,2},{2,3},{3,0},{4,5},{5,6},{6,7},{7,4},{8,9},{9,10},{10,1... | collective-permute-start | bytes 786440 | tf_op jit(solution)/shard_map/ppermute | solution.py:275
  42.3 16.9 %collective-permute-start.9 = (bf16[64,2048]{1,0:T(8,128)(2,1)S(1)}, bf16[64,2048]{1,0:T(8,128)(2,1)S(1)}, u32[]{:S(2)}, u32[]{:S(2)}) collective-permute-start(bf16[64,2048]{1,0:T(8,128)(2,1)S(1)} %fusion.9), channel_id=1, source_target_pairs={{0,1},{1,2},{2,3},{3,0},{4,5},{5,6},{6,7},{7,4},{8,9},{9,10},{10,1... | collective-permute-start | bytes 786440 | tf_op jit(solution)/shard_map/ppermute | solution.py:275
  53.7 11.1 %collective-permute-start.13 = (bf16[64,2048]{1,0:T(8,128)(2,1)S(1)}, bf16[64,2048]{1,0:T(8,128)(2,1)S(1)}, u32[]{:S(2)}, u32[]{:S(2)}) collective-permute-start(bf16[64,2048]{1,0:T(8,128)(2,1)S(1)} %pad_maximum_fusion), channel_id=1, source_target_pairs={{0,1},{1,2},{2,3},{3,0},{4,5},{5,6},{6,7},{7,4},{8,9},{9,10},{10,1... | collective-permute-start | bytes 786440 | tf_op jit(solution)/shard_map/ppermute | solution.py:275
  53.8 16.8 %collective-permute-start.14 = (bf16[64,2048]{1,0:T(8,128)(2,1)S(1)}, bf16[64,2048]{1,0:T(8,128)(2,1)S(1)}, u32[]{:S(2)}, u32[]{:S(2)}) collective-permute-start(bf16[64,2048]{1,0:T(8,128)(2,1)S(1)} %pad_maximum_fusion), channel_id=1, source_target_pairs={{0,3},{1,0},{2,1},{3,2},{4,7},{5,4},{6,5},{7,6},{8,11},{9,8},{10,9... | collective-permute-start | bytes 786440 | tf_op jit(solution)/shard_map/ppermute | solution.py:275
  59.5 16.6 %collective-permute-start.17 = (bf16[64,2048]{1,0:T(8,128)(2,1)S(1)}, bf16[64,2048]{1,0:T(8,128)(2,1)S(1)}, u32[]{:S(2)}, u32[]{:S(2)}) collective-permute-start(bf16[64,2048]{1,0:T(8,128)(2,1)S(1)} %pad_maximum_fusion.1), channel_id=1, source_target_pairs={{0,1},{1,2},{2,3},{3,0},{4,5},{5,6},{6,7},{7,4},{8,9},{9,10},{10,1... | collective-permute-start | bytes 786440 | tf_op jit(solution)/shard_map/ppermute | solution.py:275
  59.6 22.0 %collective-permute-start.16 = (bf16[64,2048]{1,0:T(8,128)(2,1)S(1)}, bf16[64,2048]{1,0:T(8,128)(2,1)S(1)}, u32[]{:S(2)}, u32[]{:S(2)}) collective-permute-start(bf16[64,2048]{1,0:T(8,128)(2,1)S(1)} %pad_maximum_fusion.1), channel_id=1, source_target_pairs={{0,3},{1,0},{2,1},{3,2},{4,7},{5,4},{6,5},{7,6},{8,11},{9,8},{10,9... | collective-permute-start | bytes 786440 | tf_op jit(solution)/shard_map/ppermute | solution.py:275
  64.8 22.5 %collective-permute-start.15 = (bf16[64,2048]{1,0:T(8,128)(2,1)S(1)}, bf16[64,2048]{1,0:T(8,128)(2,1)S(1)}, u32[]{:S(2)}, u32[]{:S(2)}) collective-permute-start(bf16[64,2048]{1,0:T(8,128)(2,1)S(1)} %collective-permute-done.13), channel_id=1, source_target_pairs={{0,1},{1,2},{2,3},{3,0},{4,5},{5,6},{6,7},{7,4},{8,9},{9,10},{10,1... | collective-permute-start | bytes 786440 | tf_op jit(solution)/shard_map/ppermute | solution.py:275
  76.1 16.3 %collective-permute-start.18 = (bf16[64,2048]{1,0:T(8,128)(2,1)S(1)}, bf16[64,2048]{1,0:T(8,128)(2,1)S(1)}, u32[]{:S(2)}, u32[]{:S(2)}) collective-permute-start(bf16[64,2048]{1,0:T(8,128)(2,1)S(1)} %collective-permute-done.17), channel_id=1, source_target_pairs={{0,1},{1,2},{2,3},{3,0},{4,5},{5,6},{6,7},{7,4},{8,9},{9,10},{10,1... | collective-permute-start | bytes 786440 | tf_op jit(solution)/shard_map/ppermute | solution.py:275
  89.5 3.0 %collective-permute-start.19 = (bf16[256,1792]{1,0:T(8,128)(2,1)S(1)}, bf16[256,1792]{1,0:T(8,128)(2,1)S(1)}, u32[]{:S(2)}, u32[]{:S(2)}) collective-permute-start(bf16[256,1792]{1,0:T(8,128)(2,1)S(1)} %convolution_convert_fusion.1), channel_id=1, source_target_pairs={{0,4},{4,0},{8,12},{12,8},{16,20},{20,16},{24,28},{28,24},{1,5},{5... | collective-permute-start | bytes 2752520 | tf_op jit(solution)/shard_map/ppermute | solution.py:13
  94.8 10.1 %collective-permute-start.20 = (bf16[64,1792]{1,0:T(8,128)(2,1)S(1)}, bf16[64,1792]{1,0:T(8,128)(2,1)S(1)}, u32[]{:S(2)}, u32[]{:S(2)}) collective-permute-start(bf16[64,1792]{1,0:T(8,128)(2,1)S(1)} %get-tuple-element.50), channel_id=1, source_target_pairs={{0,24},{4,28},{8,16},{12,20},{16,8},{20,12},{24,0},{28,4},{1,25},{... | collective-permute-start | bytes 688136 | tf_op jit(solution)/shard_map/ppermute | solution.py:13
  96.4 11.5 %collective-permute-start.21 = (bf16[64,1792]{1,0:T(8,128)(2,1)S(1)}, bf16[64,1792]{1,0:T(8,128)(2,1)S(1)}, u32[]{:S(2)}, u32[]{:S(2)}) collective-permute-start(bf16[64,1792]{1,0:T(8,128)(2,1)S(1)} %get-tuple-element.53), channel_id=1, source_target_pairs={{0,16},{4,20},{8,24},{12,28},{16,0},{20,4},{24,8},{28,12},{1,17},{... | collective-permute-start | bytes 688136 | tf_op jit(solution)/shard_map/ppermute | solution.py:13
  97.8 10.4 %copy-start.3 = (bf16[256,128]{1,0:T(8,128)(2,1)S(1)}, bf16[256,128]{1,0:T(8,128)(2,1)}, u32[]{:S(2)}) copy-start(bf16[256,128]{1,0:T(8,128)(2,1)} %get-tuple-element.48) | copy-start | bytes 196612
  97.8 10.4 %collective-permute-start.22 = (bf16[64,1792]{1,0:T(8,128)(2,1)S(1)}, bf16[64,1792]{1,0:T(8,128)(2,1)S(1)}, u32[]{:S(2)}, u32[]{:S(2)}) collective-permute-start(bf16[64,1792]{1,0:T(8,128)(2,1)S(1)} %get-tuple-element.52), channel_id=1, source_target_pairs={{0,8},{4,12},{8,0},{12,4},{16,24},{20,28},{24,16},{28,20},{1,9},{5... | collective-permute-start | bytes 688136 | tf_op jit(solution)/shard_map/ppermute | solution.py:13
